TPU v7x, 32 devices: a whole 2x2x4 slice. The times are simulated.
32 devices in a mesh: dp: 16 (over z, y, x), fsdp: 2 (over core).
Axes of the slice: x: 2, y: 2, z: 4, core: 2. Of those that a mesh axis runs over, the one named last changes fastest.
Arguments:
- features: bfloat16 [32, 576, 1024], P(('dp', 'fsdp')), may hold values from -6 to 6
- grid_live: int32 [32], P(('dp', 'fsdp')), may hold values 0 or 1
- pos_embed: bfloat16 [576, 1024], P(None, ('dp', 'fsdp')), may hold values from -3 to 3
- w_in: bfloat16 [2, 1024, 1024], P(None, ('dp', 'fsdp')), may hold values from -0.1875 to 0.1875
- w_mid: bfloat16 [2, 9216, 1024], P(None, ('dp', 'fsdp')), may hold values from -0.0625 to 0.0625
- w_out: bfloat16 [2, 1024, 1024], P(None, ('dp', 'fsdp')), may hold values from -0.1875 to 0.1875
- norm_gain: bfloat16 [2, 3, 1024], P(None, None, ('dp', 'fsdp')), may hold values from 0.099609375 to 1.8984375
- norm_bias: bfloat16 [2, 3, 1024], P(None, None, ('dp', 'fsdp')), may hold values from -1.5 to 1.5
- readout_w: bfloat16 [1024, 4096], P(('dp', 'fsdp')), may hold values from -0.1875 to 0.1875
- readout_b: bfloat16 [4096], P(('dp', 'fsdp')), may hold values from -1.5 to 1.5
- cotangent: bfloat16 [32, 144, 4096], P(('dp', 'fsdp')), may hold values from -6 to 6
Outputs:
- output: bfloat16 [32, 144, 4096], P(('dp', 'fsdp'))
- input_grad: float32 [32, 576, 1024], P(('dp', 'fsdp'))
- pos_grad: float32 [576, 1024], P(None, ('dp', 'fsdp'))
- w_in_grad: float32 [2, 1024, 1024], P(None, ('dp', 'fsdp'))
- w_mid_grad: float32 [2, 9216, 1024], P(None, ('dp', 'fsdp'))
- w_out_grad: float32 [2, 1024, 1024], P(None, ('dp', 'fsdp'))
- gain_grad: float32 [2, 3, 1024], P(None, None, ('dp', 'fsdp'))
- bias_grad: float32 [2, 3, 1024], P(None, None, ('dp', 'fsdp'))
- readout_w_grad: float32 [1024, 4096], P(('dp', 'fsdp'))
- readout_b_grad: float32 [4096], P(('dp', 'fsdp'))
All inputs are finite; a program needn't handle non-finite values. No bound on the sum of `grid_live` on one device may be relied on, other than what follows from the above.
Results may differ from a plain program's by a relative error of at most 0.018.
Values may be sent and summed in bfloat16 or wider, within the bound.
No kernel may reach another device: no remote copies, remote signals or barrier semaphores. Data moves between devices by JAX's collectives and lax.ppermute only.
A program may use at most 448 MiB of HBM per device.

v0:
```python
import jax
import jax.numpy as jnp
from jax import lax
from jax.sharding import PartitionSpec as P

C = 1024
G = 24


def product(left, right):
    return jnp.dot(left, right, preferred_element_type=jnp.float32)


def times_transposed(left, right):
    return lax.dot_general(
        left, right, (((1,), (1,)), ((), ())), preferred_element_type=jnp.float32
    )


def outer_sum(left, right):
    return lax.dot_general(
        left, right, (((0,), (0,)), ((), ())), preferred_element_type=jnp.float32
    )


def layer_norm(hidden, gain_vec, bias_vec):
    center = hidden - jnp.mean(hidden, axis=-1, keepdims=True)
    spread = jnp.mean(center * center, axis=-1, keepdims=True)
    return center * lax.rsqrt(spread + 1e-05) * gain_vec + bias_vec


def norm_act(hidden, gain_vec, bias_vec):
    return jax.nn.silu(layer_norm(hidden, gain_vec, bias_vec))


def closing(stream, hidden, gain_vec, bias_vec):
    return jax.nn.silu(stream + layer_norm(hidden, gain_vec, bias_vec))


def columns(values, grid_side):
    channels = values.shape[-1]
    padded = jnp.pad(values.reshape(grid_side, grid_side, channels), ((1, 1), (1, 1), (0, 0)))
    pieces = [
        padded[row_tap : row_tap + grid_side, col_tap : col_tap + grid_side, :]
        for row_tap in range(3)
        for col_tap in range(3)
    ]
    return jnp.concatenate(pieces, axis=-1).reshape(grid_side * grid_side, 9 * channels)


def fold_taps(grad_taps, grid_side):
    channels = grad_taps.shape[-1] // 9
    padded = jnp.pad(
        grad_taps.reshape(grid_side, grid_side, 9, channels), ((1, 1), (1, 1), (0, 0), (0, 0))
    )
    summed = jnp.zeros((grid_side, grid_side, channels), jnp.float32)
    for row_tap in range(3):
        for col_tap in range(3):
            summed = (
                summed
                + padded[
                    2 - row_tap : 2 - row_tap + grid_side,
                    2 - col_tap : 2 - col_tap + grid_side,
                    3 * row_tap + col_tap,
                    :,
                ]
            )
    return summed.reshape(grid_side * grid_side, channels)


def block_forward(stream, weights, grid_side):
    w_first, w_middle, w_last, gain_rows, bias_rows = weights
    low_in = stream.astype(jnp.bfloat16)
    pre_first = product(low_in, w_first)
    act_first = norm_act(pre_first, gain_rows[0], bias_rows[0]).astype(jnp.bfloat16)
    taps_in = columns(act_first, grid_side)
    pre_middle = product(taps_in, w_middle)
    act_middle = norm_act(pre_middle, gain_rows[1], bias_rows[1]).astype(jnp.bfloat16)
    pre_last = product(act_middle, w_last)
    result = closing(stream, pre_last, gain_rows[2], bias_rows[2])
    return (result, (low_in, pre_first, taps_in, pre_middle, act_middle, pre_last))


def block_backward(grad_out, stream, kept, weights, grid_side):
    low_in, pre_first, taps_in, pre_middle, act_middle, pre_last = kept
    w_first, w_middle, w_last, gain_rows, bias_rows = weights
    unused, pullback = jax.vjp(closing, stream, pre_last, gain_rows[2], bias_rows[2])
    grad_stream, grad_last, gain_last, bias_last = pullback(grad_out)
    grad_last = grad_last.astype(jnp.bfloat16)
    grad_act = times_transposed(grad_last, w_last)
    wgrad_last = outer_sum(act_middle, grad_last)
    unused, pullback = jax.vjp(norm_act, pre_middle, gain_rows[1], bias_rows[1])
    grad_middle, gain_middle, bias_middle = pullback(grad_act)
    grad_middle = grad_middle.astype(jnp.bfloat16)
    grad_taps = times_transposed(grad_middle, w_middle)
    wgrad_middle = outer_sum(taps_in, grad_middle)
    unused, pullback = jax.vjp(norm_act, pre_first, gain_rows[0], bias_rows[0])
    grad_first, gain_first, bias_first = pullback(fold_taps(grad_taps, grid_side))
    grad_first = grad_first.astype(jnp.bfloat16)
    grad_stream = grad_stream + times_transposed(grad_first, w_first)
    wgrad_first = outer_sum(low_in, grad_first)
    gain_grads = jnp.stack([gain_first, gain_middle, gain_last], axis=1)
    bias_grads = jnp.stack([bias_first, bias_middle, bias_last], axis=1)
    return (grad_stream, (wgrad_first, wgrad_middle, wgrad_last, gain_grads, bias_grads))


def local(
    features,
    grid_live,
    pos_embed,
    w_in,
    w_mid,
    w_out,
    norm_gain,
    norm_bias,
    readout_w,
    readout_b,
    cotangent,
):
    first = (
        lax.all_gather(pos_embed, ("dp", "fsdp"), axis=1, tiled=True),
        lax.all_gather(w_in[0], ("dp", "fsdp"), axis=0, tiled=True),
        lax.all_gather(w_mid[0], ("dp", "fsdp"), axis=0, tiled=True),
        lax.all_gather(w_out[0], ("dp", "fsdp"), axis=0, tiled=True),
        lax.all_gather(norm_gain[0], ("dp", "fsdp"), axis=1, tiled=True),
        lax.all_gather(norm_bias[0], ("dp", "fsdp"), axis=1, tiled=True),
    )
    second = (
        lax.all_gather(w_in[1], ("dp", "fsdp"), axis=0, tiled=True),
        lax.all_gather(w_mid[1], ("dp", "fsdp"), axis=0, tiled=True),
        lax.all_gather(w_out[1], ("dp", "fsdp"), axis=0, tiled=True),
        lax.all_gather(norm_gain[1], ("dp", "fsdp"), axis=1, tiled=True),
        lax.all_gather(norm_bias[1], ("dp", "fsdp"), axis=1, tiled=True),
        lax.all_gather(readout_w, ("dp", "fsdp"), axis=0, tiled=True),
        lax.all_gather(readout_b, ("dp", "fsdp"), axis=0, tiled=True),
    )
    first_block = (
        first[1],
        first[2],
        first[3],
        first[4].astype(jnp.float32),
        first[5].astype(jnp.float32),
    )
    second_block = (
        second[0],
        second[1],
        second[2],
        second[3].astype(jnp.float32),
        second[4].astype(jnp.float32),
    )
    stream_in = features[0].astype(jnp.float32) + first[0].astype(jnp.float32)
    stream_mid, first_kept = block_forward(stream_in, first_block, G)
    half_side = G // 2
    pooled = jnp.mean(stream_mid.reshape(half_side, 2, half_side, 2, C), axis=(1, 3)).reshape(
        half_side * half_side, C
    )
    stream_out, second_kept = block_forward(pooled, second_block, half_side)
    low_out = stream_out.astype(jnp.bfloat16)
    live_value = grid_live[0].astype(jnp.float32)

    def readout_act(logits):
        return jax.nn.gelu(logits, approximate=False) * live_value

    logits = product(low_out, second[5]) + second[6].astype(jnp.float32)
    output = readout_act(logits).astype(jnp.bfloat16)
    unused, pullback = jax.vjp(readout_act, logits)
    grad_logits = pullback(cotangent[0].astype(jnp.float32))[0].astype(jnp.bfloat16)
    back_readout = second[5]
    grad_readout_w = outer_sum(low_out, grad_logits)
    grad_readout_b = jnp.sum(grad_logits.astype(jnp.float32), axis=0)
    grad_top = times_transposed(grad_logits, back_readout)
    grad_pooled, second_grads = block_backward(
        grad_top, pooled, second_kept, second_block, half_side
    )
    top_first, top_middle, top_last, top_gain, top_bias = second_grads
    grad_mid = jnp.broadcast_to(
        (grad_pooled * 0.25).reshape(half_side, 1, half_side, 1, C), (half_side, 2, half_side, 2, C)
    ).reshape(G * G, C)
    second_owned = (
        lax.psum_scatter(top_first, ("dp", "fsdp"), scatter_dimension=0, tiled=True),
        lax.psum_scatter(top_middle, ("dp", "fsdp"), scatter_dimension=0, tiled=True),
        lax.psum_scatter(top_last, ("dp", "fsdp"), scatter_dimension=0, tiled=True),
        lax.psum_scatter(top_gain, ("dp", "fsdp"), scatter_dimension=0, tiled=True),
        lax.psum_scatter(top_bias, ("dp", "fsdp"), scatter_dimension=0, tiled=True),
        lax.psum_scatter(grad_readout_w, ("dp", "fsdp"), scatter_dimension=0, tiled=True),
        lax.psum_scatter(grad_readout_b, ("dp", "fsdp"), scatter_dimension=0, tiled=True),
    )
    grad_in, first_grads = block_backward(grad_mid, stream_in, first_kept, first_block, G)
    low_first, low_middle, low_last, low_gain, low_bias = first_grads
    first_owned = (
        lax.psum_scatter(grad_in.T, ("dp", "fsdp"), scatter_dimension=0, tiled=True),
        lax.psum_scatter(low_first, ("dp", "fsdp"), scatter_dimension=0, tiled=True),
        lax.psum_scatter(low_middle, ("dp", "fsdp"), scatter_dimension=0, tiled=True),
        lax.psum_scatter(low_last, ("dp", "fsdp"), scatter_dimension=0, tiled=True),
        lax.psum_scatter(low_gain, ("dp", "fsdp"), scatter_dimension=0, tiled=True),
        lax.psum_scatter(low_bias, ("dp", "fsdp"), scatter_dimension=0, tiled=True),
    )
    return (
        output[None],
        grad_in[None],
        first_owned[0].T,
        jnp.stack([first_owned[1], second_owned[0]]),
        jnp.stack([first_owned[2], second_owned[1]]),
        jnp.stack([first_owned[3], second_owned[2]]),
        jnp.stack([first_owned[4].T, second_owned[3].T]),
        jnp.stack([first_owned[5].T, second_owned[4].T]),
        second_owned[5],
        second_owned[6],
    )


def solution(mesh):
    return jax.shard_map(
        local,
        mesh=mesh,
        in_specs=(
            P(("dp", "fsdp"), None, None),
            P(("dp", "fsdp")),
            P(None, ("dp", "fsdp")),
            P(None, ("dp", "fsdp"), None),
            P(None, ("dp", "fsdp"), None),
            P(None, ("dp", "fsdp"), None),
            P(None, None, ("dp", "fsdp")),
            P(None, None, ("dp", "fsdp")),
            P(("dp", "fsdp"), None),
            P(("dp", "fsdp")),
            P(("dp", "fsdp"), None, None),
        ),
        out_specs=(
            P(("dp", "fsdp"), None, None),
            P(("dp", "fsdp"), None, None),
            P(None, ("dp", "fsdp")),
            P(None, ("dp", "fsdp"), None),
            P(None, ("dp", "fsdp"), None),
            P(None, ("dp", "fsdp"), None),
            P(None, None, ("dp", "fsdp")),
            P(None, None, ("dp", "fsdp")),
            P(("dp", "fsdp"), None),
            P(("dp", "fsdp")),
        ),
        check_vma=False,
    )
```

profile of v0, /device:TPU:0, one launch (start us, length us, event | category | flops | bytes accessed | tf_op | source)
XLA Modules:
  0.0 2831.4 jit_solution(13852400920368302998)
XLA Ops:
  9.6 2.3 fusion.110
  15.8 43.1 %all-gather.10 = bf16[32,1,128]{2,1,0:T(2,128)(2,1)S(1)} all-gather(bf16[1,1,128]{2,1,0:T(2,128)(2,1)S(1)} %bitcast.191), channel_id=1, replica_groups=mesh['dp'=16,'fsdp'=2] {'dp','fsdp'}, dimensions={0}, use_global_device_ids=true | all-gather | bytes 8448 | tf_op jit(solution)/shard_map/all_gather | solution.py:135
  58.9 38.1 %all-gather.1 = bf16[1,3,1024]{1,0,2:T(2,128)(2,1)S(1)} all-gather(bf16[1,3,32]{1,0,2:T(2,128)(2,1)S(1)} %copy.62), channel_id=3, replica_groups=mesh['dp'=16,'fsdp'=2] {'dp','fsdp'}, dimensions={2}, use_global_device_ids=true | all-gather | bytes 6336 | tf_op jit(solution)/shard_map/all_gather | solution.py:125
  97.5 10.8 slice_reduce_fusion.9
  108.3 39.8 %all-gather.2 = bf16[1,3,1024]{1,0,2:T(2,128)(2,1)S(1)} all-gather(bf16[1,3,32]{1,0,2:T(2,128)(2,1)S(1)} %copy.63), channel_id=4, replica_groups=mesh['dp'=16,'fsdp'=2] {'dp','fsdp'}, dimensions={2}, use_global_device_ids=true | all-gather | bytes 6336 | tf_op jit(solution)/shard_map/all_gather | solution.py:126
  148.1 39.9 %all-gather.6 = bf16[1,3,1024]{1,0,2:T(2,128)(2,1)S(1)} all-gather(bf16[1,3,32]{1,0,2:T(2,128)(2,1)S(1)} %copy.64), channel_id=8, replica_groups=mesh['dp'=16,'fsdp'=2] {'dp','fsdp'}, dimensions={2}, use_global_device_ids=true | all-gather | bytes 6336 | tf_op jit(solution)/shard_map/all_gather | solution.py:132
  190.4 42.5 %all-gather.7 = bf16[1,3,1024]{1,0,2:T(2,128)(2,1)S(1)} all-gather(bf16[1,3,32]{1,0,2:T(2,128)(2,1)S(1)} %copy.65), channel_id=9, replica_groups=mesh['dp'=16,'fsdp'=2] {'dp','fsdp'}, dimensions={2}, use_global_device_ids=true | all-gather | bytes 6336 | tf_op jit(solution)/shard_map/all_gather | solution.py:133
  233.5 10.7 slice_reduce_fusion.8
  244.3 10.3 slice_reduce_fusion.3
  254.6 10.6 slice_reduce_fusion.2
  266.8 3.5 fusion.115
  271.6 3.2 pad_slice_fusion.16
  286.0 17.0 fusion.116
  306.0 14.5 all-gather.28.cloned.1.call-done
  320.4 4.0 fusion.117
  326.1 2.5 fusion.35
  328.7 3.9 reshape.294
  332.6 3.4 reduce_sum.343
  338.1 40.8 %all-gather.30.cloned.1.call-done = bf16[1,1024,1024]{2,1,0:T(8,128)(2,1)} async-done(((bf16[1,32,1024]{2,1,0:T(8,128)(2,1)}), bf16[1,1024,1024]{2,1,0:T(8,128)(2,1)}) %all-gather.30.cloned.1.call-update) | async-done | bytes 2097168 | tf_op jit(solution)/shard_map/all_gather | solution.py:129
  379.0 2.2 fusion.118
  386.0 4.7 pad_slice_fusion.24
  415.9 89.4 %all-gather.32.cloned.1.call-done = bf16[1,9216,1024]{2,1,0:T(8,128)(2,1)} async-done(((bf16[1,288,1024]{2,1,0:T(8,128)(2,1)}), bf16[1,9216,1024]{2,1,0:T(8,128)(2,1)}) %all-gather.32.cloned.1.call-update) | async-done | bytes 18874384 | tf_op jit(solution)/shard_map/all_gather | solution.py:130
  505.3 8.8 fusion.119
  516.3 47.0 %all-gather.34.cloned.1.call-done = bf16[1,1024,1024]{2,1,0:T(8,128)(2,1)} async-done(((bf16[1,32,1024]{2,1,0:T(8,128)(2,1)}), bf16[1,1024,1024]{2,1,0:T(8,128)(2,1)}) %all-gather.34.cloned.1.call-update) | async-done | bytes 2097168 | tf_op jit(solution)/shard_map/all_gather | solution.py:131
  563.3 2.5 fusion.120
  567.9 74.5 %all-gather.22.cloned.1.call-done = bf16[1024,4096]{1,0:T(8,128)(2,1)} async-done(((bf16[32,4096]{1,0:T(8,128)(2,1)}), bf16[1024,4096]{1,0:T(8,128)(2,1)}) %all-gather.22.cloned.1.call-update) | async-done | bytes 8388624 | tf_op jit(solution)/shard_map/all_gather | solution.py:134
  642.5 12.6 convert_reduce_fusion
  655.3 3.7 multiply_reduce_fusion.9
  661.4 15.3 fusion
  676.7 7.3 reshape.296
  684.1 17.0 fusion.81
  701.0 2.1 reshape.306
  703.1 2.4 multiply_reduce_fusion.11
  712.0 2.4 broadcast_in_dim.40
  714.4 4.3 reshape.297
  718.8 4.7 multiply_reduce_fusion
  727.5 3.3 multiply_reduce_fusion.1
  731.6 20.0 fusion.4
  751.6 26.2 reshape.298
  777.8 52.5 %fusion.14 = f32[24,24,1,1024]{3,2,1,0:T(1,128)} fusion(f32[24,24,9,1024]{3,2,1,0:T(8,128)} %reshape.298), kind=kLoop, calls=%fused_computation.38 | loop fusion | flops 4718592 | bytes 42467328 | tf_op jit(solution)/shard_map/add | solution.py:60
  830.4 2.4 copy.61
  844.3 4.1 fusion.94
  848.5 6.6 fusion.96
  855.8 4.0 fusion.85
  861.2 2.5 fusion.101
  865.1 4.0 fusion.82
  870.8 24.0 fusion.97
  895.9 16.7 fusion.95
  914.3 5.2 fusion.53
  919.4 3.2 copy.49
  924.3 8.2 fusion.98
  933.2 39.5 %all-reduce.4 = f32[4096]{0:T(1024)S(1)} all-reduce(f32[4096]{0:T(1024)S(1)} %copy-done.81), channel_id=24, replica_groups=mesh['dp'=16,'fsdp'=2] {'dp','fsdp'}, use_global_device_ids=true, to_apply=%region_50.51.clone | all-reduce | flops 4096 | bytes 32768
  973.3 3.0 fusion.64
  978.5 130.3 %reduce-scatter.41.cloned.1.call-done = f32[32,3]{1,0:T(8,128)} async-done(((f32[1024,3]{1,0:T(8,128)}), f32[32,3]{1,0:T(8,128)}) %reduce-scatter.41.cloned.1.call-update) | async-done | bytes 400
  1109.6 131.4 %reduce-scatter.39.cloned.1.call-done = f32[32,3]{1,0:T(8,128)} async-done(((f32[1024,3]{1,0:T(8,128)}), f32[32,3]{1,0:T(8,128)}) %reduce-scatter.39.cloned.1.call-update) | async-done | bytes 400
  1242.4 137.7 %reduce-scatter.33.cloned.1.call-done = f32[32,1024]{1,0:T(8,128)} async-done(((f32[1024,1024]{1,0:T(8,128)}), f32[32,1024]{1,0:T(8,128)}) %reduce-scatter.33.cloned.1.call-update) | async-done | bytes 131088 | tf_op jit(solution)/shard_map/reduce_scatter | solution.py:182
  1380.1 139.0 %reduce-scatter.31.cloned.1.call-done = f32[32,1024]{1,0:T(8,128)} async-done(((f32[1024,1024]{1,0:T(8,128)}), f32[32,1024]{1,0:T(8,128)}) %reduce-scatter.31.cloned.1.call-update) | async-done | bytes 131088 | tf_op jit(solution)/shard_map/reduce_scatter | solution.py:194
  1520.8 137.3 %reduce-scatter.25.cloned.1.call-done = f32[32,1024]{1,0:T(8,128)} async-done(((f32[1024,1024]{1,0:T(8,128)}), f32[32,1024]{1,0:T(8,128)}) %reduce-scatter.25.cloned.1.call-update) | async-done | bytes 131088 | tf_op jit(solution)/shard_map/reduce_scatter | solution.py:180
  1658.1 138.9 %reduce-scatter.23.cloned.1.call-done = f32[32,1024]{1,0:T(8,128)} async-done(((f32[1024,1024]{1,0:T(8,128)}), f32[32,1024]{1,0:T(8,128)}) %reduce-scatter.23.cloned.1.call-update) | async-done | bytes 131088 | tf_op jit(solution)/shard_map/reduce_scatter | solution.py:192
  1798.6 349.0 %reduce-scatter.27.cloned.1.call-done = f32[288,1024]{1,0:T(8,128)} async-done(((f32[9216,1024]{1,0:T(8,128)}), f32[288,1024]{1,0:T(8,128)}) %reduce-scatter.27.cloned.1.call-update) | async-done | bytes 1179664 | tf_op jit(solution)/shard_map/reduce_scatter | solution.py:193
  2147.6 355.4 %reduce-scatter.29.cloned.1.call-done = f32[288,1024]{1,0:T(8,128)} async-done(((f32[9216,1024]{1,0:T(8,128)}), f32[288,1024]{1,0:T(8,128)}) %reduce-scatter.29.cloned.1.call-update) | async-done | bytes 1179664 | tf_op jit(solution)/shard_map/reduce_scatter | solution.py:181
  2502.9 3.3 pad_maximum_fusion
  2506.3 136.6 %reduce-scatter.37.cloned.1.call-done = f32[32,576]{1,0:T(8,128)} async-done(((f32[1024,576]{1,0:T(8,128)}), f32[32,576]{1,0:T(8,128)}) %reduce-scatter.37.cloned.1.call-update) | async-done | bytes 73744
  2642.8 181.6 %reduce-scatter.35.cloned.1.call-done = f32[32,4096]{1,0:T(8,128)} async-done(((f32[1024,4096]{1,0:T(8,128)}), f32[32,4096]{1,0:T(8,128)}) %reduce-scatter.35.cloned.1.call-update) | async-done | bytes 524304 | tf_op jit(solution)/shard_map/reduce_scatter | solution.py:185
  (367 shorter events, 107.5 us)
Async XLA Ops:
  7.2 4.8 copy-start.45
  7.2 8.2 copy-start.95
  7.2 8.2 copy-start.96
  7.2 8.6 copy-start.105
  7.2 258.0 %all-gather.20.cloned.1.call-start = ((), (), s32[]{:S(2)}) async-start(), calls=%async_computation.12 | async-start | bytes 1351680 | tf_op jit(solution)/shard_map/all_gather | solution.py:121
  8.0 258.9 %all-gather.24.cloned.1.call-start = ((), (), s32[]{:S(2)}) async-start(), calls=%async_computation.21 | async-start | bytes 2162688 | tf_op jit(solution)/shard_map/all_gather | solution.py:122
  9.6 276.4 %all-gather.26.cloned.1.call-start = ((), (), s32[]{:S(2)}) async-start(), calls=%async_computation.22 | async-start | bytes 19464192 | tf_op jit(solution)/shard_map/all_gather | solution.py:123
  12.0 308.5 %all-gather.28.cloned.1.call-start = ((), (), s32[]{:S(2)}) async-start(), calls=%async_computation.23 | async-start | bytes 2162688 | tf_op jit(solution)/shard_map/all_gather | solution.py:124
  12.7 366.3 %all-gather.30.cloned.1.call-start = ((), (), s32[]{:S(2)}) async-start(), calls=%async_computation.24 | async-start | bytes 2162688 | tf_op jit(solution)/shard_map/all_gather | solution.py:129
  13.3 492.0 %all-gather.32.cloned.1.call-start = ((), (), s32[]{:S(2)}) async-start(), calls=%async_computation.25 | async-start | bytes 19464192 | tf_op jit(solution)/shard_map/all_gather | solution.py:130
  13.9 549.4 %all-gather.34.cloned.1.call-start = ((), (), s32[]{:S(2)}) async-start(), calls=%async_computation.26 | async-start | bytes 2162688 | tf_op jit(solution)/shard_map/all_gather | solution.py:131
  14.6 627.9 %all-gather.22.cloned.1.call-start = ((), (), s32[]{:S(2)}) async-start(), calls=%async_computation.13 | async-start | bytes 8650752 | tf_op jit(solution)/shard_map/all_gather | solution.py:134
  15.4 960.9 %reduce-scatter.45.cloned.1.call-start = ((), (), s32[]{:S(2)}) async-start(), calls=%async_computation.31 | async-start | bytes 540672
  108.3 171.2 %copy-start.39 = (f32[1024]{0:T(1024)}, f32[1024]{0:T(1024)S(1)}, u32[]{:S(2)}) copy-start(f32[1024]{0:T(1024)S(1)} %get-tuple-element.75) | copy-start | bytes 12292
  244.3 35.2 %copy-start.52 = (f32[1024]{0:T(1024)}, f32[1024]{0:T(1024)S(1)}, u32[]{:S(2)}) copy-start(f32[1024]{0:T(1024)S(1)} %get-tuple-element.78) | copy-start | bytes 12292
  254.6 404.4 %copy-start.43 = (f32[1024]{0:T(1024)}, f32[1024]{0:T(1024)S(1)}, u32[]{:S(2)}) copy-start(f32[1024]{0:T(1024)S(1)} %get-tuple-element.70) | copy-start | bytes 12292
  254.6 12.3 copy-start.20
  265.1 390.0 %copy-start.46 = (f32[1024]{0:T(1024)}, f32[1024]{0:T(1024)S(1)}, u32[]{:S(2)}) copy-start(f32[1024]{0:T(1024)S(1)} %get-tuple-element.73) | copy-start | bytes 12292
  266.8 58.8 %copy-start.3 = (bf16[576,1024]{1,0:T(8,128)(2,1)}, bf16[576,1024]{1,0:T(8,128)(2,1)S(1)}, u32[]{:S(2)}) copy-start(bf16[576,1024]{1,0:T(8,128)(2,1)S(1)} %copy.41) | copy-start | bytes 3538948
  270.3 9.2 copy-start
  270.3 9.2 copy-start.37
  270.7 4.1 copy-start.63
  270.7 8.8 copy-start.41
  303.0 21.5 copy-start.61
  338.1 317.0 %copy-start.9 = (f32[144,1024]{1,0:T(8,128)}, f32[144,1024]{1,0:T(8,128)S(1)}, u32[]{:S(2)}) copy-start(f32[144,1024]{1,0:T(8,128)S(1)} %div.169) | copy-start | bytes 1769476
  404.9 7.0 copy-start.54
  404.9 7.0 copy-start.59
  404.9 7.0 copy-start.71
  404.9 8.0 copy-start.34
  404.9 8.7 copy-start.33
  404.9 9.5 copy-start.32
  406.7 8.5 copy-start.31
  642.5 12.7 copy-start.18
  642.5 12.7 copy-start.73
  642.5 12.7 copy-start.85
  642.5 12.7 copy-start.106
  655.2 4.1 copy-start.12
  661.4 15.3 copy-start.14
  661.4 15.3 copy-start.75
  684.0 19.1 copy-start.55
  684.0 19.1 copy-start.60
  701.0 7.0 copy-start.30
  703.1 4.9 copy-start.13
  712.0 265.2 %reduce-scatter.43.cloned.1.call-start = ((), (), s32[]{:S(2)}) async-start(), calls=%async_computation.30 | async-start | bytes 540672
  714.4 4.3 copy-start.4
  714.4 4.3 copy-start.49
  714.4 4.3 copy-start.51
  714.4 4.3 copy-start.57
  718.8 4.7 copy-start.68
  724.9 5.9 copy-start.26
  724.9 5.9 copy-start.103
  731.6 20.0 copy-start.24
  731.6 20.0 copy-start.101
  838.0 270.9 %reduce-scatter.41.cloned.1.call-start = ((), (), s32[]{:S(2)}) async-start(), calls=%async_computation.29 | async-start | bytes 540672
  841.2 399.9 %reduce-scatter.39.cloned.1.call-start = ((), (), s32[]{:S(2)}) async-start(), calls=%async_computation.28 | async-start | bytes 540672
  844.3 535.8 %reduce-scatter.33.cloned.1.call-start = ((), (), s32[]{:S(2)}) async-start(), calls=%async_computation.19 | async-start | bytes 4325376 | tf_op jit(solution)/shard_map/reduce_scatter | solution.py:182
  848.5 670.7 %reduce-scatter.31.cloned.1.call-start = ((), (), s32[]{:S(2)}) async-start(), calls=%async_computation.18 | async-start | bytes 4325376 | tf_op jit(solution)/shard_map/reduce_scatter | solution.py:194
  855.2 802.9 %reduce-scatter.25.cloned.1.call-start = ((), (), s32[]{:S(2)}) async-start(), calls=%async_computation.15 | async-start | bytes 4325376 | tf_op jit(solution)/shard_map/reduce_scatter | solution.py:180
  859.8 937.1 %reduce-scatter.23.cloned.1.call-start = ((), (), s32[]{:S(2)}) async-start(), calls=%async_computation.14 | async-start | bytes 4325376 | tf_op jit(solution)/shard_map/reduce_scatter | solution.py:192
  869.2 1278.4 %reduce-scatter.27.cloned.1.call-start = ((), (), s32[]{:S(2)}) async-start(), calls=%async_computation.16 | async-start | bytes 38928384 | tf_op jit(solution)/shard_map/reduce_scatter | solution.py:193
  894.8 1608.1 %reduce-scatter.29.cloned.1.call-start = ((), (), s32[]{:S(2)}) async-start(), calls=%async_computation.17 | async-start | bytes 38928384 | tf_op jit(solution)/shard_map/reduce_scatter | solution.py:181
  912.6 1730.2 %reduce-scatter.37.cloned.1.call-start = ((), (), s32[]{:S(2)}) async-start(), calls=%async_computation.27 | async-start | bytes 2703360
  922.7 1901.7 %reduce-scatter.35.cloned.1.call-start = ((), (), s32[]{:S(2)}) async-start(), calls=%async_computation.20 | async-start | bytes 17301504 | tf_op jit(solution)/shard_map/reduce_scatter | solution.py:185
  932.5 40.8 %copy-start.23 = (f32[144,4096]{1,0:T(8,128)S(1)}, f32[144,4096]{1,0:T(8,128)}, u32[]{:S(2)}) copy-start(f32[144,4096]{1,0:T(8,128)} %get-tuple-element.82) | copy-start | bytes 7077892
  (65 other events, 125.5 us)
Sparse Core Ops, SparseCore 0:
  10.9 57.5 all-gather.19
  72.0 55.5 all-gather.23
  131.0 130.7 all-gather.25
  265.0 55.3 all-gather.27
  323.7 55.2 all-gather.29
  381.7 123.5 all-gather.31
  508.7 54.5 all-gather.33
  566.1 76.2 all-gather.21
  712.1 132.4 reduce-scatter.44
  846.7 130.0 reduce-scatter.42
  979.0 129.7 reduce-scatter.40
  1111.0 129.9 reduce-scatter.38
  1243.3 136.7 reduce-scatter.32
  1382.2 136.8 reduce-scatter.30
  1521.2 136.7 reduce-scatter.24
  1660.2 136.6 reduce-scatter.22
  1803.2 344.3 reduce-scatter.26
  2155.0 347.8 reduce-scatter.28
  2505.8 136.9 reduce-scatter.36
  2645.5 178.7 reduce-scatter.34
where the time goes:
time: 2840 us; the launch traced here: 2830 us
  waiting for transfers between devices  2110 us (74%)
  blocking collectives  243 us (9%)
  local copies, waits for them, and re-layouts  177 us (6%)
  matrix products  169 us (6%)
  other arithmetic  118 us (4%)
    unnamed x25, waiting for transfers between devices  402 us
    reduce_scatter x1, waiting for transfers between devices, local(): lax.psum_scatter(top_middle, ('dp', 'fsdp'), scatter_dimension=0, tiled=T...  355 us
    reduce_scatter x1, waiting for transfers between devices, local(): lax.psum_scatter(low_middle, ('dp', 'fsdp'), scatter_dimension=0, tiled=T...  349 us
    reduce_scatter x1, waiting for transfers between devices, local(): lax.psum_scatter(grad_readout_w, ('dp', 'fsdp'), scatter_dimension=0, til...  182 us
    reduce_scatter x1, waiting for transfers between devices, local(): lax.psum_scatter(low_last, ('dp', 'fsdp'), scatter_dimension=0, tiled=True)  139 us
    reduce_scatter x1, waiting for transfers between devices, local(): lax.psum_scatter(low_first, ('dp', 'fsdp'), scatter_dimension=0, tiled=True)  139 us
    reduce_scatter x1, waiting for transfers between devices, local(): lax.psum_scatter(top_last, ('dp', 'fsdp'), scatter_dimension=0, tiled=True)  138 us
    reduce_scatter x1, waiting for transfers between devices, local(): lax.psum_scatter(top_first, ('dp', 'fsdp'), scatter_dimension=0, tiled=True)  137 us
  transfers between devices with their start and end apart: 20, of which 15 were waited for; matrix products, arithmetic and copies ran while one was open for 13% of the time, Pallas kernels for 0%

commit v1 on v0

v1 whole, which is shorter than its diff:
```python
import functools

import jax
import jax.numpy as jnp
from jax import lax
from jax.experimental import pallas as pl
from jax.experimental.pallas import tpu as pltpu
from jax.sharding import PartitionSpec as P

C = 1024
G = 24


def product(left, right):
    return jnp.dot(left, right, preferred_element_type=jnp.float32)


def times_transposed(left, right):
    return lax.dot_general(
        left, right, (((1,), (1,)), ((), ())), preferred_element_type=jnp.float32
    )


def outer_sum(left, right):
    return lax.dot_general(
        left, right, (((0,), (0,)), ((), ())), preferred_element_type=jnp.float32
    )


def layer_norm(hidden, gain_vec, bias_vec):
    center = hidden - jnp.mean(hidden, axis=-1, keepdims=True)
    spread = jnp.mean(center * center, axis=-1, keepdims=True)
    return center * lax.rsqrt(spread + 1e-05) * gain_vec + bias_vec


def norm_act(hidden, gain_vec, bias_vec):
    return jax.nn.silu(layer_norm(hidden, gain_vec, bias_vec))


def closing(stream, hidden, gain_vec, bias_vec):
    return jax.nn.silu(stream + layer_norm(hidden, gain_vec, bias_vec))


def columns(values, grid_side):
    channels = values.shape[-1]
    padded = jnp.pad(values.reshape(grid_side, grid_side, channels), ((1, 1), (1, 1), (0, 0)))
    pieces = [
        padded[row_tap : row_tap + grid_side, col_tap : col_tap + grid_side, :]
        for row_tap in range(3)
        for col_tap in range(3)
    ]
    return jnp.concatenate(pieces, axis=-1).reshape(grid_side * grid_side, 9 * channels)


def back_columns(values, grid_side):
    channels = values.shape[-1]
    padded = jnp.pad(values.reshape(grid_side, grid_side, channels), ((1, 1), (1, 1), (0, 0)))
    pieces = [
        padded[2 - row_tap : 2 - row_tap + grid_side, 2 - col_tap : 2 - col_tap + grid_side, :]
        for row_tap in range(3)
        for col_tap in range(3)
    ]
    return jnp.concatenate(pieces, axis=-1).reshape(grid_side * grid_side, 9 * channels)


def block_forward(stream, weights, grid_side):
    w_first, w_middle, w_last, gain_rows, bias_rows = weights
    low_in = stream.astype(jnp.bfloat16)
    pre_first = product(low_in, w_first)
    act_first = norm_act(pre_first, gain_rows[0], bias_rows[0]).astype(jnp.bfloat16)
    taps_in = columns(act_first, grid_side)
    pre_middle = product(taps_in, w_middle)
    act_middle = norm_act(pre_middle, gain_rows[1], bias_rows[1]).astype(jnp.bfloat16)
    pre_last = product(act_middle, w_last)
    result = closing(stream, pre_last, gain_rows[2], bias_rows[2])
    return (result, (low_in, pre_first, taps_in, pre_middle, act_middle, pre_last))


def block_backward(grad_out, stream, kept, weights, grid_side):
    low_in, pre_first, taps_in, pre_middle, act_middle, pre_last = kept
    w_first, w_middle, w_last, gain_rows, bias_rows = weights
    unused, pullback = jax.vjp(closing, stream, pre_last, gain_rows[2], bias_rows[2])
    grad_stream, grad_last, gain_last, bias_last = pullback(grad_out)
    grad_last = grad_last.astype(jnp.bfloat16)
    grad_act = times_transposed(grad_last, w_last)
    wgrad_last = outer_sum(act_middle, grad_last)
    unused, pullback = jax.vjp(norm_act, pre_middle, gain_rows[1], bias_rows[1])
    grad_middle, gain_middle, bias_middle = pullback(grad_act)
    grad_middle = grad_middle.astype(jnp.bfloat16)
    tapped = back_columns(grad_middle, grid_side).reshape(-1, 9, C)
    grad_act_first = lax.dot_general(
        tapped,
        w_middle.reshape(9, C, C),
        (((1, 2), (0, 2)), ((), ())),
        preferred_element_type=jnp.float32,
    )
    wgrad_middle = outer_sum(taps_in, grad_middle)
    unused, pullback = jax.vjp(norm_act, pre_first, gain_rows[0], bias_rows[0])
    grad_first, gain_first, bias_first = pullback(grad_act_first)
    grad_first = grad_first.astype(jnp.bfloat16)
    grad_stream = grad_stream + times_transposed(grad_first, w_first)
    wgrad_first = outer_sum(low_in, grad_first)
    gain_grads = jnp.stack([gain_first, gain_middle, gain_last], axis=1)
    bias_grads = jnp.stack([bias_first, bias_middle, bias_last], axis=1)
    return (grad_stream, (wgrad_first, wgrad_middle, wgrad_last, gain_grads, bias_grads))

PLANE = 4


class Movement:
    def __init__(self, mesh):
        self.dp = mesh.shape["dp"]
        self.cores = mesh.shape["fsdp"]
        self.line = self.dp // PLANE

    def flip(self, value, bits):
        return lax.ppermute(value, "dp", [(i, i ^ bits) for i in range(self.dp)])

    def up(self, value, first, last):
        pairs = [(i, i + PLANE) for i in range(self.dp - PLANE) if first <= i // PLANE <= last]
        return lax.ppermute(value, "dp", pairs)

    def down(self, value, first, last):
        pairs = [(i, i - PLANE) for i in range(PLANE, self.dp) if first <= i // PLANE <= last]
        return lax.ppermute(value, "dp", pairs)

    def turn(self, value, step):
        return lax.ppermute(value, "fsdp", [(i, (i + step) % self.cores) for i in range(self.cores)])

    def place(self):
        index = lax.axis_index("dp")
        return index // PLANE, index % PLANE, lax.axis_index("fsdp")

    def gather_line(self, own):
        line = self.line
        height = self.place()[0]
        rising, falling, above, below = own, own, [], []
        for step in range(1, line):
            rising = self.up(rising, step - 1, line - 2)
            falling = self.down(falling, 1, line - step)
            below.append(rising)
            above.append(falling)
        stacked = jnp.stack(below[::-1] + [own] + above)
        return lax.dynamic_slice_in_dim(stacked, line - 1 - height, line)

    def gather_pieces(self, own):
        held = self.gather_line(own)
        half = held.shape[-1] // 2
        first = self.flip(held, 1)
        second = self.flip(held, 2)
        far = (self.flip(first[..., :half], 2), self.flip(second[..., half:], 1))
        pieces = [(0, 0, (held,)), (1, 0, (first,)), (2, 0, (second,)), (3, 0, far)]
        for step in range(1, self.cores):
            pieces += [(chip, step, tuple(self.turn(part, step) for part in parts)) for chip, _, parts in pieces[:4]]
        return pieces

    def gather(self, own_parts):
        gathered = [self.gather_pieces(part) for part in own_parts]
        columns = own_parts[0].shape[-1]
        rows = [part.shape[0] for part in own_parts]
        total = sum(rows)
        operands, plan, start = [], [], 0
        for pieces, count in zip(gathered, rows):
            for chip, step, parts in pieces:
                left = 0
                for part in parts:
                    operands.append(part)
                    plan.append((chip, step, start, count, left, part.shape[-1]))
                    left += part.shape[-1]
            start += count
        cores = self.cores

        def kernel(*refs):
            sources, target, arrived = refs[:-2], refs[-2], refs[-1]
            near = lax.rem(lax.axis_index("dp"), PLANE)
            core = lax.axis_index("fsdp")
            copies = []
            for number, (chip, step, start, count, left, width) in enumerate(plan):
                across = near if chip == 0 else lax.bitwise_xor(near, chip)
                turned = lax.rem(core + (cores - step), cores)
                copies.append(
                    pltpu.make_async_copy(
                        sources[number],
                        target.at[:, across, turned, pl.ds(start, count), pl.ds(left, width)],
                        arrived.at[number],
                    )
                )
            for copy in copies:
                copy.start()
            for copy in copies:
                copy.wait()

        shape = (self.line, PLANE, cores, total, columns)
        whole = pl.pallas_call(
            kernel,
            out_shape=jax.ShapeDtypeStruct(shape, own_parts[0].dtype),
            in_specs=[pl.BlockSpec(memory_space=pl.ANY)] * len(operands),
            out_specs=pl.BlockSpec(memory_space=pl.ANY),
            scratch_shapes=[pltpu.SemaphoreType.DMA((len(operands),))],
            cost_estimate=pl.CostEstimate(
                flops=0,
                bytes_accessed=4 * self.dp * cores * total * columns,
                transcendentals=0,
            ),
        )(*operands)
        return whole

    def scatter(self, terms):
        line, cores = self.line, self.cores
        height, near, core = self.place()
        columns = terms.shape[-1]
        terms = terms.reshape(line, PLANE, cores, -1, columns)
        half = columns // 2

        def of_core(step):
            return lax.dynamic_index_in_dim(terms, (core + step) % cores, 2, keepdims=False)

        summed = of_core(0).astype(jnp.float32)
        for step in range(1, cores):
            summed = summed + self.turn(of_core(step), step).astype(jnp.float32)

        def of_chip(bits):
            return lax.dynamic_index_in_dim(summed, near ^ bits, 1, keepdims=False)

        low = jnp.bfloat16
        far = of_chip(3).astype(low)
        far_first = self.flip(far[..., :half], 2).astype(jnp.float32)
        far_second = self.flip(far[..., half:], 1).astype(jnp.float32)
        first = of_chip(1)
        first = jnp.concatenate([first[..., :half] + far_first, first[..., half:]], -1)
        second = of_chip(2)
        second = jnp.concatenate([second[..., :half], second[..., half:] + far_second], -1)
        first = self.flip(first.astype(low), 1).astype(jnp.float32)
        second = self.flip(second.astype(low), 2).astype(jnp.float32)
        held = of_chip(0) + first + second

        def of_line(distance):
            return lax.dynamic_index_in_dim(held, jnp.clip(height + distance, 0, line - 1), 0, keepdims=False)

        rising = falling = None
        for distance in range(line - 1, 0, -1):
            to_up, to_down = of_line(distance), of_line(-distance)
            if rising is not None:
                to_up, to_down = to_up + rising, to_down + falling
            rising = self.up(to_up.astype(low), 0, line - 1 - distance).astype(jnp.float32)
            falling = self.down(to_down.astype(low), distance, line - 1).astype(jnp.float32)
        return of_line(0) + rising + falling


def local(
    move,
    features,
    grid_live,
    pos_embed,
    w_in,
    w_mid,
    w_out,
    norm_gain,
    norm_bias,
    readout_w,
    readout_b,
    cotangent,
):
    devices = move.dp * move.cores
    low = jnp.bfloat16
    own_rows = w_in.shape[1]
    width = norm_gain.shape[-1]
    wide = readout_b.shape[0]
    cells = pos_embed.shape[0]
    scales = jnp.concatenate([norm_gain.reshape(-1), norm_bias.reshape(-1), readout_b])
    small = jnp.concatenate([pos_embed.T.reshape(-1), scales])
    small_rows = -(-small.shape[0] // (16 * C)) * 16
    small = jnp.pad(small, (0, small_rows * C - small.shape[0])).reshape(small_rows, C)
    thirds = w_mid.shape[1] // 3
    small_all = move.gather([small]).reshape(devices, -1)
    w_in_0 = move.gather([w_in[0]]).reshape(C, C)

    def middle(block):
        if thirds % 16:
            return move.gather([w_mid[block]]).reshape(9 * C, C)
        return move.gather([w_mid[block, i * thirds : (i + 1) * thirds] for i in range(3)]).reshape(9 * C, C)

    w_mid_0 = middle(0)
    w_out_0 = move.gather([w_out[0]]).reshape(C, C)
    w_in_1 = move.gather([w_in[1]]).reshape(C, C)
    w_mid_1 = middle(1)
    w_out_1 = move.gather([w_out[1]]).reshape(C, C)
    readout_all = move.gather([readout_w]).reshape(C, -1)
    pos_all = small_all[:, : cells * width].reshape(C, cells).T
    at = cells * width
    count = 6 * width
    gains = small_all[:, at : at + count].reshape(devices, 2, 3, width)
    gains = jnp.moveaxis(gains, 0, 2).reshape(2, 3, C).astype(jnp.float32)
    biases = small_all[:, at + count : at + 2 * count].reshape(devices, 2, 3, width)
    biases = jnp.moveaxis(biases, 0, 2).reshape(2, 3, C).astype(jnp.float32)
    readout_bias = small_all[:, at + 2 * count : at + 2 * count + wide].reshape(-1).astype(jnp.float32)

    first_block = (w_in_0, w_mid_0, w_out_0, gains[0], biases[0])
    second_block = (w_in_1, w_mid_1, w_out_1, gains[1], biases[1])
    stream_in = features[0].astype(jnp.float32) + pos_all.astype(jnp.float32)
    stream_mid, first_kept = block_forward(stream_in, first_block, G)
    half_side = G // 2
    pooled = jnp.mean(stream_mid.reshape(half_side, 2, half_side, 2, C), axis=(1, 3)).reshape(
        half_side * half_side, C
    )
    stream_out, second_kept = block_forward(pooled, second_block, half_side)
    low_out = stream_out.astype(jnp.bfloat16)
    live_value = grid_live[0].astype(jnp.float32)

    def readout_act(logits):
        return jax.nn.gelu(logits, approximate=False) * live_value

    logits = product(low_out, readout_all) + readout_bias
    output = readout_act(logits).astype(jnp.bfloat16)
    unused, pullback = jax.vjp(readout_act, logits)
    grad_logits = pullback(cotangent[0].astype(jnp.float32))[0].astype(jnp.bfloat16)
    grad_readout_w = outer_sum(low_out, grad_logits).astype(low)
    grad_readout_b = jnp.sum(grad_logits.astype(jnp.float32), axis=0)
    grad_top = times_transposed(grad_logits, readout_all)
    readout_owned = move.scatter(grad_readout_w)
    grad_pooled, second_grads = block_backward(
        grad_top, pooled, second_kept, second_block, half_side
    )
    top_first, top_middle, top_last, top_gain, top_bias = second_grads
    last_owned_1 = move.scatter(top_last.astype(low))
    middle_owned_1 = move.scatter(top_middle.astype(low))
    first_owned_1 = move.scatter(top_first.astype(low))
    grad_mid = jnp.broadcast_to(
        (grad_pooled * 0.25).reshape(half_side, 1, half_side, 1, C), (half_side, 2, half_side, 2, C)
    ).reshape(G * G, C)
    grad_in, first_grads = block_backward(grad_mid, stream_in, first_kept, first_block, G)
    low_first, low_middle, low_last, low_gain, low_bias = first_grads
    last_owned_0 = move.scatter(low_last.astype(low))
    middle_owned_0 = move.scatter(low_middle.astype(low))
    first_owned_0 = move.scatter(low_first.astype(low))
    gain_terms = jnp.stack([low_gain, top_gain]).reshape(2, devices, width, 3)
    bias_terms = jnp.stack([low_bias, top_bias]).reshape(2, devices, width, 3)
    small_terms = jnp.concatenate(
        [
            grad_in.T.reshape(devices, -1),
            gain_terms.transpose(1, 0, 3, 2).reshape(devices, -1),
            bias_terms.transpose(1, 0, 3, 2).reshape(devices, -1),
            grad_readout_b.reshape(devices, -1),
        ],
        axis=1,
    ).astype(low)
    rest = small_rows * C - small_terms.shape[1]
    small_terms = jnp.pad(small_terms, ((0, 0), (0, rest))).reshape(devices * small_rows, C)
    small_owned = move.scatter(small_terms).reshape(-1)
    pos_owned = small_owned[:at].reshape(width, cells).T
    return (
        output[None],
        grad_in[None],
        pos_owned,
        jnp.stack([first_owned_0, first_owned_1]),
        jnp.stack([middle_owned_0, middle_owned_1]),
        jnp.stack([last_owned_0, last_owned_1]),
        small_owned[at : at + count].reshape(2, 3, width),
        small_owned[at + count : at + 2 * count].reshape(2, 3, width),
        readout_owned,
        small_owned[at + 2 * count : at + 2 * count + wide],
    )


def solution(mesh):
    return jax.shard_map(
        functools.partial(local, Movement(mesh)),
        mesh=mesh,
        in_specs=(
            P(("dp", "fsdp"), None, None),
            P(("dp", "fsdp")),
            P(None, ("dp", "fsdp")),
            P(None, ("dp", "fsdp"), None),
            P(None, ("dp", "fsdp"), None),
            P(None, ("dp", "fsdp"), None),
            P(None, None, ("dp", "fsdp")),
            P(None, None, ("dp", "fsdp")),
            P(("dp", "fsdp"), None),
            P(("dp", "fsdp")),
            P(("dp", "fsdp"), None, None),
        ),
        out_specs=(
            P(("dp", "fsdp"), None, None),
            P(("dp", "fsdp"), None, None),
            P(None, ("dp", "fsdp")),
            P(None, ("dp", "fsdp"), None),
            P(None, ("dp", "fsdp"), None),
            P(None, ("dp", "fsdp"), None),
            P(None, None, ("dp", "fsdp")),
            P(None, None, ("dp", "fsdp")),
            P(("dp", "fsdp"), None),
            P(("dp", "fsdp")),
        ),
        check_vma=False,
    )
```

time: 2840 us -> 3130 us (1.10)
  Pallas kernels: 0 us -> 1730 us
  waiting for transfers between devices: 2110 us -> 403 us
  starting transfers between devices: 1.39 us -> 410 us
  blocking collectives: 243 us -> 0 us
  local copies, waits for them, and re-layouts: 177 us -> 283 us
    pallas_call x0 -> x8, Pallas kernels: none -> 1730 us  [gather(): pl.pallas_call(kernel, out_shape=jax.ShapeDtypeStruct(shape, own_parts[0]...]
    reduce_scatter x7 -> x0, waiting for transfers between devices: 1440 us -> none  [the longest x1 355 us: local(): lax.psum_scatter(top_middle, ('dp', 'fsdp'), scatter_dimension=0, tiled=T...]
    ppermute x0 -> x268, starting transfers between devices: none -> 410 us  [the longest x60 211 us: up(): return lax.ppermute(value, 'dp', pairs)]
    ppermute x0 -> x268, waiting for transfers between devices: none -> 403 us  [the longest x80 227 us: flip(): return lax.ppermute(value, 'dp', [(i, i ^ bits) for i in range(self.dp)])]
    unnamed x25 -> x0, waiting for transfers between devices: 402 us -> none
    all_gather x8 -> x0, waiting for transfers between devices: 266 us -> none  [the longest x1 89.4 us: local(): lax.all_gather(w_mid[1], ('dp', 'fsdp'), axis=0, tiled=True)]
    all_gather x5 -> x0, blocking collectives: 203 us -> none  [the longest x1 43.1 us: local(): lax.all_gather(readout_b, ('dp', 'fsdp'), axis=0, tiled=True)]
    dot_general x0 -> x2, matrix products: none -> 72.4 us  [block_backward(): lax.dot_general(tapped, w_middle.reshape(9, C, C), (((1, 2), (0, 2)), (()...]
  transfers between devices with their start and end apart: 20 -> 268, of which waited for: 15 -> 88; matrix products, arithmetic and copies ran while one was open for 13% -> 14% of each run, Pallas kernels for 0% -> 47%
where the time goes in v1:
time: 3130 us; the launch traced here: 3110 us
  Pallas kernels  1730 us (55%)
  starting transfers between devices  410 us (13%)
  waiting for transfers between devices  403 us (13%)
  local copies, waits for them, and re-layouts  283 us (9%)
  matrix products  185 us (6%)
  other arithmetic  101 us (3%)
    pallas_call x8, Pallas kernels, gather(): pl.pallas_call(kernel, out_shape=jax.ShapeDtypeStruct(shape, own_parts[0]...  1730 us
    ppermute x80, waiting for transfers between devices, flip(): return lax.ppermute(value, 'dp', [(i, i ^ bits) for i in range(self.dp)])  227 us
    ppermute x60, starting transfers between devices, up(): return lax.ppermute(value, 'dp', pairs)  211 us
    ppermute x60, waiting for transfers between devices, down(): return lax.ppermute(value, 'dp', pairs)  129 us
    ppermute x80, starting transfers between devices, flip(): return lax.ppermute(value, 'dp', [(i, i ^ bits) for i in range(self.dp)])  96.3 us
    ppermute x60, starting transfers between devices, down(): return lax.ppermute(value, 'dp', pairs)  89.2 us
    unnamed x462, local copies, waits for them, and re-layouts  75.7 us
    dot_general x2, matrix products, block_backward(): lax.dot_general(tapped, w_middle.reshape(9, C, C), (((1, 2), (0, 2)), (()...  72.4 us
  transfers between devices with their start and end apart: 268, of which 88 were waited for; matrix products, arithmetic and copies ran while one was open for 14% of the time, Pallas kernels for 47%

profile of v1, /device:TPU:0, one launch (start us, length us, event | category | flops | bytes accessed | tf_op | source)
XLA Modules:
  0.0 3113.5 jit_solution(12904852689528280268)
XLA Ops:
  1.6 4.9 collective-permute-start.75
  20.8 4.7 collective-permute-start.15
  46.9 16.6 collective-permute-start.120
  67.5 13.4 collective-permute-start.154
  122.4 5.2 collective-permute-start.45
  151.3 5.1 collective-permute-start.105
  171.3 23.5 collective-permute-done.33
  196.2 13.4 collective-permute-done.139
  210.9 6.2 collective-permute-done.34
  218.4 6.2 collective-permute-done.140
  226.0 6.2 collective-permute-done.35
  240.3 5.6 collective-permute-done.109
  259.9 10.9 collective-permute-done.50
  287.5 64.7 %shard_map.186 = bf16[4,4,2,32,1024]{4,3,2,1,0:T(8,128)(2,1)} custom-call(bf16[4,32,1024]{2,1,0:T(8,128)(2,1)} %copy-done.72, bf16[4,32,1024]{2,1,0:T(8,128)(2,1)} %copy-done.87, bf16[4,32,1024]{2,1,0:T(8,128)(2,1)} %copy-done.86, bf16[4,32,512]{2,1,0:T(8,128)(2,1)} %copy-done.130, bf16[4,32,512]{2,1,0:T(8,128)(2,1)} %copy-done.129, ...), custom_call_target="tpu_custom_call" | custom-call | bytes 4194304 | tf_op jit(solution)/shard_map/pallas_call | solution.py:194
  368.6 64.7 %shard_map.187 = bf16[4,4,2,32,1024]{4,3,2,1,0:T(8,128)(2,1)} custom-call(bf16[4,32,1024]{2,1,0:T(8,128)(2,1)} %copy-done.71, bf16[4,32,1024]{2,1,0:T(8,128)(2,1)} %collective-permute-done.21.refs_1_, bf16[4,32,1024]{2,1,0:T(8,128)(2,1)} %collective-permute-done.22.refs_2_, bf16[4,32,512]{2,1,0:T(8,128)(2,1)} %collective-permute-done.23.refs_3_, ...), custom_call_target="tpu_custom_call" | custom-call | bytes 4194304 | tf_op jit(solution)/shard_map/pallas_call | solution.py:194
  462.9 6.4 collective-permute-done.170
  471.6 9.0 collective-permute-done.142.refs_22_
  483.3 14.2 collective-permute-done.37.refs_2_
  501.2 13.1 collective-permute-done.52.refs_12_
  517.2 14.1 collective-permute-done.67.refs_22_
  535.0 13.1 collective-permute-done.112.refs_2_
  548.1 7.0 collective-permute-start.172
  555.2 6.2 collective-permute-start.171
  566.2 7.8 collective-permute-done.39.refs_4_
  579.0 16.8 collective-permute-done.38.refs_3_
  596.4 8.5 collective-permute-done.54.refs_14_
  627.1 64.7 %shard_map.192 = bf16[4,4,2,32,1024]{4,3,2,1,0:T(8,128)(2,1)} custom-call(bf16[4,32,1024]{2,1,0:T(8,128)(2,1)} %copy-done.68, bf16[4,32,1024]{2,1,0:T(8,128)(2,1)} %copy-done.81, bf16[4,32,1024]{2,1,0:T(8,128)(2,1)} %copy-done.79, bf16[4,32,512]{2,1,0:T(8,128)(2,1)} %copy-done.120, bf16[4,32,512]{2,1,0:T(8,128)(2,1)} %copy-done.118, ...), custom_call_target="tpu_custom_call" | custom-call | bytes 4194304 | tf_op jit(solution)/shard_map/pallas_call | solution.py:194
  691.8 64.7 %shard_map.189 = bf16[4,4,2,32,1024]{4,3,2,1,0:T(8,128)(2,1)} custom-call(bf16[4,32,1024]{2,1,0:T(8,128)(2,1)} %copy-done.69, bf16[4,32,1024]{2,1,0:T(8,128)(2,1)} %copy-done.84, bf16[4,32,1024]{2,1,0:T(8,128)(2,1)} %copy-done.82, bf16[4,32,512]{2,1,0:T(8,128)(2,1)} %copy-done.122, bf16[4,32,512]{2,1,0:T(8,128)(2,1)} %copy-done.119, ...), custom_call_target="tpu_custom_call" | custom-call | bytes 4194304 | tf_op jit(solution)/shard_map/pallas_call | solution.py:194
  756.6 64.7 %shard_map.190 = bf16[4,4,2,32,1024]{4,3,2,1,0:T(8,128)(2,1)} custom-call(bf16[4,32,1024]{2,1,0:T(8,128)(2,1)} %copy-done.70, bf16[4,32,1024]{2,1,0:T(8,128)(2,1)} %copy-done.85, bf16[4,32,1024]{2,1,0:T(8,128)(2,1)} %copy-done.83, bf16[4,32,512]{2,1,0:T(8,128)(2,1)} %copy-done.123, bf16[4,32,512]{2,1,0:T(8,128)(2,1)} %copy-done.121, ...), custom_call_target="tpu_custom_call" | custom-call | bytes 4194304 | tf_op jit(solution)/shard_map/pallas_call | solution.py:194
  835.0 573.1 %shard_map.188 = bf16[4,4,2,288,1024]{4,3,2,1,0:T(8,128)(2,1)} custom-call(bf16[4,96,1024]{2,1,0:T(8,128)(2,1)} %constant_dynamic-slice_fusion.23.refs_0_, bf16[4,96,1024]{2,1,0:T(8,128)(2,1)} %copy-done.61, bf16[4,96,1024]{2,1,0:T(8,128)(2,1)} %copy-done.60, bf16[4,96,512]{2,1,0:T(8,128)(2,1)} %copy-done.92, bf16[4,96,512]{2,1,0:T(8,128)(2,1)} %copy-done.91, ...), custom_call_target="tpu_custom_call" | custom-call | bytes 37748736 | tf_op jit(solution)/shard_map/pallas_call | solution.py:194
  1408.1 16.9 fusion.180
  1449.0 5.5 collective-permute-done.114.refs_4_
  1503.9 573.1 %shard_map.191 = bf16[4,4,2,288,1024]{4,3,2,1,0:T(8,128)(2,1)} custom-call(bf16[4,96,1024]{2,1,0:T(8,128)(2,1)} %constant_dynamic-slice_fusion.18.refs_0_, bf16[4,96,1024]{2,1,0:T(8,128)(2,1)} %collective-permute-done.111.refs_1_, bf16[4,96,1024]{2,1,0:T(8,128)(2,1)} %collective-permute-done.112.refs_2_, bf16[4,96,512]{2,1,0:T(8,128)(2,1)} %copy-done.96, ...), custom_call_target="tpu_custom_call" | custom-call | bytes 37748736 | tf_op jit(solution)/shard_map/pallas_call | solution.py:194
  2077.1 9.1 fusion.183
  2090.3 255.3 %shard_map.193 = bf16[4,4,2,32,4096]{4,3,2,1,0:T(8,128)(2,1)} custom-call(bf16[4,32,4096]{2,1,0:T(8,128)(2,1)} %copy-done.30, bf16[4,32,4096]{2,1,0:T(8,128)(2,1)} %copy-done.43, bf16[4,32,4096]{2,1,0:T(8,128)(2,1)} %copy-done.41, bf16[4,32,2048]{2,1,0:T(8,128)(2,1)} %collective-permute-done.173.refs_3_, ...), custom_call_target="tpu_custom_call" | custom-call | bytes 16777216 | tf_op jit(solution)/shard_map/pallas_call | solution.py:194
  2345.7 12.4 fusion.157
  2376.0 7.0 reshape_reshape.15
  2383.1 14.4 multiply_reduce_fusion.11
  2426.9 5.9 convolution_convert_fusion.2
  2432.8 11.4 convolution_convert_fusion
  2457.7 6.3 constant_dynamic-slice_fusion.1
  2466.9 22.4 convolution_convert_fusion.1
  2501.8 20.3 reshape_reshape.17
  2522.1 58.0 %multiply_reduce_fusion.2 = (bf16[1024]{0:T(1024)(128)(2,1)}, f32[576]{0:T(1024)S(1)}, bf16[1024]{0:T(1024)(128)(2,1)}, f32[576,1024]{1,0:T(8,128)}) fusion(f32[576,1024]{1,0:T(8,128)S(1)} %copy-done.3, f32[576]{0:T(1024)S(1)} %copy-done.139, f32[576]{0:T(1024)S(1)} %copy-done.136, f32[1024]{0:T(1024)} %bitcast.18, f32[1024]{0:T(1024)S(1)} %bitcast.759, ...), kind=kOutput, calls=%fused_computation.74 | convolution fusion | flops 10882839552 | bytes 34228992 | tf_op jit(solution)/shard_map/dot_general | solution.py:91
  2595.1 26.6 constant_dynamic-slice_fusion.7
  2633.5 8.8 copy.113
  2642.3 8.9 copy.114
  2706.9 6.5 collective-permute-start.240
  2776.5 32.4 %collective-permute-start.253 = (bf16[32,1024]{1,0:T(8,128)(2,1)S(1)}, bf16[32,1024]{1,0:T(8,128)(2,1)S(1)}, u32[]{:S(2)}, u32[]{:S(2)}) collective-permute-start(bf16[32,1024]{1,0:T(8,128)(2,1)S(1)} %get-tuple-element.131), channel_id=1, source_target_pairs={{0,8},{2,10},{4,12},{6,14},{8,16},{10,18},{12,20},{14,22},{16,24},... | collective-permute-start | bytes 196616 | tf_op jit(solution)/shard_map/ppermute | solution.py:121
  2841.8 12.4 collective-permute-done.260
  2858.6 6.7 convert_add_fusion.1
  2869.8 11.2 convert_add_fusion
  2881.0 6.5 copy-done.1
  2898.4 4.9 dynamic-slice_bitcast_fusion.1
  2914.0 14.0 collective-permute-done.227
  2950.8 34.6 %collective-permute-done.217 = bf16[4,288,1024]{2,1,0:T(8,128)(2,1)} collective-permute-done((bf16[4,288,1024]{2,1,0:T(8,128)(2,1)S(1)}, bf16[4,288,1024]{2,1,0:T(8,128)(2,1)}, u32[]{:S(2)}, u32[]{:S(2)}) %collective-permute-start.217) | collective-permute-done | bytes 2359328 | tf_op jit(solution)/shard_map/ppermute | solution.py:117
  2988.9 5.0 fusion.3
  2998.1 12.6 collective-permute-done.228
  3012.1 5.0 fusion.2
  3025.1 7.7 collective-permute-done.229
  3052.3 10.0 collective-permute-done.230
  3080.0 5.9 collective-permute-done.220
  3085.8 14.6 collective-permute-done.223
  3100.7 10.8 collective-permute-done.234
  (1280 shorter events, 708.7 us)
Async XLA Ops:
  9.8 37.1 %collective-permute-start.3 = (bf16[32,1024]{1,0:T(8,128)(2,1)S(1)}, bf16[32,1024]{1,0:T(8,128)(2,1)S(1)}, u32[]{:S(2)}, u32[]{:S(2)}) collective-permute-start(bf16[32,1024]{1,0:T(8,128)(2,1)S(1)} %reshape.494), channel_id=1, source_target_pairs={{8,0},{10,2},{12,4},{14,6},{16,8},{18,10},{20,12},{22,14},{24,16},... | collective-permute-start | bytes 196616 | tf_op jit(solution)/shard_map/ppermute | solution.py:125
  46.9 58.1 %collective-permute-start.120 = (bf16[96,1024]{1,0:T(8,128)(2,1)S(1)}, bf16[96,1024]{1,0:T(8,128)(2,1)S(1)}, u32[]{:S(2)}, u32[]{:S(2)}) collective-permute-start(bf16[96,1024]{1,0:T(8,128)(2,1)S(1)} %get-tuple-element.114), channel_id=1, source_target_pairs={{0,8},{2,10},{4,12},{6,14},{8,16},{10,18},{12,20},{14,22},{16,24},... | collective-permute-start | bytes 589832 | tf_op jit(solution)/shard_map/ppermute | solution.py:121
  159.8 76.5 %collective-permute-start.108 = (bf16[96,1024]{1,0:T(8,128)(2,1)S(1)}, bf16[96,1024]{1,0:T(8,128)(2,1)S(1)}, u32[]{:S(2)}, u32[]{:S(2)}) collective-permute-start(bf16[96,1024]{1,0:T(8,128)(2,1)S(1)} %get-tuple-element.110), channel_id=1, source_target_pairs={{8,0},{10,2},{12,4},{14,6},{16,8},{18,10},{20,12},{22,14},{24,16},... | collective-permute-start | bytes 589832 | tf_op jit(solution)/shard_map/ppermute | solution.py:125
  163.6 72.7 %collective-permute-start.63 = (bf16[96,1024]{1,0:T(8,128)(2,1)S(1)}, bf16[96,1024]{1,0:T(8,128)(2,1)S(1)}, u32[]{:S(2)}, u32[]{:S(2)}) collective-permute-start(bf16[96,1024]{1,0:T(8,128)(2,1)S(1)} %get-tuple-element.111), channel_id=1, source_target_pairs={{8,0},{10,2},{12,4},{14,6},{16,8},{18,10},{20,12},{22,14},{24,16},... | collective-permute-start | bytes 589832 | tf_op jit(solution)/shard_map/ppermute | solution.py:125
  166.4 71.3 %collective-permute-start.48 = (bf16[96,1024]{1,0:T(8,128)(2,1)S(1)}, bf16[96,1024]{1,0:T(8,128)(2,1)S(1)}, u32[]{:S(2)}, u32[]{:S(2)}) collective-permute-start(bf16[96,1024]{1,0:T(8,128)(2,1)S(1)} %get-tuple-element.112), channel_id=1, source_target_pairs={{8,0},{10,2},{12,4},{14,6},{16,8},{18,10},{20,12},{22,14},{24,16},... | collective-permute-start | bytes 589832 | tf_op jit(solution)/shard_map/ppermute | solution.py:125
  170.0 69.0 %collective-permute-start.123 = (bf16[96,1024]{1,0:T(8,128)(2,1)S(1)}, bf16[96,1024]{1,0:T(8,128)(2,1)S(1)}, u32[]{:S(2)}, u32[]{:S(2)}) collective-permute-start(bf16[96,1024]{1,0:T(8,128)(2,1)S(1)} %get-tuple-element.114), channel_id=1, source_target_pairs={{8,0},{10,2},{12,4},{14,6},{16,8},{18,10},{20,12},{22,14},{24,16},... | collective-permute-start | bytes 589832 | tf_op jit(solution)/shard_map/ppermute | solution.py:125
  232.2 47.0 %collective-permute-start.165 = (bf16[32,4096]{1,0:T(8,128)(2,1)S(1)}, bf16[32,4096]{1,0:T(8,128)(2,1)}, u32[]{:S(2)}, u32[]{:S(2)}) collective-permute-start(bf16[32,4096]{1,0:T(8,128)(2,1)S(1)} %copy-done.111), channel_id=1, source_target_pairs={{0,8},{2,10},{4,12},{6,14},{8,16},{10,18},{12,20},{14,22},{16,24},... | collective-permute-start | bytes 786440 | tf_op jit(solution)/shard_map/ppermute | solution.py:121
  236.3 45.9 %collective-permute-start.10 = (bf16[4,32,1024]{2,1,0:T(8,128)(2,1)S(1)}, bf16[4,32,1024]{2,1,0:T(8,128)(2,1)S(1)}, u32[]{:S(2)}, u32[]{:S(2)}) collective-permute-start(bf16[4,32,1024]{2,1,0:T(8,128)(2,1)S(1)} %constant_dynamic-slice_fusion.25.refs_0_), channel_id=1, source_target_pairs={{0,1},{1,0},{2,3},{3,2},{4,5},{5,4},{6,7},{7,6},{8,9},{9,8},{10,11... | collective-permute-start | bytes 786440 | tf_op jit(solution)/shard_map/ppermute | solution.py:128
  282.2 74.4 %collective-permute-start.168 = (bf16[32,4096]{1,0:T(8,128)(2,1)S(1)}, bf16[32,4096]{1,0:T(8,128)(2,1)S(1)}, u32[]{:S(2)}, u32[]{:S(2)}) collective-permute-start(bf16[32,4096]{1,0:T(8,128)(2,1)S(1)} %copy-done.111), channel_id=1, source_target_pairs={{8,0},{10,2},{12,4},{14,6},{16,8},{18,10},{20,12},{22,14},{24,16},... | collective-permute-start | bytes 786440 | tf_op jit(solution)/shard_map/ppermute | solution.py:125
  283.5 73.1 %collective-permute-start.25 = (bf16[4,32,1024]{2,1,0:T(8,128)(2,1)S(1)}, bf16[4,32,1024]{2,1,0:T(8,128)(2,1)S(1)}, u32[]{:S(2)}, u32[]{:S(2)}) collective-permute-start(bf16[4,32,1024]{2,1,0:T(8,128)(2,1)S(1)} %constant_dynamic-slice_fusion.24.refs_0_), channel_id=1, source_target_pairs={{0,1},{1,0},{2,3},{3,2},{4,5},{5,4},{6,7},{7,6},{8,9},{9,8},{10,11... | collective-permute-start | bytes 786440 | tf_op jit(solution)/shard_map/ppermute | solution.py:128
  283.7 81.6 %collective-permute-start.166 = (bf16[32,4096]{1,0:T(8,128)(2,1)}, bf16[32,4096]{1,0:T(8,128)(2,1)}, u32[]{:S(2)}, u32[]{:S(2)}) collective-permute-start(bf16[32,4096]{1,0:T(8,128)(2,1)} %collective-permute-done.165), channel_id=1, source_target_pairs={{8,16},{10,18},{12,20},{14,22},{16,24},{18,26},{20,28},{22,30},{9,... | collective-permute-start | bytes 786440 | tf_op jit(solution)/shard_map/ppermute | solution.py:121
  285.4 78.0 %collective-permute-start.24 = (bf16[4,32,512]{2,1,0:T(8,128)(2,1)}, bf16[4,32,512]{2,1,0:T(8,128)(2,1)}, u32[]{:S(2)}, u32[]{:S(2)}) collective-permute-start(bf16[4,32,512]{2,1,0:T(8,128)(2,1)} %slice.601), channel_id=1, source_target_pairs={{0,2},{2,0},{4,6},{6,4},{8,10},{10,8},{12,14},{14,12},{16,18},{18,... | collective-permute-start | bytes 393224 | tf_op jit(solution)/shard_map/ppermute | solution.py:117
  286.0 77.4 %collective-permute-start.23 = (bf16[4,32,512]{2,1,0:T(8,128)(2,1)}, bf16[4,32,512]{2,1,0:T(8,128)(2,1)}, u32[]{:S(2)}, u32[]{:S(2)}) collective-permute-start(bf16[4,32,512]{2,1,0:T(8,128)(2,1)} %slice.600), channel_id=1, source_target_pairs={{0,4},{2,6},{4,0},{6,2},{8,12},{10,14},{12,8},{14,10},{16,20},{18,... | collective-permute-start | bytes 393224 | tf_op jit(solution)/shard_map/ppermute | solution.py:117
  365.3 76.2 %collective-permute-start.160 = (bf16[4,32,1024]{2,1,0:T(8,128)(2,1)}, bf16[4,32,1024]{2,1,0:T(8,128)(2,1)}, u32[]{:S(2)}, u32[]{:S(2)}) collective-permute-start(bf16[4,32,1024]{2,1,0:T(8,128)(2,1)} %copy-done.68), channel_id=1, source_target_pairs={{0,1},{1,0},{2,3},{3,2},{4,5},{5,4},{6,7},{7,6},{8,9},{9,8},{10,11... | collective-permute-start | bytes 786440 | tf_op jit(solution)/shard_map/ppermute | solution.py:128
  365.4 77.6 %collective-permute-start.85 = (bf16[4,32,1024]{2,1,0:T(8,128)(2,1)}, bf16[4,32,1024]{2,1,0:T(8,128)(2,1)}, u32[]{:S(2)}, u32[]{:S(2)}) collective-permute-start(bf16[4,32,1024]{2,1,0:T(8,128)(2,1)} %copy-done.69), channel_id=1, source_target_pairs={{0,1},{1,0},{2,3},{3,2},{4,5},{5,4},{6,7},{7,6},{8,9},{9,8},{10,11... | collective-permute-start | bytes 786440 | tf_op jit(solution)/shard_map/ppermute | solution.py:128
  365.9 77.9 %collective-permute-start.100 = (bf16[4,32,1024]{2,1,0:T(8,128)(2,1)}, bf16[4,32,1024]{2,1,0:T(8,128)(2,1)}, u32[]{:S(2)}, u32[]{:S(2)}) collective-permute-start(bf16[4,32,1024]{2,1,0:T(8,128)(2,1)} %copy-done.70), channel_id=1, source_target_pairs={{0,1},{1,0},{2,3},{3,2},{4,5},{5,4},{6,7},{7,6},{8,9},{9,8},{10,11... | collective-permute-start | bytes 786440 | tf_op jit(solution)/shard_map/ppermute | solution.py:128
  366.0 80.6 %collective-permute-start.169 = (bf16[32,4096]{1,0:T(8,128)(2,1)}, bf16[32,4096]{1,0:T(8,128)(2,1)}, u32[]{:S(2)}, u32[]{:S(2)}) collective-permute-start(bf16[32,4096]{1,0:T(8,128)(2,1)} %copy-done.112), channel_id=1, source_target_pairs={{8,0},{10,2},{12,4},{14,6},{16,8},{18,10},{20,12},{22,14},{9,1},{1... | collective-permute-start | bytes 786440 | tf_op jit(solution)/shard_map/ppermute | solution.py:125
  367.3 77.1 %collective-permute-start.167 = (bf16[32,4096]{1,0:T(8,128)(2,1)}, bf16[32,4096]{1,0:T(8,128)(2,1)}, u32[]{:S(2)}, u32[]{:S(2)}) collective-permute-start(bf16[32,4096]{1,0:T(8,128)(2,1)} %collective-permute-done.166), channel_id=1, source_target_pairs={{16,24},{18,26},{20,28},{22,30},{17,25},{19,27},{21,29},{23,31}} | collective-permute-start | bytes 786440 | tf_op jit(solution)/shard_map/ppermute | solution.py:121
  461.5 36.0 %collective-permute-start.37 = (bf16[4,96,1024]{2,1,0:T(8,128)(2,1)S(1)}, bf16[4,96,1024]{2,1,0:T(8,128)(2,1)S(1)}, u32[]{:S(2)}, u32[]{:S(2)}) collective-permute-start(bf16[4,96,1024]{2,1,0:T(8,128)(2,1)S(1)} %copy-done.34), channel_id=1, source_target_pairs={{0,4},{2,6},{4,0},{6,2},{8,12},{10,14},{12,8},{14,10},{16,20},{18,... | collective-permute-start | bytes 2359304 | tf_op jit(solution)/shard_map/ppermute | solution.py:117
  514.3 33.8 %collective-permute-start.112 = (bf16[4,96,1024]{2,1,0:T(8,128)(2,1)}, bf16[4,96,1024]{2,1,0:T(8,128)(2,1)}, u32[]{:S(2)}, u32[]{:S(2)}) collective-permute-start(bf16[4,96,1024]{2,1,0:T(8,128)(2,1)} %constant_dynamic-slice_fusion.18.refs_0_), channel_id=1, source_target_pairs={{0,4},{2,6},{4,0},{6,2},{8,12},{10,14},{12,8},{14,10},{16,20},{18,... | collective-permute-start | bytes 2359304 | tf_op jit(solution)/shard_map/ppermute | solution.py:117
  515.1 40.0 %collective-permute-start.111 = (bf16[4,96,1024]{2,1,0:T(8,128)(2,1)}, bf16[4,96,1024]{2,1,0:T(8,128)(2,1)}, u32[]{:S(2)}, u32[]{:S(2)}) collective-permute-start(bf16[4,96,1024]{2,1,0:T(8,128)(2,1)} %constant_dynamic-slice_fusion.18.refs_0_), channel_id=1, source_target_pairs={{0,2},{2,0},{4,6},{6,4},{8,10},{10,8},{12,14},{14,12},{16,18},{18,... | collective-permute-start | bytes 2359304 | tf_op jit(solution)/shard_map/ppermute | solution.py:117
  515.7 49.2 %collective-permute-start.127 = (bf16[4,96,1024]{2,1,0:T(8,128)(2,1)}, bf16[4,96,1024]{2,1,0:T(8,128)(2,1)S(1)}, u32[]{:S(2)}, u32[]{:S(2)}) collective-permute-start(bf16[4,96,1024]{2,1,0:T(8,128)(2,1)} %constant_dynamic-slice_fusion.17.refs_10_), channel_id=1, source_target_pairs={{0,4},{2,6},{4,0},{6,2},{8,12},{10,14},{12,8},{14,10},{16,20},{18,... | collective-permute-start | bytes 2359304 | tf_op jit(solution)/shard_map/ppermute | solution.py:117
  531.3 34.3 %collective-permute-start.126 = (bf16[4,96,1024]{2,1,0:T(8,128)(2,1)}, bf16[4,96,1024]{2,1,0:T(8,128)(2,1)S(1)}, u32[]{:S(2)}, u32[]{:S(2)}) collective-permute-start(bf16[4,96,1024]{2,1,0:T(8,128)(2,1)} %constant_dynamic-slice_fusion.17.refs_10_), channel_id=1, source_target_pairs={{0,2},{2,0},{4,6},{6,4},{8,10},{10,8},{12,14},{14,12},{16,18},{18,... | collective-permute-start | bytes 2359304 | tf_op jit(solution)/shard_map/ppermute | solution.py:117
  532.0 42.0 %collective-permute-start.39 = (bf16[4,96,512]{2,1,0:T(8,128)(2,1)S(1)}, bf16[4,96,512]{2,1,0:T(8,128)(2,1)S(1)}, u32[]{:S(2)}, u32[]{:S(2)}) collective-permute-start(bf16[4,96,512]{2,1,0:T(8,128)(2,1)S(1)} %slice.607), channel_id=1, source_target_pairs={{0,2},{2,0},{4,6},{6,4},{8,10},{10,8},{12,14},{14,12},{16,18},{18,... | collective-permute-start | bytes 1179656 | tf_op jit(solution)/shard_map/ppermute | solution.py:117
  548.1 68.4 %collective-permute-start.172 = (bf16[4,32,4096]{2,1,0:T(8,128)(2,1)S(1)}, bf16[4,32,4096]{2,1,0:T(8,128)(2,1)S(1)}, u32[]{:S(2)}, u32[]{:S(2)}) collective-permute-start(bf16[4,32,4096]{2,1,0:T(8,128)(2,1)S(1)} %constant_dynamic-slice_fusion.14.refs_0_), channel_id=1, source_target_pairs={{0,4},{2,6},{4,0},{6,2},{8,12},{10,14},{12,8},{14,10},{16,20},{18,... | collective-permute-start | bytes 3145736 | tf_op jit(solution)/shard_map/ppermute | solution.py:117
  555.2 61.9 %collective-permute-start.171 = (bf16[4,32,4096]{2,1,0:T(8,128)(2,1)S(1)}, bf16[4,32,4096]{2,1,0:T(8,128)(2,1)S(1)}, u32[]{:S(2)}, u32[]{:S(2)}) collective-permute-start(bf16[4,32,4096]{2,1,0:T(8,128)(2,1)S(1)} %constant_dynamic-slice_fusion.14.refs_0_), channel_id=1, source_target_pairs={{0,2},{2,0},{4,6},{6,4},{8,10},{10,8},{12,14},{14,12},{16,18},{18,... | collective-permute-start | bytes 3145736 | tf_op jit(solution)/shard_map/ppermute | solution.py:117
  565.6 39.3 %collective-permute-start.54 = (bf16[4,96,512]{2,1,0:T(8,128)(2,1)S(1)}, bf16[4,96,512]{2,1,0:T(8,128)(2,1)S(1)}, u32[]{:S(2)}, u32[]{:S(2)}) collective-permute-start(bf16[4,96,512]{2,1,0:T(8,128)(2,1)S(1)} %slice.609), channel_id=1, source_target_pairs={{0,2},{2,0},{4,6},{6,4},{8,10},{10,8},{12,14},{14,12},{16,18},{18,... | collective-permute-start | bytes 1179656 | tf_op jit(solution)/shard_map/ppermute | solution.py:117
  620.5 211.8 %collective-permute-start.56 = (bf16[4,96,1024]{2,1,0:T(8,128)(2,1)}, bf16[4,96,1024]{2,1,0:T(8,128)(2,1)}, u32[]{:S(2)}, u32[]{:S(2)}) collective-permute-start(bf16[4,96,1024]{2,1,0:T(8,128)(2,1)} %collective-permute-done.51.refs_11_), channel_id=1, source_target_pairs={{0,1},{1,0},{2,3},{3,2},{4,5},{5,4},{6,7},{7,6},{8,9},{9,8},{10,11... | collective-permute-start | bytes 2359304 | tf_op jit(solution)/shard_map/ppermute | solution.py:128
  620.9 211.9 %collective-permute-start.72 = (bf16[4,96,1024]{2,1,0:T(8,128)(2,1)}, bf16[4,96,1024]{2,1,0:T(8,128)(2,1)}, u32[]{:S(2)}, u32[]{:S(2)}) collective-permute-start(bf16[4,96,1024]{2,1,0:T(8,128)(2,1)} %collective-permute-done.67.refs_22_), channel_id=1, source_target_pairs={{0,1},{1,0},{2,3},{3,2},{4,5},{5,4},{6,7},{7,6},{8,9},{9,8},{10,11... | collective-permute-start | bytes 2359304 | tf_op jit(solution)/shard_map/ppermute | solution.py:128
  621.0 212.6 %collective-permute-start.71 = (bf16[4,96,1024]{2,1,0:T(8,128)(2,1)}, bf16[4,96,1024]{2,1,0:T(8,128)(2,1)}, u32[]{:S(2)}, u32[]{:S(2)}) collective-permute-start(bf16[4,96,1024]{2,1,0:T(8,128)(2,1)} %collective-permute-done.66.refs_21_), channel_id=1, source_target_pairs={{0,1},{1,0},{2,3},{3,2},{4,5},{5,4},{6,7},{7,6},{8,9},{9,8},{10,11... | collective-permute-start | bytes 2359304 | tf_op jit(solution)/shard_map/ppermute | solution.py:128
  624.6 207.7 %collective-permute-start.74 = (bf16[4,96,512]{2,1,0:T(8,128)(2,1)}, bf16[4,96,512]{2,1,0:T(8,128)(2,1)}, u32[]{:S(2)}, u32[]{:S(2)}) collective-permute-start(bf16[4,96,512]{2,1,0:T(8,128)(2,1)} %collective-permute-done.69.refs_24_), channel_id=1, source_target_pairs={{0,1},{1,0},{2,3},{3,2},{4,5},{5,4},{6,7},{7,6},{8,9},{9,8},{10,11... | collective-permute-start | bytes 1179656 | tf_op jit(solution)/shard_map/ppermute | solution.py:128
  625.5 207.4 %collective-permute-start.73 = (bf16[4,96,512]{2,1,0:T(8,128)(2,1)}, bf16[4,96,512]{2,1,0:T(8,128)(2,1)}, u32[]{:S(2)}, u32[]{:S(2)}) collective-permute-start(bf16[4,96,512]{2,1,0:T(8,128)(2,1)} %collective-permute-done.68.refs_23_), channel_id=1, source_target_pairs={{0,1},{1,0},{2,3},{3,2},{4,5},{5,4},{6,7},{7,6},{8,9},{9,8},{10,11... | collective-permute-start | bytes 1179656 | tf_op jit(solution)/shard_map/ppermute | solution.py:128
  832.3 610.0 %collective-permute-start.145 = (bf16[4,96,1024]{2,1,0:T(8,128)(2,1)}, bf16[4,96,1024]{2,1,0:T(8,128)(2,1)}, u32[]{:S(2)}, u32[]{:S(2)}) collective-permute-start(bf16[4,96,1024]{2,1,0:T(8,128)(2,1)} %constant_dynamic-slice_fusion.16.refs_20_), channel_id=1, source_target_pairs={{0,1},{1,0},{2,3},{3,2},{4,5},{5,4},{6,7},{7,6},{8,9},{9,8},{10,11... | collective-permute-start | bytes 2359304 | tf_op jit(solution)/shard_map/ppermute | solution.py:128
  832.4 613.5 %collective-permute-start.115 = (bf16[4,96,1024]{2,1,0:T(8,128)(2,1)}, bf16[4,96,1024]{2,1,0:T(8,128)(2,1)}, u32[]{:S(2)}, u32[]{:S(2)}) collective-permute-start(bf16[4,96,1024]{2,1,0:T(8,128)(2,1)} %constant_dynamic-slice_fusion.18.refs_0_), channel_id=1, source_target_pairs={{0,1},{1,0},{2,3},{3,2},{4,5},{5,4},{6,7},{7,6},{8,9},{9,8},{10,11... | collective-permute-start | bytes 2359304 | tf_op jit(solution)/shard_map/ppermute | solution.py:128
  832.8 614.0 %collective-permute-start.130 = (bf16[4,96,1024]{2,1,0:T(8,128)(2,1)}, bf16[4,96,1024]{2,1,0:T(8,128)(2,1)}, u32[]{:S(2)}, u32[]{:S(2)}) collective-permute-start(bf16[4,96,1024]{2,1,0:T(8,128)(2,1)} %constant_dynamic-slice_fusion.17.refs_10_), channel_id=1, source_target_pairs={{0,1},{1,0},{2,3},{3,2},{4,5},{5,4},{6,7},{7,6},{8,9},{9,8},{10,11... | collective-permute-start | bytes 2359304 | tf_op jit(solution)/shard_map/ppermute | solution.py:128
  832.9 614.7 %collective-permute-start.144 = (bf16[4,96,512]{2,1,0:T(8,128)(2,1)}, bf16[4,96,512]{2,1,0:T(8,128)(2,1)}, u32[]{:S(2)}, u32[]{:S(2)}) collective-permute-start(bf16[4,96,512]{2,1,0:T(8,128)(2,1)} %slice.627), channel_id=1, source_target_pairs={{0,2},{2,0},{4,6},{6,4},{8,10},{10,8},{12,14},{14,12},{16,18},{18,... | collective-permute-start | bytes 1179656 | tf_op jit(solution)/shard_map/ppermute | solution.py:117
  833.6 615.4 %collective-permute-start.143 = (bf16[4,96,512]{2,1,0:T(8,128)(2,1)}, bf16[4,96,512]{2,1,0:T(8,128)(2,1)}, u32[]{:S(2)}, u32[]{:S(2)}) collective-permute-start(bf16[4,96,512]{2,1,0:T(8,128)(2,1)} %slice.626), channel_id=1, source_target_pairs={{0,4},{2,6},{4,0},{6,2},{8,12},{10,14},{12,8},{14,10},{16,20},{18,... | collective-permute-start | bytes 1179656 | tf_op jit(solution)/shard_map/ppermute | solution.py:117
  1501.9 586.4 %collective-permute-start.175 = (bf16[4,32,4096]{2,1,0:T(8,128)(2,1)}, bf16[4,32,4096]{2,1,0:T(8,128)(2,1)}, u32[]{:S(2)}, u32[]{:S(2)}) collective-permute-start(bf16[4,32,4096]{2,1,0:T(8,128)(2,1)} %copy-done.30), channel_id=1, source_target_pairs={{0,1},{1,0},{2,3},{3,2},{4,5},{5,4},{6,7},{7,6},{8,9},{9,8},{10,11... | collective-permute-start | bytes 3145736 | tf_op jit(solution)/shard_map/ppermute | solution.py:128
  1502.0 585.3 %collective-permute-start.174 = (bf16[4,32,2048]{2,1,0:T(8,128)(2,1)}, bf16[4,32,2048]{2,1,0:T(8,128)(2,1)}, u32[]{:S(2)}, u32[]{:S(2)}) collective-permute-start(bf16[4,32,2048]{2,1,0:T(8,128)(2,1)} %slice.635), channel_id=1, source_target_pairs={{0,2},{2,0},{4,6},{6,4},{8,10},{10,8},{12,14},{14,12},{16,18},{18,... | collective-permute-start | bytes 1572872 | tf_op jit(solution)/shard_map/ppermute | solution.py:117
  1502.7 584.7 %collective-permute-start.173 = (bf16[4,32,2048]{2,1,0:T(8,128)(2,1)}, bf16[4,32,2048]{2,1,0:T(8,128)(2,1)}, u32[]{:S(2)}, u32[]{:S(2)}) collective-permute-start(bf16[4,32,2048]{2,1,0:T(8,128)(2,1)} %slice.634), channel_id=1, source_target_pairs={{0,4},{2,6},{4,0},{6,2},{8,12},{10,14},{12,8},{14,10},{16,20},{18,... | collective-permute-start | bytes 1572872 | tf_op jit(solution)/shard_map/ppermute | solution.py:117
  1503.4 586.2 %collective-permute-start.177 = (bf16[4,32,4096]{2,1,0:T(8,128)(2,1)}, bf16[4,32,4096]{2,1,0:T(8,128)(2,1)}, u32[]{:S(2)}, u32[]{:S(2)}) collective-permute-start(bf16[4,32,4096]{2,1,0:T(8,128)(2,1)} %copy-done.41), channel_id=1, source_target_pairs={{0,1},{1,0},{2,3},{3,2},{4,5},{5,4},{6,7},{7,6},{8,9},{9,8},{10,11... | collective-permute-start | bytes 3145736 | tf_op jit(solution)/shard_map/ppermute | solution.py:128
  1503.4 586.9 %collective-permute-start.176 = (bf16[4,32,4096]{2,1,0:T(8,128)(2,1)}, bf16[4,32,4096]{2,1,0:T(8,128)(2,1)}, u32[]{:S(2)}, u32[]{:S(2)}) collective-permute-start(bf16[4,32,4096]{2,1,0:T(8,128)(2,1)} %copy-done.43), channel_id=1, source_target_pairs={{0,1},{1,0},{2,3},{3,2},{4,5},{5,4},{6,7},{7,6},{8,9},{9,8},{10,11... | collective-permute-start | bytes 3145736 | tf_op jit(solution)/shard_map/ppermute | solution.py:128
  2457.2 194.1 %collective-permute-start.235 = (bf16[4,4,32,1024]{3,2,0,1:T(8,128)(2,1)}, bf16[4,4,32,1024]{3,2,0,1:T(8,128)(2,1)}, u32[]{:S(2)}, u32[]{:S(2)}) collective-permute-start(bf16[4,4,32,1024]{3,2,0,1:T(8,128)(2,1)} %bitcast.678), channel_id=1, source_target_pairs={{0,1},{1,0},{2,3},{3,2},{4,5},{5,4},{6,7},{7,6},{8,9},{9,8},{10,11... | collective-permute-start | bytes 3145736 | tf_op jit(solution)/shard_map/ppermute | solution.py:128
  2457.3 196.8 %collective-permute-start.246 = (bf16[4,4,32,1024]{3,2,0,1:T(8,128)(2,1)}, bf16[4,4,32,1024]{3,2,0,1:T(8,128)(2,1)}, u32[]{:S(2)}, u32[]{:S(2)}) collective-permute-start(bf16[4,4,32,1024]{3,2,0,1:T(8,128)(2,1)} %bitcast.677), channel_id=1, source_target_pairs={{0,1},{1,0},{2,3},{3,2},{4,5},{5,4},{6,7},{7,6},{8,9},{9,8},{10,11... | collective-permute-start | bytes 3145736 | tf_op jit(solution)/shard_map/ppermute | solution.py:128
  2466.2 368.3 %collective-permute-start.257 = (bf16[4,4,32,4096]{3,2,0,1:T(8,128)(2,1)}, bf16[4,4,32,4096]{3,2,0,1:T(8,128)(2,1)}, u32[]{:S(2)}, u32[]{:S(2)}) collective-permute-start(bf16[4,4,32,4096]{3,2,0,1:T(8,128)(2,1)} %bitcast.676), channel_id=1, source_target_pairs={{0,1},{1,0},{2,3},{3,2},{4,5},{5,4},{6,7},{7,6},{8,9},{9,8},{10,11... | collective-permute-start | bytes 12582920 | tf_op jit(solution)/shard_map/ppermute | solution.py:128
  2593.1 62.8 %collective-permute-start.191 = (bf16[4,4,32,1024]{3,2,0,1:T(8,128)(2,1)}, bf16[4,4,32,1024]{3,2,0,1:T(8,128)(2,1)}, u32[]{:S(2)}, u32[]{:S(2)}) collective-permute-start(bf16[4,4,32,1024]{3,2,0,1:T(8,128)(2,1)} %bitcast.680), channel_id=1, source_target_pairs={{0,1},{1,0},{2,3},{3,2},{4,5},{5,4},{6,7},{7,6},{8,9},{9,8},{10,11... | collective-permute-start | bytes 3145736 | tf_op jit(solution)/shard_map/ppermute | solution.py:128
  2593.3 64.3 %collective-permute-start.202 = (bf16[4,4,32,1024]{3,2,0,1:T(8,128)(2,1)}, bf16[4,4,32,1024]{3,2,0,1:T(8,128)(2,1)}, u32[]{:S(2)}, u32[]{:S(2)}) collective-permute-start(bf16[4,4,32,1024]{3,2,0,1:T(8,128)(2,1)} %bitcast.679), channel_id=1, source_target_pairs={{0,1},{1,0},{2,3},{3,2},{4,5},{5,4},{6,7},{7,6},{8,9},{9,8},{10,11... | collective-permute-start | bytes 3145736 | tf_op jit(solution)/shard_map/ppermute | solution.py:128
  2696.4 162.2 %collective-permute-start.213 = (bf16[4,4,288,1024]{3,2,0,1:T(8,128)(2,1)S(1)}, bf16[4,4,288,1024]{3,2,0,1:T(8,128)(2,1)}, u32[]{:S(2)}, u32[]{:S(2)}) collective-permute-start(bf16[4,4,288,1024]{3,2,0,1:T(8,128)(2,1)S(1)} %bitcast.703), channel_id=1, source_target_pairs={{0,1},{1,0},{2,3},{3,2},{4,5},{5,4},{6,7},{7,6},{8,9},{9,8},{10,11... | collective-permute-start | bytes 28311560 | tf_op jit(solution)/shard_map/ppermute | solution.py:128
  2698.0 171.8 %collective-permute-start.224 = (bf16[4,4,288,1024]{3,2,0,1:T(8,128)(2,1)}, bf16[4,4,288,1024]{3,2,0,1:T(8,128)(2,1)}, u32[]{:S(2)}, u32[]{:S(2)}) collective-permute-start(bf16[4,4,288,1024]{3,2,0,1:T(8,128)(2,1)} %bitcast.674), channel_id=1, source_target_pairs={{0,1},{1,0},{2,3},{3,2},{4,5},{5,4},{6,7},{7,6},{8,9},{9,8},{10,11... | collective-permute-start | bytes 28311560 | tf_op jit(solution)/shard_map/ppermute | solution.py:128
  2775.1 34.0 %collective-permute-start.245 = (bf16[32,1024]{1,0:T(8,128)(2,1)S(1)}, bf16[32,1024]{1,0:T(8,128)(2,1)S(1)}, u32[]{:S(2)}, u32[]{:S(2)}) collective-permute-start(bf16[32,1024]{1,0:T(8,128)(2,1)S(1)} %fusion.111), channel_id=1, source_target_pairs={{8,0},{10,2},{12,4},{14,6},{16,8},{18,10},{20,12},{22,14},{24,16},... | collective-permute-start | bytes 196616 | tf_op jit(solution)/shard_map/ppermute | solution.py:125
  2776.5 34.3 %collective-permute-start.253 = (bf16[32,1024]{1,0:T(8,128)(2,1)S(1)}, bf16[32,1024]{1,0:T(8,128)(2,1)S(1)}, u32[]{:S(2)}, u32[]{:S(2)}) collective-permute-start(bf16[32,1024]{1,0:T(8,128)(2,1)S(1)} %get-tuple-element.131), channel_id=1, source_target_pairs={{0,8},{2,10},{4,12},{6,14},{8,16},{10,18},{12,20},{14,22},{16,24},... | collective-permute-start | bytes 196616 | tf_op jit(solution)/shard_map/ppermute | solution.py:121
  2855.4 82.7 %collective-permute-start.261 = (bf16[4,32,4096]{2,1,0:T(8,128)(2,1)}, bf16[4,32,4096]{2,1,0:T(8,128)(2,1)}, u32[]{:S(2)}, u32[]{:S(2)}) collective-permute-start(bf16[4,32,4096]{2,1,0:T(8,128)(2,1)} %pad_maximum_fusion.6), channel_id=1, source_target_pairs={{0,4},{2,6},{4,0},{6,2},{8,12},{10,14},{12,8},{14,10},{16,20},{18,... | collective-permute-start | bytes 3145736 | tf_op jit(solution)/shard_map/ppermute | solution.py:117
  2857.9 86.3 %collective-permute-start.259 = (bf16[4,32,4096]{2,1,0:T(8,128)(2,1)}, bf16[4,32,4096]{2,1,0:T(8,128)(2,1)}, u32[]{:S(2)}, u32[]{:S(2)}) collective-permute-start(bf16[4,32,4096]{2,1,0:T(8,128)(2,1)} %pad_maximum_fusion.5), channel_id=1, source_target_pairs={{0,2},{2,0},{4,6},{6,4},{8,10},{10,8},{12,14},{14,12},{16,18},{18,... | collective-permute-start | bytes 3145736 | tf_op jit(solution)/shard_map/ppermute | solution.py:117
  2867.8 41.3 %collective-permute-start.214 = (bf16[4,288,512]{2,1,0:T(8,128)(2,1)}, bf16[4,288,512]{2,1,0:T(8,128)(2,1)}, u32[]{:S(2)}, u32[]{:S(2)}) collective-permute-start(bf16[4,288,512]{2,1,0:T(8,128)(2,1)} %get-tuple-element.75), channel_id=1, source_target_pairs={{0,4},{2,6},{4,0},{6,2},{8,12},{10,14},{12,8},{14,10},{16,20},{18,... | collective-permute-start | bytes 3538952 | tf_op jit(solution)/shard_map/ppermute | solution.py:117
  2868.4 37.1 %collective-permute-start.216 = (bf16[4,288,512]{2,1,0:T(8,128)(2,1)}, bf16[4,288,512]{2,1,0:T(8,128)(2,1)}, u32[]{:S(2)}, u32[]{:S(2)}) collective-permute-start(bf16[4,288,512]{2,1,0:T(8,128)(2,1)} %get-tuple-element.76), channel_id=1, source_target_pairs={{0,2},{2,0},{4,6},{6,4},{8,10},{10,8},{12,14},{14,12},{16,18},{18,... | collective-permute-start | bytes 3538952 | tf_op jit(solution)/shard_map/ppermute | solution.py:117
  2892.4 35.6 %collective-permute-start.227 = (bf16[4,288,512]{2,1,0:T(8,128)(2,1)}, bf16[4,288,512]{2,1,0:T(8,128)(2,1)}, u32[]{:S(2)}, u32[]{:S(2)}) collective-permute-start(bf16[4,288,512]{2,1,0:T(8,128)(2,1)} %get-tuple-element.78), channel_id=1, source_target_pairs={{0,2},{2,0},{4,6},{6,4},{8,10},{10,8},{12,14},{14,12},{16,18},{18,... | collective-permute-start | bytes 3538952 | tf_op jit(solution)/shard_map/ppermute | solution.py:117
  2909.1 76.3 %collective-permute-start.217 = (bf16[4,288,1024]{2,1,0:T(8,128)(2,1)S(1)}, bf16[4,288,1024]{2,1,0:T(8,128)(2,1)}, u32[]{:S(2)}, u32[]{:S(2)}) collective-permute-start(bf16[4,288,1024]{2,1,0:T(8,128)(2,1)S(1)} %pad_maximum_fusion.1), channel_id=1, source_target_pairs={{0,4},{2,6},{4,0},{6,2},{8,12},{10,14},{12,8},{14,10},{16,20},{18,... | collective-permute-start | bytes 7077896 | tf_op jit(solution)/shard_map/ppermute | solution.py:117
  2928.0 60.8 %collective-permute-start.215 = (bf16[4,288,1024]{2,1,0:T(8,128)(2,1)}, bf16[4,288,1024]{2,1,0:T(8,128)(2,1)}, u32[]{:S(2)}, u32[]{:S(2)}) collective-permute-start(bf16[4,288,1024]{2,1,0:T(8,128)(2,1)} %pad_maximum_fusion), channel_id=1, source_target_pairs={{0,2},{2,0},{4,6},{6,4},{8,10},{10,8},{12,14},{14,12},{16,18},{18,... | collective-permute-start | bytes 7077896 | tf_op jit(solution)/shard_map/ppermute | solution.py:117
  2935.3 75.4 %collective-permute-start.228 = (bf16[4,288,1024]{2,1,0:T(8,128)(2,1)}, bf16[4,288,1024]{2,1,0:T(8,128)(2,1)}, u32[]{:S(2)}, u32[]{:S(2)}) collective-permute-start(bf16[4,288,1024]{2,1,0:T(8,128)(2,1)} %pad_maximum_fusion.3), channel_id=1, source_target_pairs={{0,4},{2,6},{4,0},{6,2},{8,12},{10,14},{12,8},{14,10},{16,20},{18,... | collective-permute-start | bytes 7077896 | tf_op jit(solution)/shard_map/ppermute | solution.py:117
  2938.1 74.0 %collective-permute-start.226 = (bf16[4,288,1024]{2,1,0:T(8,128)(2,1)}, bf16[4,288,1024]{2,1,0:T(8,128)(2,1)}, u32[]{:S(2)}, u32[]{:S(2)}) collective-permute-start(bf16[4,288,1024]{2,1,0:T(8,128)(2,1)} %pad_maximum_fusion.2), channel_id=1, source_target_pairs={{0,2},{2,0},{4,6},{6,4},{8,10},{10,8},{12,14},{14,12},{16,18},{18,... | collective-permute-start | bytes 7077896 | tf_op jit(solution)/shard_map/ppermute | solution.py:117
  2946.9 74.3 %collective-permute-start.262 = (bf16[32,4096]{1,0:T(8,128)(2,1)S(1)}, bf16[32,4096]{1,0:T(8,128)(2,1)S(1)}, u32[]{:S(2)}, u32[]{:S(2)}) collective-permute-start(bf16[32,4096]{1,0:T(8,128)(2,1)S(1)} %get-tuple-element.81), channel_id=1, source_target_pairs={{0,8},{2,10},{4,12},{6,14},{1,9},{3,11},{5,13},{7,15}} | collective-permute-start | bytes 786440 | tf_op jit(solution)/shard_map/ppermute | solution.py:121
  2985.4 52.0 %collective-permute-start.265 = (bf16[32,4096]{1,0:T(8,128)(2,1)S(1)}, bf16[32,4096]{1,0:T(8,128)(2,1)S(1)}, u32[]{:S(2)}, u32[]{:S(2)}) collective-permute-start(bf16[32,4096]{1,0:T(8,128)(2,1)S(1)} %get-tuple-element.82), channel_id=1, source_target_pairs={{24,16},{26,18},{28,20},{30,22},{25,17},{27,19},{29,21},{31,23}} | collective-permute-start | bytes 786440 | tf_op jit(solution)/shard_map/ppermute | solution.py:125
  3039.2 38.6 %collective-permute-start.264 = (bf16[32,4096]{1,0:T(8,128)(2,1)S(1)}, bf16[32,4096]{1,0:T(8,128)(2,1)S(1)}, u32[]{:S(2)}, u32[]{:S(2)}) collective-permute-start(bf16[32,4096]{1,0:T(8,128)(2,1)S(1)} %get-tuple-element.79), channel_id=1, source_target_pairs={{0,8},{2,10},{4,12},{6,14},{8,16},{10,18},{12,20},{14,22},{16,24},... | collective-permute-start | bytes 786440 | tf_op jit(solution)/shard_map/ppermute | solution.py:121
  3077.8 33.7 %collective-permute-start.234 = (bf16[288,1024]{1,0:T(8,128)(2,1)S(1)}, bf16[288,1024]{1,0:T(8,128)(2,1)S(1)}, u32[]{:S(2)}, u32[]{:S(2)}) collective-permute-start(bf16[288,1024]{1,0:T(8,128)(2,1)S(1)} %fusion.50), channel_id=1, source_target_pairs={{8,0},{10,2},{12,4},{14,6},{16,8},{18,10},{20,12},{22,14},{24,16},... | collective-permute-start | bytes 1769480 | tf_op jit(solution)/shard_map/ppermute | solution.py:125
  (384 other events, 6681.7 us)

commit v2 on v0

v2 whole, which is shorter than its diff:
```python
import functools

import jax
import jax.numpy as jnp
from jax import lax
from jax.experimental import pallas as pl
from jax.experimental.pallas import tpu as pltpu
from jax.sharding import PartitionSpec as P

C = 1024
G = 24
PLANE = 4
TILE = 256
ROWS = 48
PAD = 24
MISC = 16
HEAD = 1664
VMEM = 60 * 1024 * 1024


def low(value):
    return value.astype(jnp.bfloat16)


def wide(value):
    return value.astype(jnp.float32)


def dot(left, right):
    return jnp.dot(left, right, preferred_element_type=jnp.float32)


def dot_rows(left, right):
    return lax.dot_general(left, right, (((1,), (1,)), ((), ())), preferred_element_type=jnp.float32)


def dot_sums(left, right):
    return lax.dot_general(left, right, (((0,), (0,)), ((), ())), preferred_element_type=jnp.float32)


def sigmoid(value):
    return 1.0 / (1.0 + jnp.exp(-value))


def centered(value):
    center = value - jnp.mean(value, axis=-1, keepdims=True)
    spread = jnp.mean(center * center, axis=-1, keepdims=True)
    scale = lax.rsqrt(spread + 1e-05)
    return center * scale, scale


def norm_back(grad, normal, scale, gain):
    inner = grad * gain
    first = jnp.mean(inner, axis=-1, keepdims=True)
    second = jnp.mean(inner * normal, axis=-1, keepdims=True)
    return scale * (inner - first - normal * second)


def silu_back(value):
    gate = sigmoid(value)
    return gate * (1.0 + value * (1.0 - gate))


def tiles(extent, size, body):
    def step(i, carry):
        body(pl.ds(pl.multiple_of(i * size, size), size))
        return carry

    lax.fori_loop(0, extent // size, step, 0)


def fold(value):
    return jnp.sum(value.reshape(-1, 8, value.shape[-1]), axis=0)


def columns_of(cells, side, lanes):
    index = lax.broadcasted_iota(jnp.int32, (cells, lanes), 0).astype(jnp.float32)
    return index - side * jnp.floor((index + 0.5) * (1.0 / side))


def beside(value, side, step):
    cells = value.shape[0]
    column = columns_of(cells, side, value.shape[1])
    inside = column < side - 1 if step > 0 else column > 0
    return jnp.where(inside, pltpu.roll(value, (cells - step) % cells, 0), 0.0)


class Blocks:
    def __init__(self, parts, block_rows, columns=slice(None)):
        self.parts = parts
        self.block_rows = block_rows
        self.columns = columns
        self.operands = [array for part in parts for array in part[0]]
        self.copies = sum(array.shape[0] for array in self.operands)

    def bind(self, refs, places, matrix, sems, to_blocks=False, base=0):
        made = []
        number = 0
        for arrays, source, rows, target in self.parts:
            offset = 0
            for array in arrays:
                count = array.shape[0]
                for i in range(count):
                    at = target
                    if count > 1:
                        at = pl.multiple_of(places[offset + i] * self.block_rows + target, 16)
                    inside = matrix.at[pl.ds(at, rows), :]
                    outside = refs[number].at[i, pl.ds(source, rows), self.columns]
                    pair = (inside, outside) if to_blocks else (outside, inside)
                    made.append(pltpu.make_async_copy(*pair, sems.at[base + len(made)]))
                offset += count
                number += 1
        return made


def start(copies):
    for copy in copies:
        copy.start()


def wait(copies):
    for copy in copies:
        copy.wait()


ANY = pl.BlockSpec(memory_space=pl.ANY)
IN = pl.BlockSpec(memory_space=pltpu.VMEM)
SMEM = pl.BlockSpec(memory_space=pltpu.SMEM)


def call(kernel, name, ins, in_specs, outs, out_specs, scratch, flops, moved):
    return pl.pallas_call(
        kernel,
        name=name,
        out_shape=outs,
        in_specs=in_specs,
        out_specs=out_specs,
        scratch_shapes=scratch,
        compiler_params=pltpu.CompilerParams(vmem_limit_bytes=VMEM),
        cost_estimate=pl.CostEstimate(flops=int(flops), bytes_accessed=int(moved), transcendentals=0),
    )(*ins)


def shaped(*shape, dtype=jnp.float32):
    return jax.ShapeDtypeStruct(shape, dtype)


def forward_block(places, number, side, stream, features, misc, w_first, w_middle, w_last):
    cells = side * side
    opening = features is not None
    n_first, n_middle, n_last = len(w_first.operands), len(w_middle.operands), len(w_last.operands)
    given = [features] if opening else [stream, misc]
    given_count = len(given)
    bf16 = jnp.bfloat16

    def kernel(places_ref, *refs):
        refs = list(refs)
        heads = [refs.pop(0) for _ in range(given_count)]
        firsts = [refs.pop(0) for _ in range(n_first)]
        middles = [refs.pop(0) for _ in range(n_middle)]
        lasts = [refs.pop(0) for _ in range(n_last)]
        if opening:
            misc_ref, u_ref = refs.pop(0), refs.pop(0)
        else:
            u_ref, misc_ref = heads
        result_ref, pre1, pre2, pre3, act1 = [refs.pop(0) for _ in range(5)]
        wi, wm, wo, taps, lowered, above, below, work, pairs, sems = refs
        first_copies = w_first.bind(firsts, places_ref, wi, sems)
        middle_copies = w_middle.bind(middles, places_ref, wm, sems, base=len(first_copies))
        last_copies = w_last.bind(lasts, places_ref, wo, sems, base=len(first_copies) + len(middle_copies))
        start(first_copies)
        start(middle_copies)
        start(last_copies)
        wait(first_copies)
        if opening:

            def place(cut):
                turned = jnp.transpose(wide(wi[cut, C:HEAD]))
                u_ref[:, cut] = wide(heads[0][:, cut]) + turned[:cells]
                misc_ref[:, cut] = turned[cells : cells + MISC]

            tiles(C, 128, place)

        def lower(rows):
            lowered[rows, :] = low(u_ref[rows, :])

        tiles(cells, ROWS, lower)

        def first(cut):
            pre1[:, cut] = dot(lowered[...], wi[:, cut])

        tiles(C, TILE, first)

        def norm_act(source, target, norm):
            gain = misc_ref[3 * number + norm : 3 * number + norm + 1, :]
            bias = misc_ref[6 + 3 * number + norm : 7 + 3 * number + norm, :]

            def rows_of(rows):
                normal, _ = centered(source[rows, :])
                hidden = normal * gain + bias
                target[rows, :] = hidden * sigmoid(hidden)

            tiles(cells, ROWS, rows_of)

        norm_act(pre1, work, 0)

        def spread(i, carry):
            cut = pl.ds(pl.multiple_of(i * 128, 128), 128)
            value = work[:, cut]
            act1[:, cut] = low(value)
            taps[:, pl.ds(pl.multiple_of(i * 128, 128), 128)] = low(beside(value, side, -1))
            taps[:, pl.ds(pl.multiple_of(C + i * 128, 128), 128)] = low(value)
            taps[:, pl.ds(pl.multiple_of(2 * C + i * 128, 128), 128)] = low(beside(value, side, 1))
            return carry

        lax.fori_loop(0, C // 128, spread, 0)
        zeros = jnp.zeros((PAD, TILE), jnp.float32)
        for ref in (above, below):
            ref[:PAD, :] = zeros
            ref[PAD + cells :, :] = zeros
        wait(middle_copies)

        def middle(cut):
            above[PAD : PAD + cells, :] = dot(taps[...], wm[0 : 3 * C, cut])
            below[PAD : PAD + cells, :] = dot(taps[...], wm[6 * C : 9 * C, cut])
            same = dot(taps[...], wm[3 * C : 6 * C, cut])
            pre2[:, cut] = same + above[PAD - side : PAD - side + cells, :] + below[PAD + side : PAD + side + cells, :]

        tiles(C, TILE, middle)
        norm_act(pre2, work, 1)

        def lower_second(rows):
            lowered[rows, :] = low(work[rows, :])

        tiles(cells, ROWS, lower_second)
        wait(last_copies)

        def last(cut):
            pre3[:, cut] = dot(lowered[...], wo[:, cut])

        tiles(C, TILE, last)
        gain = misc_ref[3 * number + 2 : 3 * number + 3, :]
        bias = misc_ref[8 + 3 * number : 9 + 3 * number, :]

        def close(rows):
            normal, _ = centered(pre3[rows, :])
            total = u_ref[rows, :] + (normal * gain + bias)
            value = total * sigmoid(total)
            if opening:
                work[rows, :] = value
            else:
                result_ref[rows, :] = low(value)

        tiles(cells, ROWS, close)
        if opening:
            half = side // 2

            def pool(cut):
                value = work[:, cut].reshape(half, 2, side, 128)
                pairs[...] = (value[:, 0] + value[:, 1]).reshape(half * side, 128)
                result_ref[:, cut] = 0.25 * (
                    pairs[pl.ds(0, half * half, 2), :] + pairs[pl.ds(1, half * half, 2), :]
                )

            tiles(C, 128, pool)

    outs, out_specs = [], []
    if opening:
        outs += [shaped(MISC, C), shaped(cells, C), shaped(cells // 4, C)]
    else:
        outs += [shaped(cells, C, dtype=bf16)]
    outs += [shaped(cells, C)] * 3 + [shaped(cells, C, dtype=bf16)]
    copies = w_first.copies + w_middle.copies + w_last.copies
    scratch = [
        pltpu.VMEM((C, HEAD if opening else C), bf16),
        pltpu.VMEM((9 * C, C), bf16),
        pltpu.VMEM((C, C), bf16),
        pltpu.VMEM((cells, 3 * C), bf16),
        pltpu.VMEM((cells, C), bf16),
        pltpu.VMEM((cells + 2 * PAD, TILE), jnp.float32),
        pltpu.VMEM((cells + 2 * PAD, TILE), jnp.float32),
        pltpu.VMEM((cells, C), jnp.float32),
        pltpu.VMEM((cells // 2, 128), jnp.float32),
        pltpu.SemaphoreType.DMA((copies,)),
    ]
    weights = w_first.operands + w_middle.operands + w_last.operands
    return call(
        kernel,
        "forward_block",
        [places] + given + weights,
        [SMEM] + [IN] * given_count + [ANY] * len(weights),
        outs,
        [IN] * len(outs),
        scratch,
        2 * cells * 11 * C * C,
        22 * C * C + 20 * cells * C,
    )


def readout(places, live, lowered, bias, cotangent, weights, out_blocks):
    cells, columns = cotangent.shape
    n_weights, n_outs = len(weights.operands), len(out_blocks.operands)
    bf16 = jnp.bfloat16
    cut_size = 512

    def kernel(places_in, places_out, live_ref, low_ref, bias_ref, cot_ref, *refs):
        refs = list(refs)
        sources = [refs.pop(0) for _ in range(n_weights)]
        output, grad_stream, grad_bias = refs.pop(0), refs.pop(0), refs.pop(0)
        targets = [refs.pop(0) for _ in range(n_outs)]
        matrix, grad, turned, sems = refs
        copies = weights.bind(sources, places_in, matrix, sems)
        start(copies)
        factor = wide(live_ref[0])
        grad_stream[...] = jnp.zeros((cells, C), jnp.float32)
        turned[...] = low(jnp.transpose(wide(low_ref[...])))
        wait(copies)

        def part(cut):
            logits = dot(low_ref[...], matrix[:, cut]) + bias_ref[:, cut]
            share = 0.5 * (1.0 + lax.erf(logits * (0.5**0.5)))
            output[:, cut] = low(logits * share * factor)
            slope = share + logits * (jnp.exp(-0.5 * logits * logits) * (0.5 / jnp.pi) ** 0.5)
            grad_logits = low(wide(cot_ref[:, cut]) * factor * slope)
            grad_bias[:, cut] = jnp.sum(wide(grad_logits), axis=0, keepdims=True)
            grad[:, cut] = low(dot(turned[...], grad_logits))
            grad_stream[...] += dot_rows(grad_logits, matrix[:, cut])

        tiles(columns, cut_size, part)
        out_copies = out_blocks.bind(targets, places_out, grad, sems, to_blocks=True)
        start(out_copies)
        wait(out_copies)

    outs = [shaped(cells, columns, dtype=bf16), shaped(cells, C), shaped(1, columns)]
    outs += [shaped(*array.shape, dtype=bf16) for array in out_blocks.operands]
    scratch = [
        pltpu.VMEM((C, columns), bf16),
        pltpu.VMEM((C, columns), bf16),
        pltpu.VMEM((C, cells), bf16),
        pltpu.SemaphoreType.DMA((max(weights.copies, out_blocks.copies),)),
    ]
    return call(
        kernel,
        "readout",
        [places[0], places[1], live, lowered, bias, cotangent] + weights.operands,
        [SMEM] * 3 + [IN] * 3 + [ANY] * n_weights,
        outs,
        [IN] * 3 + [ANY] * n_outs,
        scratch,
        6 * cells * C * columns,
        4 * C * columns + 4 * cells * columns,
    )


def back_last(places, number, side, grad_out, stream, pre3, pre2, misc, w_last, out_blocks):
    cells = side * side
    n_weights, n_outs = len(w_last.operands), len(out_blocks.operands)
    bf16 = jnp.bfloat16

    def kernel(places_in, places_out, grad_ref, u_ref, pre3_ref, pre2_ref, misc_ref, *refs):
        refs = list(refs)
        sources = [refs.pop(0) for _ in range(n_weights)]
        direct, grad_pre2, sums = refs.pop(0), refs.pop(0), refs.pop(0)
        targets = [refs.pop(0) for _ in range(n_outs)]
        matrix, grad, grad_pre3, act2, work, parts, sems = refs
        copies = w_last.bind(sources, places_in, matrix, sems)
        start(copies)
        parts[...] = jnp.zeros_like(parts)
        gain = misc_ref[3 * number + 2 : 3 * number + 3, :]
        bias = misc_ref[8 + 3 * number : 9 + 3 * number, :]

        def close(rows):
            normal, scale = centered(pre3_ref[rows, :])
            total = u_ref[rows, :] + (normal * gain + bias)
            inner = grad_ref[rows, :] * silu_back(total)
            direct[rows, :] = inner
            parts[0:8, :] += fold(inner * normal)
            parts[8:16, :] += fold(inner)
            grad_pre3[rows, :] = low(norm_back(inner, normal, scale, gain))

        tiles(cells, ROWS, close)
        gain = misc_ref[3 * number + 1 : 3 * number + 2, :]
        bias = misc_ref[7 + 3 * number : 8 + 3 * number, :]

        def again(rows):
            normal, _ = centered(pre2_ref[rows, :])
            hidden = normal * gain + bias
            act2[rows, :] = low(hidden * sigmoid(hidden))

        tiles(cells, ROWS, again)

        def weight_term(cut):
            grad[cut, :] = low(dot_sums(act2[:, cut], grad_pre3[...]))

        tiles(C, TILE, weight_term)
        wait(copies)
        out_copies = out_blocks.bind(targets, places_out, grad, sems, to_blocks=True)
        start(out_copies)

        def last(cut):
            work[:, cut] = dot_rows(grad_pre3[...], matrix[cut, :])

        tiles(C, TILE, last)

        def norm(rows):
            normal, scale = centered(pre2_ref[rows, :])
            hidden = normal * gain + bias
            inner = work[rows, :] * silu_back(hidden)
            parts[16:24, :] += fold(inner * normal)
            parts[24:32, :] += fold(inner)
            grad_pre2[rows, :] = low(norm_back(inner, normal, scale, gain))

        tiles(cells, ROWS, norm)
        sums[...] = jnp.sum(parts[...].reshape(4, 8, C), axis=1)
        wait(out_copies)

    outs = [shaped(cells, C), shaped(cells, C, dtype=bf16), shaped(4, C)]
    outs += [shaped(*array.shape, dtype=bf16) for array in out_blocks.operands]
    scratch = [
        pltpu.VMEM((C, C), bf16),
        pltpu.VMEM((C, C), bf16),
        pltpu.VMEM((cells, C), bf16),
        pltpu.VMEM((cells, C), bf16),
        pltpu.VMEM((cells, C), jnp.float32),
        pltpu.VMEM((32, C), jnp.float32),
        pltpu.SemaphoreType.DMA((max(w_last.copies, out_blocks.copies),)),
    ]
    return call(
        kernel,
        "back_last",
        [places[0], places[1], grad_out, stream, pre3, pre2, misc] + w_last.operands,
        [SMEM] * 2 + [IN] * 5 + [ANY] * n_weights,
        outs,
        [IN] * 3 + [ANY] * n_outs,
        scratch,
        4 * cells * C * C,
        8 * C * C + 24 * cells * C,
    )


def back_middle(places, side, act1, grad_pre2, out_blocks):
    cells = side * side
    n_outs = len(out_blocks.operands)
    bf16 = jnp.bfloat16

    def kernel(places_out, act_ref, grad_ref, *refs):
        refs = list(refs)
        targets = [refs.pop(0) for _ in range(n_outs)]
        grad, taps, shifted, padded, sems = refs
        copies = out_blocks.bind(targets, places_out, grad, sems, to_blocks=True)
        padded[:PAD, :] = jnp.zeros((PAD, 128), jnp.float32)
        padded[PAD + cells :, :] = jnp.zeros((PAD, 128), jnp.float32)

        def spread(i, carry):
            cut = pl.ds(pl.multiple_of(i * 128, 128), 128)
            value = wide(act_ref[:, cut])
            taps[:, cut] = low(beside(value, side, -1))
            taps[:, pl.ds(pl.multiple_of(C + i * 128, 128), 128)] = act_ref[:, cut]
            taps[:, pl.ds(pl.multiple_of(2 * C + i * 128, 128), 128)] = low(beside(value, side, 1))
            padded[PAD : PAD + cells, :] = wide(grad_ref[:, cut])
            shifted[0, :, cut] = low(padded[PAD + side : PAD + side + cells, :])
            shifted[1, :, cut] = grad_ref[:, cut]
            shifted[2, :, cut] = low(padded[PAD - side : PAD - side + cells, :])
            return carry

        lax.fori_loop(0, C // 128, spread, 0)
        for row_tap in range(3):

            def part(i, carry, row_tap=row_tap):
                cut = pl.ds(pl.multiple_of(i * TILE, TILE), TILE)
                target = pl.ds(pl.multiple_of(row_tap * 3 * C + i * TILE, TILE), TILE)
                grad[target, :] = low(dot_sums(taps[:, cut], shifted[row_tap]))
                return carry

            lax.fori_loop(0, 3 * C // TILE, part, 0)
        start(copies)
        wait(copies)

    outs = [shaped(*array.shape, dtype=bf16) for array in out_blocks.operands]
    scratch = [
        pltpu.VMEM((9 * C, C), bf16),
        pltpu.VMEM((cells, 3 * C), bf16),
        pltpu.VMEM((3, cells, C), bf16),
        pltpu.VMEM((cells + 2 * PAD, 128), jnp.float32),
        pltpu.SemaphoreType.DMA((out_blocks.copies,)),
    ]
    return call(
        kernel,
        "back_middle",
        [places[1], act1, grad_pre2],
        [SMEM] + [IN] * 2,
        outs,
        [ANY] * n_outs,
        scratch,
        2 * cells * 9 * C * C,
        18 * C * C + 4 * cells * C,
    )


def back_first(places, number, side, grad_pre2, pre1, stream, direct, misc, rest, w_middle, w_first, out_blocks):
    cells = side * side
    closing = rest is not None
    n_middle, n_first, n_outs = len(w_middle.operands), len(w_first.operands), len(out_blocks.operands)
    bf16 = jnp.bfloat16
    extra = [rest] if closing else []

    def kernel(places_in, places_out, grad_ref, pre1_ref, u_ref, direct_ref, misc_ref, *refs):
        refs = list(refs)
        rest_ref = refs.pop(0) if closing else None
        middles = [refs.pop(0) for _ in range(n_middle)]
        firsts = [refs.pop(0) for _ in range(n_first)]
        grad_u, sums = refs.pop(0), refs.pop(0)
        targets = [refs.pop(0) for _ in range(n_outs)]
        wm, wi, grad, taps, above, below, work, lowered, grad_pre1, parts, sems = refs
        middle_copies = w_middle.bind(middles, places_in, wm, sems)
        first_copies = w_first.bind(firsts, places_in, wi, sems, base=len(middle_copies))
        start(middle_copies)
        start(first_copies)
        parts[...] = jnp.zeros_like(parts)
        zeros = jnp.zeros((PAD, TILE), jnp.float32)
        for ref in (above, below):
            ref[:PAD, :] = zeros
            ref[PAD + cells :, :] = zeros

        def spread(i, carry):
            cut = pl.ds(pl.multiple_of(i * 128, 128), 128)
            value = wide(grad_ref[:, cut])
            taps[:, cut] = low(beside(value, side, 1))
            taps[:, pl.ds(pl.multiple_of(C + i * 128, 128), 128)] = grad_ref[:, cut]
            taps[:, pl.ds(pl.multiple_of(2 * C + i * 128, 128), 128)] = low(beside(value, side, -1))
            return carry

        lax.fori_loop(0, C // 128, spread, 0)

        def lower(rows):
            lowered[rows, :] = low(u_ref[rows, :])

        tiles(cells, ROWS, lower)
        wait(middle_copies)

        def middle(i, carry):
            def row(tap):
                total = None
                for column in range(3):
                    source = pl.ds(pl.multiple_of((3 * tap + column) * C + i * TILE, TILE), TILE)
                    term = dot_rows(taps[:, column * C : (column + 1) * C], wm[source, :])
                    total = term if total is None else total + term
                return total

            above[PAD : PAD + cells, :] = row(0)
            below[PAD : PAD + cells, :] = row(2)
            cut = pl.ds(pl.multiple_of(i * TILE, TILE), TILE)
            work[:, cut] = (
                row(1) + above[PAD + side : PAD + side + cells, :] + below[PAD - side : PAD - side + cells, :]
            )
            return carry

        lax.fori_loop(0, C // TILE, middle, 0)
        gain = misc_ref[3 * number : 3 * number + 1, :]
        bias = misc_ref[6 + 3 * number : 7 + 3 * number, :]

        def norm(rows):
            normal, scale = centered(pre1_ref[rows, :])
            hidden = normal * gain + bias
            inner = work[rows, :] * silu_back(hidden)
            parts[0:8, :] += fold(inner * normal)
            parts[8:16, :] += fold(inner)
            grad_pre1[rows, :] = low(norm_back(inner, normal, scale, gain))

        tiles(cells, ROWS, norm)
        sums[...] = jnp.sum(parts[...].reshape(2, 8, C), axis=1)

        def weight_term(cut):
            grad[cut, :C] = low(dot_sums(lowered[:, cut], grad_pre1[...]))

        tiles(C, TILE, weight_term)
        wait(first_copies)

        def first(cut):
            grad_u[:, cut] = direct_ref[:, cut] + dot_rows(grad_pre1[...], wi[cut, :])

        tiles(C, TILE, first)
        if closing:

            def turn(cut):
                stacked = jnp.concatenate(
                    [
                        grad_u[:, cut],
                        sums[0:1, cut],
                        rest_ref[1:6, cut],
                        sums[1:2, cut],
                        rest_ref[7:MISC, cut],
                        jnp.zeros((HEAD - C - cells - MISC, 128), jnp.float32),
                    ]
                )
                grad[cut, C:HEAD] = low(jnp.transpose(stacked))

            tiles(C, 128, turn)
        out_copies = out_blocks.bind(targets, places_out, grad, sems, to_blocks=True)
        start(out_copies)
        wait(out_copies)

    outs = [shaped(cells, C), shaped(2, C)]
    outs += [shaped(*array.shape, dtype=bf16) for array in out_blocks.operands]
    scratch = [
        pltpu.VMEM((9 * C, C), bf16),
        pltpu.VMEM((C, C), bf16),
        pltpu.VMEM((C, HEAD if closing else C), bf16),
        pltpu.VMEM((cells, 3 * C), bf16),
        pltpu.VMEM((cells + 2 * PAD, TILE), jnp.float32),
        pltpu.VMEM((cells + 2 * PAD, TILE), jnp.float32),
        pltpu.VMEM((cells, C), jnp.float32),
        pltpu.VMEM((cells, C), bf16),
        pltpu.VMEM((cells, C), bf16),
        pltpu.VMEM((16, C), jnp.float32),
        pltpu.SemaphoreType.DMA((max(w_middle.copies + w_first.copies, out_blocks.copies),)),
    ]
    weights = w_middle.operands + w_first.operands
    return call(
        kernel,
        "back_first",
        [places[0], places[1], grad_pre2, pre1, stream, direct, misc] + extra + weights,
        [SMEM] * 2 + [IN] * (5 + len(extra)) + [ANY] * len(weights),
        outs,
        [IN] * 2 + [ANY] * n_outs,
        scratch,
        2 * cells * 11 * C * C,
        24 * C * C + 24 * cells * C,
    )


def after(value, *earlier):
    return lax.optimization_barrier((value, earlier))[0]


class Movement:
    def __init__(self, mesh):
        self.dp = mesh.shape["dp"]
        self.cores = mesh.shape["fsdp"]
        self.line = self.dp // PLANE
        self.devices = self.dp * self.cores
        self.ring = [0] + list(range(1, self.line, 2)) + list(range(2, self.line, 2))[::-1]
        self.paired = self.cores == 2 and self.line == 4

    def flip(self, value, bits):
        return lax.ppermute(value, "dp", [(i, i ^ bits) for i in range(self.dp)])

    def along(self, value):
        pairs = []
        for position, level in enumerate(self.ring):
            following = self.ring[(position + 1) % self.line]
            pairs += [(level * PLANE + near, following * PLANE + near) for near in range(PLANE)]
        return lax.ppermute(value, "dp", pairs)

    def swap(self, value):
        return lax.ppermute(value, "fsdp", [(0, 1), (1, 0)])

    def places(self, direction):
        if not self.paired:
            return jnp.zeros((1,), jnp.int32)
        index = lax.axis_index("dp")
        ring = jnp.array(self.ring, jnp.int32)
        position = jnp.argmax(ring == index // PLANE).astype(jnp.int32)
        level = ring[(position + direction * jnp.arange(self.line, dtype=jnp.int32)) % self.line]
        near = (index % PLANE) ^ jnp.arange(PLANE, dtype=jnp.int32)
        core = (lax.axis_index("fsdp") + jnp.arange(2, dtype=jnp.int32)) % 2
        chip = level[None, None, :] * PLANE + near[None, :, None]
        return (chip * 2 + core[:, None, None]).reshape(-1)

    def gather(self, pieces):
        if not self.paired:
            return [[lax.all_gather(own, ("dp", "fsdp"), axis=0, tiled=False).reshape(1, -1, own.shape[1])] for own in pieces]
        line_done, plane_done, gathered = (), (), []
        for own in pieces:
            own = after(own, *line_done) if line_done else own
            one = self.along(own)
            two = self.along(one)
            three = self.along(two)
            line_done = (two,)
            held = jnp.stack([own, one, two, three])
            held = after(held, *plane_done) if plane_done else held
            first = self.flip(held, 1)
            second = self.flip(held, 2)
            plane_done = (first, second)
            far = (self.flip(first[:2], 2), self.flip(second[2:], 1))
            here = jnp.concatenate([held, first, second, *far])
            gathered.append([here, self.swap(here)])
        return gathered


class Sum:
    def __init__(self, move, arrays):
        self.move = move
        self.arrays = arrays
        if not move.paired:
            self.owned = lax.psum_scatter(wide(arrays[0][0]), ("dp", "fsdp"), scatter_dimension=0, tiled=True)

    def turn(self):
        move = self.move
        shape = (PLANE, move.line) + self.arrays[0].shape[1:]
        self.here = self.arrays[0].reshape(shape)
        self.there = move.swap(self.arrays[1]).reshape(shape)
        return self.there

    def pair(self, chip, steps):
        return wide(self.here[chip, steps]) + wide(self.there[chip, steps])

    def diagonal(self):
        half = self.move.line // 2
        self.far = (
            self.move.flip(low(self.pair(3, slice(None, half))), 2),
            self.move.flip(low(self.pair(3, slice(half, None))), 1),
        )
        return self.far

    def plane(self):
        half = self.move.line // 2
        near, rest = slice(None, half), slice(half, None)
        first = jnp.concatenate([self.pair(1, near) + wide(self.far[0]), self.pair(1, rest)])
        second = jnp.concatenate([self.pair(2, near), self.pair(2, rest) + wide(self.far[1])])
        self.sides = (self.move.flip(low(first), 1), self.move.flip(low(second), 2))
        return self.sides

    def finish(self):
        held = self.pair(0, slice(None)) + wide(self.sides[0]) + wide(self.sides[1])
        three = self.move.along(low(held[3]))
        two = self.move.along(low(held[2] + wide(three)))
        one = self.move.along(low(held[1] + wide(two)))
        self.owned = held[0] + wide(one)
        return self.owned


def local(
    move,
    features,
    grid_live,
    pos_embed,
    w_in,
    w_mid,
    w_out,
    norm_gain,
    norm_bias,
    readout_w,
    readout_b,
    cotangent,
):
    rows, middle_rows, width = w_in.shape[1], w_mid.shape[1], readout_w.shape[1]
    cells = pos_embed.shape[0]
    pooled_cells = cells // 4
    misc_at = C + cells
    half_side = G // 2
    spare = jnp.zeros((rows, HEAD - misc_at - MISC), jnp.bfloat16)
    head = jnp.concatenate(
        [w_in[0], pos_embed.T, norm_gain.reshape(6, rows).T, norm_bias.reshape(6, rows).T, readout_b.reshape(rows, 4), spare],
        axis=1,
    )
    outer = jnp.concatenate([w_out[0], w_in[1], w_out[1]])
    parts_0, parts_1 = (3, 2) if move.paired else (1, 1)
    cut_0, cut_1 = middle_rows // parts_0, middle_rows // parts_1
    pieces = [head]
    pieces += [w_mid[0, i * cut_0 : (i + 1) * cut_0] for i in range(parts_0)]
    pieces += [outer]
    pieces += [w_mid[1, i * cut_1 : (i + 1) * cut_1] for i in range(parts_1)]
    pieces += [readout_w]
    if move.paired:
        gathered = move.gather(pieces)
        heads, middles_0, outers = gathered[0], gathered[1 : 1 + parts_0], gathered[1 + parts_0]
        middles_1, readouts = gathered[2 + parts_0 : -1], gathered[-1]
        outers = [[(outers, i * rows, rows, 0)] for i in range(3)]
    else:
        heads, middle_0, last_0, first_1, last_1, middle_1, readouts = move.gather(
            [head, w_mid[0], w_out[0], w_in[1], w_out[1], w_mid[1], readout_w]
        )
        middles_0, middles_1 = [middle_0], [middle_1]
        outers = [[(whole, 0, C, 0)] for whole in (last_0, first_1, last_1)]

    def middle_blocks(groups, cut):
        count = cut if move.paired else 9 * C
        return Blocks([(arrays, 0, count, i * cut) for i, arrays in enumerate(groups)], middle_rows)

    count = rows if move.paired else C
    head_blocks = Blocks([(heads, 0, count, 0)], rows)
    first_0 = Blocks([(heads, 0, count, 0)], rows, pl.ds(0, C))
    mid_0, mid_1 = middle_blocks(middles_0, cut_0), middle_blocks(middles_1, cut_1)
    last_0, first_1, last_1 = [Blocks(parts, rows) for parts in outers]
    readout_blocks = Blocks([(readouts, 0, count, 0)], rows)

    def out_blocks(block_rows, columns, parts=1):
        if not move.paired:
            return Blocks([([shaped(1, move.devices * block_rows, columns)], 0, move.devices * block_rows, 0)], block_rows)
        cut = block_rows // parts
        return Blocks([([shaped(move.dp, cut, columns)] * 2, 0, cut, i * cut) for i in range(parts)], block_rows)

    places = (move.places(-1), move.places(1))
    misc, stream_in, pooled, pre1_0, pre2_0, pre3_0, act1_0 = forward_block(
        places[0], 0, G, None, features[0], None, head_blocks, mid_0, last_0
    )
    low_out, pre1_1, pre2_1, pre3_1, act1_1 = forward_block(
        places[0], 1, half_side, pooled, None, misc, first_1, mid_1, last_1
    )
    readout_bias = misc[12:].T.reshape(1, width)
    output, grad_top, grad_readout_b, *readout_terms = readout(
        places, grid_live, low_out, readout_bias, cotangent[0], readout_blocks, out_blocks(rows, width)
    )
    sum_readout = Sum(move, readout_terms)
    direct_1, grad_pre2_1, sums_1, *last_terms_1 = back_last(
        places, 1, half_side, grad_top, pooled, pre3_1, pre2_1, misc, last_1, out_blocks(rows, C)
    )
    hold = after if move.paired else lambda value, *earlier: value
    if move.paired:
        grad_pre2_1 = after(grad_pre2_1, sum_readout.turn())
    middle_terms_1 = back_middle(places, half_side, act1_1, grad_pre2_1, out_blocks(middle_rows, C, parts_1))
    step = 2 if move.paired else 1
    sums_middle_1 = [Sum(move, middle_terms_1[i * step : (i + 1) * step]) for i in range(parts_1)]
    if move.paired:
        grad_pre2_1 = after(grad_pre2_1, middle_terms_1, *sum_readout.diagonal())
    grad_pooled, sums_first_1, *first_terms_1 = back_first(
        places, 1, half_side, grad_pre2_1, pre1_1, pooled, direct_1, misc, None, mid_1, first_1, out_blocks(rows, C)
    )
    if move.paired:
        waited = [*sum_readout.plane(), sums_middle_1[0].turn(), sums_middle_1[1].turn(), *sums_middle_1[0].diagonal()]
        grad_pooled = after(grad_pooled, *waited)
    grad_mid = jnp.broadcast_to(
        (grad_pooled * 0.25).reshape(half_side, 1, half_side, 1, C), (half_side, 2, half_side, 2, C)
    ).reshape(cells, C)
    direct_0, grad_pre2_0, sums_0, *last_terms_0 = back_last(
        places, 0, G, grad_mid, stream_in, pre3_0, pre2_0, misc, last_0, out_blocks(rows, C)
    )
    if move.paired:
        outer_terms = [jnp.concatenate(pair, axis=1) for pair in zip(last_terms_0, first_terms_1, last_terms_1)]
        sum_outer = Sum(move, outer_terms)
        waited = [sum_readout.finish(), *sums_middle_1[0].plane(), *sums_middle_1[1].diagonal()]
        grad_pre2_0 = after(grad_pre2_0, *waited)
    middle_terms_0 = back_middle(places, G, act1_0, grad_pre2_0, out_blocks(middle_rows, C, parts_0))
    sums_middle_0 = [Sum(move, middle_terms_0[i * step : (i + 1) * step]) for i in range(parts_0)]
    if move.paired:
        waited = [sums_middle_1[0].finish(), *sums_middle_1[1].plane(), sum_outer.turn(), *sum_outer.diagonal()]
        grad_pre2_0 = after(grad_pre2_0, middle_terms_0, *waited)
    blank = jnp.zeros((1, C), jnp.float32)
    rest = jnp.concatenate(
        [
            blank, sums_0[2:3], sums_0[0:1], sums_first_1[0:1], sums_1[2:3], sums_1[0:1],
            blank, sums_0[3:4], sums_0[1:2], sums_first_1[1:2], sums_1[3:4], sums_1[1:2],
            grad_readout_b.reshape(C, 4).T,
        ]
    )
    grad_in, _, *head_terms = back_first(
        places, 0, G, grad_pre2_0, pre1_0, stream_in, direct_0, misc, rest, mid_0, first_0, out_blocks(rows, HEAD)
    )
    sum_head = Sum(move, head_terms)
    if move.paired:
        sums_middle_1[1].finish()
        sum_outer.plane()
        for total in sums_middle_0:
            total.turn()
        sums_middle_0[0].diagonal()
        sum_outer.finish()
        sums_middle_0[0].plane()
        sums_middle_0[1].diagonal()
        sums_middle_0[0].finish()
        sums_middle_0[1].plane()
        sums_middle_0[2].diagonal()
        sums_middle_0[1].finish()
        sums_middle_0[2].plane()
        sum_head.turn()
        sum_head.diagonal()
        sums_middle_0[2].finish()
        sum_head.plane()
        sum_head.finish()
        outer_owned = sum_outer.owned.reshape(3, rows, C)
    else:
        outer_owned = [Sum(move, terms).owned for terms in (last_terms_0, first_terms_1, last_terms_1)]
    head_owned = sum_head.owned
    scales = head_owned[:, misc_at : misc_at + MISC]
    return (
        output[None],
        grad_in[None],
        head_owned[:, C:misc_at].T,
        jnp.stack([head_owned[:, :C], outer_owned[1]]),
        jnp.stack(
            [
                jnp.concatenate([total.owned for total in sums_middle_0]),
                jnp.concatenate([total.owned for total in sums_middle_1]),
            ]
        ),
        jnp.stack([outer_owned[0], outer_owned[2]]),
        scales[:, 0:6].T.reshape(2, 3, rows),
        scales[:, 6:12].T.reshape(2, 3, rows),
        sum_readout.owned,
        scales[:, 12:].reshape(-1),
    )


def solution(mesh):
    return jax.shard_map(
        functools.partial(local, Movement(mesh)),
        mesh=mesh,
        in_specs=(
            P(("dp", "fsdp"), None, None),
            P(("dp", "fsdp")),
            P(None, ("dp", "fsdp")),
            P(None, ("dp", "fsdp"), None),
            P(None, ("dp", "fsdp"), None),
            P(None, ("dp", "fsdp"), None),
            P(None, None, ("dp", "fsdp")),
            P(None, None, ("dp", "fsdp")),
            P(("dp", "fsdp"), None),
            P(("dp", "fsdp")),
            P(("dp", "fsdp"), None, None),
        ),
        out_specs=(
            P(("dp", "fsdp"), None, None),
            P(("dp", "fsdp"), None, None),
            P(None, ("dp", "fsdp")),
            P(None, ("dp", "fsdp"), None),
            P(None, ("dp", "fsdp"), None),
            P(None, ("dp", "fsdp"), None),
            P(None, None, ("dp", "fsdp")),
            P(None, None, ("dp", "fsdp")),
            P(("dp", "fsdp"), None),
            P(("dp", "fsdp")),
        ),
        check_vma=False,
    )
```

time: 2840 us -> 819 us (0.29)
  waiting for transfers between devices: 2110 us -> 319 us
  blocking collectives: 243 us -> 0 us
  Pallas kernels: 0 us -> 221 us
  matrix products: 169 us -> 0 us
  starting transfers between devices: 1.39 us -> 147 us
  local copies, waits for them, and re-layouts: 177 us -> 51.5 us
  other arithmetic: 118 us -> 68.8 us
    reduce_scatter x7 -> x0, waiting for transfers between devices: 1440 us -> none  [the longest x1 355 us: local(): lax.psum_scatter(top_middle, ('dp', 'fsdp'), scatter_dimension=0, tiled=T...]
    unnamed x25 -> x0, waiting for transfers between devices: 402 us -> none
    ppermute x0 -> x128, waiting for transfers between devices: none -> 319 us  [the longest x64 204 us: flip(): return lax.ppermute(value, 'dp', [(i, i ^ bits) for i in range(self.dp)])]
    all_gather x8 -> x0, waiting for transfers between devices: 266 us -> none  [the longest x1 89.4 us: local(): lax.all_gather(w_mid[1], ('dp', 'fsdp'), axis=0, tiled=True)]
    pallas_call x0 -> x9, Pallas kernels: none -> 221 us  [call(): pl.pallas_call(kernel, name=name, out_shape=outs, in_specs=in_specs, out_...]
    all_gather x5 -> x0, blocking collectives: 203 us -> none  [the longest x1 43.1 us: local(): lax.all_gather(readout_b, ('dp', 'fsdp'), axis=0, tiled=True)]
    dot_general x21 -> x0, matrix products: 169 us -> none  [the longest x7 67.7 us: outer_sum(): lax.dot_general(left, right, (((0,), (0,)), ((), ())), preferred_element_...]
    ppermute x0 -> x128, starting transfers between devices: none -> 147 us  [the longest x64 82.1 us: flip(): return lax.ppermute(value, 'dp', [(i, i ^ bits) for i in range(self.dp)])]
  transfers between devices with their start and end apart: 20 -> 128, of which waited for: 15 -> 59; matrix products, arithmetic and copies ran while one was open for 13% -> 13% of each run, Pallas kernels for 0% -> 25%
where the time goes in v2:
time: 819 us; the launch traced here: 810 us
  waiting for transfers between devices  319 us (39%)
  Pallas kernels  221 us (27%)
  starting transfers between devices  147 us (18%)
  other arithmetic  68.8 us (8%)
  local copies, waits for them, and re-layouts  51.5 us (6%)
    pallas_call x9, Pallas kernels, call(): pl.pallas_call(kernel, name=name, out_shape=outs, in_specs=in_specs, out_...  221 us
    ppermute x64, waiting for transfers between devices, flip(): return lax.ppermute(value, 'dp', [(i, i ^ bits) for i in range(self.dp)])  204 us
    ppermute x48, waiting for transfers between devices, along(): return lax.ppermute(value, 'dp', pairs)  108 us
    ppermute x64, starting transfers between devices, flip(): return lax.ppermute(value, 'dp', [(i, i ^ bits) for i in range(self.dp)])  82.1 us
    ppermute x48, starting transfers between devices, along(): return lax.ppermute(value, 'dp', pairs)  61.8 us
    unnamed x95, local copies, waits for them, and re-layouts  24.9 us
  transfers between devices with their start and end apart: 128, of which 59 were waited for; matrix products, arithmetic and copies ran while one was open for 13% of the time, Pallas kernels for 25%

profile of v2, /device:TPU:0, one launch (start us, length us, event | category | flops | bytes accessed | tf_op | source)
XLA Modules:
  0.0 810.3 jit_solution(4825632812757128686)
XLA Ops:
  5.0 3.1 collective-permute-start
  8.1 4.0 collective-permute-done
  14.1 3.5 collective-permute-done.1
  18.5 3.3 collective-permute-start.2
  21.9 2.8 collective-permute-done.8
  31.7 3.4 collective-permute-start.16
  42.3 7.0 collective-permute-done.17
  50.1 3.4 collective-permute-start.18
  53.5 3.6 collective-permute-done.24
  67.6 3.0 collective-permute-done.26
  71.1 8.8 %collective-permute-done.20 = bf16[4,96,1024]{2,1,0:T(8,128)(2,1)S(1)} collective-permute-done((bf16[4,96,1024]{2,1,0:T(8,128)(2,1)S(1)}, bf16[4,96,1024]{2,1,0:T(8,128)(2,1)S(1)}, u32[]{:S(2)}, u32[]{:S(2)}) %collective-permute-start.20) | collective-permute-done | bytes 786464 | tf_op jit(solution)/shard_map/ppermute | solution.py:646
  85.0 6.2 collective-permute-done.33
  91.5 3.4 collective-permute-start.34
  94.9 7.8 collective-permute-done.34
  107.5 4.2 collective-permute-done.41
  111.8 16.2 %collective-permute-done.13 = bf16[2,96,1024]{2,1,0:T(8,128)(2,1)S(1)} collective-permute-done((bf16[2,96,1024]{2,1,0:T(8,128)(2,1)S(1)}, bf16[2,96,1024]{2,1,0:T(8,128)(2,1)S(1)}, u32[]{:S(2)}, u32[]{:S(2)}) %collective-permute-start.13) | collective-permute-done | bytes 393248 | tf_op jit(solution)/shard_map/ppermute | solution.py:646
  128.0 3.3 collective-permute-start.48
  134.1 3.9 collective-permute-start.43
  139.4 9.7 %collective-permute-done.49 = bf16[144,1024]{1,0:T(8,128)(2,1)S(1)} collective-permute-done((bf16[144,1024]{1,0:T(8,128)(2,1)S(1)}, bf16[144,1024]{1,0:T(8,128)(2,1)S(1)}, u32[]{:S(2)}, u32[]{:S(2)}) %collective-permute-start.49) | collective-permute-done | bytes 294944 | tf_op jit(solution)/shard_map/ppermute | solution.py:653
  149.0 8.0 collective-permute-done.21
  157.1 3.1 collective-permute-start.50
  164.7 3.5 collective-permute-start.30
  180.4 27.1 %collective-permute-done.37 = bf16[2,96,1024]{2,1,0:T(8,128)(2,1)S(1)} collective-permute-done((bf16[2,96,1024]{2,1,0:T(8,128)(2,1)S(1)}, bf16[2,96,1024]{2,1,0:T(8,128)(2,1)S(1)}, u32[]{:S(2)}, u32[]{:S(2)}) %collective-permute-start.37) | collective-permute-done | bytes 393248 | tf_op jit(solution)/shard_map/ppermute | solution.py:646
  216.4 7.4 collective-permute-done.45
  227.0 9.4 %collective-permute-done.54 = bf16[2,144,1024]{2,1,0:T(8,128)(2,1)S(1)} collective-permute-done((bf16[2,144,1024]{2,1,0:T(8,128)(2,1)S(1)}, bf16[2,144,1024]{2,1,0:T(8,128)(2,1)S(1)}, u32[]{:S(2)}, u32[]{:S(2)}) %collective-permute-start.54) | collective-permute-done | bytes 589856 | tf_op jit(solution)/shard_map/ppermute | solution.py:646
  244.1 13.4 %collective-permute-done.60 = bf16[4,32,4096]{2,1,0:T(8,128)(2,1)S(1)} collective-permute-done((bf16[4,32,4096]{2,1,0:T(8,128)(2,1)S(1)}, bf16[4,32,4096]{2,1,0:T(8,128)(2,1)S(1)}, u32[]{:S(2)}, u32[]{:S(2)}) %collective-permute-start.60) | collective-permute-done | bytes 1048608 | tf_op jit(solution)/shard_map/ppermute | solution.py:646
  264.7 6.5 collective-permute-done.62
  280.1 37.9 %forward_block.2 = (f32[16,1024]{1,0:T(8,128)}, f32[576,1024]{1,0:T(8,128)}, f32[144,1024]{1,0:T(8,128)}, f32[576,1024]{1,0:T(8,128)}, f32[576,1024]{1,0:T(8,128...) custom-call(s32[32]{0:T(128)} %add.628.places_ref.places_in, bf16[576,1024]{1,0:T(8,128)(2,1)} %bitcast.430, ...), custom_call_target="tpu_custom_call" | custom-call | flops 13287555072 | bytes 34865152 | tf_op jit(solution)/shard_map/forward_block/pallas_call | solution.py:132
  320.0 16.8 %forward_block.3 = (bf16[144,1024]{1,0:T(8,128)(2,1)}, f32[144,1024]{1,0:T(8,128)}, f32[144,1024]{1,0:T(8,128)}, f32[144,1024]{1,0:T(8,128)}, bf16[144,1024]{1,0:T(8,128)(2,1)}) custom-call(s32[32]{0:T(128)} %add.628.places_ref.places_in, f32[144,1024]{1,0:T(8,128)} %get-tuple-element.85.refs_0_.u_ref, f32[16,1024]{1,0:T(8,128)} %get-tuple-element.86.refs_1_.misc_ref, ...), custom_call_target="tpu_custom_call" | custom-call | flops 3321888768 | bytes 26017792 | tf_op jit(solution)/shard_map/forward_block/pallas_call | solution.py:132
  336.8 19.0 %readout.1 = (bf16[144,4096]{1,0:T(8,128)(2,1)}, f32[144,1024]{1,0:T(8,128)}, f32[1,4096]{1,0:T(1,128)}, bf16[16,32,4096]{2,1,0:T(8,128)(2,1)}, bf16[16,32,4096]{2,1,0:T(8,128)(2,1)}) custom-call(s32[32]{0:T(128)} %add.628.places_ref.places_in, s32[32]{0:T(128)} %add.637.places_out, s32[1]{0:T(128)S(6)} %copy.75.live_ref, ...), custom_call_target="tpu_custom_call" | custom-call | flops 3623878656 | bytes 19136512 | tf_op jit(solution)/shard_map/readout/pallas_call | solution.py:132
  356.4 7.0 collective-permute-done.64
  363.4 3.8 fusion.35
  369.8 11.7 %collective-permute-done.66 = bf16[2,32,4096]{2,1,0:T(8,128)(2,1)S(1)} collective-permute-done((bf16[2,32,4096]{2,1,0:T(8,128)(2,1)S(1)}, bf16[2,32,4096]{2,1,0:T(8,128)(2,1)S(1)}, u32[]{:S(2)}, u32[]{:S(2)}) %collective-permute-start.66) | collective-permute-done | bytes 524320 | tf_op jit(solution)/shard_map/ppermute | solution.py:646
  386.5 9.4 %back_last.2 = (f32[144,1024]{1,0:T(8,128)}, bf16[144,1024]{1,0:T(8,128)(2,1)}, f32[4,1024]{1,0:T(4,128)}, bf16[16,32,1024]{2,1,0:T(8,128)(2,1)}, bf16[16,32,1024]{2,1,0:T(8,128)(2,1)}) custom-call(s32[32]{0:T(128)} %add.628.places_ref.places_in, s32[32]{0:T(128)} %add.637.places_out, f32[144,1024]{1,0:T(8,128)} %get-tuple-element.95.grad_ref, ...), custom_call_target="tpu_custom_call" | custom-call | flops 603979776 | bytes 11927552 | tf_op jit(solution)/shard_map/back_last/pallas_call | solution.py:132
  395.9 21.2 %back_middle.2 = (bf16[16,144,1024]{2,1,0:T(8,128)(2,1)}, bf16[16,144,1024]{2,1,0:T(8,128)(2,1)}, bf16[16,144,1024]{2,1,0:T(8,128)(2,1)}, bf16[16,144,1024]{2,1,0:T(8,128)(2,1)}) custom-call(s32[32]{0:T(128)} %add.637.places_out, bf16[144,1024]{1,0:T(8,128)(2,1)} %get-tuple-element.101.act_ref, bf16[144,1024]{1,0:T(8,128)(2,1)} %get-tuple-element.107.grad_ref), custom_call_target="tpu_custom_call" | custom-call | flops 2717908992 | bytes 19464192 | tf_op jit(solution)/shard_map/back_middle/pallas_call | solution.py:132
  423.8 6.0 collective-permute-done.73
  429.9 21.6 %back_first.2 = (f32[144,1024]{1,0:T(8,128)}, f32[2,1024]{1,0:T(2,128)}, bf16[16,32,1024]{2,1,0:T(8,128)(2,1)}, bf16[16,32,1024]{2,1,0:T(8,128)(2,1)}) custom-call(s32[32]{0:T(128)} %add.628.places_ref.places_in, s32[32]{0:T(128)} %add.637.places_out, bf16[144,1024]{1,0:T(8,128)(2,1)} %get-tuple-element.107.grad_ref, ...), custom_call_target="tpu_custom_call" | custom-call | flops 3321888768 | bytes 28704768 | tf_op jit(solution)/shard_map/back_first/pallas_call | solution.py:132
  454.3 3.5 fusion.17
  462.6 3.9 fusion.21
  467.8 6.3 collective-permute-done.72
  483.6 2.9 reshape.528.grad_ref
  494.0 23.5 %back_last.3 = (f32[576,1024]{1,0:T(8,128)}, bf16[576,1024]{1,0:T(8,128)(2,1)}, f32[4,1024]{1,0:T(4,128)}, bf16[16,32,1024]{2,1,0:T(8,128)(2,1)}, bf16[16,32,1024]{2,1,0:T(8,128)(2,1)}) custom-call(s32[32]{0:T(128)} %add.628.places_ref.places_in, s32[32]{0:T(128)} %add.637.places_out, f32[576,1024]{1,0:T(8,128)} %reshape.528.grad_ref, ...), custom_call_target="tpu_custom_call" | custom-call | flops 2415919104 | bytes 22544384 | tf_op jit(solution)/shard_map/back_last/pallas_call | solution.py:132
  517.5 3.4 pad_maximum_fusion
  524.2 3.5 convert_add_fusion.1
  528.9 6.3 collective-permute-done.83
  536.5 2.9 convert_add_fusion
  544.8 2.8 concatenate.128.refs_0_
  547.6 2.8 collective-permute-done.125
  552.3 4.5 collective-permute-done.81
  559.0 35.0 %back_middle.3 = (bf16[16,96,1024]{2,1,0:T(8,128)(2,1)}, bf16[16,96,1024]{2,1,0:T(8,128)(2,1)}, bf16[16,96,1024]{2,1,0:T(8,128)(2,1)}, bf16[16,96,1024]{2,1,0:T(...) custom-call(s32[32]{0:T(128)} %add.637.places_out, ...), custom_call_target="tpu_custom_call" | custom-call | flops 10871635968 | bytes 21233664 | tf_op jit(solution)/shard_map/back_middle/pallas_call | solution.py:132
  601.7 3.3 collective-permute-done.127
  605.8 6.2 collective-permute-done.87
  612.0 3.7 collective-permute-done.86
  619.9 36.5 %back_first.3 = (f32[576,1024]{1,0:T(8,128)}, f32[2,1024]{1,0:T(2,128)}, bf16[16,32,1664]{2,1,0:T(8,128)(2,1)}, bf16[16,32,1664]{2,1,0:T(8,128)(2,1)}) custom-call(s32[32]{0:T(128)} %add.628.places_ref.places_in, s32[32]{0:T(128)} %add.637.places_out, bf16[576,1024]{1,0:T(8,128)(2,1)} %get-tuple-element.130.grad_ref, ...), custom_call_target="tpu_custom_call" | custom-call | flops 13287555072 | bytes 39321600 | tf_op jit(solution)/shard_map/back_first/pallas_call | solution.py:132
  670.7 3.5 collective-permute-done.102
  679.0 3.6 collective-permute-done.99
  687.5 3.6 collective-permute-done.118
  699.2 29.3 %collective-permute-done.89 = bf16[2,32,1664]{2,1,0:T(8,128)(2,1)S(1)} collective-permute-done((bf16[2,32,1664]{2,1,0:T(8,128)(2,1)S(1)}, bf16[2,32,1664]{2,1,0:T(8,128)(2,1)S(1)}, u32[]{:S(2)}, u32[]{:S(2)}) %collective-permute-start.89) | collective-permute-done | bytes 213024 | tf_op jit(solution)/shard_map/ppermute | solution.py:646
  735.8 13.2 %collective-permute-done.111 = bf16[4,96,1024]{2,1,0:T(8,128)(2,1)S(1)} collective-permute-done((bf16[4,96,1024]{2,1,0:T(8,128)(2,1)S(1)}, bf16[4,96,1024]{2,1,0:T(8,128)(2,1)S(1)}, u32[]{:S(2)}, u32[]{:S(2)}) %collective-permute-start.111) | collective-permute-done | bytes 786464 | tf_op jit(solution)/shard_map/ppermute | solution.py:646
  753.3 12.5 %collective-permute-done.119 = bf16[4,96,1024]{2,1,0:T(8,128)(2,1)S(1)} collective-permute-done((bf16[4,96,1024]{2,1,0:T(8,128)(2,1)S(1)}, bf16[4,96,1024]{2,1,0:T(8,128)(2,1)S(1)}, u32[]{:S(2)}, u32[]{:S(2)}) %collective-permute-start.119) | collective-permute-done | bytes 786464 | tf_op jit(solution)/shard_map/ppermute | solution.py:646
  771.4 4.9 collective-permute-done.122
  781.1 3.7 collective-permute-done.115
  785.3 5.9 collective-permute-done.93
  793.7 6.9 collective-permute-done.94
  (459 shorter events, 236.0 us)
Async XLA Ops:
  37.9 21.4 %collective-permute-start.12 = (bf16[4,96,1024]{2,1,0:T(8,128)(2,1)S(1)}, bf16[4,96,1024]{2,1,0:T(8,128)(2,1)S(1)}, u32[]{:S(2)}, u32[]{:S(2)}) collective-permute-start(bf16[4,96,1024]{2,1,0:T(8,128)(2,1)S(1)} %pad_maximum_fusion.11), channel_id=1, source_target_pairs={{0,4},{2,6},{4,0},{6,2},{8,12},{10,14},{12,8},{14,10},{16,20},{18,... | collective-permute-start | bytes 2359304 | tf_op jit(solution)/shard_map/ppermute | solution.py:646
  39.2 20.1 %collective-permute-start.11 = (bf16[4,96,1024]{2,1,0:T(8,128)(2,1)S(1)}, bf16[4,96,1024]{2,1,0:T(8,128)(2,1)S(1)}, u32[]{:S(2)}, u32[]{:S(2)}) collective-permute-start(bf16[4,96,1024]{2,1,0:T(8,128)(2,1)S(1)} %pad_maximum_fusion.11), channel_id=1, source_target_pairs={{0,2},{2,0},{4,6},{6,4},{8,10},{10,8},{12,14},{14,12},{16,18},{18,... | collective-permute-start | bytes 2359304 | tf_op jit(solution)/shard_map/ppermute | solution.py:646
  59.3 20.5 %collective-permute-start.20 = (bf16[4,96,1024]{2,1,0:T(8,128)(2,1)S(1)}, bf16[4,96,1024]{2,1,0:T(8,128)(2,1)S(1)}, u32[]{:S(2)}, u32[]{:S(2)}) collective-permute-start(bf16[4,96,1024]{2,1,0:T(8,128)(2,1)S(1)} %pad_maximum_fusion.12), channel_id=1, source_target_pairs={{0,4},{2,6},{4,0},{6,2},{8,12},{10,14},{12,8},{14,10},{16,20},{18,... | collective-permute-start | bytes 2359304 | tf_op jit(solution)/shard_map/ppermute | solution.py:646
  60.7 20.5 %collective-permute-start.19 = (bf16[4,96,1024]{2,1,0:T(8,128)(2,1)S(1)}, bf16[4,96,1024]{2,1,0:T(8,128)(2,1)S(1)}, u32[]{:S(2)}, u32[]{:S(2)}) collective-permute-start(bf16[4,96,1024]{2,1,0:T(8,128)(2,1)S(1)} %pad_maximum_fusion.12), channel_id=1, source_target_pairs={{0,2},{2,0},{4,6},{6,4},{8,10},{10,8},{12,14},{14,12},{16,18},{18,... | collective-permute-start | bytes 2359304 | tf_op jit(solution)/shard_map/ppermute | solution.py:646
  64.4 42.1 %collective-permute-start.6 = (bf16[2,32,1664]{2,1,0:T(8,128)(2,1)S(1)}, bf16[2,32,1664]{2,1,0:T(8,128)(2,1)S(1)}, u32[]{:S(2)}, u32[]{:S(2)}) collective-permute-start(bf16[2,32,1664]{2,1,0:T(8,128)(2,1)S(1)} %slice.797), channel_id=1, source_target_pairs={{0,2},{2,0},{4,6},{6,4},{8,10},{10,8},{12,14},{14,12},{16,18},{18,... | collective-permute-start | bytes 638984 | tf_op jit(solution)/shard_map/ppermute | solution.py:646
  66.0 25.5 %collective-permute-start.5 = (bf16[2,32,1664]{2,1,0:T(8,128)(2,1)S(1)}, bf16[2,32,1664]{2,1,0:T(8,128)(2,1)S(1)}, u32[]{:S(2)}, u32[]{:S(2)}) collective-permute-start(bf16[2,32,1664]{2,1,0:T(8,128)(2,1)S(1)} %slice.796), channel_id=1, source_target_pairs={{0,4},{2,6},{4,0},{6,2},{8,12},{10,14},{12,8},{14,10},{16,20},{18,... | collective-permute-start | bytes 638984 | tf_op jit(solution)/shard_map/ppermute | solution.py:646
  81.2 21.6 %collective-permute-start.28 = (bf16[4,96,1024]{2,1,0:T(8,128)(2,1)S(1)}, bf16[4,96,1024]{2,1,0:T(8,128)(2,1)S(1)}, u32[]{:S(2)}, u32[]{:S(2)}) collective-permute-start(bf16[4,96,1024]{2,1,0:T(8,128)(2,1)S(1)} %pad_maximum_fusion.13), channel_id=1, source_target_pairs={{0,4},{2,6},{4,0},{6,2},{8,12},{10,14},{12,8},{14,10},{16,20},{18,... | collective-permute-start | bytes 2359304 | tf_op jit(solution)/shard_map/ppermute | solution.py:646
  81.9 21.0 %collective-permute-start.27 = (bf16[4,96,1024]{2,1,0:T(8,128)(2,1)S(1)}, bf16[4,96,1024]{2,1,0:T(8,128)(2,1)S(1)}, u32[]{:S(2)}, u32[]{:S(2)}) collective-permute-start(bf16[4,96,1024]{2,1,0:T(8,128)(2,1)S(1)} %pad_maximum_fusion.13), channel_id=1, source_target_pairs={{0,2},{2,0},{4,6},{6,4},{8,10},{10,8},{12,14},{14,12},{16,18},{18,... | collective-permute-start | bytes 2359304 | tf_op jit(solution)/shard_map/ppermute | solution.py:646
  102.9 28.6 %collective-permute-start.36 = (bf16[4,96,1024]{2,1,0:T(8,128)(2,1)S(1)}, bf16[4,96,1024]{2,1,0:T(8,128)(2,1)S(1)}, u32[]{:S(2)}, u32[]{:S(2)}) collective-permute-start(bf16[4,96,1024]{2,1,0:T(8,128)(2,1)S(1)} %pad_maximum_fusion.14), channel_id=1, source_target_pairs={{0,4},{2,6},{4,0},{6,2},{8,12},{10,14},{12,8},{14,10},{16,20},{18,... | collective-permute-start | bytes 2359304 | tf_op jit(solution)/shard_map/ppermute | solution.py:646
  104.0 27.5 %collective-permute-start.35 = (bf16[4,96,1024]{2,1,0:T(8,128)(2,1)S(1)}, bf16[4,96,1024]{2,1,0:T(8,128)(2,1)S(1)}, u32[]{:S(2)}, u32[]{:S(2)}) collective-permute-start(bf16[4,96,1024]{2,1,0:T(8,128)(2,1)S(1)} %pad_maximum_fusion.14), channel_id=1, source_target_pairs={{0,2},{2,0},{4,6},{6,4},{8,10},{10,8},{12,14},{14,12},{16,18},{18,... | collective-permute-start | bytes 2359304 | tf_op jit(solution)/shard_map/ppermute | solution.py:646
  106.5 31.4 %collective-permute-start.14 = (bf16[2,96,1024]{2,1,0:T(8,128)(2,1)S(1)}, bf16[2,96,1024]{2,1,0:T(8,128)(2,1)S(1)}, u32[]{:S(2)}, u32[]{:S(2)}) collective-permute-start(bf16[2,96,1024]{2,1,0:T(8,128)(2,1)S(1)} %slice.799), channel_id=1, source_target_pairs={{0,2},{2,0},{4,6},{6,4},{8,10},{10,8},{12,14},{14,12},{16,18},{18,... | collective-permute-start | bytes 1179656 | tf_op jit(solution)/shard_map/ppermute | solution.py:646
  106.6 21.4 %collective-permute-start.13 = (bf16[2,96,1024]{2,1,0:T(8,128)(2,1)S(1)}, bf16[2,96,1024]{2,1,0:T(8,128)(2,1)S(1)}, u32[]{:S(2)}, u32[]{:S(2)}) collective-permute-start(bf16[2,96,1024]{2,1,0:T(8,128)(2,1)S(1)} %slice.798), channel_id=1, source_target_pairs={{0,4},{2,6},{4,0},{6,2},{8,12},{10,14},{12,8},{14,10},{16,20},{18,... | collective-permute-start | bytes 1179656 | tf_op jit(solution)/shard_map/ppermute | solution.py:646
  111.7 19.6 %collective-permute-start.42 = (bf16[144,1024]{1,0:T(8,128)(2,1)S(1)}, bf16[144,1024]{1,0:T(8,128)(2,1)S(1)}, u32[]{:S(2)}, u32[]{:S(2)}) collective-permute-start(bf16[144,1024]{1,0:T(8,128)(2,1)S(1)} %collective-permute-done.41), channel_id=1, source_target_pairs={{0,8},{2,10},{4,12},{6,14},{8,24},{10,26},{12,28},{14,30},{24,16},... | collective-permute-start | bytes 884744 | tf_op jit(solution)/shard_map/ppermute | solution.py:653
  131.5 39.1 %collective-permute-start.44 = (bf16[4,144,1024]{2,1,0:T(8,128)(2,1)S(1)}, bf16[4,144,1024]{2,1,0:T(8,128)(2,1)S(1)}, u32[]{:S(2)}, u32[]{:S(2)}) collective-permute-start(bf16[4,144,1024]{2,1,0:T(8,128)(2,1)S(1)} %pad_maximum_fusion.2), channel_id=1, source_target_pairs={{0,4},{2,6},{4,0},{6,2},{8,12},{10,14},{12,8},{14,10},{16,20},{18,... | collective-permute-start | bytes 3538952 | tf_op jit(solution)/shard_map/ppermute | solution.py:646
  134.1 36.6 %collective-permute-start.43 = (bf16[4,144,1024]{2,1,0:T(8,128)(2,1)S(1)}, bf16[4,144,1024]{2,1,0:T(8,128)(2,1)S(1)}, u32[]{:S(2)}, u32[]{:S(2)}) collective-permute-start(bf16[4,144,1024]{2,1,0:T(8,128)(2,1)S(1)} %pad_maximum_fusion.2), channel_id=1, source_target_pairs={{0,2},{2,0},{4,6},{6,4},{8,10},{10,8},{12,14},{14,12},{16,18},{18,... | collective-permute-start | bytes 3538952 | tf_op jit(solution)/shard_map/ppermute | solution.py:646
  138.0 22.5 %collective-permute-start.22 = (bf16[2,96,1024]{2,1,0:T(8,128)(2,1)S(1)}, bf16[2,96,1024]{2,1,0:T(8,128)(2,1)S(1)}, u32[]{:S(2)}, u32[]{:S(2)}) collective-permute-start(bf16[2,96,1024]{2,1,0:T(8,128)(2,1)S(1)} %slice.801), channel_id=1, source_target_pairs={{0,2},{2,0},{4,6},{6,4},{8,10},{10,8},{12,14},{14,12},{16,18},{18,... | collective-permute-start | bytes 1179656 | tf_op jit(solution)/shard_map/ppermute | solution.py:646
  138.1 18.9 %collective-permute-start.21 = (bf16[2,96,1024]{2,1,0:T(8,128)(2,1)S(1)}, bf16[2,96,1024]{2,1,0:T(8,128)(2,1)S(1)}, u32[]{:S(2)}, u32[]{:S(2)}) collective-permute-start(bf16[2,96,1024]{2,1,0:T(8,128)(2,1)S(1)} %slice.800), channel_id=1, source_target_pairs={{0,4},{2,6},{4,0},{6,2},{8,12},{10,14},{12,8},{14,10},{16,20},{18,... | collective-permute-start | bytes 1179656 | tf_op jit(solution)/shard_map/ppermute | solution.py:646
  170.6 93.5 %collective-permute-start.15 = (bf16[16,96,1024]{2,1,0:T(8,128)(2,1)S(1)}, bf16[16,96,1024]{2,1,0:T(8,128)(2,1)S(1)}, u32[]{:S(2)}, u32[]{:S(2)}) collective-permute-start(bf16[16,96,1024]{2,1,0:T(8,128)(2,1)S(1)} %constant_dynamic-update-slice_fusion.8.refs_3_.refs_1_), channel_id=1, source_target_pairs={{0,1},{1,0},{2,3},{3,2},{4,5},{5,4},{6,7},{7,6},{8,9},{9,8},{10,11... | collective-permute-start | bytes 9437192 | tf_op jit(solution)/shard_map/ppermute | solution.py:656
  170.7 38.2 %collective-permute-start.52 = (bf16[4,144,1024]{2,1,0:T(8,128)(2,1)S(1)}, bf16[4,144,1024]{2,1,0:T(8,128)(2,1)S(1)}, u32[]{:S(2)}, u32[]{:S(2)}) collective-permute-start(bf16[4,144,1024]{2,1,0:T(8,128)(2,1)S(1)} %pad_maximum_fusion.3), channel_id=1, source_target_pairs={{0,4},{2,6},{4,0},{6,2},{8,12},{10,14},{12,8},{14,10},{16,20},{18,... | collective-permute-start | bytes 3538952 | tf_op jit(solution)/shard_map/ppermute | solution.py:646
  174.8 32.7 %collective-permute-start.37 = (bf16[2,96,1024]{2,1,0:T(8,128)(2,1)S(1)}, bf16[2,96,1024]{2,1,0:T(8,128)(2,1)S(1)}, u32[]{:S(2)}, u32[]{:S(2)}) collective-permute-start(bf16[2,96,1024]{2,1,0:T(8,128)(2,1)S(1)} %slice.804), channel_id=1, source_target_pairs={{0,4},{2,6},{4,0},{6,2},{8,12},{10,14},{12,8},{14,10},{16,20},{18,... | collective-permute-start | bytes 1179656 | tf_op jit(solution)/shard_map/ppermute | solution.py:646
  176.9 36.8 %collective-permute-start.51 = (bf16[4,144,1024]{2,1,0:T(8,128)(2,1)S(1)}, bf16[4,144,1024]{2,1,0:T(8,128)(2,1)S(1)}, u32[]{:S(2)}, u32[]{:S(2)}) collective-permute-start(bf16[4,144,1024]{2,1,0:T(8,128)(2,1)S(1)} %pad_maximum_fusion.3), channel_id=1, source_target_pairs={{0,2},{2,0},{4,6},{6,4},{8,10},{10,8},{12,14},{14,12},{16,18},{18,... | collective-permute-start | bytes 3538952 | tf_op jit(solution)/shard_map/ppermute | solution.py:646
  179.1 31.8 %collective-permute-start.38 = (bf16[2,96,1024]{2,1,0:T(8,128)(2,1)S(1)}, bf16[2,96,1024]{2,1,0:T(8,128)(2,1)S(1)}, u32[]{:S(2)}, u32[]{:S(2)}) collective-permute-start(bf16[2,96,1024]{2,1,0:T(8,128)(2,1)S(1)} %slice.805), channel_id=1, source_target_pairs={{0,2},{2,0},{4,6},{6,4},{8,10},{10,8},{12,14},{14,12},{16,18},{18,... | collective-permute-start | bytes 1179656 | tf_op jit(solution)/shard_map/ppermute | solution.py:646
  210.9 25.4 %collective-permute-start.54 = (bf16[2,144,1024]{2,1,0:T(8,128)(2,1)S(1)}, bf16[2,144,1024]{2,1,0:T(8,128)(2,1)S(1)}, u32[]{:S(2)}, u32[]{:S(2)}) collective-permute-start(bf16[2,144,1024]{2,1,0:T(8,128)(2,1)S(1)} %slice.809), channel_id=1, source_target_pairs={{0,2},{2,0},{4,6},{6,4},{8,10},{10,8},{12,14},{14,12},{16,18},{18,... | collective-permute-start | bytes 1769480 | tf_op jit(solution)/shard_map/ppermute | solution.py:646
  213.8 26.4 %collective-permute-start.53 = (bf16[2,144,1024]{2,1,0:T(8,128)(2,1)S(1)}, bf16[2,144,1024]{2,1,0:T(8,128)(2,1)S(1)}, u32[]{:S(2)}, u32[]{:S(2)}) collective-permute-start(bf16[2,144,1024]{2,1,0:T(8,128)(2,1)S(1)} %slice.808), channel_id=1, source_target_pairs={{0,4},{2,6},{4,0},{6,2},{8,12},{10,14},{12,8},{14,10},{16,20},{18,... | collective-permute-start | bytes 1769480 | tf_op jit(solution)/shard_map/ppermute | solution.py:646
  223.7 49.8 %collective-permute-start.23 = (bf16[16,96,1024]{2,1,0:T(8,128)(2,1)S(1)}, bf16[16,96,1024]{2,1,0:T(8,128)(2,1)S(1)}, u32[]{:S(2)}, u32[]{:S(2)}) collective-permute-start(bf16[16,96,1024]{2,1,0:T(8,128)(2,1)S(1)} %constant_dynamic-update-slice_fusion.13.refs_5_.refs_3_), channel_id=1, source_target_pairs={{0,1},{1,0},{2,3},{3,2},{4,5},{5,4},{6,7},{7,6},{8,9},{9,8},{10,11... | collective-permute-start | bytes 9437192 | tf_op jit(solution)/shard_map/ppermute | solution.py:656
  225.7 31.8 %collective-permute-start.60 = (bf16[4,32,4096]{2,1,0:T(8,128)(2,1)S(1)}, bf16[4,32,4096]{2,1,0:T(8,128)(2,1)S(1)}, u32[]{:S(2)}, u32[]{:S(2)}) collective-permute-start(bf16[4,32,4096]{2,1,0:T(8,128)(2,1)S(1)} %pad_maximum_fusion.8), channel_id=1, source_target_pairs={{0,4},{2,6},{4,0},{6,2},{8,12},{10,14},{12,8},{14,10},{16,20},{18,... | collective-permute-start | bytes 3145736 | tf_op jit(solution)/shard_map/ppermute | solution.py:646
  236.4 24.5 %collective-permute-start.59 = (bf16[4,32,4096]{2,1,0:T(8,128)(2,1)S(1)}, bf16[4,32,4096]{2,1,0:T(8,128)(2,1)S(1)}, u32[]{:S(2)}, u32[]{:S(2)}) collective-permute-start(bf16[4,32,4096]{2,1,0:T(8,128)(2,1)S(1)} %pad_maximum_fusion.8), channel_id=1, source_target_pairs={{0,2},{2,0},{4,6},{6,4},{8,10},{10,8},{12,14},{14,12},{16,18},{18,... | collective-permute-start | bytes 3145736 | tf_op jit(solution)/shard_map/ppermute | solution.py:646
  240.1 24.0 %collective-permute-start.7 = (bf16[16,32,1664]{2,1,0:T(8,128)(2,1)S(1)}, bf16[16,32,1664]{2,1,0:T(8,128)(2,1)S(1)}, u32[]{:S(2)}, u32[]{:S(2)}) collective-permute-start(bf16[16,32,1664]{2,1,0:T(8,128)(2,1)S(1)} %constant_dynamic-update-slice_fusion.refs_1_.refs_7_), channel_id=1, source_target_pairs={{0,1},{1,0},{2,3},{3,2},{4,5},{5,4},{6,7},{7,6},{8,9},{9,8},{10,11... | collective-permute-start | bytes 5111816 | tf_op jit(solution)/shard_map/ppermute | solution.py:656
  271.2 48.8 %collective-permute-start.47 = (bf16[16,144,1024]{2,1,0:T(8,128)(2,1)}, bf16[16,144,1024]{2,1,0:T(8,128)(2,1)}, u32[]{:S(2)}, u32[]{:S(2)}) collective-permute-start(bf16[16,144,1024]{2,1,0:T(8,128)(2,1)} %constant_dynamic-update-slice_fusion.28.refs_4_.refs_0_), channel_id=1, source_target_pairs={{0,1},{1,0},{2,3},{3,2},{4,5},{5,4},{6,7},{7,6},{8,9},{9,8},{10,11... | collective-permute-start | bytes 14155784 | tf_op jit(solution)/shard_map/ppermute | solution.py:656
  271.9 48.2 %collective-permute-start.55 = (bf16[16,144,1024]{2,1,0:T(8,128)(2,1)}, bf16[16,144,1024]{2,1,0:T(8,128)(2,1)}, u32[]{:S(2)}, u32[]{:S(2)}) collective-permute-start(bf16[16,144,1024]{2,1,0:T(8,128)(2,1)} %constant_dynamic-update-slice_fusion.33.refs_6_.refs_2_), channel_id=1, source_target_pairs={{0,1},{1,0},{2,3},{3,2},{4,5},{5,4},{6,7},{7,6},{8,9},{9,8},{10,11... | collective-permute-start | bytes 14155784 | tf_op jit(solution)/shard_map/ppermute | solution.py:656
  273.6 63.2 %collective-permute-start.63 = (bf16[16,32,4096]{2,1,0:T(8,128)(2,1)}, bf16[16,32,4096]{2,1,0:T(8,128)(2,1)}, u32[]{:S(2)}, u32[]{:S(2)}) collective-permute-start(bf16[16,32,4096]{2,1,0:T(8,128)(2,1)} %constant_dynamic-update-slice_fusion.38.refs_0_), channel_id=1, source_target_pairs={{0,1},{1,0},{2,3},{3,2},{4,5},{5,4},{6,7},{7,6},{8,9},{9,8},{10,11... | collective-permute-start | bytes 12582920 | tf_op jit(solution)/shard_map/ppermute | solution.py:656
  384.2 33.5 %collective-permute-start.67 = (bf16[4,32,4096]{2,1,0:T(8,128)(2,1)S(1)}, bf16[4,32,4096]{2,1,0:T(8,128)(2,1)S(1)}, u32[]{:S(2)}, u32[]{:S(2)}) collective-permute-start(bf16[4,32,4096]{2,1,0:T(8,128)(2,1)S(1)} %pad_maximum_fusion.9), channel_id=1, source_target_pairs={{0,2},{2,0},{4,6},{6,4},{8,10},{10,8},{12,14},{14,12},{16,18},{18,... | collective-permute-start | bytes 3145736 | tf_op jit(solution)/shard_map/ppermute | solution.py:646
  385.2 32.5 %collective-permute-start.68 = (bf16[4,32,4096]{2,1,0:T(8,128)(2,1)S(1)}, bf16[4,32,4096]{2,1,0:T(8,128)(2,1)}, u32[]{:S(2)}, u32[]{:S(2)}) collective-permute-start(bf16[4,32,4096]{2,1,0:T(8,128)(2,1)S(1)} %pad_maximum_fusion.10), channel_id=1, source_target_pairs={{0,4},{2,6},{4,0},{6,2},{8,12},{10,14},{12,8},{14,10},{16,20},{18,... | collective-permute-start | bytes 3145736 | tf_op jit(solution)/shard_map/ppermute | solution.py:646
  417.1 37.2 %collective-permute-start.69 = (bf16[16,144,1024]{2,1,0:T(8,128)(2,1)}, bf16[16,144,1024]{2,1,0:T(8,128)(2,1)}, u32[]{:S(2)}, u32[]{:S(2)}) collective-permute-start(bf16[16,144,1024]{2,1,0:T(8,128)(2,1)} %get-tuple-element.103), channel_id=1, source_target_pairs={{0,1},{1,0},{2,3},{3,2},{4,5},{5,4},{6,7},{7,6},{8,9},{9,8},{10,11... | collective-permute-start | bytes 14155784 | tf_op jit(solution)/shard_map/ppermute | solution.py:656
  417.2 45.3 %collective-permute-start.70 = (bf16[16,144,1024]{2,1,0:T(8,128)(2,1)}, bf16[16,144,1024]{2,1,0:T(8,128)(2,1)}, u32[]{:S(2)}, u32[]{:S(2)}) collective-permute-start(bf16[16,144,1024]{2,1,0:T(8,128)(2,1)} %get-tuple-element.105), channel_id=1, source_target_pairs={{0,1},{1,0},{2,3},{3,2},{4,5},{5,4},{6,7},{7,6},{8,9},{9,8},{10,11... | collective-permute-start | bytes 14155784 | tf_op jit(solution)/shard_map/ppermute | solution.py:656
  429.8 23.1 %collective-permute-start.74 = (bf16[32,4096]{1,0:T(8,128)(2,1)S(1)}, bf16[32,4096]{1,0:T(8,128)(2,1)S(1)}, u32[]{:S(2)}, u32[]{:S(2)}) collective-permute-start(bf16[32,4096]{1,0:T(8,128)(2,1)S(1)} %fusion.37), channel_id=1, source_target_pairs={{0,8},{2,10},{4,12},{6,14},{8,24},{10,26},{12,28},{14,30},{24,16},... | collective-permute-start | bytes 786440 | tf_op jit(solution)/shard_map/ppermute | solution.py:653
  466.5 20.4 %collective-permute-start.79 = (bf16[2,144,1024]{2,1,0:T(8,128)(2,1)}, bf16[2,144,1024]{2,1,0:T(8,128)(2,1)}, u32[]{:S(2)}, u32[]{:S(2)}) collective-permute-start(bf16[2,144,1024]{2,1,0:T(8,128)(2,1)} %get-tuple-element.162), channel_id=1, source_target_pairs={{0,2},{2,0},{4,6},{6,4},{8,10},{10,8},{12,14},{14,12},{16,18},{18,... | collective-permute-start | bytes 1769480 | tf_op jit(solution)/shard_map/ppermute | solution.py:646
  467.6 20.7 %collective-permute-start.78 = (bf16[2,144,1024]{2,1,0:T(8,128)(2,1)}, bf16[2,144,1024]{2,1,0:T(8,128)(2,1)}, u32[]{:S(2)}, u32[]{:S(2)}) collective-permute-start(bf16[2,144,1024]{2,1,0:T(8,128)(2,1)} %get-tuple-element.163), channel_id=1, source_target_pairs={{0,4},{2,6},{4,0},{6,2},{8,12},{10,14},{12,8},{14,10},{16,20},{18,... | collective-permute-start | bytes 1769480 | tf_op jit(solution)/shard_map/ppermute | solution.py:646
  479.0 45.2 %collective-permute-start.76 = (bf16[4,144,1024]{2,1,0:T(8,128)(2,1)}, bf16[4,144,1024]{2,1,0:T(8,128)(2,1)}, u32[]{:S(2)}, u32[]{:S(2)}) collective-permute-start(bf16[4,144,1024]{2,1,0:T(8,128)(2,1)} %pad_maximum_fusion.4), channel_id=1, source_target_pairs={{0,2},{2,0},{4,6},{6,4},{8,10},{10,8},{12,14},{14,12},{16,18},{18,... | collective-permute-start | bytes 3538952 | tf_op jit(solution)/shard_map/ppermute | solution.py:646
  480.7 43.5 %collective-permute-start.77 = (bf16[4,144,1024]{2,1,0:T(8,128)(2,1)}, bf16[4,144,1024]{2,1,0:T(8,128)(2,1)}, u32[]{:S(2)}, u32[]{:S(2)}) collective-permute-start(bf16[4,144,1024]{2,1,0:T(8,128)(2,1)} %pad_maximum_fusion.5), channel_id=1, source_target_pairs={{0,4},{2,6},{4,0},{6,2},{8,12},{10,14},{12,8},{14,10},{16,20},{18,... | collective-permute-start | bytes 3538952 | tf_op jit(solution)/shard_map/ppermute | solution.py:646
  491.1 44.0 %collective-permute-start.83 = (bf16[4,144,1024]{2,1,0:T(8,128)(2,1)S(1)}, bf16[4,144,1024]{2,1,0:T(8,128)(2,1)S(1)}, u32[]{:S(2)}, u32[]{:S(2)}) collective-permute-start(bf16[4,144,1024]{2,1,0:T(8,128)(2,1)S(1)} %pad_maximum_fusion.6), channel_id=1, source_target_pairs={{0,2},{2,0},{4,6},{6,4},{8,10},{10,8},{12,14},{14,12},{16,18},{18,... | collective-permute-start | bytes 3538952 | tf_op jit(solution)/shard_map/ppermute | solution.py:646
  492.2 44.3 %collective-permute-start.84 = (bf16[4,144,1024]{2,1,0:T(8,128)(2,1)S(1)}, bf16[4,144,1024]{2,1,0:T(8,128)(2,1)}, u32[]{:S(2)}, u32[]{:S(2)}) collective-permute-start(bf16[4,144,1024]{2,1,0:T(8,128)(2,1)S(1)} %pad_maximum_fusion.7), channel_id=1, source_target_pairs={{0,4},{2,6},{4,0},{6,2},{8,12},{10,14},{12,8},{14,10},{16,20},{18,... | collective-permute-start | bytes 3538952 | tf_op jit(solution)/shard_map/ppermute | solution.py:646
  520.8 77.3 %collective-permute-start.85 = (bf16[16,96,1024]{2,1,0:T(8,128)(2,1)}, bf16[16,96,1024]{2,1,0:T(8,128)(2,1)}, u32[]{:S(2)}, u32[]{:S(2)}) collective-permute-start(bf16[16,96,1024]{2,1,0:T(8,128)(2,1)} %pad_maximum_fusion), channel_id=1, source_target_pairs={{0,1},{1,0},{2,3},{3,2},{4,5},{5,4},{6,7},{7,6},{8,9},{9,8},{10,11... | collective-permute-start | bytes 9437192 | tf_op jit(solution)/shard_map/ppermute | solution.py:656
  551.2 43.3 %collective-permute-start.126 = (bf16[144,1024]{1,0:T(8,128)(2,1)}, bf16[144,1024]{1,0:T(8,128)(2,1)S(1)}, u32[]{:S(2)}, u32[]{:S(2)}) collective-permute-start(bf16[144,1024]{1,0:T(8,128)(2,1)} %fusion.23), channel_id=1, source_target_pairs={{0,8},{2,10},{4,12},{6,14},{8,24},{10,26},{12,28},{14,30},{24,16},... | collective-permute-start | bytes 884744 | tf_op jit(solution)/shard_map/ppermute | solution.py:653
  557.8 36.8 %collective-permute-start.82 = (bf16[144,1024]{1,0:T(8,128)(2,1)S(1)}, bf16[144,1024]{1,0:T(8,128)(2,1)S(1)}, u32[]{:S(2)}, u32[]{:S(2)}) collective-permute-start(bf16[144,1024]{1,0:T(8,128)(2,1)S(1)} %fusion.30), channel_id=1, source_target_pairs={{0,8},{2,10},{4,12},{6,14},{8,24},{10,26},{12,28},{14,30},{24,16},... | collective-permute-start | bytes 884744 | tf_op jit(solution)/shard_map/ppermute | solution.py:653
  593.9 66.1 %collective-permute-start.101 = (bf16[16,96,1024]{2,1,0:T(8,128)(2,1)}, bf16[16,96,1024]{2,1,0:T(8,128)(2,1)}, u32[]{:S(2)}, u32[]{:S(2)}) collective-permute-start(bf16[16,96,1024]{2,1,0:T(8,128)(2,1)} %get-tuple-element.119), channel_id=1, source_target_pairs={{0,1},{1,0},{2,3},{3,2},{4,5},{5,4},{6,7},{7,6},{8,9},{9,8},{10,11... | collective-permute-start | bytes 9437192 | tf_op jit(solution)/shard_map/ppermute | solution.py:656
  594.0 70.0 %collective-permute-start.109 = (bf16[16,96,1024]{2,1,0:T(8,128)(2,1)}, bf16[16,96,1024]{2,1,0:T(8,128)(2,1)}, u32[]{:S(2)}, u32[]{:S(2)}) collective-permute-start(bf16[16,96,1024]{2,1,0:T(8,128)(2,1)} %get-tuple-element.121), channel_id=1, source_target_pairs={{0,1},{1,0},{2,3},{3,2},{4,5},{5,4},{6,7},{7,6},{8,9},{9,8},{10,11... | collective-permute-start | bytes 9437192 | tf_op jit(solution)/shard_map/ppermute | solution.py:656
  594.5 72.8 %collective-permute-start.117 = (bf16[16,96,1024]{2,1,0:T(8,128)(2,1)}, bf16[16,96,1024]{2,1,0:T(8,128)(2,1)}, u32[]{:S(2)}, u32[]{:S(2)}) collective-permute-start(bf16[16,96,1024]{2,1,0:T(8,128)(2,1)} %get-tuple-element.123), channel_id=1, source_target_pairs={{0,1},{1,0},{2,3},{3,2},{4,5},{5,4},{6,7},{7,6},{8,9},{9,8},{10,11... | collective-permute-start | bytes 9437192 | tf_op jit(solution)/shard_map/ppermute | solution.py:656
  617.5 38.9 %collective-permute-start.97 = (bf16[4,96,1024]{2,1,0:T(8,128)(2,1)S(1)}, bf16[4,96,1024]{2,1,0:T(8,128)(2,1)S(1)}, u32[]{:S(2)}, u32[]{:S(2)}) collective-permute-start(bf16[4,96,1024]{2,1,0:T(8,128)(2,1)S(1)} %pad_maximum_fusion.16), channel_id=1, source_target_pairs={{0,4},{2,6},{4,0},{6,2},{8,12},{10,14},{12,8},{14,10},{16,20},{18,... | collective-permute-start | bytes 2359304 | tf_op jit(solution)/shard_map/ppermute | solution.py:646
  619.2 37.3 %collective-permute-start.96 = (bf16[4,96,1024]{2,1,0:T(8,128)(2,1)}, bf16[4,96,1024]{2,1,0:T(8,128)(2,1)S(1)}, u32[]{:S(2)}, u32[]{:S(2)}) collective-permute-start(bf16[4,96,1024]{2,1,0:T(8,128)(2,1)} %pad_maximum_fusion.15), channel_id=1, source_target_pairs={{0,2},{2,0},{4,6},{6,4},{8,10},{10,8},{12,14},{14,12},{16,18},{18,... | collective-permute-start | bytes 2359304 | tf_op jit(solution)/shard_map/ppermute | solution.py:646
  656.4 39.3 %collective-permute-start.88 = (bf16[16,32,1664]{2,1,0:T(8,128)(2,1)}, bf16[16,32,1664]{2,1,0:T(8,128)(2,1)S(1)}, u32[]{:S(2)}, u32[]{:S(2)}) collective-permute-start(bf16[16,32,1664]{2,1,0:T(8,128)(2,1)} %get-tuple-element.139), channel_id=1, source_target_pairs={{0,1},{1,0},{2,3},{3,2},{4,5},{5,4},{6,7},{7,6},{8,9},{9,8},{10,11... | collective-permute-start | bytes 5111816 | tf_op jit(solution)/shard_map/ppermute | solution.py:656
  684.4 47.2 %collective-permute-start.105 = (bf16[4,96,1024]{2,1,0:T(8,128)(2,1)S(1)}, bf16[4,96,1024]{2,1,0:T(8,128)(2,1)S(1)}, u32[]{:S(2)}, u32[]{:S(2)}) collective-permute-start(bf16[4,96,1024]{2,1,0:T(8,128)(2,1)S(1)} %pad_maximum_fusion.18), channel_id=1, source_target_pairs={{0,4},{2,6},{4,0},{6,2},{8,12},{10,14},{12,8},{14,10},{16,20},{18,... | collective-permute-start | bytes 2359304 | tf_op jit(solution)/shard_map/ppermute | solution.py:646
  691.1 41.5 %collective-permute-start.103 = (bf16[4,96,1024]{2,1,0:T(8,128)(2,1)S(1)}, bf16[4,96,1024]{2,1,0:T(8,128)(2,1)S(1)}, u32[]{:S(2)}, u32[]{:S(2)}) collective-permute-start(bf16[4,96,1024]{2,1,0:T(8,128)(2,1)S(1)} %pad_maximum_fusion.17), channel_id=1, source_target_pairs={{0,2},{2,0},{4,6},{6,4},{8,10},{10,8},{12,14},{14,12},{16,18},{18,... | collective-permute-start | bytes 2359304 | tf_op jit(solution)/shard_map/ppermute | solution.py:646
  692.2 42.4 %collective-permute-start.113 = (bf16[4,96,1024]{2,1,0:T(8,128)(2,1)S(1)}, bf16[4,96,1024]{2,1,0:T(8,128)(2,1)S(1)}, u32[]{:S(2)}, u32[]{:S(2)}) collective-permute-start(bf16[4,96,1024]{2,1,0:T(8,128)(2,1)S(1)} %pad_maximum_fusion.20), channel_id=1, source_target_pairs={{0,4},{2,6},{4,0},{6,2},{8,12},{10,14},{12,8},{14,10},{16,20},{18,... | collective-permute-start | bytes 2359304 | tf_op jit(solution)/shard_map/ppermute | solution.py:646
  697.1 31.3 %collective-permute-start.89 = (bf16[2,32,1664]{2,1,0:T(8,128)(2,1)S(1)}, bf16[2,32,1664]{2,1,0:T(8,128)(2,1)S(1)}, u32[]{:S(2)}, u32[]{:S(2)}) collective-permute-start(bf16[2,32,1664]{2,1,0:T(8,128)(2,1)S(1)} %get-tuple-element.204), channel_id=1, source_target_pairs={{0,4},{2,6},{4,0},{6,2},{8,12},{10,14},{12,8},{14,10},{16,20},{18,... | collective-permute-start | bytes 638984 | tf_op jit(solution)/shard_map/ppermute | solution.py:646
  697.5 32.1 %collective-permute-start.91 = (bf16[2,32,1664]{2,1,0:T(8,128)(2,1)S(1)}, bf16[2,32,1664]{2,1,0:T(8,128)(2,1)S(1)}, u32[]{:S(2)}, u32[]{:S(2)}) collective-permute-start(bf16[2,32,1664]{2,1,0:T(8,128)(2,1)S(1)} %get-tuple-element.205), channel_id=1, source_target_pairs={{0,2},{2,0},{4,6},{6,4},{8,10},{10,8},{12,14},{14,12},{16,18},{18,... | collective-permute-start | bytes 638984 | tf_op jit(solution)/shard_map/ppermute | solution.py:646
  728.5 20.5 %collective-permute-start.111 = (bf16[4,96,1024]{2,1,0:T(8,128)(2,1)S(1)}, bf16[4,96,1024]{2,1,0:T(8,128)(2,1)S(1)}, u32[]{:S(2)}, u32[]{:S(2)}) collective-permute-start(bf16[4,96,1024]{2,1,0:T(8,128)(2,1)S(1)} %pad_maximum_fusion.19), channel_id=1, source_target_pairs={{0,2},{2,0},{4,6},{6,4},{8,10},{10,8},{12,14},{14,12},{16,18},{18,... | collective-permute-start | bytes 2359304 | tf_op jit(solution)/shard_map/ppermute | solution.py:646
  729.6 22.5 %collective-permute-start.121 = (bf16[4,96,1024]{2,1,0:T(8,128)(2,1)S(1)}, bf16[4,96,1024]{2,1,0:T(8,128)(2,1)S(1)}, u32[]{:S(2)}, u32[]{:S(2)}) collective-permute-start(bf16[4,96,1024]{2,1,0:T(8,128)(2,1)S(1)} %pad_maximum_fusion.22), channel_id=1, source_target_pairs={{0,4},{2,6},{4,0},{6,2},{8,12},{10,14},{12,8},{14,10},{16,20},{18,... | collective-permute-start | bytes 2359304 | tf_op jit(solution)/shard_map/ppermute | solution.py:646
  731.6 34.2 %collective-permute-start.119 = (bf16[4,96,1024]{2,1,0:T(8,128)(2,1)S(1)}, bf16[4,96,1024]{2,1,0:T(8,128)(2,1)S(1)}, u32[]{:S(2)}, u32[]{:S(2)}) collective-permute-start(bf16[4,96,1024]{2,1,0:T(8,128)(2,1)S(1)} %pad_maximum_fusion.21), channel_id=1, source_target_pairs={{0,2},{2,0},{4,6},{6,4},{8,10},{10,8},{12,14},{14,12},{16,18},{18,... | collective-permute-start | bytes 2359304 | tf_op jit(solution)/shard_map/ppermute | solution.py:646
  732.6 44.3 %collective-permute-start.92 = (bf16[4,32,1664]{2,1,0:T(8,128)(2,1)S(1)}, bf16[4,32,1664]{2,1,0:T(8,128)(2,1)S(1)}, u32[]{:S(2)}, u32[]{:S(2)}) collective-permute-start(bf16[4,32,1664]{2,1,0:T(8,128)(2,1)S(1)} %pad_maximum_fusion.25), channel_id=1, source_target_pairs={{0,4},{2,6},{4,0},{6,2},{8,12},{10,14},{12,8},{14,10},{16,20},{18,... | collective-permute-start | bytes 1277960 | tf_op jit(solution)/shard_map/ppermute | solution.py:646
  734.6 42.3 %collective-permute-start.90 = (bf16[4,32,1664]{2,1,0:T(8,128)(2,1)S(1)}, bf16[4,32,1664]{2,1,0:T(8,128)(2,1)S(1)}, u32[]{:S(2)}, u32[]{:S(2)}) collective-permute-start(bf16[4,32,1664]{2,1,0:T(8,128)(2,1)S(1)} %pad_maximum_fusion.24), channel_id=1, source_target_pairs={{0,2},{2,0},{4,6},{6,4},{8,10},{10,8},{12,14},{14,12},{16,18},{18,... | collective-permute-start | bytes 1277960 | tf_op jit(solution)/shard_map/ppermute | solution.py:646
  748.9 20.0 %collective-permute-start.106 = (bf16[96,1024]{1,0:T(8,128)(2,1)S(1)}, bf16[96,1024]{1,0:T(8,128)(2,1)S(1)}, u32[]{:S(2)}, u32[]{:S(2)}) collective-permute-start(bf16[96,1024]{1,0:T(8,128)(2,1)S(1)} %fusion.92), channel_id=1, source_target_pairs={{0,8},{2,10},{4,12},{6,14},{8,24},{10,26},{12,28},{14,30},{24,16},... | collective-permute-start | bytes 589832 | tf_op jit(solution)/shard_map/ppermute | solution.py:653
  752.0 17.9 %collective-permute-start.114 = (bf16[96,1024]{1,0:T(8,128)(2,1)S(1)}, bf16[96,1024]{1,0:T(8,128)(2,1)S(1)}, u32[]{:S(2)}, u32[]{:S(2)}) collective-permute-start(bf16[96,1024]{1,0:T(8,128)(2,1)S(1)} %fusion.93), channel_id=1, source_target_pairs={{0,8},{2,10},{4,12},{6,14},{8,24},{10,26},{12,28},{14,30},{24,16},... | collective-permute-start | bytes 589832 | tf_op jit(solution)/shard_map/ppermute | solution.py:653
  780.6 20.6 %collective-permute-start.108 = (bf16[96,1024]{1,0:T(8,128)(2,1)S(1)}, bf16[96,1024]{1,0:T(8,128)(2,1)S(1)}, u32[]{:S(2)}, u32[]{:S(2)}) collective-permute-start(bf16[96,1024]{1,0:T(8,128)(2,1)S(1)} %fusion.72), channel_id=1, source_target_pairs={{0,8},{2,10},{4,12},{6,14},{8,24},{10,26},{12,28},{14,30},{24,16},... | collective-permute-start | bytes 589832 | tf_op jit(solution)/shard_map/ppermute | solution.py:653
  (91 other events, 1167.3 us)

commit v3 on v2

v3 whole, which is shorter than its diff:
```python
import functools

import jax
import jax.numpy as jnp
import numpy as np
from jax import lax
from jax.experimental import pallas as pl
from jax.experimental.pallas import tpu as pltpu
from jax.sharding import PartitionSpec as P

C = 1024
G = 24
PLANE = 4
TILE = 256
ROWS = 144
PAD = 24
MISC = 16
HEAD = 1664
SIDE = 384
STEPS, LEVELS, OUT_STEPS, OUT_LEVELS, OUT_LINE, CORE, TABLE = 0, 32, 64, 80, 96, 112, 113
COST = 30
COSTS = {"forward_block": 50}
VMEM = 60 * 1024 * 1024


def low(value):
    return value.astype(jnp.bfloat16)


def wide(value):
    return value.astype(jnp.float32)


def dot(left, right):
    return jnp.dot(left, right, preferred_element_type=jnp.float32)


def dot_rows(left, right):
    return lax.dot_general(left, right, (((1,), (1,)), ((), ())), preferred_element_type=jnp.float32)


def dot_sums(left, right):
    return lax.dot_general(left, right, (((0,), (0,)), ((), ())), preferred_element_type=jnp.float32)


def sigmoid(value):
    return 1.0 / (1.0 + jnp.exp(-value))


def centered(value):
    center = value - jnp.mean(value, axis=-1, keepdims=True)
    spread = jnp.mean(center * center, axis=-1, keepdims=True)
    scale = lax.rsqrt(spread + 1e-05)
    return center * scale, scale


def norm_back(grad, normal, scale, gain):
    inner = grad * gain
    first = jnp.mean(inner, axis=-1, keepdims=True)
    second = jnp.mean(inner * normal, axis=-1, keepdims=True)
    return scale * (inner - first - normal * second)


def silu_back(value):
    gate = sigmoid(value)
    return gate * (1.0 + value * (1.0 - gate))


def tiles(extent, size, body):
    def step(i, carry):
        body(pl.ds(pl.multiple_of(i * size, size), size))
        return carry

    lax.fori_loop(0, extent // size, step, 0)


def fold(value):
    return jnp.sum(value.reshape(-1, 8, value.shape[-1]), axis=0)


def columns_of(cells, side, lanes):
    index = lax.broadcasted_iota(jnp.int32, (cells, lanes), 0).astype(jnp.float32)
    return index - side * jnp.floor((index + 0.5) * (1.0 / side))


def beside(value, side, step):
    cells = value.shape[0]
    column = columns_of(cells, side, value.shape[1])
    inside = column < side - 1 if step > 0 else column > 0
    return jnp.where(inside, pltpu.roll(value, (cells - step) % cells, 0), 0.0)


class Blocks:
    def __init__(self, block_rows):
        self.block_rows = block_rows
        self.operands = []
        self.moves = []

    def operand(self, array):
        for number, known in enumerate(self.operands):
            if known is array:
                return number
        self.operands.append(array)
        return len(self.operands) - 1

    def add(self, array, block, row, column, place, to_row, to_column, rows, columns):
        self.moves.append((self.operand(array), block, row, column, place, to_row, to_column, rows, columns))

    @property
    def copies(self):
        return len(self.moves)

    def bind(self, refs, places, matrix, sems, to_blocks=False, base=0):
        made = []
        for number, block, row, column, place, to_row, to_column, rows, columns in self.moves:
            first = to_row
            if place is not None:
                first = pl.multiple_of(places[place] * self.block_rows + to_row, 16)
            inside = matrix.at[pl.ds(first, rows), pl.ds(to_column, columns)]
            outside = refs[number] if block is None else refs[number].at[block]
            outside = outside.at[pl.ds(row, rows), pl.ds(column, columns)]
            pair = (inside, outside) if to_blocks else (outside, inside)
            made.append(pltpu.make_async_copy(*pair, sems.at[base + len(made)]))
        return made


def start(copies):
    for copy in copies:
        copy.start()


def wait(copies):
    for copy in copies:
        copy.wait()


ANY = pl.BlockSpec(memory_space=pl.ANY)
IN = pl.BlockSpec(memory_space=pltpu.VMEM)
SMEM = pl.BlockSpec(memory_space=pltpu.SMEM)


def call(kernel, name, ins, in_specs, outs, out_specs, scratch, flops, moved):
    short = COSTS.get(name, COST)
    return pl.pallas_call(
        kernel,
        name=name,
        out_shape=outs,
        in_specs=in_specs,
        out_specs=out_specs,
        scratch_shapes=scratch,
        compiler_params=pltpu.CompilerParams(vmem_limit_bytes=VMEM),
        cost_estimate=pl.CostEstimate(flops=int(flops) // short, bytes_accessed=int(moved) // short, transcendentals=0),
    )(*ins)


class Traffic:
    def __init__(self, sems):
        self.sems = sems
        self.used = 0
        self.sent = []

    def begin(self, source, target):
        copy = pltpu.make_async_copy(source, target, self.sems.at[self.used])
        self.used += 1
        copy.start()
        return copy

    def send(self, source, target):
        self.sent.append(self.begin(source, target))

    def load(self, blocks, refs, places, matrix):
        copies = blocks.bind(refs, places, matrix, self.sems, base=self.used)
        self.used += len(copies)
        start(copies)
        return copies

    def store(self, blocks, refs, places, matrix):
        copies = blocks.bind(refs, places, matrix, self.sems, to_blocks=True, base=self.used)
        self.used += len(copies)
        start(copies)
        self.sent += copies

    def finish(self):
        wait(self.sent)


def shaped(*shape, dtype=jnp.float32):
    return jax.ShapeDtypeStruct(shape, dtype)


def forward_block(table, number, side, stream, features, misc, w_first, w_middle, w_last):
    cells = side * side
    opening = features is not None
    n_first, n_middle, n_last = len(w_first.operands), len(w_middle.operands), len(w_last.operands)
    given = [features] if opening else [stream, misc]
    given_count = len(given)
    bf16 = jnp.bfloat16
    n_lefts = 3 if opening else 4

    def kernel(table_ref, *refs):
        refs = list(refs)
        heads = [refs.pop(0) for _ in range(given_count)]
        firsts = [refs.pop(0) for _ in range(n_first)]
        middles = [refs.pop(0) for _ in range(n_middle)]
        lasts = [refs.pop(0) for _ in range(n_last)]
        if opening:
            misc_ref, pooled_ref, u_out = refs.pop(0), refs.pop(0), refs.pop(0)
            u_ref = refs.pop(0 - 1)
        else:
            u_ref, misc_ref = heads
        lefts_out, pre1_out, pre2_out, pre3_out = [refs.pop(0) for _ in range(4)]
        wi, wm, wo, taps, lefts, above, below, work, pairs, pre1, pre2, pre3, sems = refs
        traffic = Traffic(sems)
        first_copies = traffic.load(w_first, firsts, table_ref, wi)
        middle_copies = traffic.load(w_middle, middles, table_ref, wm)
        last_copies = traffic.load(w_last, lasts, table_ref, wo)
        wait(first_copies)
        if opening:

            def place(cut):
                turned = jnp.transpose(wide(wi[cut, C:HEAD]))
                u_ref[:, cut] = wide(heads[0][:, cut]) + turned[:cells]
                misc_ref[:, cut] = turned[cells : cells + MISC]

            tiles(C, 128, place)
            traffic.send(u_ref, u_out)

        def lower(rows):
            lefts[0, rows, :] = low(u_ref[rows, :])

        tiles(cells, ROWS, lower)

        def first(cut):
            pre1[:, cut] = dot(lefts[0], wi[:, cut])

        tiles(C, TILE, first)
        traffic.send(pre1, pre1_out)

        def norm_act(source, norm, store):
            gain = misc_ref[3 * number + norm : 3 * number + norm + 1, :]
            bias = misc_ref[6 + 3 * number + norm : 7 + 3 * number + norm, :]

            def rows_of(rows):
                normal, _ = centered(source[rows, :])
                hidden = normal * gain + bias
                store(rows, hidden * sigmoid(hidden))

            tiles(cells, ROWS, rows_of)

        def keep_first(rows, value):
            work[rows, :] = value
            lefts[1, rows, :] = low(value)

        norm_act(pre1, 0, keep_first)

        def spread(i, carry):
            cut = pl.ds(pl.multiple_of(i * 128, 128), 128)
            value = work[:, cut]
            taps[:, pl.ds(pl.multiple_of(i * 128, 128), 128)] = low(beside(value, side, -1))
            taps[:, pl.ds(pl.multiple_of(C + i * 128, 128), 128)] = low(value)
            taps[:, pl.ds(pl.multiple_of(2 * C + i * 128, 128), 128)] = low(beside(value, side, 1))
            return carry

        lax.fori_loop(0, C // 128, spread, 0)
        zeros = jnp.zeros((PAD, TILE), jnp.float32)
        for ref in (above, below):
            ref[:PAD, :] = zeros
            ref[PAD + cells :, :] = zeros
        wait(middle_copies)

        def middle(cut):
            above[PAD : PAD + cells, :] = dot(taps[...], wm[0 : 3 * C, cut])
            below[PAD : PAD + cells, :] = dot(taps[...], wm[6 * C : 9 * C, cut])
            same = dot(taps[...], wm[3 * C : 6 * C, cut])
            pre2[:, cut] = same + above[PAD - side : PAD - side + cells, :] + below[PAD + side : PAD + side + cells, :]

        tiles(C, TILE, middle)
        traffic.send(pre2, pre2_out)

        def keep_second(rows, value):
            lefts[2, rows, :] = low(value)

        norm_act(pre2, 1, keep_second)
        if opening:
            traffic.send(lefts, lefts_out)
        wait(last_copies)

        def last(cut):
            pre3[:, cut] = dot(lefts[2], wo[:, cut])

        tiles(C, TILE, last)
        traffic.send(pre3, pre3_out)
        gain = misc_ref[3 * number + 2 : 3 * number + 3, :]
        bias = misc_ref[8 + 3 * number : 9 + 3 * number, :]

        def close(rows):
            normal, _ = centered(pre3[rows, :])
            total = u_ref[rows, :] + (normal * gain + bias)
            value = total * sigmoid(total)
            if opening:
                work[rows, :] = value
            else:
                lefts[3, rows, :] = low(value)

        tiles(cells, ROWS, close)
        if opening:
            half = side // 2

            def pool(cut):
                value = work[:, cut].reshape(half, 2, side, 128)
                pairs[...] = (value[:, 0] + value[:, 1]).reshape(half * side, 128)
                pooled_ref[:, cut] = 0.25 * (
                    pairs[pl.ds(0, half * half, 2), :] + pairs[pl.ds(1, half * half, 2), :]
                )

            tiles(C, 128, pool)
        else:
            traffic.send(lefts, lefts_out)
        traffic.finish()

    outs, out_specs = [], []
    if opening:
        outs += [shaped(MISC, C), shaped(cells // 4, C), shaped(cells, C)]
        out_specs += [IN, IN, ANY]
    outs += [shaped(n_lefts, cells, C, dtype=bf16)] + [shaped(cells, C)] * 3
    out_specs += [ANY] * 4
    copies = w_first.copies + w_middle.copies + w_last.copies + 5
    scratch = [
        pltpu.VMEM((C, HEAD if opening else C), bf16),
        pltpu.VMEM((9 * C, C), bf16),
        pltpu.VMEM((C, C), bf16),
        pltpu.VMEM((cells, 3 * C), bf16),
        pltpu.VMEM((n_lefts, cells, C), bf16),
        pltpu.VMEM((cells + 2 * PAD, TILE), jnp.float32),
        pltpu.VMEM((cells + 2 * PAD, TILE), jnp.float32),
        pltpu.VMEM((cells, C), jnp.float32),
        pltpu.VMEM((cells // 2, 128), jnp.float32),
        pltpu.VMEM((cells, C), jnp.float32),
        pltpu.VMEM((cells, C), jnp.float32),
        pltpu.VMEM((cells, C), jnp.float32),
        pltpu.SemaphoreType.DMA((copies,)),
    ]
    if opening:
        scratch.append(pltpu.VMEM((cells, C), jnp.float32))
    weights = w_first.operands + w_middle.operands + w_last.operands
    return call(
        kernel,
        "forward_block",
        [table] + given + weights,
        [SMEM] + [IN] * given_count + [ANY] * len(weights),
        outs,
        out_specs,
        scratch,
        2 * cells * 11 * C * C,
        22 * C * C + 20 * cells * C,
    )


def readout(table, live, lefts, bias, cotangent, weights):
    cells, columns = cotangent.shape
    n_weights = len(weights.operands)
    bf16 = jnp.bfloat16
    cut_size = 512
    half = columns // 2

    def kernel(table_ref, live_ref, lefts_ref, bias_ref, cot_ref, *refs):
        refs = list(refs)
        sources = [refs.pop(0) for _ in range(n_weights)]
        output, grad_stream, grad_bias, own, other, matrix, low_ref, sems = refs
        traffic = Traffic(sems)
        given = traffic.begin(lefts_ref.at[3], low_ref)
        copies = traffic.load(weights, sources, table_ref, matrix)
        factor = wide(live_ref[0])
        core = table_ref[CORE]
        grad_stream[...] = jnp.zeros((cells, C), jnp.float32)
        given.wait()
        wait(copies)
        for part in range(2):

            def step(cut, part=part):
                here = pl.ds(pl.multiple_of(part * half + cut.start, cut_size), cut_size)
                logits = dot(low_ref[...], matrix[:, here]) + bias_ref[:, here]
                share = 0.5 * (1.0 + lax.erf(logits * (0.5**0.5)))
                output[:, here] = low(logits * share * factor)
                slope = share + logits * (jnp.exp(-0.5 * logits * logits) * (0.5 / jnp.pi) ** 0.5)
                grad_logits = low(wide(cot_ref[:, here]) * factor * slope)
                grad_bias[:, here] = jnp.sum(wide(grad_logits), axis=0, keepdims=True)

                @pl.when(core == part)
                def _():
                    own[:, cut] = grad_logits

                @pl.when(core != part)
                def _():
                    other[:, cut] = grad_logits

                grad_stream[...] += dot_rows(grad_logits, matrix[:, here])

            tiles(half, cut_size, step)

    outs = [shaped(cells, columns, dtype=bf16), shaped(cells, C), shaped(1, columns)]
    outs += [shaped(cells, half, dtype=bf16)] * 2
    scratch = [
        pltpu.VMEM((C, columns), bf16),
        pltpu.VMEM((cells, C), bf16),
        pltpu.SemaphoreType.DMA((weights.copies + 1,)),
    ]
    return call(
        kernel,
        "readout",
        [table, live, lefts, bias, cotangent] + weights.operands,
        [SMEM] * 2 + [ANY] + [IN] * 2 + [ANY] * n_weights,
        outs,
        [IN] * 5,
        scratch,
        4 * cells * C * columns,
        2 * C * columns + 4 * cells * columns,
    )


def back_last(table, number, side, grad_out, stream, pre3, pre2, misc, w_last):
    cells = side * side
    pooled = grad_out.shape[0] != cells
    n_weights = len(w_last.operands)
    bf16 = jnp.bfloat16
    half = C // 2

    def kernel(table_ref, grad_ref, u_in, pre3_in, pre2_in, misc_ref, *refs):
        refs = list(refs)
        sources = [refs.pop(0) for _ in range(n_weights)]
        direct_out, grads, other, sums, matrix, direct, u_ref, pre3_ref, pre2_ref, work, parts, pairs, sems = refs
        traffic = Traffic(sems)
        opened = [traffic.begin(u_in, u_ref), traffic.begin(pre3_in, pre3_ref)]
        later = traffic.begin(pre2_in, pre2_ref)
        copies = traffic.load(w_last, sources, table_ref, matrix)
        parts[...] = jnp.zeros_like(parts)
        gain = misc_ref[3 * number + 2 : 3 * number + 3, :]
        bias = misc_ref[8 + 3 * number : 9 + 3 * number, :]
        if pooled:

            def spread(cut):
                value = 0.25 * grad_ref[:, cut]
                pairs[pl.ds(0, cells // 4, 2), :] = value
                pairs[pl.ds(1, cells // 4, 2), :] = value
                twice = pairs[...].reshape(side // 2, 1, side, 128)
                work[:, cut] = jnp.broadcast_to(twice, (side // 2, 2, side, 128)).reshape(cells, 128)

            tiles(C, 128, spread)
        grad_from = work if pooled else grad_ref
        wait(opened)

        def close(rows):
            normal, scale = centered(pre3_ref[rows, :])
            total = u_ref[rows, :] + (normal * gain + bias)
            inner = grad_from[rows, :] * silu_back(total)
            direct[rows, :] = inner
            parts[0:8, :] += fold(inner * normal)
            parts[8:16, :] += fold(inner)
            grads[0, rows, :] = low(norm_back(inner, normal, scale, gain))

        tiles(cells, ROWS, close)
        traffic.send(direct, direct_out)
        gain = misc_ref[3 * number + 1 : 3 * number + 2, :]
        bias = misc_ref[7 + 3 * number : 8 + 3 * number, :]
        wait(copies)

        def last(cut):
            work[:, cut] = dot_rows(grads[0], matrix[cut, :])

        tiles(C, TILE, last)
        later.wait()

        def norm(rows):
            normal, scale = centered(pre2_ref[rows, :])
            hidden = normal * gain + bias
            inner = work[rows, :] * silu_back(hidden)
            parts[16:24, :] += fold(inner * normal)
            parts[24:32, :] += fold(inner)
            grads[1, rows, :] = low(norm_back(inner, normal, scale, gain))

        tiles(cells, ROWS, norm)
        sums[...] = jnp.sum(parts[...].reshape(4, 8, C), axis=1)
        there = pl.ds(pl.multiple_of((1 - table_ref[CORE]) * half, half), half)
        for i in range(2):
            other[i] = grads[i, :, there]
        traffic.finish()

    outs = [shaped(cells, C), shaped(2, cells, C, dtype=bf16), shaped(2, cells, half, dtype=bf16), shaped(4, C)]
    f32 = jnp.float32
    scratch = [pltpu.VMEM((C, C), bf16)] + [pltpu.VMEM((cells, C), f32)] * 5
    scratch += [pltpu.VMEM((32, C), f32), pltpu.VMEM((cells // 2, 128), f32), pltpu.SemaphoreType.DMA((w_last.copies + 4,))]
    return call(
        kernel,
        "back_last",
        [table, grad_out, stream, pre3, pre2, misc] + w_last.operands,
        [SMEM, IN, ANY, ANY, ANY, IN] + [ANY] * n_weights,
        outs,
        [ANY, IN, IN, IN],
        scratch,
        2 * cells * C * C,
        2 * C * C + 24 * cells * C,
    )


def middle_terms(table, side, lefts, lefts_other, grads, grads_other, out_blocks):
    cells = side * side
    n_outs = len(out_blocks.operands)
    bf16 = jnp.bfloat16
    pair = lefts_other is not None
    both = 2 * cells if pair else cells
    half = C // 2 if pair else C
    given = [lefts, grads] + ([lefts_other, grads_other] if pair else [])

    def kernel(table_ref, *refs):
        refs = list(refs)
        sources = [refs.pop(0) for _ in given]
        targets = [refs.pop(0) for _ in range(n_outs)]
        act, right, grad, taps, shifted, padded, sems = refs
        traffic = Traffic(sems)
        copies = [traffic.begin(sources[0].at[1], act.at[pl.ds(0, cells), :])]
        if pair:
            mine = pl.ds(pl.multiple_of(table_ref[CORE] * half, half), half)
            copies += [
                traffic.begin(sources[1].at[1, :, mine], right.at[pl.ds(0, cells), :]),
                traffic.begin(sources[2].at[1], act.at[pl.ds(cells, cells), :]),
                traffic.begin(sources[3].at[1], right.at[pl.ds(cells, cells), :]),
            ]
        else:
            copies += [traffic.begin(sources[1].at[1], right.at[pl.ds(0, cells), :])]
        padded[:PAD, :] = jnp.zeros((PAD, 128), jnp.float32)
        padded[PAD + cells :, :] = jnp.zeros((PAD, 128), jnp.float32)
        wait(copies)
        for first in range(0, both, cells):
            rows = slice(first, first + cells)

            def spread(i, carry, rows=rows):
                cut = pl.ds(pl.multiple_of(i * 128, 128), 128)
                value = wide(act[rows, cut])
                taps[rows, cut] = low(beside(value, side, -1))
                taps[rows, pl.ds(pl.multiple_of(C + i * 128, 128), 128)] = act[rows, cut]
                taps[rows, pl.ds(pl.multiple_of(2 * C + i * 128, 128), 128)] = low(beside(value, side, 1))
                return carry

            def shift(i, carry, rows=rows):
                cut = pl.ds(pl.multiple_of(i * 128, 128), 128)
                padded[PAD : PAD + cells, :] = wide(right[rows, cut])
                shifted[0, rows, cut] = low(padded[PAD + side : PAD + side + cells, :])
                shifted[1, rows, cut] = right[rows, cut]
                shifted[2, rows, cut] = low(padded[PAD - side : PAD - side + cells, :])
                return carry

            lax.fori_loop(0, C // 128, spread, 0)
            lax.fori_loop(0, half // 128, shift, 0)
        size = 512
        for row_tap in range(3):

            def part(i, carry, row_tap=row_tap):
                cut = pl.ds(pl.multiple_of(i * size, size), size)
                target = pl.ds(pl.multiple_of(row_tap * 3 * C + i * size, size), size)
                grad[target, :] = low(dot_sums(taps[:, cut], shifted[row_tap]))
                return carry

            lax.fori_loop(0, 3 * C // size, part, 0)
        traffic.store(out_blocks, targets, table_ref, grad)
        traffic.finish()

    outs = [shaped(*array.shape, dtype=bf16) for array in out_blocks.operands]
    scratch = [
        pltpu.VMEM((both, C), bf16),
        pltpu.VMEM((both, half), bf16),
        pltpu.VMEM((9 * C, half), bf16),
        pltpu.VMEM((both, 3 * C), bf16),
        pltpu.VMEM((3, both, half), bf16),
        pltpu.VMEM((cells + 2 * PAD, 128), jnp.float32),
        pltpu.SemaphoreType.DMA((out_blocks.copies + 4,)),
    ]
    return call(
        kernel,
        "middle_terms",
        [table] + given,
        [SMEM] + [ANY] * len(given),
        outs,
        [ANY] * n_outs,
        scratch,
        2 * cells * 9 * C * C,
        18 * C * half + 8 * cells * C,
    )


def plain_terms(table, products, sides, out_blocks):
    bf16 = jnp.bfloat16
    pair = products[0][2] is not None
    given = []
    for left, _, left_other, right, _, right_other, _ in products:
        given += [left, right] + ([left_other, right_other] if pair else [])
    n_given = len(given)
    n_outs = len(out_blocks.operands)
    columns = out_blocks.operands[0].shape[-1]
    width = columns
    rows_of = [product[0].shape[-2] for product in products]

    def kernel(table_ref, *refs):
        refs = list(refs)
        sources = [refs.pop(0) for _ in range(n_given)]
        beside_refs = [refs.pop(0) for _ in range(len(sides) * (2 if pair else 1))]
        targets = [refs.pop(0) for _ in range(n_outs)]
        grad, sems = refs.pop(0), refs.pop(0)
        traffic = Traffic(sems)
        waits = []
        for (_, left_at, _, _, right_at, _, other_at), cells in zip(products, rows_of):
            left, right = refs.pop(0), refs.pop(0)
            left_in, right_in = sources.pop(0), sources.pop(0)
            copies = [traffic.begin(left_in.at[left_at], left.at[pl.ds(0, cells), :])]
            if right_at is not None:
                right_in = right_in.at[right_at]
                if pair:
                    right_in = right_in.at[:, pl.ds(pl.multiple_of(table_ref[CORE] * width, width), width)]
            copies.append(traffic.begin(right_in, right.at[pl.ds(0, cells), :]))
            if pair:
                left_in, right_in = sources.pop(0), sources.pop(0)
                copies.append(traffic.begin(left_in.at[left_at], left.at[pl.ds(cells, cells), :]))
                if other_at is not None:
                    right_in = right_in.at[other_at]
                copies.append(traffic.begin(right_in, right.at[pl.ds(cells, cells), :]))
            waits.append((copies, left, right))
        at, below = 0, len(products) * C
        for side in sides:
            extent = side[0].shape[-1]
            total = beside_refs.pop(0)[...]
            if pair:
                total = low(wide(total) + wide(beside_refs.pop(0)[...]))
            grad[below:, at : at + extent] = total
            at += extent
        if sides:
            grad[below:, at:] = jnp.zeros((C, columns - at), bf16)
        for number, (copies, left, right) in enumerate(waits):
            wait(copies)

            def part(cut, number=number, left=left, right=right):
                target = pl.ds(pl.multiple_of(number * C + cut.start, TILE), TILE)
                grad[target, :] = low(dot_sums(left[:, cut], right[...]))

            tiles(C, TILE, part)
        traffic.store(out_blocks, targets, table_ref, grad)
        traffic.finish()

    factor = 2 if pair else 1
    outs = [shaped(*array.shape, dtype=bf16) for array in out_blocks.operands]
    scratch = [
        pltpu.VMEM(((len(products) + (1 if sides else 0)) * C, columns), bf16),
        pltpu.SemaphoreType.DMA((out_blocks.copies + 4 * len(products),)),
    ]
    for cells in rows_of:
        scratch += [pltpu.VMEM((factor * cells, C), bf16), pltpu.VMEM((factor * cells, width), bf16)]
    besides = [array for side in sides for array in side if array is not None]
    return call(
        kernel,
        "plain_terms",
        [table] + given + besides,
        [SMEM] + [ANY] * n_given + [IN] * len(besides),
        outs,
        [ANY] * n_outs,
        scratch,
        sum(2 * factor * cells * C * width for cells in rows_of),
        2 * len(products) * C * columns + sum(4 * factor * cells * C for cells in rows_of),
    )


def back_first(table, number, side, grads, pre1, direct, misc, rest, w_middle, w_first):
    cells = side * side
    closing = rest is not None
    n_middle, n_first = len(w_middle.operands), len(w_first.operands)
    bf16 = jnp.bfloat16
    extra = [rest] if closing else []
    half = C // 2
    side_half = SIDE

    def kernel(table_ref, grads_in, pre1_in, direct_in, misc_ref, *refs):
        refs = list(refs)
        rest_ref = refs.pop(0) if closing else None
        middles = [refs.pop(0) for _ in range(n_middle)]
        firsts = [refs.pop(0) for _ in range(n_first)]
        grad_u, sums, grad_pre1, other = [refs.pop(0) for _ in range(4)]
        turned = [refs.pop(0), refs.pop(0)] if closing else None
        wm, wi, grad_ref, pre1_ref, direct_ref, taps, above, below, work, parts, sems = refs
        traffic = Traffic(sems)
        given = traffic.begin(grads_in.at[1], grad_ref)
        middle_copies = traffic.load(w_middle, middles, table_ref, wm)
        pre1_copy = traffic.begin(pre1_in, pre1_ref)
        first_copies = traffic.load(w_first, firsts, table_ref, wi)
        direct_copy = traffic.begin(direct_in, direct_ref)
        parts[...] = jnp.zeros_like(parts)
        zeros = jnp.zeros((PAD, TILE), jnp.float32)
        for ref in (above, below):
            ref[:PAD, :] = zeros
            ref[PAD + cells :, :] = zeros
        given.wait()

        def spread(i, carry):
            cut = pl.ds(pl.multiple_of(i * 128, 128), 128)
            value = wide(grad_ref[:, cut])
            taps[:, cut] = low(beside(value, side, 1))
            taps[:, pl.ds(pl.multiple_of(C + i * 128, 128), 128)] = grad_ref[:, cut]
            taps[:, pl.ds(pl.multiple_of(2 * C + i * 128, 128), 128)] = low(beside(value, side, -1))
            return carry

        lax.fori_loop(0, C // 128, spread, 0)
        wait(middle_copies)

        def middle(i, carry):
            def row(tap):
                total = None
                for column in range(3):
                    source = pl.ds(pl.multiple_of((3 * tap + column) * C + i * TILE, TILE), TILE)
                    term = dot_rows(taps[:, column * C : (column + 1) * C], wm[source, :])
                    total = term if total is None else total + term
                return total

            above[PAD : PAD + cells, :] = row(0)
            below[PAD : PAD + cells, :] = row(2)
            cut = pl.ds(pl.multiple_of(i * TILE, TILE), TILE)
            work[:, cut] = (
                row(1) + above[PAD + side : PAD + side + cells, :] + below[PAD - side : PAD - side + cells, :]
            )
            return carry

        lax.fori_loop(0, C // TILE, middle, 0)
        gain = misc_ref[3 * number : 3 * number + 1, :]
        bias = misc_ref[6 + 3 * number : 7 + 3 * number, :]
        pre1_copy.wait()

        def norm(rows):
            normal, scale = centered(pre1_ref[rows, :])
            hidden = normal * gain + bias
            inner = work[rows, :] * silu_back(hidden)
            parts[0:8, :] += fold(inner * normal)
            parts[8:16, :] += fold(inner)
            grad_pre1[0, rows, :] = low(norm_back(inner, normal, scale, gain))

        tiles(cells, ROWS, norm)
        sums[...] = jnp.sum(parts[...].reshape(2, 8, C), axis=1)
        core = table_ref[CORE]
        other[...] = grad_pre1[0, :, pl.ds(pl.multiple_of((1 - core) * half, half), half)]
        wait(first_copies)
        direct_copy.wait()

        def first(cut):
            grad_u[:, cut] = direct_ref[:, cut] + dot_rows(grad_pre1[0], wi[cut, :])

        tiles(C, TILE, first)
        if closing:

            def turn(cut):
                stacked = jnp.concatenate(
                    [
                        grad_u[:, cut],
                        sums[0:1, cut],
                        rest_ref[1:6, cut],
                        sums[1:2, cut],
                        rest_ref[7:MISC, cut],
                        jnp.zeros((2 * side_half - cells - MISC, 128), jnp.float32),
                    ]
                )
                parts_of = low(jnp.transpose(stacked))
                for part in range(2):
                    piece = parts_of[:, part * side_half : (part + 1) * side_half]

                    @pl.when(core == part)
                    def _(piece=piece):
                        turned[0][cut, :] = piece

                    @pl.when(core != part)
                    def _(piece=piece):
                        turned[1][cut, :] = piece

            tiles(C, 128, turn)

    outs = [shaped(cells, C), shaped(2, C), shaped(1, cells, C, dtype=bf16), shaped(cells, half, dtype=bf16)]
    if closing:
        outs += [shaped(C, side_half, dtype=bf16)] * 2
    f32 = jnp.float32
    scratch = [
        pltpu.VMEM((9 * C, C), bf16),
        pltpu.VMEM((C, C), bf16),
        pltpu.VMEM((cells, C), bf16),
        pltpu.VMEM((cells, C), f32),
        pltpu.VMEM((cells, C), f32),
        pltpu.VMEM((cells, 3 * C), bf16),
        pltpu.VMEM((cells + 2 * PAD, TILE), f32),
        pltpu.VMEM((cells + 2 * PAD, TILE), f32),
        pltpu.VMEM((cells, C), f32),
        pltpu.VMEM((16, C), f32),
        pltpu.SemaphoreType.DMA((w_middle.copies + w_first.copies + 3,)),
    ]
    weights = w_middle.operands + w_first.operands
    return call(
        kernel,
        "back_first",
        [table, grads, pre1, direct, misc] + extra + weights,
        [SMEM] + [ANY] * 3 + [IN] * (1 + len(extra)) + [ANY] * len(weights),
        outs,
        [IN] * len(outs),
        scratch,
        2 * cells * 10 * C * C,
        20 * C * C + 24 * cells * C,
    )


def after(value, *earlier):
    return lax.optimization_barrier((value, earlier))[0]


class Movement:
    def __init__(self, mesh):
        self.dp = mesh.shape["dp"]
        self.cores = mesh.shape["fsdp"]
        self.line = self.dp // PLANE
        self.devices = self.dp * self.cores
        self.ring = [0] + list(range(1, self.line, 2)) + list(range(2, self.line, 2))[::-1]
        self.paired = self.cores == 2 and self.line == 4

    def flip(self, value, bits):
        return lax.ppermute(value, "dp", [(i, i ^ bits) for i in range(self.dp)])

    def along(self, value):
        pairs = []
        for position, level in enumerate(self.ring):
            following = self.ring[(position + 1) % self.line]
            pairs += [(level * PLANE + near, following * PLANE + near) for near in range(PLANE)]
        return lax.ppermute(value, "dp", pairs)

    def swap(self, value):
        return lax.ppermute(value, "fsdp", [(0, 1), (1, 0)])

    def lines(self):
        return [[level * PLANE + near for level in range(self.line)] for near in range(PLANE)]

    def table(self):
        if not self.paired:
            return jnp.zeros((TABLE,), jnp.int32)
        steps, chips = range(self.line), range(PLANE)
        halves = [(1, 0), (1, 1), (3, 0), (3, 1), (2, 2), (2, 3), (3, 2), (3, 3), (1, 2), (1, 3), (2, 0), (2, 1)]
        halves += [(0, step) for step in steps]
        rows = []
        for device in range(self.devices):
            chip, core = divmod(device, 2)
            level, near = divmod(chip, PLANE)
            position = self.ring.index(level)

            def chip_at(far, level, near=near):
                return level * PLANE + (near ^ far)

            def step_at(step, position=position):
                return self.ring[(position + step) % self.line]

            row = [chip_at(far, step_at(-step)) * 2 + (core + k) % 2 for k in range(2) for far in chips for step in steps]
            row += [chip_at(far, step) * 2 + (core + k) % 2 for k in range(2) for far in chips for step in steps]
            row += [chip_at(far, step_at(step)) for far, step in halves]
            row += [chip_at(far, step) for far, step in halves]
            row += [chip_at(far, step_at(step)) for step in reversed(steps) for far in chips]
            rows.append(row + [core])
        index = lax.axis_index("dp") * self.cores + lax.axis_index("fsdp")
        return lax.dynamic_index_in_dim(jnp.asarray(np.array(rows, np.int32)), index, 0, keepdims=False)


class Piece:
    def __init__(self, move, own, name):
        self.move = move
        self.own = own
        self.name = name
        self.rows = own.shape[0]
        self.at = STEPS
        self.found = []

    def keep(self, array, far, steps, first=0, other=None):
        for i, step in enumerate(steps):
            for core, held in enumerate((array, other)):
                self.found.append((held, first + i * self.rows, self.at + 16 * core + 4 * far + step))

    def line(self, second, third):
        with jax.named_scope(self.name + "_line"):
            one = self.move.along(self.own)
            two = self.move.along(after(one, *second) if second else one)
            three = self.move.along(after(two, *third))
        self.passed = (one, two, three)
        self.held = jnp.concatenate([self.own, one, two, three])

    def levels(self, *earlier):
        with jax.named_scope(self.name + "_levels"):
            own = after(self.own, *earlier) if earlier else self.own
            self.held = lax.all_gather(own, "dp", axis_index_groups=self.move.lines(), axis=0, tiled=True)
        self.at = LEVELS

    def settle_line(self, *earlier):
        with jax.named_scope("swap"):
            other = self.move.swap(after(self.held, *earlier) if earlier else self.held)
        self.keep(self.held, 0, range(4), other=other)

    def plane_first(self):
        half = self.rows // 2
        with jax.named_scope(self.name + "_plane"):
            first, second = self.sides = self.move.flip(self.own, 1), self.move.flip(self.own, 2)
            self.fars = (self.move.flip(first[:half], 2), self.move.flip(second[half:], 1))
            self.passed = (jnp.concatenate([self.own, first, second, *self.fars]),)

    def pass_on(self, *earlier):
        with jax.named_scope(self.name + "_line"):
            self.passed += (self.move.along(after(self.passed[-1], *earlier)),)

    def end_line(self, *earlier):
        for step, array in enumerate(after(self.passed, *earlier)):
            other = self.move.swap(array)
            for far in range(PLANE):
                self.keep(array, far, [step], first=far * self.rows, other=other)


def cross(move, pieces, fars, *earlier):
    over_first = [piece.held for piece in pieces] + [piece.second[2 * piece.rows : 4 * piece.rows] for piece in fars]
    over_second = [piece.held for piece in pieces] + [piece.first[: 2 * piece.rows] for piece in fars]
    over_first, over_second = [jnp.concatenate(parts) if len(parts) > 1 else parts[0] for parts in (over_first, over_second)]
    if earlier:
        over_first, over_second = after((over_first, over_second), *earlier)
    with jax.named_scope("_".join(piece.name for piece in pieces + fars) + "_plane"):
        first, second = move.flip(over_first, 1), move.flip(over_second, 2)
    row = 0
    for piece in pieces:
        piece.sides = (first, second, row)
        piece.first = first[row : row + 4 * piece.rows]
        piece.second = second[row : row + 4 * piece.rows]
        row += 4 * piece.rows
    for piece in fars:
        piece.far_sides = (first, second, row)
        piece.far_first = first
        row += 2 * piece.rows
    return first, second


def settle(move, pieces, fars, *earlier):
    first, second = (pieces[0].sides if pieces else fars[0].far_sides)[:2]
    if earlier:
        first, second = after((first, second), *earlier)
    with jax.named_scope("swap"):
        first_other, second_other = move.swap(first), move.swap(second)
    for piece in pieces:
        row = piece.sides[2]
        piece.first = first[row : row + 4 * piece.rows]
        piece.second = second[row : row + 4 * piece.rows]
        piece.keep(first, 1, range(4), first=row, other=first_other)
        piece.keep(second, 2, range(4), first=row, other=second_other)
    for piece in fars:
        row = piece.far_sides[2]
        piece.keep(first, 3, (2, 3), first=row, other=first_other)
        piece.keep(second, 3, (0, 1), first=row, other=second_other)


class Sum:
    def __init__(self, move, arrays, name, levels=False):
        self.move = move
        self.arrays = arrays
        self.name = name
        self.levels = levels

    def across(self, *earlier):
        first, second = after(tuple(self.arrays[:2]), *earlier) if earlier else self.arrays[:2]
        with jax.named_scope(self.name + "_across"):
            self.first = self.move.flip(first, 1)
            self.second = self.move.flip(second, 2)
        return self.first, self.second

    def prepare(self, *earlier):
        self.first, self.second = after((self.first, self.second), *earlier)
        with jax.named_scope(self.name + "_onward"):
            self.rests = (
                low(wide(self.arrays[2]) + wide(self.second[2:])),
                low(wide(self.arrays[3]) + wide(self.first[2:])),
            )
        return self.rests

    def onward(self):
        with jax.named_scope(self.name + "_onward"):
            self.rests = (self.move.flip(self.rests[0], 1), self.move.flip(self.rests[1], 2))
        return self.rests

    def gather(self, *earlier):
        rests = after(self.rests, *earlier) if earlier else self.rests
        with jax.named_scope(self.name + "_held"):
            held = self.arrays[4]
            self.near = wide(held[:2]) + wide(self.first[:2]) + wide(rests[1])
            self.far = wide(held[2:]) + wide(self.second[:2]) + wide(rests[0])
            if self.levels:
                held = jnp.concatenate([low(self.near), low(self.far)])
                self.held = held.reshape(-1, held.shape[-1])
                return self.held

    def finish(self, *earlier):
        with jax.named_scope(self.name + "_line"):
            if self.levels:
                lines = self.move.lines()
                owned = lax.psum_scatter(self.held, "dp", axis_index_groups=lines, scatter_dimension=0, tiled=True)
                self.owned = wide(owned)
            else:
                three = self.move.along(low(self.far[1]))
                if earlier:
                    three = after(three, *earlier)
                two = self.move.along(low(self.far[0] + wide(three)))
                one = self.move.along(low(self.near[1] + wide(two)))
                self.owned = self.near[0] + wide(one)


class LineSum:
    def __init__(self, move, arrays, name):
        self.move = move
        self.arrays = arrays
        self.name = name
        self.next = arrays[0]

    def line(self, step):
        with jax.named_scope(f"{self.name}_line{step}"):
            self.sent = self.move.along(self.next)

    def prepare(self, step, *earlier):
        with jax.named_scope(f"{self.name}_line{step}"):
            sent = after(self.sent, *earlier) if earlier else self.sent
            self.next = low(wide(self.arrays[step]) + wide(sent))
        return self.next

    def across(self):
        with jax.named_scope(self.name + "_across"):
            held = wide(self.arrays[3]) + wide(self.sent)
            half = held.shape[1] // 2
            self.near, self.rest = held[:, :half], held[:, half:]
            self.operands = (low(self.near[1::2]), low(self.rest[2:]))
            self.first = self.move.flip(self.operands[0], 1)
            self.second = self.move.flip(self.operands[1], 2)

    def finish(self):
        with jax.named_scope(self.name + "_onward"):
            first_rest = self.move.flip(low(self.rest[1] + wide(self.second[1])), 1)
            second_rest = self.move.flip(low(self.near[2] + wide(self.first[1])), 2)
            near = self.near[0] + wide(self.first[0]) + wide(second_rest)
            rest = self.rest[0] + wide(self.second[0]) + wide(first_rest)
            self.owned = jnp.concatenate([near, rest])


def unite(move, owned, matrices):
    blocks = owned.reshape(matrices, 2, -1, owned.shape[-1])
    core = lax.axis_index("fsdp")
    mine = lax.dynamic_index_in_dim(blocks, core, 1, keepdims=False)
    other = move.swap(lax.dynamic_index_in_dim(blocks, 1 - core, 1, keepdims=False))
    return jnp.where(core == 0, jnp.stack([mine, other], 2), jnp.stack([other, mine], 2))


def local(
    move,
    features,
    grid_live,
    pos_embed,
    w_in,
    w_mid,
    w_out,
    norm_gain,
    norm_bias,
    readout_w,
    readout_b,
    cotangent,
):
    rows, middle_rows, width = w_in.shape[1], w_mid.shape[1], readout_w.shape[1]
    cells = pos_embed.shape[0]
    half_side = G // 2
    paired = move.paired
    scales = [norm_gain.reshape(6, rows).T, norm_bias.reshape(6, rows).T, readout_b.reshape(rows, 4)]
    beside = jnp.concatenate([pos_embed.T, *scales, jnp.zeros((rows, C - cells - MISC), jnp.bfloat16)], axis=1)
    if paired:
        cut = middle_rows // 2
        stacks = [
            [w_in[0], beside, w_out[0]],
            [w_mid[0, :cut]],
            [w_mid[0, cut:], w_in[1], w_out[1]],
            [w_mid[1]],
            [readout_w[:, i * C : (i + 1) * C] for i in range(width // C)],
        ]
        one, two, three, four, top = [
            Piece(move, jnp.concatenate(stack) if len(stack) > 1 else stack[0], name)
            for stack, name in zip(stacks, ("one", "two", "three", "four", "top"))
        ]
        top.plane_first()
        one.line((), top.sides)
        two.line(one.passed[1:2], one.passed[2:])
        three.line(two.passed[1:2], two.passed[2:])
        four.levels(three.passed[1])
        cross(move, [one], [], *top.fars)
        cross(move, [two], [one], one.first)
        one.settle_line(one.first)
        settle(move, [one], [], one.first)
        cross(move, [three], [two], two.first)
        two.settle_line(two.first)
        settle(move, [two], [one], two.first)
        top.pass_on(two.first)
        cross(move, [], [three], three.first)
        three.settle_line(three.first)
        settle(move, [three], [two], three.first)
        cross(move, [four], [], three.far_first)
        top.pass_on(three.far_first)
        settle(move, [], [three], three.far_first)
        lies = {
            "first_0": [(one, 0, rows, 0, 0, C)],
            "head_0": [(one, 0, rows, 0, 0, C), (one, rows, rows, 0, C, HEAD - C)],
            "middle_0": [(two, 0, cut, 0, 0, C), (three, 0, cut, cut, 0, C)],
            "last_0": [(one, 2 * rows, rows, 0, 0, C)],
            "first_1": [(three, cut, rows, 0, 0, C)],
            "last_1": [(three, cut + rows, rows, 0, 0, C)],
            "middle_1": [(four, 0, middle_rows, 0, 0, C)],
            "readout": [(top, i * rows, rows, 0, i * C, C) for i in range(width // C)],
        }
    else:

        def whole(own):
            return lax.all_gather(own, ("dp", "fsdp"), axis=0, tiled=True)

        first_all = whole(w_in[0])
        lies = {
            "first_0": [(first_all, 0)],
            "head_0": [(first_all, 0), (whole(beside[:, : HEAD - C]), C)],
            "middle_0": [(whole(w_mid[0]), 0)],
            "last_0": [(whole(w_out[0]), 0)],
            "first_1": [(whole(w_in[1]), 0)],
            "last_1": [(whole(w_out[1]), 0)],
            "middle_1": [(whole(w_mid[1]), 0)],
            "readout": [(whole(readout_w), 0)],
        }

    def matrix(name):
        blocks = Blocks(middle_rows if name.startswith("middle") else rows)
        if not paired:
            for array, column in lies[name]:
                blocks.add(array, None, 0, 0, None, 0, column, *array.shape)
            return blocks
        for piece, row, extent, to_row, to_column, columns in lies[name]:
            for array, first, place in piece.found:
                blocks.add(array, None, first + row, 0, place, to_row, to_column, extent, columns)
        return blocks

    def sums_of(block_rows, columns, matrices=1, parts=1, levels=False, last_line=False):
        if not paired:
            extent = matrices * move.devices * block_rows
            blocks = Blocks(block_rows)
            blocks.add(shaped(1, extent, columns), 0, 0, 0, None, 0, 0, extent, columns)
            return blocks
        chip_rows = 2 * block_rows
        cut = chip_rows // parts
        blocks = Blocks(chip_rows)
        for part in range(parts):
            line_first = last_line and part == parts - 1
            place = OUT_LINE if line_first else OUT_LEVELS if levels else OUT_STEPS
            for count in (4, 4, 4, 4) if line_first else (4, 4, 2, 2, 4):
                array = shaped(count, matrices * cut, columns)
                for block in range(count):
                    for i in range(matrices):
                        blocks.add(array, block, i * cut, 0, place, i * C + part * cut, 0, cut, columns)
                    place += 1
        return blocks

    def swap(value):
        return move.swap(value) if paired else None

    def tie(value, *earlier):
        return after(value, *earlier) if paired else value

    def scattered(terms, matrices=1):
        total = wide(terms[0][0]).reshape(matrices, -1, terms[0].shape[-1])
        return lax.psum_scatter(total, ("dp", "fsdp"), scatter_dimension=1, tiled=True)

    half = 2 if paired else 1
    table = move.table()
    mid_0, last_0 = matrix("middle_0"), matrix("last_0")
    misc, pooled, stream_in, lefts_0, pre1_0, pre2_0, pre3_0 = forward_block(
        table, 0, G, None, features[0], None, matrix("head_0"), mid_0, last_0
    )
    lefts_other_0 = swap(lefts_0)
    if paired:
        settle(move, [four], [], pooled)
        cross(move, [], [four])
        top.pass_on(pooled)
        four.settle_line(pooled)
        settle(move, [], [four])
    first_1, mid_1, last_1 = matrix("first_1"), matrix("middle_1"), matrix("last_1")
    lefts_1, pre1_1, pre2_1, pre3_1 = forward_block(table, 1, half_side, pooled, None, misc, first_1, mid_1, last_1)
    lefts_other_1 = swap(lefts_1)
    if paired:
        top.end_line(lefts_1)
    readout_bias = misc[12:].T.reshape(1, width)
    output, grad_top, grad_readout_b, grad_logits, grad_logits_other = readout(
        table, grid_live, lefts_1, readout_bias, cotangent[0], matrix("readout")
    )
    if paired:
        grad_logits_other = swap(grad_logits_other)
    else:
        grad_logits, grad_logits_other = jnp.concatenate([grad_logits, grad_logits_other], axis=1), None
    direct_1, grads_1, grads_other_1, sums_1 = back_last(
        table, 1, half_side, grad_top, pooled, pre3_1, pre2_1, misc, last_1
    )
    grads_other_1 = swap(grads_other_1)
    readout_terms = plain_terms(
        table,
        [(lefts_1, 3, lefts_other_1, tie(grad_logits, sums_1), None, grad_logits_other, None)],
        [],
        sums_of(rows, width // half, levels=True),
    )
    middle_terms_1 = middle_terms(
        table,
        half_side,
        tie(lefts_1, *readout_terms),
        lefts_other_1,
        grads_1,
        grads_other_1,
        sums_of(middle_rows, C // half, parts=2 if paired else 1, levels=True),
    )
    if paired:
        sum_readout = Sum(move, readout_terms, "readout", levels=True)
        sums_middle_1 = [Sum(move, middle_terms_1[5 * i : 5 * i + 5], f"middle_1_{i}", levels=True) for i in range(2)]
        sum_readout.across()
        sums_middle_1[0].across()
        grads_1 = tie(grads_1, *middle_terms_1)
    grad_pooled, sums_first_1, grad_first_1, grad_first_other_1 = back_first(
        table, 1, half_side, grads_1, pre1_1, direct_1, misc, None, mid_1, first_1
    )
    grad_first_other_1 = swap(grad_first_other_1)
    if paired:
        grad_pooled = tie(grad_pooled, *sum_readout.prepare(grad_pooled))
        sum_readout.onward()
    direct_0, grads_0, grads_other_0, sums_0 = back_last(
        table, 0, G, grad_pooled, stream_in, pre3_0, pre2_0, misc, last_0
    )
    grads_other_0 = swap(grads_other_0)
    if paired:
        held = sum_readout.gather(sums_0)
        lefts_other_0 = tie(lefts_other_0, held, *sums_middle_1[0].prepare(sums_0))
        sum_readout.finish()
        sums_middle_1[0].onward()
        sums_middle_1[1].across(sums_0)
    middle_terms_0 = middle_terms(
        table,
        G,
        lefts_0,
        lefts_other_0,
        grads_0,
        grads_other_0,
        sums_of(middle_rows, C // half, parts=2 if paired else 1, last_line=True),
    )
    if paired:
        sum_middle_0 = Sum(move, middle_terms_0[:5], "middle_0_0")
        line_middle_0 = LineSum(move, middle_terms_0[5:], "middle_0_1")
        waited = [sums_middle_1[0].gather(*middle_terms_0), *sums_middle_1[1].prepare(*middle_terms_0)]
        grads_0 = tie(grads_0, *middle_terms_0, *waited)
        sums_middle_1[0].finish()
        sums_middle_1[1].onward()
        sum_middle_0.across()
        line_middle_0.line(0)
    blank = jnp.zeros((1, C), jnp.float32)
    rest = jnp.concatenate(
        [
            blank, sums_0[2:3], sums_0[0:1], sums_first_1[0:1], sums_1[2:3], sums_1[0:1],
            blank, sums_0[3:4], sums_0[1:2], sums_first_1[1:2], sums_1[3:4], sums_1[1:2],
            grad_readout_b.reshape(C, 4).T,
        ]
    )
    grad_in, _, grad_first_0, grad_first_other_0, side, side_other = back_first(
        table, 0, G, grads_0, pre1_0, direct_0, misc, rest, mid_0, matrix("first_0")
    )
    grad_first_other_0 = swap(grad_first_other_0)
    if paired:
        sides = [(side, swap(side_other))]
        waited = [line_middle_0.prepare(1, grad_in), *sum_middle_0.prepare(grad_in), sums_middle_1[1].gather(grad_in)]
        lefts_other_0 = tie(lefts_other_0, *waited)
        line_middle_0.line(1)
        sum_middle_0.onward()
        sums_middle_1[1].finish()
    else:
        sides = [(side, None), (side_other, None)]
    last_terms = plain_terms(
        table,
        [
            (lefts_0, 2, lefts_other_0, grads_0, 0, grads_other_0, 0),
            (lefts_1, 0, lefts_other_1, grad_first_1, 0, grad_first_other_1, None),
            (lefts_1, 2, lefts_other_1, grads_1, 0, grads_other_1, 0),
            (lefts_0, 0, lefts_other_0, grad_first_0, 0, grad_first_other_0, None),
        ],
        sides,
        sums_of(rows, C // half, matrices=5),
    )
    if paired:
        sum_last = Sum(move, last_terms, "last")
        sum_last.across()
        waited = sum_middle_0.gather(*last_terms)
        next_line = line_middle_0.prepare(2, *last_terms)
        line_middle_0.line(2)
        sum_middle_0.finish(next_line)
        sum_last.prepare(next_line)
        sum_last.onward()
        line_middle_0.across()
        sum_last.gather(*line_middle_0.operands)
        sum_last.finish()
        line_middle_0.finish()
        readout_owned = unite(move, sum_readout.owned, 1).reshape(rows, width)
        owned_1 = jnp.concatenate([total.owned for total in sums_middle_1])
        owned_0 = jnp.concatenate([sum_middle_0.owned, line_middle_0.owned])
        middle_owned = [unite(move, owned, 1).reshape(middle_rows, C) for owned in (owned_0, owned_1)]
        last_owned = unite(move, sum_last.owned, 5)
        side_owned = jnp.concatenate([last_owned[4, :, i, :SIDE] for i in range(2)], axis=1)
        last_owned = last_owned.reshape(5, rows, C)
    else:
        readout_owned = scattered(readout_terms)[0]
        middle_owned = [scattered(terms)[0] for terms in (middle_terms_0, middle_terms_1)]
        last_owned = scattered(last_terms, 5)
        side_owned = last_owned[4]
    scales = side_owned[:, cells : cells + MISC]
    return (
        output[None],
        grad_in[None],
        side_owned[:, :cells].T,
        jnp.stack([last_owned[3], last_owned[1]]),
        jnp.stack(middle_owned),
        jnp.stack([last_owned[0], last_owned[2]]),
        scales[:, 0:6].T.reshape(2, 3, rows),
        scales[:, 6:12].T.reshape(2, 3, rows),
        readout_owned,
        scales[:, 12:].reshape(-1),
    )


def solution(mesh):
    return jax.shard_map(
        functools.partial(local, Movement(mesh)),
        mesh=mesh,
        in_specs=(
            P(("dp", "fsdp"), None, None),
            P(("dp", "fsdp")),
            P(None, ("dp", "fsdp")),
            P(None, ("dp", "fsdp"), None),
            P(None, ("dp", "fsdp"), None),
            P(None, ("dp", "fsdp"), None),
            P(None, None, ("dp", "fsdp")),
            P(None, None, ("dp", "fsdp")),
            P(("dp", "fsdp"), None),
            P(("dp", "fsdp")),
            P(("dp", "fsdp"), None, None),
        ),
        out_specs=(
            P(("dp", "fsdp"), None, None),
            P(("dp", "fsdp"), None, None),
            P(None, ("dp", "fsdp")),
            P(None, ("dp", "fsdp"), None),
            P(None, ("dp", "fsdp"), None),
            P(None, ("dp", "fsdp"), None),
            P(None, None, ("dp", "fsdp")),
            P(None, None, ("dp", "fsdp")),
            P(("dp", "fsdp"), None),
            P(("dp", "fsdp")),
        ),
        check_vma=False,
    )
```

time: 819 us -> 668 us (0.82)
  waiting for transfers between devices: 319 us -> 253 us
  starting transfers between devices: 147 us -> 92.3 us
  Pallas kernels: 221 us -> 192 us
  other arithmetic: 68.8 us -> 53.3 us
  between operations: 3.23 us -> 16.3 us
    ppermute x64 -> x40, waiting for transfers between devices: 204 us -> 88 us  [flip(): return lax.ppermute(value, 'dp', [(i, i ^ bits) for i in range(self.dp)])]
    ppermute x48 -> x21, waiting for transfers between devices: 108 us -> 148 us  [along(): return lax.ppermute(value, 'dp', pairs)]
    ppermute x64 -> x40, starting transfers between devices: 82.1 us -> 49.1 us  [flip(): return lax.ppermute(value, 'dp', [(i, i ^ bits) for i in range(self.dp)])]
    pallas_call x9 -> x11, Pallas kernels: 221 us -> 192 us  [call(): pl.pallas_call(kernel, name=name, out_shape=outs, in_specs=in_specs, out_...]
    add x21 -> x6, other arithmetic: 32.3 us -> 6.28 us  [the longest x2 3.18 us: gather(): self.far = wide(held[2:]) + wide(self.second[:2]) + wide(rests[0])]
    ppermute x48 -> x21, starting transfers between devices: 61.8 us -> 37.5 us  [along(): return lax.ppermute(value, 'dp', pairs)]
    convert_element_type x20, other arithmetic: 9.11 us -> 29.2 us  [low(): return value.astype(jnp.bfloat16)]
    another operation x22 -> x3, other arithmetic: 18.3 us -> 3 us  [the longest x1 1.56 us: local(): jnp.stack(middle_owned)]
  transfers between devices with their start and end apart: 128 -> 97, of which waited for: 59 -> 33; matrix products, arithmetic and copies ran while one was open for 13% -> 12% of each run, Pallas kernels for 25% -> 28%
where the time goes in v3:
time: 668 us; the launch traced here: 658 us
  waiting for transfers between devices  253 us (38%)
  Pallas kernels  192 us (29%)
  starting transfers between devices  92.3 us (14%)
  other arithmetic  53.3 us (8%)
  local copies, waits for them, and re-layouts  51.2 us (8%)
  between operations  16.3 us (2%)
    pallas_call x11, Pallas kernels, call(): pl.pallas_call(kernel, name=name, out_shape=outs, in_specs=in_specs, out_...  192 us
    ppermute x21, waiting for transfers between devices, along(): return lax.ppermute(value, 'dp', pairs)  148 us
    ppermute x40, waiting for transfers between devices, flip(): return lax.ppermute(value, 'dp', [(i, i ^ bits) for i in range(self.dp)])  88 us
    ppermute x40, starting transfers between devices, flip(): return lax.ppermute(value, 'dp', [(i, i ^ bits) for i in range(self.dp)])  49.1 us
    ppermute x21, starting transfers between devices, along(): return lax.ppermute(value, 'dp', pairs)  37.5 us
    convert_element_type x20, other arithmetic, low(): return value.astype(jnp.bfloat16)  29.2 us
    unnamed x168, local copies, waits for them, and re-layouts  28 us
    ppermute x32, waiting for transfers between devices, swap(): return lax.ppermute(value, 'fsdp', [(0, 1), (1, 0)])  17 us
  transfers between devices with their start and end apart: 97, of which 33 were waited for; matrix products, arithmetic and copies ran while one was open for 12% of the time, Pallas kernels for 28%

profile of v3, /device:TPU:0, one launch (start us, length us, event | category | flops | bytes accessed | tf_op | source)
XLA Modules:
  0.0 658.0 jit_solution(15042593871717231665)
XLA Ops:
  13.5 3.0 collective-permute-start.2
  20.3 2.6 collective-permute-start.12
  24.5 2.9 collective-permute-done
  28.9 7.3 %collective-permute-done.1 = bf16[96,1024]{1,0:T(8,128)(2,1)S(1)} collective-permute-done((bf16[96,1024]{1,0:T(8,128)(2,1)S(1)}, bf16[96,1024]{1,0:T(8,128)(2,1)S(1)}, u32[]{:S(2)}, u32[]{:S(2)}) %collective-permute-start.1) | collective-permute-done | bytes 196640 | tf_op jit(solution)/shard_map/one_line/ppermute | solution.py:830
  38.2 4.5 collective-permute-done.4
  43.4 3.8 collective-permute-start.13
  48.9 5.5 collective-permute-done.13
  54.4 2.5 collective-permute-start.14
  56.9 5.4 collective-permute-done.14
  63.1 2.5 collective-permute-start.15
  67.1 2.9 collective-permute-start.16
  70.0 9.0 %collective-permute-done.20 = bf16[208,1024]{1,0:T(8,128)(2,1)S(1)} collective-permute-done((bf16[208,1024]{1,0:T(8,128)(2,1)S(1)}, bf16[208,1024]{1,0:T(8,128)(2,1)S(1)}, u32[]{:S(2)}, u32[]{:S(2)}) %collective-permute-start.20) | collective-permute-done | bytes 426016 | tf_op jit(solution)/shard_map/three_line/ppermute | solution.py:830
  79.7 11.7 %collective-permute-done.21 = bf16[208,1024]{1,0:T(8,128)(2,1)S(1)} collective-permute-done((bf16[208,1024]{1,0:T(8,128)(2,1)S(1)}, bf16[208,1024]{1,0:T(8,128)(2,1)S(1)}, u32[]{:S(2)}, u32[]{:S(2)}) %collective-permute-start.21) | collective-permute-done | bytes 426016 | tf_op jit(solution)/shard_map/three_line/ppermute | solution.py:830
  93.4 7.0 %collective-permute-done.22 = bf16[208,1024]{1,0:T(8,128)(2,1)S(1)} collective-permute-done((bf16[208,1024]{1,0:T(8,128)(2,1)S(1)}, bf16[208,1024]{1,0:T(8,128)(2,1)S(1)}, u32[]{:S(2)}, u32[]{:S(2)}) %collective-permute-start.22) | collective-permute-done | bytes 426016 | tf_op jit(solution)/shard_map/three_line/ppermute | solution.py:830
  101.5 3.2 copy.72
  106.7 2.4 collective-permute-start.24
  113.4 33.1 %collective-permute-done.41.refs_2_ = bf16[512,1024]{1,0:T(8,128)(2,1)} collective-permute-done((bf16[512,1024]{1,0:T(8,128)(2,1)}, bf16[512,1024]{1,0:T(8,128)(2,1)}, u32[]{:S(2)}, u32[]{:S(2)}) %collective-permute-start.41) | collective-permute-done | bytes 1048608 | tf_op jit(solution)/shard_map/top_line/ppermute | solution.py:830
  149.9 1.8 slice.418
  151.9 1.8 collective-permute-start.29
  153.7 19.0 %collective-permute-done.28.refs_23_.refs_8_.refs_28_.refs_6_.refs_16_.refs_13_ = bf16[416,1024]{1,0:T(8,128)(2,1)S(1)} collective-permute-done((bf16[416,1024]{1,0:T(8,128)(2,1)S(1)}, bf16[416,1024]{1,0:T(8,128)(2,1)S(1)}, u32[]{:S(2)}, u32[]{:S(2)}) %collective-permute-start.28) | collective-permute-done | bytes 852000 | tf_op jit(solution)/shard_map/three_plane/ppermute | solution.py:823
  176.0 4.9 collective-permute-done.30.refs_24_.refs_9_.refs_29_.refs_7_.refs_17_.refs_14_
  180.9 2.2 collective-permute-done.31.refs_26_.refs_11_.refs_31_.refs_9_.refs_19_.refs_16_
  185.8 1.9 collective-permute-start.42
  187.8 30.4 %forward_block.2 = (f32[16,1024]{1,0:T(8,128)}, f32[144,1024]{1,0:T(8,128)}, f32[576,1024]{1,0:T(8,128)}, bf16[3,576,1024]{2,1,0:T(8,128)(2,1)}, f32[576,1024]{1...) custom-call(s32[113]{0:T(128)} %fusion.21.table_ref, bf16[576,1024]{1,0:T(8,128)(2,1)} %bitcast.161, ...), custom_call_target="tpu_custom_call" | custom-call | flops 265751104 | bytes 697303 | tf_op jit(solution)/shard_map/forward_block/pallas_call | solution.py:144
  218.3 16.2 %collective-permute-done.32.refs_12_.refs_0_ = bf16[1152,1024]{1,0:T(8,128)(2,1)} collective-permute-done((bf16[1152,1024]{1,0:T(8,128)(2,1)}, bf16[1152,1024]{1,0:T(8,128)(2,1)}, u32[]{:S(2)}, u32[]{:S(2)}) %collective-permute-start.32) | collective-permute-done | bytes 2359328 | tf_op jit(solution)/shard_map/four_plane/ppermute | solution.py:823
  234.5 2.2 collective-permute-done.33.refs_14_.refs_2_
  241.9 23.5 %collective-permute-done.37.refs_18_.refs_6_ = bf16[576,1024]{1,0:T(8,128)(2,1)S(1)} collective-permute-done((bf16[576,1024]{1,0:T(8,128)(2,1)S(1)}, bf16[576,1024]{1,0:T(8,128)(2,1)S(1)}, u32[]{:S(2)}, u32[]{:S(2)}) %collective-permute-start.37) | collective-permute-done | bytes 1179680 | tf_op jit(solution)/shard_map/four_plane/ppermute | solution.py:823
  268.2 2.6 collective-permute-start.43
  272.9 15.9 %forward_block.3 = (bf16[4,144,1024]{2,1,0:T(8,128)(2,1)}, f32[144,1024]{1,0:T(8,128)}, f32[144,1024]{1,0:T(8,128)}, f32[144,1024]{1,0:T(8,128)}) custom-call(s32[113]{0:T(128)} %fusion.21.table_ref, f32[144,1024]{1,0:T(8,128)} %get-tuple-element.164.refs_0_.u_in, f32[16,1024]{1,0:T(8,128)} %get-tuple-element.165.refs_1_.misc_ref, ...), custom_call_target="tpu_custom_call" | custom-call | flops 66437776 | bytes 520355 | tf_op jit(solution)/shard_map/forward_block/pallas_call | solution.py:144
  288.8 6.5 collective-permute-done.43.refs_6_
  300.9 1.9 collective-permute-done.46.refs_5_
  302.8 15.2 %readout.1 = (bf16[144,4096]{1,0:T(8,128)(2,1)}, f32[144,1024]{1,0:T(8,128)}, f32[1,4096]{1,0:T(1,128)}, bf16[144,2048]{1,0:T(8,128)(2,1)}, bf16[144,2048]{1,0:T(8,128)(2,1)}) custom-call(s32[113]{0:T(128)} %fusion.21.table_ref, s32[1]{0:T(128)S(6)} %copy.77.live_ref, bf16[4,144,1024]{2,1,0:T(8,128)(2,1)} %get-tuple-element.193.lefts_ref.refs_0_.refs_4_.refs_8_, ...), custom_call_target="tpu_custom_call" | custom-call | flops 80530640 | bytes 358263 | tf_op jit(solution)/shard_map/readout/pallas_call | solution.py:144
  318.2 6.4 back_last.2
  324.6 7.6 %plain_terms.2 = (bf16[4,64,2048]{2,1,0:T(8,128)(2,1)}, bf16[4,64,2048]{2,1,0:T(8,128)(2,1)}, bf16[2,64,2048]{2,1,0:T(8,128)(2,1)}, bf16[2,64,2048]{2,1,0:T(8,128)(2,1)}, bf16[4,64,2048]{2,1,0:T(8,128)(2,1)}) custom-call(s32[113]{0:T(128)} %fusion.21.table_ref, bf16[4,144,1024]{2,1,0:T(8,128)(2,1)} %get-tuple-element.193.lefts_ref.refs_0_.refs_4_.refs_8_, ...), custom_call_target="tpu_custom_call" | custom-call | flops 40265320 | bytes 179131 | tf_op jit(solution)/shard_map/plain_terms/pallas_call | solution.py:144
  336.1 6.0 collective-permute-done.50.refs_3_.refs_11_
  342.7 15.3 %middle_terms.2 = (bf16[4,288,512]{2,1,0:T(8,128)(2,1)}, bf16[4,288,512]{2,1,0:T(8,128)(2,1)}, bf16[2,288,512]{2,1,0:T(8,128)(2,1)}, bf16[2,288,512]{2,1,0:T(8,1...) custom-call(s32[113]{0:T(128)} %fusion.21.table_ref, ...), custom_call_target="tpu_custom_call" | custom-call | flops 90596968 | bytes 353894 | tf_op jit(solution)/shard_map/middle_terms/pallas_call | solution.py:144
  358.1 17.8 %back_first.2 = (f32[144,1024]{1,0:T(8,128)}, f32[2,1024]{1,0:T(2,128)}, bf16[1,144,1024]{2,1,0:T(8,128)(2,1)}, bf16[144,512]{1,0:T(8,128)(2,1)}) custom-call(s32[113]{0:T(128)} %fusion.21.table_ref, bf16[2,144,1024]{2,1,0:T(8,128)(2,1)} %get-tuple-element.205.refs_1_.grads_in.refs_9_, f32[144,1024]{1,0:T(8,128)} %get-tuple-element.206.pre1_in, ...), custom_call_target="tpu_custom_call" | custom-call | flops 100663296 | bytes 817015 | tf_op jit(solution)/shard_map/back_first/pallas_call | solution.py:144
  375.9 2.0 add_convert_fusion.16
  383.3 13.5 %back_last.3 = (f32[576,1024]{1,0:T(8,128)}, bf16[2,576,1024]{2,1,0:T(8,128)(2,1)}, bf16[2,576,512]{2,1,0:T(8,128)(2,1)}, f32[4,1024]{1,0:T(4,128)}) custom-call(s32[113]{0:T(128)} %fusion.21.table_ref, f32[144,1024]{1,0:T(8,128)} %get-tuple-element.211.grad_ref, f32[576,1024]{1,0:T(8,128)} %get-tuple-element.212.u_in, ...), custom_call_target="tpu_custom_call" | custom-call | flops 40265320 | bytes 541764 | tf_op jit(solution)/shard_map/back_last/pallas_call | solution.py:144
  396.8 2.4 add_convert_fusion.15
  400.8 19.1 %collective-permute-done.56 = bf16[4,288,512]{2,1,0:T(8,128)(2,1)} collective-permute-done((bf16[4,288,512]{2,1,0:T(8,128)(2,1)}, bf16[4,288,512]{2,1,0:T(8,128)(2,1)}, u32[]{:S(2)}, u32[]{:S(2)}) %collective-permute-start.56) | collective-permute-done | bytes 1179680 | tf_op jit(solution)/shard_map/middle_1_0_across/ppermute | solution.py:823
  421.4 2.2 add_convert_fusion.12
  424.1 2.0 add_convert_fusion.13
  426.5 26.6 %middle_terms.3 = (bf16[4,288,512]{2,1,0:T(8,128)(2,1)}, bf16[4,288,512]{2,1,0:T(8,128)(2,1)}, bf16[2,288,512]{2,1,0:T(8,128)(2,1)}, bf16[2,288,512]{2,1,0:T(8,1...) custom-call(s32[113]{0:T(128)} %fusion.21.table_ref, ...), custom_call_target="tpu_custom_call" | custom-call | flops 362387872 | bytes 471859 | tf_op jit(solution)/shard_map/middle_terms/pallas_call | solution.py:144
  457.9 3.8 collective-permute-done.60
  461.7 2.1 add_convert_fusion.11
  465.0 2.1 add_convert_fusion.8
  467.3 2.0 add_convert_fusion.9
  474.5 29.3 %back_first.3 = (f32[576,1024]{1,0:T(8,128)}, f32[2,1024]{1,0:T(2,128)}, bf16[1,576,1024]{2,1,0:T(8,128)(2,1)}, bf16[576,512]{1,0:T(8,128)(2,1)}, bf16[1024,384]{1,0:T(8,128)(2,1)}, /*index=5*/bf16[1024,384]{1,0:T(8,128)(2,1)}) custom-call(s32[113]{0:T(128)} %fusion.21.table_ref, bf16[2,576,1024]{2,1,0:T(8,128)(2,1)} %get-tuple-element.239.refs_1_.grads_in, ...), custom_call_target="tpu_custom_call" | custom-call | flops 402653184 | bytes 1170909 | tf_op jit(solution)/shard_map/back_first/pallas_call | solution.py:144
  504.6 2.5 add_convert_fusion.5
  507.3 3.5 add_convert_fusion.1
  520.1 13.7 %plain_terms.3 = (bf16[4,320,512]{2,1,0:T(8,128)(2,1)}, bf16[4,320,512]{2,1,0:T(8,128)(2,1)}, bf16[2,320,512]{2,1,0:T(8,128)(2,1)}, bf16[2,320,512]{2,1,0:T(8,128)(2,1)}, bf16[4,320,512]{2,1,0:T(8,128)(2,1)}) custom-call(s32[113]{0:T(128)} %fusion.21.table_ref, bf16[3,576,1024]{2,1,0:T(8,128)(2,1)} %get-tuple-element.216.refs_0_.refs_12_, ...), custom_call_target="tpu_custom_call" | custom-call | flops 100663296 | bytes 533026 | tf_op jit(solution)/shard_map/plain_terms/pallas_call | solution.py:144
  539.4 3.3 collective-permute-start.83
  542.7 16.4 %collective-permute-done.73 = bf16[4,288,512]{2,1,0:T(8,128)(2,1)} collective-permute-done((bf16[4,288,512]{2,1,0:T(8,128)(2,1)}, bf16[4,288,512]{2,1,0:T(8,128)(2,1)}, u32[]{:S(2)}, u32[]{:S(2)}) %collective-permute-start.73) | collective-permute-done | bytes 1179680 | tf_op jit(solution)/shard_map/middle_0_1_line1/ppermute | solution.py:830
  562.4 4.7 collective-permute-done.83
  574.1 23.7 %collective-permute-done.84 = bf16[288,512]{1,0:T(8,128)(2,1)S(1)} collective-permute-done((bf16[288,512]{1,0:T(8,128)(2,1)S(1)}, bf16[288,512]{1,0:T(8,128)(2,1)S(1)}, u32[]{:S(2)}, u32[]{:S(2)}) %collective-permute-start.84) | collective-permute-done | bytes 294944 | tf_op jit(solution)/shard_map/middle_0_0_line/ppermute | solution.py:830
  602.8 1.8 convert_add_fusion
  604.8 1.8 collective-permute-start.86
  609.6 3.5 collective-permute-start.77
  617.3 2.6 collective-permute-done.77
  620.0 2.5 collective-permute-start.78
  622.7 6.5 collective-permute-done.78
  634.1 2.0 select_n.86
  639.8 2.9 maximum_select_fusion
  (423 shorter events, 134.4 us)
Async XLA Ops:
  7.2 168.8 %all-gather.2.cloned.1.call-start = ((), (), s32[]{:S(2)}) async-start(), calls=%async_computation.3 | async-start | bytes 2949120 | tf_op jit(solution)/shard_map/four_levels/all_gather | solution.py:891
  13.5 15.4 %collective-permute-start.2 = (bf16[128,1024]{1,0:T(8,128)(2,1)S(1)}, bf16[128,1024]{1,0:T(8,128)(2,1)S(1)}, u32[]{:S(2)}, u32[]{:S(2)}) collective-permute-start(bf16[128,1024]{1,0:T(8,128)(2,1)S(1)} %pad_maximum_fusion.8), channel_id=1, source_target_pairs={{0,2},{2,0},{4,6},{6,4},{8,10},{10,8},{12,14},{14,12},{16,18},{18,... | collective-permute-start | bytes 786440 | tf_op jit(solution)/shard_map/top_plane/ppermute | solution.py:823
  20.3 23.1 %collective-permute-start.12 = (bf16[144,1024]{1,0:T(8,128)(2,1)S(1)}, bf16[144,1024]{1,0:T(8,128)(2,1)S(1)}, u32[]{:S(2)}, u32[]{:S(2)}) collective-permute-start(bf16[144,1024]{1,0:T(8,128)(2,1)S(1)} %get-tuple-element.302), channel_id=1, source_target_pairs={{0,8},{2,10},{4,12},{6,14},{8,24},{10,26},{12,28},{14,30},{24,16},... | collective-permute-start | bytes 884744 | tf_op jit(solution)/shard_map/two_line/ppermute | solution.py:830
  42.8 20.2 %collective-permute-start.7 = (bf16[384,1024]{1,0:T(8,128)(2,1)S(1)}, bf16[384,1024]{1,0:T(8,128)(2,1)S(1)}, u32[]{:S(2)}, u32[]{:S(2)}) collective-permute-start(bf16[384,1024]{1,0:T(8,128)(2,1)S(1)} %constant_dynamic-update-slice_fusion.refs_1_.refs_27_.refs_0_.refs_17_), channel_id=1, source_target_pairs={{0,2},{2,0},{4,6},{6,4},{8,10},{10,8},{12,14},{14,12},{16,18},{18,... | collective-permute-start | bytes 2359304 | tf_op jit(solution)/shard_map/one_plane/ppermute | solution.py:823
  47.2 15.8 %collective-permute-start.9 = (bf16[384,1024]{1,0:T(8,128)(2,1)S(1)}, bf16[384,1024]{1,0:T(8,128)(2,1)S(1)}, u32[]{:S(2)}, u32[]{:S(2)}) collective-permute-start(bf16[384,1024]{1,0:T(8,128)(2,1)S(1)} %constant_dynamic-update-slice_fusion.refs_1_.refs_27_.refs_0_.refs_17_), channel_id=1, source_target_pairs={{0,4},{2,6},{4,0},{6,2},{8,12},{10,14},{12,8},{14,10},{16,20},{18,... | collective-permute-start | bytes 2359304 | tf_op jit(solution)/shard_map/one_plane/ppermute | solution.py:823
  63.1 41.6 %collective-permute-start.15 = (bf16[768,1024]{1,0:T(8,128)(2,1)S(1)}, bf16[768,1024]{1,0:T(8,128)(2,1)S(1)}, u32[]{:S(2)}, u32[]{:S(2)}) collective-permute-start(bf16[768,1024]{1,0:T(8,128)(2,1)S(1)} %slice_dynamic-update-slice_fusion.3), channel_id=1, source_target_pairs={{0,2},{2,0},{4,6},{6,4},{8,10},{10,8},{12,14},{14,12},{16,18},{18,... | collective-permute-start | bytes 4718600 | tf_op jit(solution)/shard_map/two_one_plane/ppermute | solution.py:823
  65.7 13.3 %collective-permute-start.20 = (bf16[208,1024]{1,0:T(8,128)(2,1)S(1)}, bf16[208,1024]{1,0:T(8,128)(2,1)S(1)}, u32[]{:S(2)}, u32[]{:S(2)}) collective-permute-start(bf16[208,1024]{1,0:T(8,128)(2,1)S(1)} %pad_maximum_fusion.7), channel_id=1, source_target_pairs={{0,8},{2,10},{4,12},{6,14},{8,24},{10,26},{12,28},{14,30},{24,16},... | collective-permute-start | bytes 1277960 | tf_op jit(solution)/shard_map/three_line/ppermute | solution.py:830
  67.1 38.4 %collective-permute-start.16 = (bf16[768,1024]{1,0:T(8,128)(2,1)S(1)}, bf16[768,1024]{1,0:T(8,128)(2,1)S(1)}, u32[]{:S(2)}, u32[]{:S(2)}) collective-permute-start(bf16[768,1024]{1,0:T(8,128)(2,1)S(1)} %slice_dynamic-update-slice_fusion.2), channel_id=1, source_target_pairs={{0,4},{2,6},{4,0},{6,2},{8,12},{10,14},{12,8},{14,10},{16,20},{18,... | collective-permute-start | bytes 4718600 | tf_op jit(solution)/shard_map/two_one_plane/ppermute | solution.py:823
  106.4 42.8 %collective-permute-start.23 = (bf16[1120,1024]{1,0:T(8,128)(2,1)}, bf16[1120,1024]{1,0:T(8,128)(2,1)S(1)}, u32[]{:S(2)}, u32[]{:S(2)}) collective-permute-start(bf16[1120,1024]{1,0:T(8,128)(2,1)} %slice_dynamic-update-slice_fusion.1), channel_id=1, source_target_pairs={{0,2},{2,0},{4,6},{6,4},{8,10},{10,8},{12,14},{14,12},{16,18},{18,... | collective-permute-start | bytes 6881288 | tf_op jit(solution)/shard_map/three_two_plane/ppermute | solution.py:823
  106.7 43.0 %collective-permute-start.24 = (bf16[1120,1024]{1,0:T(8,128)(2,1)}, bf16[1120,1024]{1,0:T(8,128)(2,1)}, u32[]{:S(2)}, u32[]{:S(2)}) collective-permute-start(bf16[1120,1024]{1,0:T(8,128)(2,1)} %slice_dynamic-update-slice_fusion), channel_id=1, source_target_pairs={{0,4},{2,6},{4,0},{6,2},{8,12},{10,14},{12,8},{14,10},{16,20},{18,... | collective-permute-start | bytes 6881288 | tf_op jit(solution)/shard_map/three_two_plane/ppermute | solution.py:823
  111.9 34.7 %collective-permute-start.41 = (bf16[512,1024]{1,0:T(8,128)(2,1)}, bf16[512,1024]{1,0:T(8,128)(2,1)}, u32[]{:S(2)}, u32[]{:S(2)}) collective-permute-start(bf16[512,1024]{1,0:T(8,128)(2,1)} %constant_dynamic-update-slice_fusion.32.refs_0_), channel_id=1, source_target_pairs={{0,8},{2,10},{4,12},{6,14},{8,24},{10,26},{12,28},{14,30},{24,16},... | collective-permute-start | bytes 3145736 | tf_op jit(solution)/shard_map/top_line/ppermute | solution.py:830
  112.8 403.0 %reduce-scatter.8.cloned.1.call-start = ((), (), s32[]{:S(2)}) async-start(), calls=%async_computation.6 | async-start | bytes 1310720 | tf_op jit(solution)/shard_map/readout_line/reduce_scatter | solution.py:999
  112.8 33.7 %collective-permute-start.10 = (bf16[384,1024]{1,0:T(8,128)(2,1)S(1)}, bf16[384,1024]{1,0:T(8,128)(2,1)S(1)}, u32[]{:S(2)}, u32[]{:S(2)}) collective-permute-start(bf16[384,1024]{1,0:T(8,128)(2,1)S(1)} %collective-permute-done.7.refs_3_.refs_29_.refs_2_.refs_19_), channel_id=1, source_target_pairs={{0,1},{1,0},{2,3},{3,2},{4,5},{5,4},{6,7},{7,6},{8,9},{9,8},{10,11... | collective-permute-start | bytes 2359304 | tf_op jit(solution)/shard_map/swap/ppermute | solution.py:833
  112.9 38.8 %collective-permute-start.11 = (bf16[384,1024]{1,0:T(8,128)(2,1)}, bf16[384,1024]{1,0:T(8,128)(2,1)S(1)}, u32[]{:S(2)}, u32[]{:S(2)}) collective-permute-start(bf16[384,1024]{1,0:T(8,128)(2,1)} %copy-done.9), channel_id=1, source_target_pairs={{0,1},{1,0},{2,3},{3,2},{4,5},{5,4},{6,7},{7,6},{8,9},{9,8},{10,11... | collective-permute-start | bytes 2359304 | tf_op jit(solution)/shard_map/swap/ppermute | solution.py:833
  147.5 25.8 %collective-permute-start.17 = (bf16[768,1024]{1,0:T(8,128)(2,1)}, bf16[768,1024]{1,0:T(8,128)(2,1)S(1)}, u32[]{:S(2)}, u32[]{:S(2)}) collective-permute-start(bf16[768,1024]{1,0:T(8,128)(2,1)} %copy-done.1), channel_id=1, source_target_pairs={{0,1},{1,0},{2,3},{3,2},{4,5},{5,4},{6,7},{7,6},{8,9},{9,8},{10,11... | collective-permute-start | bytes 4718600 | tf_op jit(solution)/shard_map/swap/ppermute | solution.py:833
  149.3 23.9 %collective-permute-start.19 = (bf16[576,1024]{1,0:T(8,128)(2,1)S(1)}, bf16[576,1024]{1,0:T(8,128)(2,1)S(1)}, u32[]{:S(2)}, u32[]{:S(2)}) collective-permute-start(bf16[576,1024]{1,0:T(8,128)(2,1)S(1)} %pad_maximum_fusion.1.refs_11_.refs_1_), channel_id=1, source_target_pairs={{0,1},{1,0},{2,3},{3,2},{4,5},{5,4},{6,7},{7,6},{8,9},{9,8},{10,11... | collective-permute-start | bytes 3538952 | tf_op jit(solution)/shard_map/swap/ppermute | solution.py:833
  149.7 24.0 %collective-permute-start.18 = (bf16[768,1024]{1,0:T(8,128)(2,1)S(1)}, bf16[768,1024]{1,0:T(8,128)(2,1)S(1)}, u32[]{:S(2)}, u32[]{:S(2)}) collective-permute-start(bf16[768,1024]{1,0:T(8,128)(2,1)S(1)} %copy-done.3), channel_id=1, source_target_pairs={{0,1},{1,0},{2,3},{3,2},{4,5},{5,4},{6,7},{7,6},{8,9},{9,8},{10,11... | collective-permute-start | bytes 4718600 | tf_op jit(solution)/shard_map/swap/ppermute | solution.py:833
  151.7 20.9 %collective-permute-start.28 = (bf16[416,1024]{1,0:T(8,128)(2,1)S(1)}, bf16[416,1024]{1,0:T(8,128)(2,1)S(1)}, u32[]{:S(2)}, u32[]{:S(2)}) collective-permute-start(bf16[416,1024]{1,0:T(8,128)(2,1)S(1)} %slice.418), channel_id=1, source_target_pairs={{0,2},{2,0},{4,6},{6,4},{8,10},{10,8},{12,14},{14,12},{16,18},{18,... | collective-permute-start | bytes 2555912 | tf_op jit(solution)/shard_map/three_plane/ppermute | solution.py:823
  151.9 21.0 %collective-permute-start.29 = (bf16[416,1024]{1,0:T(8,128)(2,1)S(1)}, bf16[416,1024]{1,0:T(8,128)(2,1)}, u32[]{:S(2)}, u32[]{:S(2)}) collective-permute-start(bf16[416,1024]{1,0:T(8,128)(2,1)S(1)} %slice.419), channel_id=1, source_target_pairs={{0,4},{2,6},{4,0},{6,2},{8,12},{10,14},{12,8},{14,10},{16,20},{18,... | collective-permute-start | bytes 2555912 | tf_op jit(solution)/shard_map/three_plane/ppermute | solution.py:823
  172.6 15.1 %collective-permute-start.25 = (bf16[1120,1024]{1,0:T(8,128)(2,1)S(1)}, bf16[1120,1024]{1,0:T(8,128)(2,1)}, u32[]{:S(2)}, u32[]{:S(2)}) collective-permute-start(bf16[1120,1024]{1,0:T(8,128)(2,1)S(1)} %collective-permute-done.23.refs_17_.refs_4_.refs_24_.refs_2_.refs_12_.refs_7_), channel_id=1, source_target_pairs={{0,1},{1,0},{2,3},{3,2},{4,5},{5,4},{6,7},{7,6},{8,9},{9,8},{10,11... | collective-permute-start | bytes 6881288 | tf_op jit(solution)/shard_map/swap/ppermute | solution.py:833
  172.8 14.9 %collective-permute-start.26 = (bf16[1120,1024]{1,0:T(8,128)(2,1)}, bf16[1120,1024]{1,0:T(8,128)(2,1)}, u32[]{:S(2)}, u32[]{:S(2)}) collective-permute-start(bf16[1120,1024]{1,0:T(8,128)(2,1)} %collective-permute-done.24.refs_19_.refs_6_.refs_26_.refs_4_.refs_14_.refs_9_), channel_id=1, source_target_pairs={{0,1},{1,0},{2,3},{3,2},{4,5},{5,4},{6,7},{7,6},{8,9},{9,8},{10,11... | collective-permute-start | bytes 6881288 | tf_op jit(solution)/shard_map/swap/ppermute | solution.py:833
  180.9 53.6 %collective-permute-start.32 = (bf16[1152,1024]{1,0:T(8,128)(2,1)}, bf16[1152,1024]{1,0:T(8,128)(2,1)}, u32[]{:S(2)}, u32[]{:S(2)}) collective-permute-start(bf16[1152,1024]{1,0:T(8,128)(2,1)} %all-gather.2.cloned.1.call-done.refs_16_.refs_4_), channel_id=1, source_target_pairs={{0,2},{2,0},{4,6},{6,4},{8,10},{10,8},{12,14},{14,12},{16,18},{18,... | collective-permute-start | bytes 7077896 | tf_op jit(solution)/shard_map/four_plane/ppermute | solution.py:823
  183.1 53.6 %collective-permute-start.33 = (bf16[1152,1024]{1,0:T(8,128)(2,1)}, bf16[1152,1024]{1,0:T(8,128)(2,1)}, u32[]{:S(2)}, u32[]{:S(2)}) collective-permute-start(bf16[1152,1024]{1,0:T(8,128)(2,1)} %all-gather.2.cloned.1.call-done.refs_16_.refs_4_), channel_id=1, source_target_pairs={{0,4},{2,6},{4,0},{6,2},{8,12},{10,14},{12,8},{14,10},{16,20},{18,... | collective-permute-start | bytes 7077896 | tf_op jit(solution)/shard_map/four_plane/ppermute | solution.py:823
  185.8 55.5 %collective-permute-start.42 = (bf16[512,1024]{1,0:T(8,128)(2,1)}, bf16[512,1024]{1,0:T(8,128)(2,1)}, u32[]{:S(2)}, u32[]{:S(2)}) collective-permute-start(bf16[512,1024]{1,0:T(8,128)(2,1)} %collective-permute-done.41.refs_2_), channel_id=1, source_target_pairs={{0,8},{2,10},{4,12},{6,14},{8,24},{10,26},{12,28},{14,30},{24,16},... | collective-permute-start | bytes 3145736 | tf_op jit(solution)/shard_map/top_line/ppermute | solution.py:830
  218.2 48.6 %collective-permute-start.36 = (bf16[1152,1024]{1,0:T(8,128)(2,1)S(1)}, bf16[1152,1024]{1,0:T(8,128)(2,1)S(1)}, u32[]{:S(2)}, u32[]{:S(2)}) collective-permute-start(bf16[1152,1024]{1,0:T(8,128)(2,1)S(1)} %copy-done.15), channel_id=1, source_target_pairs={{0,1},{1,0},{2,3},{3,2},{4,5},{5,4},{6,7},{7,6},{8,9},{9,8},{10,11... | collective-permute-start | bytes 7077896 | tf_op jit(solution)/shard_map/swap/ppermute | solution.py:833
  238.1 27.2 %collective-permute-start.37 = (bf16[576,1024]{1,0:T(8,128)(2,1)S(1)}, bf16[576,1024]{1,0:T(8,128)(2,1)S(1)}, u32[]{:S(2)}, u32[]{:S(2)}) collective-permute-start(bf16[576,1024]{1,0:T(8,128)(2,1)S(1)} %slice.334), channel_id=1, source_target_pairs={{0,2},{2,0},{4,6},{6,4},{8,10},{10,8},{12,14},{14,12},{16,18},{18,... | collective-permute-start | bytes 3538952 | tf_op jit(solution)/shard_map/four_plane/ppermute | solution.py:823
  239.8 27.0 %collective-permute-start.39 = (bf16[576,1024]{1,0:T(8,128)(2,1)S(1)}, bf16[576,1024]{1,0:T(8,128)(2,1)S(1)}, u32[]{:S(2)}, u32[]{:S(2)}) collective-permute-start(bf16[576,1024]{1,0:T(8,128)(2,1)S(1)} %slice.335), channel_id=1, source_target_pairs={{0,4},{2,6},{4,0},{6,2},{8,12},{10,14},{12,8},{14,10},{16,20},{18,... | collective-permute-start | bytes 3538952 | tf_op jit(solution)/shard_map/four_plane/ppermute | solution.py:823
  241.4 30.5 %collective-permute-start.34 = (bf16[1152,1024]{1,0:T(8,128)(2,1)}, bf16[1152,1024]{1,0:T(8,128)(2,1)}, u32[]{:S(2)}, u32[]{:S(2)}) collective-permute-start(bf16[1152,1024]{1,0:T(8,128)(2,1)} %collective-permute-done.32.refs_12_.refs_0_), channel_id=1, source_target_pairs={{0,1},{1,0},{2,3},{3,2},{4,5},{5,4},{6,7},{7,6},{8,9},{9,8},{10,11... | collective-permute-start | bytes 7077896 | tf_op jit(solution)/shard_map/swap/ppermute | solution.py:833
  241.4 31.5 %collective-permute-start.35 = (bf16[1152,1024]{1,0:T(8,128)(2,1)}, bf16[1152,1024]{1,0:T(8,128)(2,1)}, u32[]{:S(2)}, u32[]{:S(2)}) collective-permute-start(bf16[1152,1024]{1,0:T(8,128)(2,1)} %collective-permute-done.33.refs_14_.refs_2_), channel_id=1, source_target_pairs={{0,1},{1,0},{2,3},{3,2},{4,5},{5,4},{6,7},{7,6},{8,9},{9,8},{10,11... | collective-permute-start | bytes 7077896 | tf_op jit(solution)/shard_map/swap/ppermute | solution.py:833
  268.2 27.1 %collective-permute-start.43 = (bf16[512,1024]{1,0:T(8,128)(2,1)}, bf16[512,1024]{1,0:T(8,128)(2,1)S(1)}, u32[]{:S(2)}, u32[]{:S(2)}) collective-permute-start(bf16[512,1024]{1,0:T(8,128)(2,1)} %collective-permute-done.42.refs_4_), channel_id=1, source_target_pairs={{0,8},{2,10},{4,12},{6,14},{8,24},{10,26},{12,28},{14,30},{24,16},... | collective-permute-start | bytes 3145736 | tf_op jit(solution)/shard_map/top_line/ppermute | solution.py:830
  296.3 28.3 %collective-permute-start.48 = (bf16[4,144,1024]{2,1,0:T(8,128)(2,1)}, bf16[4,144,1024]{2,1,0:T(8,128)(2,1)}, u32[]{:S(2)}, u32[]{:S(2)}) collective-permute-start(bf16[4,144,1024]{2,1,0:T(8,128)(2,1)} %get-tuple-element.193.lefts_ref.refs_0_.refs_4_.refs_8_), channel_id=1, source_target_pairs={{0,1},{1,0},{2,3},{3,2},{4,5},{5,4},{6,7},{7,6},{8,9},{9,8},{10,11... | collective-permute-start | bytes 3538952 | tf_op jit(solution)/shard_map/ppermute | solution.py:833
  332.2 43.7 %collective-permute-start.51 = (bf16[4,64,2048]{2,1,0:T(8,128)(2,1)}, bf16[4,64,2048]{2,1,0:T(8,128)(2,1)}, u32[]{:S(2)}, u32[]{:S(2)}) collective-permute-start(bf16[4,64,2048]{2,1,0:T(8,128)(2,1)} %get-tuple-element.188), channel_id=1, source_target_pairs={{0,2},{2,0},{4,6},{6,4},{8,10},{10,8},{12,14},{14,12},{16,18},{18,... | collective-permute-start | bytes 3145736 | tf_op jit(solution)/shard_map/readout_across/ppermute | solution.py:823
  334.0 41.9 %collective-permute-start.52 = (bf16[4,64,2048]{2,1,0:T(8,128)(2,1)}, bf16[4,64,2048]{2,1,0:T(8,128)(2,1)}, u32[]{:S(2)}, u32[]{:S(2)}) collective-permute-start(bf16[4,64,2048]{2,1,0:T(8,128)(2,1)} %get-tuple-element.189), channel_id=1, source_target_pairs={{0,4},{2,6},{4,0},{6,2},{8,12},{10,14},{12,8},{14,10},{16,20},{18,... | collective-permute-start | bytes 3145736 | tf_op jit(solution)/shard_map/readout_across/ppermute | solution.py:823
  335.6 90.6 %collective-permute-start.53 = (bf16[3,576,1024]{2,1,0:T(8,128)(2,1)S(1)}, bf16[3,576,1024]{2,1,0:T(8,128)(2,1)}, u32[]{:S(2)}, u32[]{:S(2)}) collective-permute-start(bf16[3,576,1024]{2,1,0:T(8,128)(2,1)S(1)} %copy-done.6), channel_id=1, source_target_pairs={{0,1},{1,0},{2,3},{3,2},{4,5},{5,4},{6,7},{7,6},{8,9},{9,8},{10,11... | collective-permute-start | bytes 10616840 | tf_op jit(solution)/shard_map/ppermute | solution.py:833
  379.1 17.7 %collective-permute-start.55 = (bf16[2,64,2048]{2,1,0:T(8,128)(2,1)}, bf16[2,64,2048]{2,1,0:T(8,128)(2,1)}, u32[]{:S(2)}, u32[]{:S(2)}) collective-permute-start(bf16[2,64,2048]{2,1,0:T(8,128)(2,1)} %add_convert_fusion.16), channel_id=1, source_target_pairs={{0,4},{2,6},{4,0},{6,2},{8,12},{10,14},{12,8},{14,10},{16,20},{18,... | collective-permute-start | bytes 1572872 | tf_op jit(solution)/shard_map/readout_onward/ppermute | solution.py:823
  379.7 17.1 %collective-permute-start.54 = (bf16[2,64,2048]{2,1,0:T(8,128)(2,1)S(1)}, bf16[2,64,2048]{2,1,0:T(8,128)(2,1)}, u32[]{:S(2)}, u32[]{:S(2)}) collective-permute-start(bf16[2,64,2048]{2,1,0:T(8,128)(2,1)S(1)} %add_convert_fusion.17), channel_id=1, source_target_pairs={{0,2},{2,0},{4,6},{6,4},{8,10},{10,8},{12,14},{14,12},{16,18},{18,... | collective-permute-start | bytes 1572872 | tf_op jit(solution)/shard_map/readout_onward/ppermute | solution.py:823
  380.0 39.8 %collective-permute-start.56 = (bf16[4,288,512]{2,1,0:T(8,128)(2,1)}, bf16[4,288,512]{2,1,0:T(8,128)(2,1)}, u32[]{:S(2)}, u32[]{:S(2)}) collective-permute-start(bf16[4,288,512]{2,1,0:T(8,128)(2,1)} %get-tuple-element.195), channel_id=1, source_target_pairs={{0,2},{2,0},{4,6},{6,4},{8,10},{10,8},{12,14},{14,12},{16,18},{18,... | collective-permute-start | bytes 3538952 | tf_op jit(solution)/shard_map/middle_1_0_across/ppermute | solution.py:823
  381.7 39.7 %collective-permute-start.57 = (bf16[4,288,512]{2,1,0:T(8,128)(2,1)}, bf16[4,288,512]{2,1,0:T(8,128)(2,1)}, u32[]{:S(2)}, u32[]{:S(2)}) collective-permute-start(bf16[4,288,512]{2,1,0:T(8,128)(2,1)} %get-tuple-element.196), channel_id=1, source_target_pairs={{0,4},{2,6},{4,0},{6,2},{8,12},{10,14},{12,8},{14,10},{16,20},{18,... | collective-permute-start | bytes 3538952 | tf_op jit(solution)/shard_map/middle_1_0_across/ppermute | solution.py:823
  400.3 199.9 %reduce-scatter.4.cloned.1.call-start = ((), (), s32[]{:S(2)}) async-start(), calls=%async_computation.4 | async-start | bytes 1474560 | tf_op jit(solution)/shard_map/middle_1_0_line/reduce_scatter | solution.py:999
  400.4 26.1 %collective-permute-start.58 = (bf16[2,576,512]{2,1,0:T(8,128)(2,1)}, bf16[2,576,512]{2,1,0:T(8,128)(2,1)}, u32[]{:S(2)}, u32[]{:S(2)}) collective-permute-start(bf16[2,576,512]{2,1,0:T(8,128)(2,1)} %get-tuple-element.223), channel_id=1, source_target_pairs={{0,1},{1,0},{2,3},{3,2},{4,5},{5,4},{6,7},{7,6},{8,9},{9,8},{10,11... | collective-permute-start | bytes 3538952 | tf_op jit(solution)/shard_map/ppermute | solution.py:833
  400.4 54.5 %collective-permute-start.61 = (bf16[4,288,512]{2,1,0:T(8,128)(2,1)}, bf16[4,288,512]{2,1,0:T(8,128)(2,1)}, u32[]{:S(2)}, u32[]{:S(2)}) collective-permute-start(bf16[4,288,512]{2,1,0:T(8,128)(2,1)} %get-tuple-element.235), channel_id=1, source_target_pairs={{0,2},{2,0},{4,6},{6,4},{8,10},{10,8},{12,14},{14,12},{16,18},{18,... | collective-permute-start | bytes 3538952 | tf_op jit(solution)/shard_map/middle_1_1_across/ppermute | solution.py:823
  419.9 36.6 %collective-permute-start.62 = (bf16[4,288,512]{2,1,0:T(8,128)(2,1)}, bf16[4,288,512]{2,1,0:T(8,128)(2,1)}, u32[]{:S(2)}, u32[]{:S(2)}) collective-permute-start(bf16[4,288,512]{2,1,0:T(8,128)(2,1)} %get-tuple-element.236), channel_id=1, source_target_pairs={{0,4},{2,6},{4,0},{6,2},{8,12},{10,14},{12,8},{14,10},{16,20},{18,... | collective-permute-start | bytes 3538952 | tf_op jit(solution)/shard_map/middle_1_1_across/ppermute | solution.py:823
  423.6 38.1 %collective-permute-start.60 = (bf16[2,288,512]{2,1,0:T(8,128)(2,1)}, bf16[2,288,512]{2,1,0:T(8,128)(2,1)}, u32[]{:S(2)}, u32[]{:S(2)}) collective-permute-start(bf16[2,288,512]{2,1,0:T(8,128)(2,1)} %add_convert_fusion.12), channel_id=1, source_target_pairs={{0,4},{2,6},{4,0},{6,2},{8,12},{10,14},{12,8},{14,10},{16,20},{18,... | collective-permute-start | bytes 1769480 | tf_op jit(solution)/shard_map/middle_1_0_onward/ppermute | solution.py:823
  426.2 35.6 %collective-permute-start.59 = (bf16[2,288,512]{2,1,0:T(8,128)(2,1)}, bf16[2,288,512]{2,1,0:T(8,128)(2,1)}, u32[]{:S(2)}, u32[]{:S(2)}) collective-permute-start(bf16[2,288,512]{2,1,0:T(8,128)(2,1)} %add_convert_fusion.13), channel_id=1, source_target_pairs={{0,2},{2,0},{4,6},{6,4},{8,10},{10,8},{12,14},{14,12},{16,18},{18,... | collective-permute-start | bytes 1769480 | tf_op jit(solution)/shard_map/middle_1_0_onward/ppermute | solution.py:823
  453.1 54.0 %collective-permute-start.64 = (bf16[4,288,512]{2,1,0:T(8,128)(2,1)}, bf16[4,288,512]{2,1,0:T(8,128)(2,1)S(1)}, u32[]{:S(2)}, u32[]{:S(2)}) collective-permute-start(bf16[4,288,512]{2,1,0:T(8,128)(2,1)} %get-tuple-element.224), channel_id=1, source_target_pairs={{0,2},{2,0},{4,6},{6,4},{8,10},{10,8},{12,14},{14,12},{16,18},{18,... | collective-permute-start | bytes 3538952 | tf_op jit(solution)/shard_map/middle_0_0_across/ppermute | solution.py:823
  454.9 52.4 %collective-permute-start.65 = (bf16[4,288,512]{2,1,0:T(8,128)(2,1)}, bf16[4,288,512]{2,1,0:T(8,128)(2,1)S(1)}, u32[]{:S(2)}, u32[]{:S(2)}) collective-permute-start(bf16[4,288,512]{2,1,0:T(8,128)(2,1)} %get-tuple-element.225), channel_id=1, source_target_pairs={{0,4},{2,6},{4,0},{6,2},{8,12},{10,14},{12,8},{14,10},{16,20},{18,... | collective-permute-start | bytes 3538952 | tf_op jit(solution)/shard_map/middle_0_0_across/ppermute | solution.py:823
  456.4 50.9 %collective-permute-start.63 = (bf16[4,288,512]{2,1,0:T(8,128)(2,1)}, bf16[4,288,512]{2,1,0:T(8,128)(2,1)}, u32[]{:S(2)}, u32[]{:S(2)}) collective-permute-start(bf16[4,288,512]{2,1,0:T(8,128)(2,1)} %get-tuple-element.229), channel_id=1, source_target_pairs={{0,8},{2,10},{4,12},{6,14},{8,24},{10,26},{12,28},{14,30},{24,16},... | collective-permute-start | bytes 3538952 | tf_op jit(solution)/shard_map/middle_0_1_line0/ppermute | solution.py:830
  467.2 132.9 %reduce-scatter.6.cloned.1.call-start = ((), (), s32[]{:S(2)}) async-start(), calls=%async_computation.5 | async-start | bytes 1474560 | tf_op jit(solution)/shard_map/middle_1_1_line/reduce_scatter | solution.py:999
  469.3 34.4 %collective-permute-start.67 = (bf16[2,288,512]{2,1,0:T(8,128)(2,1)}, bf16[2,288,512]{2,1,0:T(8,128)(2,1)S(1)}, u32[]{:S(2)}, u32[]{:S(2)}) collective-permute-start(bf16[2,288,512]{2,1,0:T(8,128)(2,1)} %add_convert_fusion.8), channel_id=1, source_target_pairs={{0,4},{2,6},{4,0},{6,2},{8,12},{10,14},{12,8},{14,10},{16,20},{18,... | collective-permute-start | bytes 1769480 | tf_op jit(solution)/shard_map/middle_1_1_onward/ppermute | solution.py:823
  470.8 33.0 %collective-permute-start.66 = (bf16[2,288,512]{2,1,0:T(8,128)(2,1)}, bf16[2,288,512]{2,1,0:T(8,128)(2,1)}, u32[]{:S(2)}, u32[]{:S(2)}) collective-permute-start(bf16[2,288,512]{2,1,0:T(8,128)(2,1)} %add_convert_fusion.9), channel_id=1, source_target_pairs={{0,2},{2,0},{4,6},{6,4},{8,10},{10,8},{12,14},{14,12},{16,18},{18,... | collective-permute-start | bytes 1769480 | tf_op jit(solution)/shard_map/middle_1_1_onward/ppermute | solution.py:823
  503.9 16.2 %collective-permute-start.70 = (bf16[1024,384]{1,0:T(8,128)(2,1)}, bf16[1024,384]{1,0:T(8,128)(2,1)}, u32[]{:S(2)}, u32[]{:S(2)}) collective-permute-start(bf16[1024,384]{1,0:T(8,128)(2,1)} %get-tuple-element.256), channel_id=1, source_target_pairs={{0,1},{1,0},{2,3},{3,2},{4,5},{5,4},{6,7},{7,6},{8,9},{9,8},{10,11... | collective-permute-start | bytes 2359304 | tf_op jit(solution)/shard_map/ppermute | solution.py:833
  511.9 47.2 %collective-permute-start.73 = (bf16[4,288,512]{2,1,0:T(8,128)(2,1)}, bf16[4,288,512]{2,1,0:T(8,128)(2,1)}, u32[]{:S(2)}, u32[]{:S(2)}) collective-permute-start(bf16[4,288,512]{2,1,0:T(8,128)(2,1)} %add_convert_fusion.1), channel_id=1, source_target_pairs={{0,8},{2,10},{4,12},{6,14},{8,24},{10,26},{12,28},{14,30},{24,16},... | collective-permute-start | bytes 3538952 | tf_op jit(solution)/shard_map/middle_0_1_line1/ppermute | solution.py:830
  513.4 23.5 %collective-permute-start.82 = (bf16[2,288,512]{2,1,0:T(8,128)(2,1)}, bf16[2,288,512]{2,1,0:T(8,128)(2,1)S(1)}, u32[]{:S(2)}, u32[]{:S(2)}) collective-permute-start(bf16[2,288,512]{2,1,0:T(8,128)(2,1)} %add_convert_fusion.6), channel_id=1, source_target_pairs={{0,4},{2,6},{4,0},{6,2},{8,12},{10,14},{12,8},{14,10},{16,20},{18,... | collective-permute-start | bytes 1769480 | tf_op jit(solution)/shard_map/middle_0_0_onward/ppermute | solution.py:823
  516.8 20.1 %collective-permute-start.81 = (bf16[2,288,512]{2,1,0:T(8,128)(2,1)}, bf16[2,288,512]{2,1,0:T(8,128)(2,1)S(1)}, u32[]{:S(2)}, u32[]{:S(2)}) collective-permute-start(bf16[2,288,512]{2,1,0:T(8,128)(2,1)} %add_convert_fusion.7), channel_id=1, source_target_pairs={{0,2},{2,0},{4,6},{6,4},{8,10},{10,8},{12,14},{14,12},{16,18},{18,... | collective-permute-start | bytes 1769480 | tf_op jit(solution)/shard_map/middle_0_0_onward/ppermute | solution.py:823
  518.8 15.6 %collective-permute-start.92 = (f32[1,32,2048]{2,0,1:T(1,128)S(1)}, f32[1,32,2048]{2,0,1:T(1,128)S(1)}, u32[]{:S(2)}, u32[]{:S(2)}) collective-permute-start(f32[1,32,2048]{2,0,1:T(1,128)S(1)} %squeeze.105), channel_id=1, source_target_pairs={{0,1},{1,0},{2,3},{3,2},{4,5},{5,4},{6,7},{7,6},{8,9},{9,8},{10,11... | collective-permute-start | bytes 786440 | tf_op jit(solution)/shard_map/ppermute | solution.py:833
  533.8 34.8 %collective-permute-start.71 = (bf16[4,320,512]{2,1,0:T(8,128)(2,1)}, bf16[4,320,512]{2,1,0:T(8,128)(2,1)S(1)}, u32[]{:S(2)}, u32[]{:S(2)}) collective-permute-start(bf16[4,320,512]{2,1,0:T(8,128)(2,1)} %get-tuple-element.258), channel_id=1, source_target_pairs={{0,2},{2,0},{4,6},{6,4},{8,10},{10,8},{12,14},{14,12},{16,18},{18,... | collective-permute-start | bytes 3932168 | tf_op jit(solution)/shard_map/last_across/ppermute | solution.py:823
  534.4 34.2 %collective-permute-start.72 = (bf16[4,320,512]{2,1,0:T(8,128)(2,1)}, bf16[4,320,512]{2,1,0:T(8,128)(2,1)S(1)}, u32[]{:S(2)}, u32[]{:S(2)}) collective-permute-start(bf16[4,320,512]{2,1,0:T(8,128)(2,1)} %get-tuple-element.259), channel_id=1, source_target_pairs={{0,4},{2,6},{4,0},{6,2},{8,12},{10,14},{12,8},{14,10},{16,20},{18,... | collective-permute-start | bytes 3932168 | tf_op jit(solution)/shard_map/last_across/ppermute | solution.py:823
  539.4 27.7 %collective-permute-start.83 = (bf16[288,512]{1,0:T(8,128)(2,1)S(1)}, bf16[288,512]{1,0:T(8,128)(2,1)S(1)}, u32[]{:S(2)}, u32[]{:S(2)}) collective-permute-start(bf16[288,512]{1,0:T(8,128)(2,1)S(1)} %fusion.11), channel_id=1, source_target_pairs={{0,8},{2,10},{4,12},{6,14},{8,24},{10,26},{12,28},{14,30},{24,16},... | collective-permute-start | bytes 884744 | tf_op jit(solution)/shard_map/middle_0_0_line/ppermute | solution.py:830
  560.7 41.7 %collective-permute-start.76 = (bf16[4,288,512]{2,1,0:T(8,128)(2,1)S(1)}, bf16[4,288,512]{2,1,0:T(8,128)(2,1)}, u32[]{:S(2)}, u32[]{:S(2)}) collective-permute-start(bf16[4,288,512]{2,1,0:T(8,128)(2,1)S(1)} %add_convert_fusion), channel_id=1, source_target_pairs={{0,8},{2,10},{4,12},{6,14},{8,24},{10,26},{12,28},{14,30},{24,16},... | collective-permute-start | bytes 3538952 | tf_op jit(solution)/shard_map/middle_0_1_line2/ppermute | solution.py:830
  567.2 30.5 %collective-permute-start.84 = (bf16[288,512]{1,0:T(8,128)(2,1)S(1)}, bf16[288,512]{1,0:T(8,128)(2,1)S(1)}, u32[]{:S(2)}, u32[]{:S(2)}) collective-permute-start(bf16[288,512]{1,0:T(8,128)(2,1)S(1)} %fusion.6), channel_id=1, source_target_pairs={{0,8},{2,10},{4,12},{6,14},{8,24},{10,26},{12,28},{14,30},{24,16},... | collective-permute-start | bytes 884744 | tf_op jit(solution)/shard_map/middle_0_0_line/ppermute | solution.py:830
  569.8 36.7 %collective-permute-start.75 = (bf16[2,320,512]{2,1,0:T(8,128)(2,1)}, bf16[2,320,512]{2,1,0:T(8,128)(2,1)S(1)}, u32[]{:S(2)}, u32[]{:S(2)}) collective-permute-start(bf16[2,320,512]{2,1,0:T(8,128)(2,1)} %add_convert_fusion.2), channel_id=1, source_target_pairs={{0,4},{2,6},{4,0},{6,2},{8,12},{10,14},{12,8},{14,10},{16,20},{18,... | collective-permute-start | bytes 1966088 | tf_op jit(solution)/shard_map/last_onward/ppermute | solution.py:823
  572.3 35.7 %collective-permute-start.74 = (bf16[2,320,512]{2,1,0:T(8,128)(2,1)}, bf16[2,320,512]{2,1,0:T(8,128)(2,1)}, u32[]{:S(2)}, u32[]{:S(2)}) collective-permute-start(bf16[2,320,512]{2,1,0:T(8,128)(2,1)} %add_convert_fusion.3), channel_id=1, source_target_pairs={{0,2},{2,0},{4,6},{6,4},{8,10},{10,8},{12,14},{14,12},{16,18},{18,... | collective-permute-start | bytes 1966088 | tf_op jit(solution)/shard_map/last_onward/ppermute | solution.py:823
  598.6 14.6 %collective-permute-start.85 = (bf16[288,512]{1,0:T(8,128)(2,1)}, bf16[288,512]{1,0:T(8,128)(2,1)S(1)}, u32[]{:S(2)}, u32[]{:S(2)}) collective-permute-start(bf16[288,512]{1,0:T(8,128)(2,1)} %fusion.8), channel_id=1, source_target_pairs={{0,8},{2,10},{4,12},{6,14},{8,24},{10,26},{12,28},{14,30},{24,16},... | collective-permute-start | bytes 884744 | tf_op jit(solution)/shard_map/middle_0_0_line/ppermute | solution.py:830
  601.9 30.4 %collective-permute-start.91 = (f32[1,288,512]{2,0,1:T(1,128)S(1)}, f32[1,288,512]{2,0,1:T(1,128)S(1)}, u32[]{:S(2)}, u32[]{:S(2)}) collective-permute-start(f32[1,288,512]{2,0,1:T(1,128)S(1)} %squeeze.104), channel_id=1, source_target_pairs={{0,1},{1,0},{2,3},{3,2},{4,5},{5,4},{6,7},{7,6},{8,9},{9,8},{10,11... | collective-permute-start | bytes 1769480 | tf_op jit(solution)/shard_map/ppermute | solution.py:833
  (104 other events, 968.6 us)
Sparse Core Ops, SparseCore 0:
  112.9 53.8 all-gather.1
  400.4 27.9 reduce-scatter.7
  467.3 35.7 reduce-scatter.3
  520.2 46.4 reduce-scatter.5

commit v4 on v3

--- a/solution.py
+++ b/solution.py
@@ -17,8 +17,9 @@
 MISC = 16
 HEAD = 1664
 SIDE = 384
-STEPS, LEVELS, OUT_STEPS, OUT_LEVELS, OUT_LINE, CORE, TABLE = 0, 32, 64, 80, 96, 112, 113
-COST = 30
+STEPS, LEVELS, OUT_STEPS, OUT_LEVELS, OUT_LINE, CORE, WINDOWS, TABLE = 0, 32, 64, 80, 96, 112, 113, 165
+STEPPED, LEVELED, LINED = range(3)
+COST = 4
 COSTS = {"forward_block": 50}
 VMEM = 60 * 1024 * 1024
 
@@ -91,8 +92,7 @@
 
 
 class Blocks:
-    def __init__(self, block_rows):
-        self.block_rows = block_rows
+    def __init__(self):
         self.operands = []
         self.moves = []
 
@@ -103,8 +103,8 @@
         self.operands.append(array)
         return len(self.operands) - 1
 
-    def add(self, array, block, row, column, place, to_row, to_column, rows, columns):
-        self.moves.append((self.operand(array), block, row, column, place, to_row, to_column, rows, columns))
+    def add(self, array, block, row, column, place, stride, to_row, to_column, rows, columns):
+        self.moves.append((self.operand(array), block, row, column, place, stride, to_row, to_column, rows, columns))
 
     @property
     def copies(self):
@@ -112,10 +112,10 @@
 
     def bind(self, refs, places, matrix, sems, to_blocks=False, base=0):
         made = []
-        for number, block, row, column, place, to_row, to_column, rows, columns in self.moves:
+        for number, block, row, column, place, stride, to_row, to_column, rows, columns in self.moves:
             first = to_row
             if place is not None:
-                first = pl.multiple_of(places[place] * self.block_rows + to_row, 16)
+                first = pl.multiple_of(places[place] * stride + to_row, 16)
             inside = matrix.at[pl.ds(first, rows), pl.ds(to_column, columns)]
             outside = refs[number] if block is None else refs[number].at[block]
             outside = outside.at[pl.ds(row, rows), pl.ds(column, columns)]
@@ -134,7 +134,7 @@
         copy.wait()
 
 
-ANY = pl.BlockSpec(memory_space=pl.ANY)
+ANY = pl.BlockSpec(memory_space=pltpu.HBM)
 IN = pl.BlockSpec(memory_space=pltpu.VMEM)
 SMEM = pl.BlockSpec(memory_space=pltpu.SMEM)
 
@@ -208,13 +208,14 @@
             u_ref = refs.pop(0 - 1)
         else:
             u_ref, misc_ref = heads
-        lefts_out, pre1_out, pre2_out, pre3_out = [refs.pop(0) for _ in range(4)]
+        lefts_out, pre1_out, pre2_out, pre3_out, wi_out, wo_out = [refs.pop(0) for _ in range(6)]
         wi, wm, wo, taps, lefts, above, below, work, pairs, pre1, pre2, pre3, sems = refs
         traffic = Traffic(sems)
         first_copies = traffic.load(w_first, firsts, table_ref, wi)
         middle_copies = traffic.load(w_middle, middles, table_ref, wm)
         last_copies = traffic.load(w_last, lasts, table_ref, wo)
         wait(first_copies)
+        traffic.send(wi.at[:, pl.ds(0, C)], wi_out)
         if opening:
 
             def place(cut):
@@ -284,6 +285,7 @@
         if opening:
             traffic.send(lefts, lefts_out)
         wait(last_copies)
+        traffic.send(wo, wo_out)
 
         def last(cut):
             pre3[:, cut] = dot(lefts[2], wo[:, cut])
@@ -322,9 +324,9 @@
     if opening:
         outs += [shaped(MISC, C), shaped(cells // 4, C), shaped(cells, C)]
         out_specs += [IN, IN, ANY]
-    outs += [shaped(n_lefts, cells, C, dtype=bf16)] + [shaped(cells, C)] * 3
-    out_specs += [ANY] * 4
-    copies = w_first.copies + w_middle.copies + w_last.copies + 5
+    outs += [shaped(n_lefts, cells, C, dtype=bf16)] + [shaped(cells, C)] * 3 + [shaped(C, C, dtype=bf16)] * 2
+    out_specs += [ANY] * 6
+    copies = w_first.copies + w_middle.copies + w_last.copies + 7
     scratch = [
         pltpu.VMEM((C, HEAD if opening else C), bf16),
         pltpu.VMEM((9 * C, C), bf16),
@@ -502,112 +504,36 @@
     )
 
 
-def middle_terms(table, side, lefts, lefts_other, grads, grads_other, out_blocks):
-    cells = side * side
-    n_outs = len(out_blocks.operands)
+def weight_terms(table, middle, products, sides, out_blocks):
     bf16 = jnp.bfloat16
-    pair = lefts_other is not None
-    both = 2 * cells if pair else cells
-    half = C // 2 if pair else C
-    given = [lefts, grads] + ([lefts_other, grads_other] if pair else [])
-
-    def kernel(table_ref, *refs):
-        refs = list(refs)
-        sources = [refs.pop(0) for _ in given]
-        targets = [refs.pop(0) for _ in range(n_outs)]
-        act, right, grad, taps, shifted, padded, sems = refs
-        traffic = Traffic(sems)
-        copies = [traffic.begin(sources[0].at[1], act.at[pl.ds(0, cells), :])]
-        if pair:
-            mine = pl.ds(pl.multiple_of(table_ref[CORE] * half, half), half)
-            copies += [
-                traffic.begin(sources[1].at[1, :, mine], right.at[pl.ds(0, cells), :]),
-                traffic.begin(sources[2].at[1], act.at[pl.ds(cells, cells), :]),
-                traffic.begin(sources[3].at[1], right.at[pl.ds(cells, cells), :]),
-            ]
-        else:
-            copies += [traffic.begin(sources[1].at[1], right.at[pl.ds(0, cells), :])]
-        padded[:PAD, :] = jnp.zeros((PAD, 128), jnp.float32)
-        padded[PAD + cells :, :] = jnp.zeros((PAD, 128), jnp.float32)
-        wait(copies)
-        for first in range(0, both, cells):
-            rows = slice(first, first + cells)
-
-            def spread(i, carry, rows=rows):
-                cut = pl.ds(pl.multiple_of(i * 128, 128), 128)
-                value = wide(act[rows, cut])
-                taps[rows, cut] = low(beside(value, side, -1))
-                taps[rows, pl.ds(pl.multiple_of(C + i * 128, 128), 128)] = act[rows, cut]
-                taps[rows, pl.ds(pl.multiple_of(2 * C + i * 128, 128), 128)] = low(beside(value, side, 1))
-                return carry
-
-            def shift(i, carry, rows=rows):
-                cut = pl.ds(pl.multiple_of(i * 128, 128), 128)
-                padded[PAD : PAD + cells, :] = wide(right[rows, cut])
-                shifted[0, rows, cut] = low(padded[PAD + side : PAD + side + cells, :])
-                shifted[1, rows, cut] = right[rows, cut]
-                shifted[2, rows, cut] = low(padded[PAD - side : PAD - side + cells, :])
-                return carry
-
-            lax.fori_loop(0, C // 128, spread, 0)
-            lax.fori_loop(0, half // 128, shift, 0)
-        size = 512
-        for row_tap in range(3):
-
-            def part(i, carry, row_tap=row_tap):
-                cut = pl.ds(pl.multiple_of(i * size, size), size)
-                target = pl.ds(pl.multiple_of(row_tap * 3 * C + i * size, size), size)
-                grad[target, :] = low(dot_sums(taps[:, cut], shifted[row_tap]))
-                return carry
-
-            lax.fori_loop(0, 3 * C // size, part, 0)
-        traffic.store(out_blocks, targets, table_ref, grad)
-        traffic.finish()
-
-    outs = [shaped(*array.shape, dtype=bf16) for array in out_blocks.operands]
-    scratch = [
-        pltpu.VMEM((both, C), bf16),
-        pltpu.VMEM((both, half), bf16),
-        pltpu.VMEM((9 * C, half), bf16),
-        pltpu.VMEM((both, 3 * C), bf16),
-        pltpu.VMEM((3, both, half), bf16),
-        pltpu.VMEM((cells + 2 * PAD, 128), jnp.float32),
-        pltpu.SemaphoreType.DMA((out_blocks.copies + 4,)),
-    ]
-    return call(
-        kernel,
-        "middle_terms",
-        [table] + given,
-        [SMEM] + [ANY] * len(given),
-        outs,
-        [ANY] * n_outs,
-        scratch,
-        2 * cells * 9 * C * C,
-        18 * C * half + 8 * cells * C,
-    )
-
-
-def plain_terms(table, products, sides, out_blocks):
-    bf16 = jnp.bfloat16
+    if middle is not None:
+        products = [(middle[1], 1, middle[2], middle[3], 1, middle[4], 1)] + products
     pair = products[0][2] is not None
     given = []
     for left, _, left_other, right, _, right_other, _ in products:
         given += [left, right] + ([left_other, right_other] if pair else [])
     n_given = len(given)
     n_outs = len(out_blocks.operands)
-    columns = out_blocks.operands[0].shape[-1]
-    width = columns
-    rows_of = [product[0].shape[-2] for product in products]
+    width = out_blocks.operands[0].shape[-1]
+    cells_of = [product[0].shape[-2] for product in products]
+    factor = 2 if pair else 1
+    heights = [C] * len(products)
+    if middle is not None:
+        heights[0] = 9 * C
+    starts = [sum(heights[:i]) for i in range(len(heights) + 1)]
+    grid_side = middle[0] if middle is not None else 0
+    grid_cells = grid_side * grid_side
+    size = 512
 
     def kernel(table_ref, *refs):
         refs = list(refs)
         sources = [refs.pop(0) for _ in range(n_given)]
-        beside_refs = [refs.pop(0) for _ in range(len(sides) * (2 if pair else 1))]
+        beside_refs = [refs.pop(0) for _ in range(len(sides) * factor)]
         targets = [refs.pop(0) for _ in range(n_outs)]
         grad, sems = refs.pop(0), refs.pop(0)
         traffic = Traffic(sems)
         waits = []
-        for (_, left_at, _, _, right_at, _, other_at), cells in zip(products, rows_of):
+        for (_, left_at, _, _, right_at, _, other_at), cells in zip(products, cells_of):
             left, right = refs.pop(0), refs.pop(0)
             left_in, right_in = sources.pop(0), sources.pop(0)
             copies = [traffic.begin(left_in.at[left_at], left.at[pl.ds(0, cells), :])]
@@ -623,61 +549,161 @@
                     right_in = right_in.at[other_at]
                 copies.append(traffic.begin(right_in, right.at[pl.ds(cells, cells), :]))
             waits.append((copies, left, right))
-        at, below = 0, len(products) * C
+        at = 0
         for side in sides:
             extent = side[0].shape[-1]
             total = beside_refs.pop(0)[...]
             if pair:
                 total = low(wide(total) + wide(beside_refs.pop(0)[...]))
-            grad[below:, at : at + extent] = total
+            grad[starts[-1] :, at : at + extent] = total
             at += extent
         if sides:
-            grad[below:, at:] = jnp.zeros((C, columns - at), bf16)
+            grad[starts[-1] :, at:] = jnp.zeros((C, width - at), bf16)
+        if middle is not None:
+            taps, shifted, padded = refs
+            copies, act, right = waits[0]
+            padded[:PAD, :] = jnp.zeros((PAD, 128), jnp.float32)
+            padded[PAD + grid_cells :, :] = jnp.zeros((PAD, 128), jnp.float32)
+            wait(copies)
+            for first in range(0, factor * grid_cells, grid_cells):
+                rows = slice(first, first + grid_cells)
+
+                def spread(i, carry, rows=rows):
+                    cut = pl.ds(pl.multiple_of(i * 128, 128), 128)
+                    value = wide(act[rows, cut])
+                    taps[rows, cut] = low(beside(value, grid_side, -1))
+                    taps[rows, pl.ds(pl.multiple_of(C + i * 128, 128), 128)] = act[rows, cut]
+                    taps[rows, pl.ds(pl.multiple_of(2 * C + i * 128, 128), 128)] = low(beside(value, grid_side, 1))
+                    return carry
+
+                def shift(i, carry, rows=rows):
+                    cut = pl.ds(pl.multiple_of(i * 128, 128), 128)
+                    padded[PAD : PAD + grid_cells, :] = wide(right[rows, cut])
+                    shifted[0, rows, cut] = low(padded[PAD + grid_side : PAD + grid_side + grid_cells, :])
+                    shifted[1, rows, cut] = right[rows, cut]
+                    shifted[2, rows, cut] = low(padded[PAD - grid_side : PAD - grid_side + grid_cells, :])
+                    return carry
+
+                lax.fori_loop(0, C // 128, spread, 0)
+                lax.fori_loop(0, width // 128, shift, 0)
+            for row_tap in range(3):
+
+                def part(i, carry, row_tap=row_tap):
+                    cut = pl.ds(pl.multiple_of(i * size, size), size)
+                    target = pl.ds(pl.multiple_of(row_tap * 3 * C + i * size, size), size)
+                    grad[target, :] = low(dot_sums(taps[:, cut], shifted[row_tap]))
+                    return carry
+
+                lax.fori_loop(0, 3 * C // size, part, 0)
         for number, (copies, left, right) in enumerate(waits):
+            if middle is not None and number == 0:
+                continue
             wait(copies)
 
             def part(cut, number=number, left=left, right=right):
-                target = pl.ds(pl.multiple_of(number * C + cut.start, TILE), TILE)
+                target = pl.ds(pl.multiple_of(starts[number] + cut.start, TILE), TILE)
                 grad[target, :] = low(dot_sums(left[:, cut], right[...]))
 
             tiles(C, TILE, part)
         traffic.store(out_blocks, targets, table_ref, grad)
         traffic.finish()
 
-    factor = 2 if pair else 1
     outs = [shaped(*array.shape, dtype=bf16) for array in out_blocks.operands]
     scratch = [
-        pltpu.VMEM(((len(products) + (1 if sides else 0)) * C, columns), bf16),
+        pltpu.VMEM((starts[-1] + (C if sides else 0), width), bf16),
         pltpu.SemaphoreType.DMA((out_blocks.copies + 4 * len(products),)),
     ]
-    for cells in rows_of:
+    for cells in cells_of:
         scratch += [pltpu.VMEM((factor * cells, C), bf16), pltpu.VMEM((factor * cells, width), bf16)]
+    if middle is not None:
+        scratch += [
+            pltpu.VMEM((factor * grid_cells, 3 * C), bf16),
+            pltpu.VMEM((3, factor * grid_cells, width), bf16),
+            pltpu.VMEM((grid_cells + 2 * PAD, 128), jnp.float32),
+        ]
     besides = [array for side in sides for array in side if array is not None]
     return call(
         kernel,
-        "plain_terms",
+        "weight_terms",
         [table] + given + besides,
         [SMEM] + [ANY] * n_given + [IN] * len(besides),
         outs,
         [ANY] * n_outs,
         scratch,
-        sum(2 * factor * cells * C * width for cells in rows_of),
-        2 * len(products) * C * columns + sum(4 * factor * cells * C for cells in rows_of),
-    )
-
-
-def back_first(table, number, side, grads, pre1, direct, misc, rest, w_middle, w_first):
+        sum(2 * factor * cells * height * width for cells, height in zip(cells_of, heights)),
+        2 * starts[-1] * width + sum(4 * factor * cells * C for cells in cells_of),
+    )
+
+
+def plane_terms(table, side, acts, grads, block_rows):
     cells = side * side
-    closing = rest is not None
+    total = sum(array.shape[0] for array in acts)
+    bf16 = jnp.bfloat16
+    blocks = 4
+    span = 3 * 128
+
+    def kernel(table_ref, *refs):
+        refs = list(refs)
+        act_refs = [refs.pop(0) for _ in acts]
+        grad_refs = [refs.pop(0) for _ in grads]
+        target, act, right, taps, terms, sems = refs
+        traffic = Traffic(sems)
+        copies, row = [], 0
+        for source, other in zip(act_refs, grad_refs):
+            rows = pl.ds(row, source.shape[0])
+            copies += [traffic.begin(source, act.at[rows, :]), traffic.begin(other, right.at[rows, :])]
+            row += source.shape[0]
+        index = lax.broadcasted_iota(jnp.int32, (total, 128), 0).astype(jnp.float32)
+        inside = index - cells * jnp.floor((index + 0.5) * (1.0 / cells))
+        line = jnp.floor((inside + 0.5) * (1.0 / side))
+        column = inside - side * line
+        wait(copies)
+        for block in range(blocks):
+            for tile in range(3):
+                at = WINDOWS + blocks + 4 * (3 * block + tile)
+                cut = pl.ds(pl.multiple_of(table_ref[at], 128), 128)
+                value = pltpu.roll(wide(act[:, cut]), table_ref[at + 1], 0)
+                tap_line = line + (table_ref[at + 2] - 1).astype(jnp.float32)
+                tap_column = column + (table_ref[at + 3] - 1).astype(jnp.float32)
+                there = (tap_line >= 0) & (tap_line < side) & (tap_column >= 0) & (tap_column < side)
+                first = block * span + tile * 128
+                taps[:, first : first + 128] = low(jnp.where(there, value, 0.0))
+            terms[block] = low(dot_sums(taps[:, block * span : (block + 1) * span], right[...]))
+            start_row = pl.multiple_of(table_ref[WINDOWS + block], 32)
+            traffic.send(terms.at[block, pl.ds(start_row, block_rows), :], target.at[block])
+        traffic.finish()
+
+    return call(
+        kernel,
+        "plane_terms",
+        [table] + acts + grads,
+        [SMEM] + [ANY] * (2 * len(acts)),
+        shaped(blocks, block_rows, C, dtype=bf16),
+        ANY,
+        [
+            pltpu.VMEM((total, C), bf16),
+            pltpu.VMEM((total, C), bf16),
+            pltpu.VMEM((total, blocks * span), bf16),
+            pltpu.VMEM((blocks, span, C), bf16),
+            pltpu.SemaphoreType.DMA((2 * len(acts) + blocks,)),
+        ],
+        2 * total * blocks * span * C,
+        4 * total * C + 2 * blocks * block_rows * C,
+    )
+
+
+def back_first(table, number, side, grads, pre1, direct, misc, rests, w_middle, w_first):
+    cells = side * side
+    closing = rests is not None
     n_middle, n_first = len(w_middle.operands), len(w_first.operands)
     bf16 = jnp.bfloat16
-    extra = [rest] if closing else []
+    extra = rests if closing else []
     half = C // 2
     side_half = SIDE
 
     def kernel(table_ref, grads_in, pre1_in, direct_in, misc_ref, *refs):
         refs = list(refs)
-        rest_ref = refs.pop(0) if closing else None
+        rest_refs = [refs.pop(0) for _ in extra]
         middles = [refs.pop(0) for _ in range(n_middle)]
         firsts = [refs.pop(0) for _ in range(n_first)]
         grad_u, sums, grad_pre1, other = [refs.pop(0) for _ in range(4)]
@@ -750,16 +776,16 @@
         tiles(C, TILE, first)
         if closing:
 
+            last_0, first_1, last_1, bias_grad = rest_refs
+
             def turn(cut):
                 stacked = jnp.concatenate(
-                    [
-                        grad_u[:, cut],
-                        sums[0:1, cut],
-                        rest_ref[1:6, cut],
-                        sums[1:2, cut],
-                        rest_ref[7:MISC, cut],
-                        jnp.zeros((2 * side_half - cells - MISC, 128), jnp.float32),
-                    ]
+                    [grad_u[:, cut]]
+                    + [ref[row : row + 1, cut] for ref, row in ((sums, 0), (last_0, 2), (last_0, 0))]
+                    + [ref[row : row + 1, cut] for ref, row in ((first_1, 0), (last_1, 2), (last_1, 0))]
+                    + [ref[row : row + 1, cut] for ref, row in ((sums, 1), (last_0, 3), (last_0, 1))]
+                    + [ref[row : row + 1, cut] for ref, row in ((first_1, 1), (last_1, 3), (last_1, 1))]
+                    + [bias_grad[:, cut], jnp.zeros((2 * side_half - cells - MISC, 128), jnp.float32)]
                 )
                 parts_of = low(jnp.transpose(stacked))
                 for part in range(2):
@@ -806,6 +832,69 @@
     )
 
 
+def place_halves(core, pair, rest=None):
+    _, rows, half = pair[0].shape
+    extra = [] if rest is None else [rest]
+
+    def kernel(core_ref, mine, other, *refs):
+        target = refs[-1]
+        for part in range(2):
+
+            @pl.when(core_ref[0] == part)
+            def _(part=part):
+                target[0, :, part * half : (part + 1) * half] = mine[0]
+                target[0, :, (1 - part) * half : (2 - part) * half] = other[0]
+
+        if extra:
+            target[1] = wide(refs[0][0])
+
+    return call(
+        kernel,
+        "place_halves",
+        [core, *pair] + extra,
+        [SMEM] + [IN] * (2 + len(extra)),
+        shaped(1 + len(extra), rows, 2 * half),
+        IN,
+        [],
+        0,
+        16 * rows * half,
+    )
+
+
+def place_last(core, mine, other, cells):
+    _, rows, half = mine.shape
+
+    def kernel(core_ref, mine_ref, other_ref, first, last, pos, gains, biases, bias, side):
+        for part in range(2):
+
+            @pl.when(core_ref[0] == part)
+            def _(part=part):
+                for target, block, number in ((last, 0, 0), (first, 1, 1), (last, 1, 2), (first, 0, 3)):
+                    target[block, :, part * half : (part + 1) * half] = mine_ref[number]
+                    target[block, :, (1 - part) * half : (2 - part) * half] = other_ref[number]
+                side[:, part * SIDE : (part + 1) * SIDE] = mine_ref[4, :, :SIDE]
+                side[:, (1 - part) * SIDE : (2 - part) * SIDE] = other_ref[4, :, :SIDE]
+
+        turned = jnp.transpose(side[...])
+        pos[...] = turned[:cells]
+        for number in range(6):
+            gains[number // 3, number % 3 : number % 3 + 1, :] = turned[cells + number : cells + number + 1]
+            biases[number // 3, number % 3 : number % 3 + 1, :] = turned[cells + 6 + number : cells + 7 + number]
+        bias[...] = turned[cells + 12 : cells + MISC]
+
+    return call(
+        kernel,
+        "place_last",
+        [core, mine, other],
+        [SMEM, IN, IN],
+        [shaped(2, rows, 2 * half)] * 2 + [shaped(cells, rows)] + [shaped(2, 3, rows)] * 2 + [shaped(4, rows)],
+        [IN] * 6,
+        [pltpu.VMEM((rows, 2 * SIDE), jnp.float32)],
+        0,
+        32 * rows * half * 5,
+    )
+
+
 def after(value, *earlier):
     return lax.optimization_barrier((value, earlier))[0]
 
@@ -858,7 +947,18 @@
             row += [chip_at(far, step_at(step)) for far, step in halves]
             row += [chip_at(far, step) for far, step in halves]
             row += [chip_at(far, step_at(step)) for step in reversed(steps) for far in chips]
-            rows.append(row + [core])
+            row.append(core)
+            firsts = [chip_at(0, step) * 2 + core for step in steps]
+            firsts = [9 * C // self.devices * owner for owner in firsts]
+            row += [first % 128 for first in firsts]
+            side = G // 2
+            for first in firsts:
+                for tile in range(first // 128, first // 128 + 3):
+                    tap, part = divmod(tile, C // 128)
+                    tap_row, tap_column = divmod(tap, 3)
+                    away = (tap_row - 1) * side + tap_column - 1
+                    row += [128 * part, -away % (2 * PLANE * side * side), tap_row, tap_column]
+            rows.append(row)
         index = lax.axis_index("dp") * self.cores + lax.axis_index("fsdp")
         return lax.dynamic_index_in_dim(jnp.asarray(np.array(rows, np.int32)), index, 0, keepdims=False)
 
@@ -953,6 +1053,19 @@
         piece.keep(second, 3, (0, 1), first=row, other=second_other)
 
 
+class Spread:
+    def __init__(self, move, own, *earlier):
+        self.move = move
+        self.own = after(own, *earlier) if earlier else own
+        with jax.named_scope("spread"):
+            self.sides = tuple(move.flip(self.own, bits) for bits in (1, 2, 3))
+
+    def end(self, *earlier):
+        with jax.named_scope("spread_swap"):
+            here = jnp.concatenate(after((self.own, *self.sides), *earlier))
+            self.all = [here, self.move.swap(here)]
+
+
 class Sum:
     def __init__(self, move, arrays, name, levels=False):
         self.move = move
@@ -974,12 +1087,13 @@
                 low(wide(self.arrays[2]) + wide(self.second[2:])),
                 low(wide(self.arrays[3]) + wide(self.first[2:])),
             )
+        self.operands = self.rests
         return self.rests
 
-    def onward(self):
+    def onward(self, *earlier):
+        rests = after(self.rests, *earlier) if earlier else self.rests
         with jax.named_scope(self.name + "_onward"):
-            self.rests = (self.move.flip(self.rests[0], 1), self.move.flip(self.rests[1], 2))
-        return self.rests
+            self.rests = (self.move.flip(rests[0], 1), self.move.flip(rests[1], 2))
 
     def gather(self, *earlier):
         rests = after(self.rests, *earlier) if earlier else self.rests
@@ -991,6 +1105,8 @@
                 held = jnp.concatenate([low(self.near), low(self.far)])
                 self.held = held.reshape(-1, held.shape[-1])
                 return self.held
+            self.far = (self.far[0], low(self.far[1]))
+            return self.far
 
     def finish(self, *earlier):
         with jax.named_scope(self.name + "_line"):
@@ -999,11 +1115,11 @@
                 owned = lax.psum_scatter(self.held, "dp", axis_index_groups=lines, scatter_dimension=0, tiled=True)
                 self.owned = wide(owned)
             else:
-                three = self.move.along(low(self.far[1]))
-                if earlier:
-                    three = after(three, *earlier)
+                three = self.move.along(self.far[1])
                 two = self.move.along(low(self.far[0] + wide(three)))
+                two = after(two, *earlier) if earlier else two
                 one = self.move.along(low(self.near[1] + wide(two)))
+                self.passed = (three, two, one)
                 self.owned = self.near[0] + wide(one)
 
 
@@ -1014,9 +1130,10 @@
         self.name = name
         self.next = arrays[0]
 
-    def line(self, step):
+    def line(self, step, *earlier):
+        value = after(self.next, *earlier) if earlier else self.next
         with jax.named_scope(f"{self.name}_line{step}"):
-            self.sent = self.move.along(self.next)
+            self.sent = self.move.along(value)
 
     def prepare(self, step, *earlier):
         with jax.named_scope(f"{self.name}_line{step}"):
@@ -1024,30 +1141,48 @@
             self.next = low(wide(self.arrays[step]) + wide(sent))
         return self.next
 
-    def across(self):
+    def prepare_across(self, *earlier):
+        sent = after(self.sent, *earlier) if earlier else self.sent
         with jax.named_scope(self.name + "_across"):
-            held = wide(self.arrays[3]) + wide(self.sent)
+            held = wide(self.arrays[3]) + wide(sent)
             half = held.shape[1] // 2
             self.near, self.rest = held[:, :half], held[:, half:]
             self.operands = (low(self.near[1::2]), low(self.rest[2:]))
-            self.first = self.move.flip(self.operands[0], 1)
-            self.second = self.move.flip(self.operands[1], 2)
-
-    def finish(self):
+        return self.operands
+
+    def across(self, *earlier):
+        operands = after(self.operands, *earlier) if earlier else self.operands
+        with jax.named_scope(self.name + "_across"):
+            self.first = self.move.flip(operands[0], 1)
+            self.second = self.move.flip(operands[1], 2)
+
+    def prepare_onward(self, *earlier):
+        self.first, self.second = after((self.first, self.second), *earlier) if earlier else (self.first, self.second)
         with jax.named_scope(self.name + "_onward"):
-            first_rest = self.move.flip(low(self.rest[1] + wide(self.second[1])), 1)
-            second_rest = self.move.flip(low(self.near[2] + wide(self.first[1])), 2)
+            self.operands = (low(self.rest[1] + wide(self.second[1])), low(self.near[2] + wide(self.first[1])))
+        return self.operands
+
+    def finish(self, *earlier):
+        operands = after(self.operands, *earlier) if earlier else self.operands
+        with jax.named_scope(self.name + "_onward"):
+            first_rest = self.move.flip(operands[0], 1)
+            second_rest = self.move.flip(operands[1], 2)
             near = self.near[0] + wide(self.first[0]) + wide(second_rest)
             rest = self.rest[0] + wide(self.second[0]) + wide(first_rest)
             self.owned = jnp.concatenate([near, rest])
 
 
-def unite(move, owned, matrices):
+def whole_matrix(array):
+    blocks = Blocks()
+    blocks.add(array, None, 0, 0, None, 0, 0, 0, *array.shape)
+    return blocks
+
+
+def halves(move, owned, matrices):
     blocks = owned.reshape(matrices, 2, -1, owned.shape[-1])
     core = lax.axis_index("fsdp")
     mine = lax.dynamic_index_in_dim(blocks, core, 1, keepdims=False)
-    other = move.swap(lax.dynamic_index_in_dim(blocks, 1 - core, 1, keepdims=False))
-    return jnp.where(core == 0, jnp.stack([mine, other], 2), jnp.stack([other, mine], 2))
+    return mine, move.swap(lax.dynamic_index_in_dim(blocks, 1 - core, 1, keepdims=False))
 
 
 def local(
@@ -1099,11 +1234,10 @@
         cross(move, [], [three], three.first)
         three.settle_line(three.first)
         settle(move, [three], [two], three.first)
-        cross(move, [four], [], three.far_first)
+        cross(move, [four], [], three.far_first, top.passed[1])
         top.pass_on(three.far_first)
         settle(move, [], [three], three.far_first)
         lies = {
-            "first_0": [(one, 0, rows, 0, 0, C)],
             "head_0": [(one, 0, rows, 0, 0, C), (one, rows, rows, 0, C, HEAD - C)],
             "middle_0": [(two, 0, cut, 0, 0, C), (three, 0, cut, cut, 0, C)],
             "last_0": [(one, 2 * rows, rows, 0, 0, C)],
@@ -1119,7 +1253,6 @@
 
         first_all = whole(w_in[0])
         lies = {
-            "first_0": [(first_all, 0)],
             "head_0": [(first_all, 0), (whole(beside[:, : HEAD - C]), C)],
             "middle_0": [(whole(w_mid[0]), 0)],
             "last_0": [(whole(w_out[0]), 0)],
@@ -1130,33 +1263,44 @@
         }
 
     def matrix(name):
-        blocks = Blocks(middle_rows if name.startswith("middle") else rows)
+        blocks = Blocks()
         if not paired:
             for array, column in lies[name]:
-                blocks.add(array, None, 0, 0, None, 0, column, *array.shape)
+                blocks.add(array, None, 0, 0, None, 0, 0, column, *array.shape)
             return blocks
+        stride = middle_rows if name.startswith("middle") else rows
         for piece, row, extent, to_row, to_column, columns in lies[name]:
             for array, first, place in piece.found:
-                blocks.add(array, None, first + row, 0, place, to_row, to_column, extent, columns)
+                blocks.add(array, None, first + row, 0, place, stride, to_row, to_column, extent, columns)
         return blocks
 
-    def sums_of(block_rows, columns, matrices=1, parts=1, levels=False, last_line=False):
+    def sums_of(columns, matrices, pieces=((None, STEPPED),)):
+        blocks = Blocks()
         if not paired:
-            extent = matrices * move.devices * block_rows
-            blocks = Blocks(block_rows)
-            blocks.add(shaped(1, extent, columns), 0, 0, 0, None, 0, 0, extent, columns)
+            extent = sum(matrices) * move.devices
+            blocks.add(shaped(1, extent, columns), 0, 0, 0, None, 0, 0, 0, extent, columns)
             return blocks
-        chip_rows = 2 * block_rows
-        cut = chip_rows // parts
-        blocks = Blocks(chip_rows)
-        for part in range(parts):
-            line_first = last_line and part == parts - 1
-            place = OUT_LINE if line_first else OUT_LEVELS if levels else OUT_STEPS
-            for count in (4, 4, 4, 4) if line_first else (4, 4, 2, 2, 4):
-                array = shaped(count, matrices * cut, columns)
+        runs, start = [], 0
+        for block_rows in matrices:
+            runs.append((start, 2 * block_rows, 0))
+            start += move.devices * block_rows
+        for cut, kind in pieces:
+            taken = []
+            while runs and cut != 0:
+                start, stride, first = runs.pop(0)
+                extent = stride - first if cut is None else min(cut, stride - first)
+                taken.append((start + first, stride, extent))
+                if first + extent < stride:
+                    runs.insert(0, (start, stride, first + extent))
+                cut = None if cut is None else cut - extent
+            place = {STEPPED: OUT_STEPS, LEVELED: OUT_LEVELS, LINED: OUT_LINE}[kind]
+            for count in (4, 4, 4, 4) if kind == LINED else (4, 4, 2, 2, 4):
+                array = shaped(count, sum(extent for _, _, extent in taken), columns)
                 for block in range(count):
-                    for i in range(matrices):
-                        blocks.add(array, block, i * cut, 0, place, i * C + part * cut, 0, cut, columns)
+                    row = 0
+                    for first, stride, extent in taken:
+                        blocks.add(array, block, row, 0, place, stride, first, 0, extent, columns)
+                        row += extent
                     place += 1
         return blocks
 
@@ -1173,7 +1317,7 @@
     half = 2 if paired else 1
     table = move.table()
     mid_0, last_0 = matrix("middle_0"), matrix("last_0")
-    misc, pooled, stream_in, lefts_0, pre1_0, pre2_0, pre3_0 = forward_block(
+    misc, pooled, stream_in, lefts_0, pre1_0, pre2_0, pre3_0, first_0, last_0 = forward_block(
         table, 0, G, None, features[0], None, matrix("head_0"), mid_0, last_0
     )
     lefts_other_0 = swap(lefts_0)
@@ -1184,101 +1328,104 @@
         four.settle_line(pooled)
         settle(move, [], [four])
     first_1, mid_1, last_1 = matrix("first_1"), matrix("middle_1"), matrix("last_1")
-    lefts_1, pre1_1, pre2_1, pre3_1 = forward_block(table, 1, half_side, pooled, None, misc, first_1, mid_1, last_1)
+    lefts_1, pre1_1, pre2_1, pre3_1, first_1, last_1 = forward_block(
+        table, 1, half_side, pooled, None, misc, first_1, mid_1, last_1
+    )
+    first_0, last_0, first_1, last_1 = [whole_matrix(array) for array in (first_0, last_0, first_1, last_1)]
     lefts_other_1 = swap(lefts_1)
     if paired:
         top.end_line(lefts_1)
     readout_bias = misc[12:].T.reshape(1, width)
     output, grad_top, grad_readout_b, grad_logits, grad_logits_other = readout(
-        table, grid_live, lefts_1, readout_bias, cotangent[0], matrix("readout")
+        table, grid_live, tie(lefts_1, lefts_other_0), readout_bias, cotangent[0], matrix("readout")
     )
     if paired:
-        grad_logits_other = swap(grad_logits_other)
+        acts = Spread(move, lefts_1[1])
+        grad_logits_other = swap(after(grad_logits_other, *acts.sides))
+        grad_top = after(grad_top, *acts.sides)
     else:
         grad_logits, grad_logits_other = jnp.concatenate([grad_logits, grad_logits_other], axis=1), None
     direct_1, grads_1, grads_other_1, sums_1 = back_last(
         table, 1, half_side, grad_top, pooled, pre3_1, pre2_1, misc, last_1
     )
+    if paired:
+        spread = Spread(move, grads_1[1], grad_logits_other)
+        grads_other_1 = tie(grads_other_1, grad_logits_other)
     grads_other_1 = swap(grads_other_1)
-    readout_terms = plain_terms(
+    readout_terms = weight_terms(
         table,
+        None,
         [(lefts_1, 3, lefts_other_1, tie(grad_logits, sums_1), None, grad_logits_other, None)],
         [],
-        sums_of(rows, width // half, levels=True),
-    )
-    middle_terms_1 = middle_terms(
-        table,
-        half_side,
-        tie(lefts_1, *readout_terms),
-        lefts_other_1,
-        grads_1,
-        grads_other_1,
-        sums_of(middle_rows, C // half, parts=2 if paired else 1, levels=True),
+        sums_of(width // half, [rows], [(None, LEVELED)]),
     )
     if paired:
         sum_readout = Sum(move, readout_terms, "readout", levels=True)
-        sums_middle_1 = [Sum(move, middle_terms_1[5 * i : 5 * i + 5], f"middle_1_{i}", levels=True) for i in range(2)]
-        sum_readout.across()
-        sums_middle_1[0].across()
-        grads_1 = tie(grads_1, *middle_terms_1)
+        spread.sides = after(spread.sides, *readout_terms)
+        sum_readout.across(grads_other_1, *spread.sides)
+        grads_1 = tie(grads_1, *readout_terms, *spread.sides)
+    else:
+        middle_terms_1 = weight_terms(
+            table,
+            (half_side, lefts_1, lefts_other_1, grads_1, grads_other_1),
+            [],
+            [],
+            sums_of(C // half, [middle_rows]),
+        )
     grad_pooled, sums_first_1, grad_first_1, grad_first_other_1 = back_first(
         table, 1, half_side, grads_1, pre1_1, direct_1, misc, None, mid_1, first_1
     )
-    grad_first_other_1 = swap(grad_first_other_1)
-    if paired:
-        grad_pooled = tie(grad_pooled, *sum_readout.prepare(grad_pooled))
-        sum_readout.onward()
     direct_0, grads_0, grads_other_0, sums_0 = back_last(
         table, 0, G, grad_pooled, stream_in, pre3_0, pre2_0, misc, last_0
     )
-    grads_other_0 = swap(grads_other_0)
     if paired:
-        held = sum_readout.gather(sums_0)
-        lefts_other_0 = tie(lefts_other_0, held, *sums_middle_1[0].prepare(sums_0))
+        waited = [*sum_readout.prepare(sums_0), *after(spread.sides, sums_0)]
+        lefts_other_0 = tie(lefts_other_0, *waited)
+        grads_other_0, grad_first_other_1 = after((grads_other_0, grad_first_other_1), *waited)
+        spread.end(*waited)
+        acts.end(*waited)
+        sum_readout.onward(*waited)
+    grads_other_0, grad_first_other_1 = swap(grads_other_0), swap(grad_first_other_1)
+    crossed_terms = weight_terms(
+        table,
+        (G, lefts_0, lefts_other_0, grads_0, grads_other_0),
+        [],
+        [],
+        sums_of(C // half, [middle_rows]),
+    )
+    if paired:
+        sum_middle_0 = Sum(move, crossed_terms, "middle_0")
+        waited = [sum_readout.gather(*crossed_terms), *after((*spread.all, *acts.all), *crossed_terms)]
         sum_readout.finish()
-        sums_middle_1[0].onward()
-        sums_middle_1[1].across(sums_0)
-    middle_terms_0 = middle_terms(
-        table,
-        G,
-        lefts_0,
-        lefts_other_0,
-        grads_0,
-        grads_other_0,
-        sums_of(middle_rows, C // half, parts=2 if paired else 1, last_line=True),
+        sum_middle_0.across(*waited)
+        acts.all[0] = tie(acts.all[0], *waited)
+        middle_terms_1 = plane_terms(table, half_side, acts.all, spread.all, middle_rows)
+        grads_0 = tie(grads_0, middle_terms_1, *waited)
+    rests = [sums_0, sums_first_1, sums_1, grad_readout_b.reshape(C, 4).T]
+    grad_in, _, grad_first_0, grad_first_other_0, side, side_other = back_first(
+        table, 0, G, grads_0, pre1_0, direct_0, misc, rests, mid_0, first_0
     )
     if paired:
-        sum_middle_0 = Sum(move, middle_terms_0[:5], "middle_0_0")
-        line_middle_0 = LineSum(move, middle_terms_0[5:], "middle_0_1")
-        waited = [sums_middle_1[0].gather(*middle_terms_0), *sums_middle_1[1].prepare(*middle_terms_0)]
-        grads_0 = tie(grads_0, *middle_terms_0, *waited)
-        sums_middle_1[0].finish()
-        sums_middle_1[1].onward()
-        sum_middle_0.across()
-        line_middle_0.line(0)
-    blank = jnp.zeros((1, C), jnp.float32)
-    rest = jnp.concatenate(
-        [
-            blank, sums_0[2:3], sums_0[0:1], sums_first_1[0:1], sums_1[2:3], sums_1[0:1],
-            blank, sums_0[3:4], sums_0[1:2], sums_first_1[1:2], sums_1[3:4], sums_1[1:2],
-            grad_readout_b.reshape(C, 4).T,
-        ]
-    )
-    grad_in, _, grad_first_0, grad_first_other_0, side, side_other = back_first(
-        table, 0, G, grads_0, pre1_0, direct_0, misc, rest, mid_0, matrix("first_0")
-    )
-    grad_first_other_0 = swap(grad_first_other_0)
-    if paired:
-        sides = [(side, swap(side_other))]
-        waited = [line_middle_0.prepare(1, grad_in), *sum_middle_0.prepare(grad_in), sums_middle_1[1].gather(grad_in)]
+        waited = [*sum_middle_0.prepare(grad_in)]
+        grad_first_other_0, side_other = after((grad_first_other_0, side_other), *waited)
+        side_other = swap(side_other)
+        sides = [(side, side_other)]
+        sum_middle_0.onward(*waited)
+        with jax.named_scope("middle_1_levels"):
+            owned_1 = lax.psum_scatter(
+                after(middle_terms_1, *waited).reshape(-1, C),
+                "dp",
+                axis_index_groups=move.lines(),
+                scatter_dimension=0,
+                tiled=True,
+            )
         lefts_other_0 = tie(lefts_other_0, *waited)
-        line_middle_0.line(1)
-        sum_middle_0.onward()
-        sums_middle_1[1].finish()
     else:
         sides = [(side, None), (side_other, None)]
-    last_terms = plain_terms(
+    grad_first_other_0 = swap(grad_first_other_0)
+    last_terms = weight_terms(
         table,
+        None,
         [
             (lefts_0, 2, lefts_other_0, grads_0, 0, grads_other_0, 0),
             (lefts_1, 0, lefts_other_1, grad_first_1, 0, grad_first_other_1, None),
@@ -1286,45 +1433,42 @@
             (lefts_0, 0, lefts_other_0, grad_first_0, 0, grad_first_other_0, None),
         ],
         sides,
-        sums_of(rows, C // half, matrices=5),
+        sums_of(C // half, [rows] * 5),
     )
     if paired:
         sum_last = Sum(move, last_terms, "last")
-        sum_last.across()
         waited = sum_middle_0.gather(*last_terms)
-        next_line = line_middle_0.prepare(2, *last_terms)
-        line_middle_0.line(2)
-        sum_middle_0.finish(next_line)
-        sum_last.prepare(next_line)
+        sum_last.across(*waited)
+        sum_middle_0.finish()
+        core = jnp.reshape(lax.axis_index("fsdp"), (1,))
+        readout_owned = place_halves(core, halves(move, sum_readout.owned, 1))[0].reshape(rows, width)
+        sum_last.prepare(readout_owned)
         sum_last.onward()
-        line_middle_0.across()
-        sum_last.gather(*line_middle_0.operands)
-        sum_last.finish()
-        line_middle_0.finish()
-        readout_owned = unite(move, sum_readout.owned, 1).reshape(rows, width)
-        owned_1 = jnp.concatenate([total.owned for total in sums_middle_1])
-        owned_0 = jnp.concatenate([sum_middle_0.owned, line_middle_0.owned])
-        middle_owned = [unite(move, owned, 1).reshape(middle_rows, C) for owned in (owned_0, owned_1)]
-        last_owned = unite(move, sum_last.owned, 5)
-        side_owned = jnp.concatenate([last_owned[4, :, i, :SIDE] for i in range(2)], axis=1)
-        last_owned = last_owned.reshape(5, rows, C)
+        sum_last.gather()
+        middle_owned = place_halves(core, halves(move, sum_middle_0.owned, 1), owned_1[None])
+        sum_last.finish(middle_owned)
+        first_grad, last_grad, pos_grad, gain_grad, bias_grad, readout_grad = place_last(core, *halves(move, sum_last.owned, 5), cells)
+        readout_grad = readout_grad.T
     else:
         readout_owned = scattered(readout_terms)[0]
-        middle_owned = [scattered(terms)[0] for terms in (middle_terms_0, middle_terms_1)]
+        middle_owned = jnp.concatenate([scattered(terms) for terms in (crossed_terms, middle_terms_1)])
         last_owned = scattered(last_terms, 5)
-        side_owned = last_owned[4]
-    scales = side_owned[:, cells : cells + MISC]
+        first_grad, last_grad = jnp.stack([last_owned[3], last_owned[1]]), jnp.stack([last_owned[0], last_owned[2]])
+        pos_grad = last_owned[4, :, :cells].T
+        scales = last_owned[4, :, cells : cells + MISC]
+        gain_grad, bias_grad = scales[:, 0:6].T.reshape(2, 3, rows), scales[:, 6:12].T.reshape(2, 3, rows)
+        readout_grad = scales[:, 12:]
     return (
         output[None],
         grad_in[None],
-        side_owned[:, :cells].T,
-        jnp.stack([last_owned[3], last_owned[1]]),
-        jnp.stack(middle_owned),
-        jnp.stack([last_owned[0], last_owned[2]]),
-        scales[:, 0:6].T.reshape(2, 3, rows),
-        scales[:, 6:12].T.reshape(2, 3, rows),
+        pos_grad,
+        first_grad,
+        middle_owned,
+        last_grad,
+        gain_grad,
+        bias_grad,
         readout_owned,
-        scales[:, 12:].reshape(-1),
+        readout_grad.reshape(-1),
     )
 
 

time: 668 us -> 638 us (0.955)
  other arithmetic: 53.3 us -> 23.4 us
  starting transfers between devices: 92.3 us -> 63.9 us
  Pallas kernels: 192 us -> 209 us
  local copies, waits for them, and re-layouts: 51.2 us -> 62.9 us
    ppermute x21 -> x18, starting transfers between devices: 37.5 us -> 18.4 us  [along(): return lax.ppermute(value, 'dp', pairs)]
    ppermute x32 -> x33, waiting for transfers between devices: 17 us -> 34.7 us  [swap(): return lax.ppermute(value, 'fsdp', [(0, 1), (1, 0)])]
    pallas_call x11 -> x14, Pallas kernels: 192 us -> 209 us  [call(): pl.pallas_call(kernel, name=name, out_shape=outs, in_specs=in_specs, out_...]
    convert_element_type x20 -> x11, other arithmetic: 29.2 us -> 12.7 us  [low(): return value.astype(jnp.bfloat16)]
    ppermute x40 -> x34, waiting for transfers between devices: 88 us -> 77.9 us  [flip(): return lax.ppermute(value, 'dp', [(i, i ^ bits) for i in range(self.dp)])]
    unnamed x168 -> x167, local copies, waits for them, and re-layouts: 28 us -> 37.5 us
    ppermute x40 -> x34, starting transfers between devices: 49.1 us -> 40.6 us  [flip(): return lax.ppermute(value, 'dp', [(i, i ^ bits) for i in range(self.dp)])]
    ppermute x21 -> x18, waiting for transfers between devices: 148 us -> 140 us  [along(): return lax.ppermute(value, 'dp', pairs)]
  transfers between devices with their start and end apart: 97 -> 88, of which waited for: 33 -> 44; matrix products, arithmetic and copies ran while one was open for 12% -> 8% of each run, Pallas kernels for 28% -> 33%
where the time goes in v4:
time: 638 us; the launch traced here: 628 us
  waiting for transfers between devices  253 us (40%)
  Pallas kernels  209 us (33%)
  starting transfers between devices  63.9 us (10%)
  local copies, waits for them, and re-layouts  62.9 us (10%)
  other arithmetic  23.4 us (4%)
  between operations  15.9 us (2%)
    pallas_call x14, Pallas kernels, call(): pl.pallas_call(kernel, name=name, out_shape=outs, in_specs=in_specs, out_...  209 us
    ppermute x18, waiting for transfers between devices, along(): return lax.ppermute(value, 'dp', pairs)  140 us
    ppermute x34, waiting for transfers between devices, flip(): return lax.ppermute(value, 'dp', [(i, i ^ bits) for i in range(self.dp)])  77.9 us
    ppermute x34, starting transfers between devices, flip(): return lax.ppermute(value, 'dp', [(i, i ^ bits) for i in range(self.dp)])  40.6 us
    unnamed x167, local copies, waits for them, and re-layouts  37.5 us
    ppermute x33, waiting for transfers between devices, swap(): return lax.ppermute(value, 'fsdp', [(0, 1), (1, 0)])  34.7 us
    ppermute x18, starting transfers between devices, along(): return lax.ppermute(value, 'dp', pairs)  18.4 us
  transfers between devices with their start and end apart: 88, of which 44 were waited for; matrix products, arithmetic and copies ran while one was open for 8% of the time, Pallas kernels for 33%

profile of v4, /device:TPU:0, one launch (start us, length us, event | category | flops | bytes accessed | tf_op | source)
XLA Modules:
  0.0 628.4 jit_solution(18270760928388251199)
XLA Ops:
  13.4 3.0 collective-permute-start.2
  22.1 2.6 collective-permute-start.12
  26.3 2.9 collective-permute-done
  30.7 7.3 %collective-permute-done.1 = bf16[96,1024]{1,0:T(8,128)(2,1)S(1)} collective-permute-done((bf16[96,1024]{1,0:T(8,128)(2,1)S(1)}, bf16[96,1024]{1,0:T(8,128)(2,1)S(1)}, u32[]{:S(2)}, u32[]{:S(2)}) %collective-permute-start.1) | collective-permute-done | bytes 196640 | tf_op jit(solution)/shard_map/one_line/ppermute | solution.py:919
  40.1 4.5 collective-permute-done.4
  45.3 3.8 collective-permute-start.13
  50.8 5.2 collective-permute-done.13
  56.0 2.5 collective-permute-start.14
  58.6 5.1 collective-permute-done.14
  65.4 2.5 collective-permute-start.15
  69.3 2.5 collective-permute-start.16
  71.8 8.9 %collective-permute-done.20 = bf16[208,1024]{1,0:T(8,128)(2,1)S(1)} collective-permute-done((bf16[208,1024]{1,0:T(8,128)(2,1)S(1)}, bf16[208,1024]{1,0:T(8,128)(2,1)S(1)}, u32[]{:S(2)}, u32[]{:S(2)}) %collective-permute-start.20) | collective-permute-done | bytes 426016 | tf_op jit(solution)/shard_map/three_line/ppermute | solution.py:919
  81.5 10.9 %collective-permute-done.21 = bf16[208,1024]{1,0:T(8,128)(2,1)S(1)} collective-permute-done((bf16[208,1024]{1,0:T(8,128)(2,1)S(1)}, bf16[208,1024]{1,0:T(8,128)(2,1)S(1)}, u32[]{:S(2)}, u32[]{:S(2)}) %collective-permute-start.21) | collective-permute-done | bytes 426016 | tf_op jit(solution)/shard_map/three_line/ppermute | solution.py:919
  95.0 6.4 %collective-permute-done.22 = bf16[208,1024]{1,0:T(8,128)(2,1)S(1)} collective-permute-done((bf16[208,1024]{1,0:T(8,128)(2,1)S(1)}, bf16[208,1024]{1,0:T(8,128)(2,1)S(1)}, u32[]{:S(2)}, u32[]{:S(2)}) %collective-permute-start.22) | collective-permute-done | bytes 426016 | tf_op jit(solution)/shard_map/three_line/ppermute | solution.py:919
  102.4 3.2 copy.69
  105.7 1.9 slice_dynamic-update-slice_fusion
  107.6 1.9 slice_dynamic-update-slice_fusion.1
  111.2 2.7 collective-permute-start.24
  121.5 35.5 %collective-permute-done.23.refs_17_.refs_4_.refs_24_.refs_10_ = bf16[1120,1024]{1,0:T(8,128)(2,1)S(1)} collective-permute-done((bf16[1120,1024]{1,0:T(8,128)(2,1)}, bf16[1120,1024]{1,0:T(8,128)(2,1)S(1)}, u32[]{:S(2)}, u32[]{:S(2)}) %collective-permute-start.23) | collective-permute-done | bytes 2293792 | tf_op jit(solution)/shard_map/three_two_plane/ppermute | solution.py:912
  157.0 2.9 collective-permute-done.24.refs_19_.refs_6_.refs_26_.refs_12_
  161.3 2.7 collective-permute-start.29
  164.1 11.3 %collective-permute-done.32.refs_2_ = bf16[512,1024]{1,0:T(8,128)(2,1)} collective-permute-done((bf16[512,1024]{1,0:T(8,128)(2,1)}, bf16[512,1024]{1,0:T(8,128)(2,1)}, u32[]{:S(2)}, u32[]{:S(2)}) %collective-permute-start.32) | collective-permute-done | bytes 1048608 | tf_op jit(solution)/shard_map/top_line/ppermute | solution.py:919
  177.6 4.5 collective-permute-done.8.refs_2_.refs_28_
  183.2 2.2 collective-permute-done.19.refs_12_.refs_5_
  188.0 8.5 %collective-permute-done.27.refs_22_.refs_3_.refs_23_.refs_15_ = bf16[832,1024]{1,0:T(8,128)(2,1)} collective-permute-done((bf16[832,1024]{1,0:T(8,128)(2,1)}, bf16[832,1024]{1,0:T(8,128)(2,1)}, u32[]{:S(2)}, u32[]{:S(2)}) %collective-permute-start.27) | collective-permute-done | bytes 1703968 | tf_op jit(solution)/shard_map/swap/ppermute | solution.py:922
  196.5 31.1 %forward_block.2 = (f32[16,1024]{1,0:T(8,128)}, f32[144,1024]{1,0:T(8,128)}, f32[576,1024]{1,0:T(8,128)}, bf16[3,576,1024]{2,1,0:T(8,128)(2,1)}, f32[576,1024]{1...) custom-call(s32[165]{0:T(256)} %bitcast.124, ...), custom_call_target="tpu_custom_call" | custom-call | flops 265751104 | bytes 697303 | tf_op jit(solution)/shard_map/forward_block/pallas_call | solution.py:144
  227.9 11.2 %collective-permute-done.33.refs_12_.refs_0_ = bf16[1152,1024]{1,0:T(8,128)(2,1)} collective-permute-done((bf16[1152,1024]{1,0:T(8,128)(2,1)}, bf16[1152,1024]{1,0:T(8,128)(2,1)}, u32[]{:S(2)}, u32[]{:S(2)}) %collective-permute-start.33) | collective-permute-done | bytes 2359328 | tf_op jit(solution)/shard_map/four_plane/ppermute | solution.py:912
  240.5 1.8 collective-permute-start.38
  244.1 23.2 %collective-permute-done.43.refs_4_ = bf16[512,1024]{1,0:T(8,128)(2,1)} collective-permute-done((bf16[512,1024]{1,0:T(8,128)(2,1)}, bf16[512,1024]{1,0:T(8,128)(2,1)}, u32[]{:S(2)}, u32[]{:S(2)}) %collective-permute-start.43) | collective-permute-done | bytes 1048608 | tf_op jit(solution)/shard_map/top_line/ppermute | solution.py:919
  267.8 2.5 collective-permute-done.40.refs_20_.refs_8_
  270.9 4.4 collective-permute-done.39.refs_19_.refs_7_
  276.5 2.1 collective-permute-done.41.refs_21_.refs_9_
  279.7 16.6 %forward_block.3 = (bf16[4,144,1024]{2,1,0:T(8,128)(2,1)}, f32[144,1024]{1,0:T(8,128)}, f32[144,1024]{1,0:T(8,128)}, f32[144,1024]{1,0:T(8,128)}, bf16[1024,1024...) custom-call(s32[165]{0:T(256)} %bitcast.125, f32[144,1024]{1,0:T(8,128)} %get-tuple-element.183.refs_0_.u_in, ...), custom_call_target="tpu_custom_call" | custom-call | flops 66437776 | bytes 520355 | tf_op jit(solution)/shard_map/forward_block/pallas_call | solution.py:144
  296.3 5.6 collective-permute-done.44.refs_6_
  305.4 2.4 collective-permute-done.46.refs_3_
  312.5 15.1 %readout.1 = (bf16[144,4096]{1,0:T(8,128)(2,1)}, f32[144,1024]{1,0:T(8,128)}, f32[1,4096]{1,0:T(1,128)}, bf16[144,2048]{1,0:T(8,128)(2,1)}, bf16[144,2048]{1,0:T(8,128)(2,1)}) custom-call(s32[165]{0:T(256)} %bitcast.126, s32[1]{0:T(128)S(6)} %copy.80.live_ref, bf16[4,144,1024]{2,1,0:T(8,128)(2,1)} %get-tuple-element.193.lefts_ref.refs_0_.refs_4_.refs_8_, ...), custom_call_target="tpu_custom_call" | custom-call | flops 603979776 | bytes 2686976 | tf_op jit(solution)/shard_map/readout/pallas_call | solution.py:144
  328.3 6.3 %back_last.2 = (f32[144,1024]{1,0:T(8,128)}, bf16[2,144,1024]{2,1,0:T(8,128)(2,1)}, bf16[2,144,512]{2,1,0:T(8,128)(2,1)}, f32[4,1024]{1,0:T(4,128)}) custom-call(s32[165]{0:T(256)} %bitcast.127, f32[144,1024]{1,0:T(8,128)} %get-tuple-element.202.grad_ref, f32[144,1024]{1,0:T(8,128)} %get-tuple-element.183.refs_0_.u_in, ...), custom_call_target="tpu_custom_call" | custom-call | flops 75497472 | bytes 1409024 | tf_op jit(solution)/shard_map/back_last/pallas_call | solution.py:144
  340.3 7.3 %weight_terms.3 = (bf16[4,64,2048]{2,1,0:T(8,128)(2,1)}, bf16[4,64,2048]{2,1,0:T(8,128)(2,1)}, bf16[2,64,2048]{2,1,0:T(8,128)(2,1)}, bf16[2,64,2048]{2,1,0:T(8,128)(2,1)}, bf16[4,64,2048]{2,1,0:T(8,128)(2,1)}) custom-call(s32[165]{0:T(256)} %bitcast.128, bf16[4,144,1024]{2,1,0:T(8,128)(2,1)} %get-tuple-element.193.lefts_ref.refs_0_.refs_4_.refs_8_, ...), custom_call_target="tpu_custom_call" | custom-call | flops 301989888 | bytes 1343488 | tf_op jit(solution)/shard_map/weight_terms/pallas_call | solution.py:144
  347.6 5.0 collective-permute-done.55
  354.8 17.2 %back_first.2 = (f32[144,1024]{1,0:T(8,128)}, f32[2,1024]{1,0:T(2,128)}, bf16[1,144,1024]{2,1,0:T(8,128)(2,1)}, bf16[144,512]{1,0:T(8,128)(2,1)}) custom-call(s32[165]{0:T(256)} %bitcast.129, bf16[2,144,1024]{2,1,0:T(8,128)(2,1)} %get-tuple-element.221.grads_in.refs_9_, f32[144,1024]{1,0:T(8,128)} %get-tuple-element.222.pre1_in, ...), custom_call_target="tpu_custom_call" | custom-call | flops 754974720 | bytes 6127616 | tf_op jit(solution)/shard_map/back_first/pallas_call | solution.py:144
  372.0 24.3 %back_last.3 = (f32[576,1024]{1,0:T(8,128)}, bf16[2,576,1024]{2,1,0:T(8,128)(2,1)}, bf16[2,576,512]{2,1,0:T(8,128)(2,1)}, f32[4,1024]{1,0:T(4,128)}) custom-call(s32[165]{0:T(256)} %bitcast.130, f32[144,1024]{1,0:T(8,128)} %get-tuple-element.225.grad_ref, f32[576,1024]{1,0:T(8,128)} %get-tuple-element.226.u_in, f32[576,1024]{1,0:T(8,128)} %get-tuple-element.227.pre3_in, ...), custom_call_target="tpu_custom_call" | custom-call | flops 301989888 | bytes 4063232 | tf_op jit(solution)/shard_map/back_last/pallas_call | solution.py:144
  403.1 2.3 collective-permute-done.62.refs_3_
  406.4 26.4 %weight_terms.4 = (bf16[4,576,512]{2,1,0:T(8,128)(2,1)}, bf16[4,576,512]{2,1,0:T(8,128)(2,1)}, bf16[2,576,512]{2,1,0:T(8,128)(2,1)}, bf16[2,576,512]{2,1,0:T(8,128)(2,1)}, bf16[4,576,512]{2,1,0:T(8,128)(2,1)}) custom-call(s32[165]{0:T(256)} %bitcast.131, bf16[3,576,1024]{2,1,0:T(8,128)(2,1)} %get-tuple-element.192.refs_0_.refs_12_, ...), custom_call_target="tpu_custom_call" | custom-call | flops 2717908992 | bytes 3538944 | tf_op jit(solution)/shard_map/weight_terms/pallas_call | solution.py:144
  432.9 2.2 add_convert_fusion.6
  440.8 15.0 %plane_terms.1 = bf16[4,288,1024]{2,1,0:T(8,128)(2,1)} custom-call(s32[165]{0:T(256)} %bitcast.132, bf16[576,1024]{1,0:T(8,128)(2,1)} %copy-done.20, bf16[576,1024]{1,0:T(8,128)(2,1)} %collective-permute-done.64.refs_1_, bf16[576,1024]{1,0:T(8,128)(2,1)} %copy-done.19, bf16[576,1024]{1,0:T(8,128)(2,1)} %collective-permute-done.63.refs_3_), custom_call_target="tpu_custom_call" | custom-call | flops 905969664 | bytes 1769472 | tf_op jit(solution)/shard_map/plane_terms/pallas_call | solution.py:144
  455.8 28.9 %back_first.3 = (f32[576,1024]{1,0:T(8,128)}, f32[2,1024]{1,0:T(2,128)}, bf16[1,576,1024]{2,1,0:T(8,128)(2,1)}, bf16[576,512]{1,0:T(8,128)(2,1)}, bf16[1024,384]{1,0:T(8,128)(2,1)}, /*index=5*/bf16[1024,384]{1,0:T(8,128)(2,1)}) custom-call(s32[165]{0:T(256)} %bitcast.133, bf16[2,576,1024]{2,1,0:T(8,128)(2,1)} %get-tuple-element.267.refs_1_.grads_in, ...), custom_call_target="tpu_custom_call" | custom-call | flops 3019898880 | bytes 8781824 | tf_op jit(solution)/shard_map/back_first/pallas_call | solution.py:144
  484.7 4.9 collective-permute-done.65
  492.4 2.6 add_convert_fusion.1
  497.3 3.0 collective-permute-done.67.refs_7_
  501.3 14.0 %weight_terms.5 = (bf16[4,320,512]{2,1,0:T(8,128)(2,1)}, bf16[4,320,512]{2,1,0:T(8,128)(2,1)}, bf16[2,320,512]{2,1,0:T(8,128)(2,1)}, bf16[2,320,512]{2,1,0:T(8,128)(2,1)}, bf16[4,320,512]{2,1,0:T(8,128)(2,1)}) custom-call(s32[165]{0:T(256)} %bitcast.134, bf16[3,576,1024]{2,1,0:T(8,128)(2,1)} %get-tuple-element.192.refs_0_.refs_12_, ...), custom_call_target="tpu_custom_call" | custom-call | flops 754974720 | bytes 3997696 | tf_op jit(solution)/shard_map/weight_terms/pallas_call | solution.py:144
  515.3 6.8 %collective-permute-done.70 = bf16[2,576,512]{2,1,0:T(8,128)(2,1)S(1)} collective-permute-done((bf16[2,576,512]{2,1,0:T(8,128)(2,1)}, bf16[2,576,512]{2,1,0:T(8,128)(2,1)S(1)}, u32[]{:S(2)}, u32[]{:S(2)}) %collective-permute-start.70) | collective-permute-done | bytes 1179680 | tf_op jit(solution)/shard_map/middle_0_onward/ppermute | solution.py:912
  524.1 3.7 convert_add_fusion
  536.1 1.9 place_halves.2
  538.1 17.4 %collective-permute-done.79 = bf16[576,512]{1,0:T(8,128)(2,1)} collective-permute-done((bf16[576,512]{1,0:T(8,128)(2,1)}, bf16[576,512]{1,0:T(8,128)(2,1)}, u32[]{:S(2)}, u32[]{:S(2)}) %collective-permute-start.79) | collective-permute-done | bytes 589856 | tf_op jit(solution)/shard_map/middle_0_line/ppermute | solution.py:919
  564.7 7.9 %collective-permute-done.80 = bf16[576,512]{1,0:T(8,128)(2,1)S(1)} collective-permute-done((bf16[576,512]{1,0:T(8,128)(2,1)S(1)}, bf16[576,512]{1,0:T(8,128)(2,1)S(1)}, u32[]{:S(2)}, u32[]{:S(2)}) %collective-permute-start.80) | collective-permute-done | bytes 589856 | tf_op jit(solution)/shard_map/middle_0_line/ppermute | solution.py:919
  574.5 2.6 collective-permute-done.76
  577.1 2.8 convert_add_fusion.2
  579.9 1.8 collective-permute-start.77
  581.7 8.3 %collective-permute-done.81 = bf16[576,512]{1,0:T(8,128)(2,1)S(1)} collective-permute-done((bf16[576,512]{1,0:T(8,128)(2,1)S(1)}, bf16[576,512]{1,0:T(8,128)(2,1)S(1)}, u32[]{:S(2)}, u32[]{:S(2)}) %collective-permute-start.81) | collective-permute-done | bytes 589856 | tf_op jit(solution)/shard_map/middle_0_line/ppermute | solution.py:919
  591.1 3.2 collective-permute-done.77
  595.3 3.1 place_halves.3
  598.4 4.1 collective-permute-done.78
  602.6 8.0 %collective-permute-done.83 = bf16[320,512]{1,0:T(8,128)(2,1)S(1)} collective-permute-done((bf16[320,512]{1,0:T(8,128)(2,1)S(1)}, bf16[320,512]{1,0:T(8,128)(2,1)S(1)}, u32[]{:S(2)}, u32[]{:S(2)}) %collective-permute-start.83) | collective-permute-done | bytes 327712 | tf_op jit(solution)/shard_map/last_line/ppermute | solution.py:919
  613.8 2.0 place_last.1
  (359 shorter events, 117.9 us)
Async XLA Ops:
  7.2 176.0 %all-gather.2.cloned.1.call-start = ((), (), s32[]{:S(2)}) async-start(), calls=%async_computation.2 | async-start | bytes 2949120 | tf_op jit(solution)/shard_map/four_levels/all_gather | solution.py:991
  13.4 17.4 %collective-permute-start.2 = (bf16[128,1024]{1,0:T(8,128)(2,1)S(1)}, bf16[128,1024]{1,0:T(8,128)(2,1)S(1)}, u32[]{:S(2)}, u32[]{:S(2)}) collective-permute-start(bf16[128,1024]{1,0:T(8,128)(2,1)S(1)} %pad_maximum_fusion.3), channel_id=1, source_target_pairs={{0,2},{2,0},{4,6},{6,4},{8,10},{10,8},{12,14},{14,12},{16,18},{18,... | collective-permute-start | bytes 786440 | tf_op jit(solution)/shard_map/top_plane/ppermute | solution.py:912
  16.4 14.4 %collective-permute-start.3 = (bf16[128,1024]{1,0:T(8,128)(2,1)S(1)}, bf16[128,1024]{1,0:T(8,128)(2,1)S(1)}, u32[]{:S(2)}, u32[]{:S(2)}) collective-permute-start(bf16[128,1024]{1,0:T(8,128)(2,1)S(1)} %pad_maximum_fusion.3), channel_id=1, source_target_pairs={{0,4},{2,6},{4,0},{6,2},{8,12},{10,14},{12,8},{14,10},{16,20},{18,... | collective-permute-start | bytes 786440 | tf_op jit(solution)/shard_map/top_plane/ppermute | solution.py:912
  20.5 8.8 %collective-permute-start = (bf16[96,1024]{1,0:T(8,128)(2,1)S(1)}, bf16[96,1024]{1,0:T(8,128)(2,1)S(1)}, u32[]{:S(2)}, u32[]{:S(2)}) collective-permute-start(bf16[96,1024]{1,0:T(8,128)(2,1)S(1)} %pad_maximum_fusion.4), channel_id=1, source_target_pairs={{0,8},{2,10},{4,12},{6,14},{8,24},{10,26},{12,28},{14,30},{24,16},... | collective-permute-start | bytes 589832 | tf_op jit(solution)/shard_map/one_line/ppermute | solution.py:919
  22.1 23.1 %collective-permute-start.12 = (bf16[144,1024]{1,0:T(8,128)(2,1)S(1)}, bf16[144,1024]{1,0:T(8,128)(2,1)S(1)}, u32[]{:S(2)}, u32[]{:S(2)}) collective-permute-start(bf16[144,1024]{1,0:T(8,128)(2,1)S(1)} %get-tuple-element.338), channel_id=1, source_target_pairs={{0,8},{2,10},{4,12},{6,14},{8,24},{10,26},{12,28},{14,30},{24,16},... | collective-permute-start | bytes 884744 | tf_op jit(solution)/shard_map/two_line/ppermute | solution.py:919
  44.7 19.7 %collective-permute-start.7 = (bf16[384,1024]{1,0:T(8,128)(2,1)S(1)}, bf16[384,1024]{1,0:T(8,128)(2,1)}, u32[]{:S(2)}, u32[]{:S(2)}) collective-permute-start(bf16[384,1024]{1,0:T(8,128)(2,1)S(1)} %constant_dynamic-update-slice_fusion.refs_1_.refs_27_), channel_id=1, source_target_pairs={{0,2},{2,0},{4,6},{6,4},{8,10},{10,8},{12,14},{14,12},{16,18},{18,... | collective-permute-start | bytes 2359304 | tf_op jit(solution)/shard_map/one_plane/ppermute | solution.py:912
  45.3 10.7 %collective-permute-start.13 = (bf16[144,1024]{1,0:T(8,128)(2,1)S(1)}, bf16[144,1024]{1,0:T(8,128)(2,1)S(1)}, u32[]{:S(2)}, u32[]{:S(2)}) collective-permute-start(bf16[144,1024]{1,0:T(8,128)(2,1)S(1)} %collective-permute-done.12), channel_id=1, source_target_pairs={{0,8},{2,10},{4,12},{6,14},{8,24},{10,26},{12,28},{14,30},{24,16},... | collective-permute-start | bytes 884744 | tf_op jit(solution)/shard_map/two_line/ppermute | solution.py:919
  49.1 16.2 %collective-permute-start.9 = (bf16[384,1024]{1,0:T(8,128)(2,1)S(1)}, bf16[384,1024]{1,0:T(8,128)(2,1)S(1)}, u32[]{:S(2)}, u32[]{:S(2)}) collective-permute-start(bf16[384,1024]{1,0:T(8,128)(2,1)S(1)} %constant_dynamic-update-slice_fusion.refs_1_.refs_27_), channel_id=1, source_target_pairs={{0,4},{2,6},{4,0},{6,2},{8,12},{10,14},{12,8},{14,10},{16,20},{18,... | collective-permute-start | bytes 2359304 | tf_op jit(solution)/shard_map/one_plane/ppermute | solution.py:912
  65.4 40.2 %collective-permute-start.15 = (bf16[768,1024]{1,0:T(8,128)(2,1)S(1)}, bf16[768,1024]{1,0:T(8,128)(2,1)}, u32[]{:S(2)}, u32[]{:S(2)}) collective-permute-start(bf16[768,1024]{1,0:T(8,128)(2,1)S(1)} %slice_dynamic-update-slice_fusion.3), channel_id=1, source_target_pairs={{0,2},{2,0},{4,6},{6,4},{8,10},{10,8},{12,14},{14,12},{16,18},{18,... | collective-permute-start | bytes 4718600 | tf_op jit(solution)/shard_map/two_one_plane/ppermute | solution.py:912
  68.0 12.7 %collective-permute-start.20 = (bf16[208,1024]{1,0:T(8,128)(2,1)S(1)}, bf16[208,1024]{1,0:T(8,128)(2,1)S(1)}, u32[]{:S(2)}, u32[]{:S(2)}) collective-permute-start(bf16[208,1024]{1,0:T(8,128)(2,1)S(1)} %pad_maximum_fusion.2), channel_id=1, source_target_pairs={{0,8},{2,10},{4,12},{6,14},{8,24},{10,26},{12,28},{14,30},{24,16},... | collective-permute-start | bytes 1277960 | tf_op jit(solution)/shard_map/three_line/ppermute | solution.py:919
  69.3 38.3 %collective-permute-start.16 = (bf16[768,1024]{1,0:T(8,128)(2,1)S(1)}, bf16[768,1024]{1,0:T(8,128)(2,1)}, u32[]{:S(2)}, u32[]{:S(2)}) collective-permute-start(bf16[768,1024]{1,0:T(8,128)(2,1)S(1)} %slice_dynamic-update-slice_fusion.2), channel_id=1, source_target_pairs={{0,4},{2,6},{4,0},{6,2},{8,12},{10,14},{12,8},{14,10},{16,20},{18,... | collective-permute-start | bytes 4718600 | tf_op jit(solution)/shard_map/two_one_plane/ppermute | solution.py:912
  80.6 11.8 %collective-permute-start.21 = (bf16[208,1024]{1,0:T(8,128)(2,1)S(1)}, bf16[208,1024]{1,0:T(8,128)(2,1)S(1)}, u32[]{:S(2)}, u32[]{:S(2)}) collective-permute-start(bf16[208,1024]{1,0:T(8,128)(2,1)S(1)} %collective-permute-done.20), channel_id=1, source_target_pairs={{0,8},{2,10},{4,12},{6,14},{8,24},{10,26},{12,28},{14,30},{24,16},... | collective-permute-start | bytes 1277960 | tf_op jit(solution)/shard_map/three_line/ppermute | solution.py:919
  92.4 9.0 %collective-permute-start.22 = (bf16[208,1024]{1,0:T(8,128)(2,1)S(1)}, bf16[208,1024]{1,0:T(8,128)(2,1)S(1)}, u32[]{:S(2)}, u32[]{:S(2)}) collective-permute-start(bf16[208,1024]{1,0:T(8,128)(2,1)S(1)} %collective-permute-done.21), channel_id=1, source_target_pairs={{0,8},{2,10},{4,12},{6,14},{8,24},{10,26},{12,28},{14,30},{24,16},... | collective-permute-start | bytes 1277960 | tf_op jit(solution)/shard_map/three_line/ppermute | solution.py:919
  109.5 47.4 %collective-permute-start.23 = (bf16[1120,1024]{1,0:T(8,128)(2,1)}, bf16[1120,1024]{1,0:T(8,128)(2,1)S(1)}, u32[]{:S(2)}, u32[]{:S(2)}) collective-permute-start(bf16[1120,1024]{1,0:T(8,128)(2,1)} %slice_dynamic-update-slice_fusion.1), channel_id=1, source_target_pairs={{0,2},{2,0},{4,6},{6,4},{8,10},{10,8},{12,14},{14,12},{16,18},{18,... | collective-permute-start | bytes 6881288 | tf_op jit(solution)/shard_map/three_two_plane/ppermute | solution.py:912
  111.2 48.7 %collective-permute-start.24 = (bf16[1120,1024]{1,0:T(8,128)(2,1)}, bf16[1120,1024]{1,0:T(8,128)(2,1)}, u32[]{:S(2)}, u32[]{:S(2)}) collective-permute-start(bf16[1120,1024]{1,0:T(8,128)(2,1)} %slice_dynamic-update-slice_fusion), channel_id=1, source_target_pairs={{0,4},{2,6},{4,0},{6,2},{8,12},{10,14},{12,8},{14,10},{16,20},{18,... | collective-permute-start | bytes 6881288 | tf_op jit(solution)/shard_map/three_two_plane/ppermute | solution.py:912
  114.8 417.4 %reduce-scatter.3.cloned.1.call-start = ((), (), s32[]{:S(2)}) async-start(), calls=%async_computation.3 | async-start | bytes 1310720 | tf_op jit(solution)/shard_map/readout_line/reduce_scatter | solution.py:1115
  121.3 54.0 %collective-permute-start.32 = (bf16[512,1024]{1,0:T(8,128)(2,1)}, bf16[512,1024]{1,0:T(8,128)(2,1)}, u32[]{:S(2)}, u32[]{:S(2)}) collective-permute-start(bf16[512,1024]{1,0:T(8,128)(2,1)} %constant_dynamic-update-slice_fusion.32.refs_0_), channel_id=1, source_target_pairs={{0,8},{2,10},{4,12},{6,14},{8,24},{10,26},{12,28},{14,30},{24,16},... | collective-permute-start | bytes 3145736 | tf_op jit(solution)/shard_map/top_line/ppermute | solution.py:919
  121.4 54.0 %collective-permute-start.10 = (bf16[384,1024]{1,0:T(8,128)(2,1)}, bf16[384,1024]{1,0:T(8,128)(2,1)}, u32[]{:S(2)}, u32[]{:S(2)}) collective-permute-start(bf16[384,1024]{1,0:T(8,128)(2,1)} %collective-permute-done.7.refs_3_.refs_29_), channel_id=1, source_target_pairs={{0,1},{1,0},{2,3},{3,2},{4,5},{5,4},{6,7},{7,6},{8,9},{9,8},{10,11... | collective-permute-start | bytes 2359304 | tf_op jit(solution)/shard_map/swap/ppermute | solution.py:922
  161.1 15.9 %collective-permute-start.28 = (bf16[416,1024]{1,0:T(8,128)(2,1)S(1)}, bf16[416,1024]{1,0:T(8,128)(2,1)S(1)}, u32[]{:S(2)}, u32[]{:S(2)}) collective-permute-start(bf16[416,1024]{1,0:T(8,128)(2,1)S(1)} %slice.225), channel_id=1, source_target_pairs={{0,2},{2,0},{4,6},{6,4},{8,10},{10,8},{12,14},{14,12},{16,18},{18,... | collective-permute-start | bytes 2555912 | tf_op jit(solution)/shard_map/three_plane/ppermute | solution.py:912
  161.3 15.7 %collective-permute-start.29 = (bf16[416,1024]{1,0:T(8,128)(2,1)S(1)}, bf16[416,1024]{1,0:T(8,128)(2,1)}, u32[]{:S(2)}, u32[]{:S(2)}) collective-permute-start(bf16[416,1024]{1,0:T(8,128)(2,1)S(1)} %slice.226), channel_id=1, source_target_pairs={{0,4},{2,6},{4,0},{6,2},{8,12},{10,14},{12,8},{14,10},{16,20},{18,... | collective-permute-start | bytes 2555912 | tf_op jit(solution)/shard_map/three_plane/ppermute | solution.py:912
  164.1 13.5 %collective-permute-start.11 = (bf16[384,1024]{1,0:T(8,128)(2,1)S(1)}, bf16[384,1024]{1,0:T(8,128)(2,1)S(1)}, u32[]{:S(2)}, u32[]{:S(2)}) collective-permute-start(bf16[384,1024]{1,0:T(8,128)(2,1)S(1)} %copy-done.7), channel_id=1, source_target_pairs={{0,1},{1,0},{2,3},{3,2},{4,5},{5,4},{6,7},{7,6},{8,9},{9,8},{10,11... | collective-permute-start | bytes 2359304 | tf_op jit(solution)/shard_map/swap/ppermute | solution.py:922
  175.4 10.3 %collective-permute-start.17 = (bf16[768,1024]{1,0:T(8,128)(2,1)}, bf16[768,1024]{1,0:T(8,128)(2,1)}, u32[]{:S(2)}, u32[]{:S(2)}) collective-permute-start(bf16[768,1024]{1,0:T(8,128)(2,1)} %collective-permute-done.15.refs_7_.refs_13_.refs_33_.refs_6_), channel_id=1, source_target_pairs={{0,1},{1,0},{2,3},{3,2},{4,5},{5,4},{6,7},{7,6},{8,9},{9,8},{10,11... | collective-permute-start | bytes 4718600 | tf_op jit(solution)/shard_map/swap/ppermute | solution.py:922
  175.4 10.6 %collective-permute-start.18 = (bf16[768,1024]{1,0:T(8,128)(2,1)}, bf16[768,1024]{1,0:T(8,128)(2,1)}, u32[]{:S(2)}, u32[]{:S(2)}) collective-permute-start(bf16[768,1024]{1,0:T(8,128)(2,1)} %collective-permute-done.16.refs_9_.refs_15_.refs_35_.refs_8_), channel_id=1, source_target_pairs={{0,1},{1,0},{2,3},{3,2},{4,5},{5,4},{6,7},{7,6},{8,9},{9,8},{10,11... | collective-permute-start | bytes 4718600 | tf_op jit(solution)/shard_map/swap/ppermute | solution.py:922
  185.4 53.6 %collective-permute-start.33 = (bf16[1152,1024]{1,0:T(8,128)(2,1)}, bf16[1152,1024]{1,0:T(8,128)(2,1)}, u32[]{:S(2)}, u32[]{:S(2)}) collective-permute-start(bf16[1152,1024]{1,0:T(8,128)(2,1)} %all-gather.2.cloned.1.call-done.refs_16_.refs_4_), channel_id=1, source_target_pairs={{0,2},{2,0},{4,6},{6,4},{8,10},{10,8},{12,14},{14,12},{16,18},{18,... | collective-permute-start | bytes 7077896 | tf_op jit(solution)/shard_map/four_plane/ppermute | solution.py:912
  185.7 53.3 %collective-permute-start.34 = (bf16[1152,1024]{1,0:T(8,128)(2,1)}, bf16[1152,1024]{1,0:T(8,128)(2,1)}, u32[]{:S(2)}, u32[]{:S(2)}) collective-permute-start(bf16[1152,1024]{1,0:T(8,128)(2,1)} %all-gather.2.cloned.1.call-done.refs_16_.refs_4_), channel_id=1, source_target_pairs={{0,4},{2,6},{4,0},{6,2},{8,12},{10,14},{12,8},{14,10},{16,20},{18,... | collective-permute-start | bytes 7077896 | tf_op jit(solution)/shard_map/four_plane/ppermute | solution.py:912
  186.0 10.5 %collective-permute-start.25 = (bf16[1120,1024]{1,0:T(8,128)(2,1)S(1)}, bf16[1120,1024]{1,0:T(8,128)(2,1)}, u32[]{:S(2)}, u32[]{:S(2)}) collective-permute-start(bf16[1120,1024]{1,0:T(8,128)(2,1)S(1)} %collective-permute-done.23.refs_17_.refs_4_.refs_24_.refs_10_), channel_id=1, source_target_pairs={{0,1},{1,0},{2,3},{3,2},{4,5},{5,4},{6,7},{7,6},{8,9},{9,8},{10,11... | collective-permute-start | bytes 6881288 | tf_op jit(solution)/shard_map/swap/ppermute | solution.py:922
  186.1 10.5 %collective-permute-start.26 = (bf16[1120,1024]{1,0:T(8,128)(2,1)}, bf16[1120,1024]{1,0:T(8,128)(2,1)}, u32[]{:S(2)}, u32[]{:S(2)}) collective-permute-start(bf16[1120,1024]{1,0:T(8,128)(2,1)} %collective-permute-done.24.refs_19_.refs_6_.refs_26_.refs_12_), channel_id=1, source_target_pairs={{0,1},{1,0},{2,3},{3,2},{4,5},{5,4},{6,7},{7,6},{8,9},{9,8},{10,11... | collective-permute-start | bytes 6881288 | tf_op jit(solution)/shard_map/swap/ppermute | solution.py:922
  186.6 9.9 %collective-permute-start.27 = (bf16[832,1024]{1,0:T(8,128)(2,1)}, bf16[832,1024]{1,0:T(8,128)(2,1)}, u32[]{:S(2)}, u32[]{:S(2)}) collective-permute-start(bf16[832,1024]{1,0:T(8,128)(2,1)} %get-tuple-element.178.refs_21_.refs_2_.refs_22_.refs_14_), channel_id=1, source_target_pairs={{0,1},{1,0},{2,3},{3,2},{4,5},{5,4},{6,7},{7,6},{8,9},{9,8},{10,11... | collective-permute-start | bytes 5111816 | tf_op jit(solution)/shard_map/swap/ppermute | solution.py:922
  227.7 42.7 %collective-permute-start.37 = (bf16[1152,1024]{1,0:T(8,128)(2,1)}, bf16[1152,1024]{1,0:T(8,128)(2,1)}, u32[]{:S(2)}, u32[]{:S(2)}) collective-permute-start(bf16[1152,1024]{1,0:T(8,128)(2,1)} %all-gather.2.cloned.1.call-done.refs_16_.refs_4_), channel_id=1, source_target_pairs={{0,1},{1,0},{2,3},{3,2},{4,5},{5,4},{6,7},{7,6},{8,9},{9,8},{10,11... | collective-permute-start | bytes 7077896 | tf_op jit(solution)/shard_map/swap/ppermute | solution.py:922
  240.5 27.2 %collective-permute-start.38 = (bf16[576,1024]{1,0:T(8,128)(2,1)S(1)}, bf16[576,1024]{1,0:T(8,128)(2,1)S(1)}, u32[]{:S(2)}, u32[]{:S(2)}) collective-permute-start(bf16[576,1024]{1,0:T(8,128)(2,1)S(1)} %slice.186), channel_id=1, source_target_pairs={{0,2},{2,0},{4,6},{6,4},{8,10},{10,8},{12,14},{14,12},{16,18},{18,... | collective-permute-start | bytes 3538952 | tf_op jit(solution)/shard_map/four_plane/ppermute | solution.py:912
  242.3 25.0 %collective-permute-start.43 = (bf16[512,1024]{1,0:T(8,128)(2,1)}, bf16[512,1024]{1,0:T(8,128)(2,1)}, u32[]{:S(2)}, u32[]{:S(2)}) collective-permute-start(bf16[512,1024]{1,0:T(8,128)(2,1)} %collective-permute-done.32.refs_2_), channel_id=1, source_target_pairs={{0,8},{2,10},{4,12},{6,14},{8,24},{10,26},{12,28},{14,30},{24,16},... | collective-permute-start | bytes 3145736 | tf_op jit(solution)/shard_map/top_line/ppermute | solution.py:919
  243.7 26.6 %collective-permute-start.40 = (bf16[576,1024]{1,0:T(8,128)(2,1)S(1)}, bf16[576,1024]{1,0:T(8,128)(2,1)S(1)}, u32[]{:S(2)}, u32[]{:S(2)}) collective-permute-start(bf16[576,1024]{1,0:T(8,128)(2,1)S(1)} %slice.187), channel_id=1, source_target_pairs={{0,4},{2,6},{4,0},{6,2},{8,12},{10,14},{12,8},{14,10},{16,20},{18,... | collective-permute-start | bytes 3538952 | tf_op jit(solution)/shard_map/four_plane/ppermute | solution.py:912
  244.1 58.8 %collective-permute-start.42 = (bf16[3,576,1024]{2,1,0:T(8,128)(2,1)S(1)}, bf16[3,576,1024]{2,1,0:T(8,128)(2,1)}, u32[]{:S(2)}, u32[]{:S(2)}) collective-permute-start(bf16[3,576,1024]{2,1,0:T(8,128)(2,1)S(1)} %copy-done.1), channel_id=1, source_target_pairs={{0,1},{1,0},{2,3},{3,2},{4,5},{5,4},{6,7},{7,6},{8,9},{9,8},{10,11... | collective-permute-start | bytes 10616840 | tf_op jit(solution)/shard_map/ppermute | solution.py:922
  267.3 11.3 %collective-permute-start.35 = (bf16[1152,1024]{1,0:T(8,128)(2,1)}, bf16[1152,1024]{1,0:T(8,128)(2,1)}, u32[]{:S(2)}, u32[]{:S(2)}) collective-permute-start(bf16[1152,1024]{1,0:T(8,128)(2,1)} %collective-permute-done.33.refs_12_.refs_0_), channel_id=1, source_target_pairs={{0,1},{1,0},{2,3},{3,2},{4,5},{5,4},{6,7},{7,6},{8,9},{9,8},{10,11... | collective-permute-start | bytes 7077896 | tf_op jit(solution)/shard_map/swap/ppermute | solution.py:922
  267.8 11.9 %collective-permute-start.36 = (bf16[1152,1024]{1,0:T(8,128)(2,1)}, bf16[1152,1024]{1,0:T(8,128)(2,1)}, u32[]{:S(2)}, u32[]{:S(2)}) collective-permute-start(bf16[1152,1024]{1,0:T(8,128)(2,1)} %collective-permute-done.34.refs_14_.refs_2_), channel_id=1, source_target_pairs={{0,1},{1,0},{2,3},{3,2},{4,5},{5,4},{6,7},{7,6},{8,9},{9,8},{10,11... | collective-permute-start | bytes 7077896 | tf_op jit(solution)/shard_map/swap/ppermute | solution.py:922
  275.2 26.7 %collective-permute-start.44 = (bf16[512,1024]{1,0:T(8,128)(2,1)}, bf16[512,1024]{1,0:T(8,128)(2,1)}, u32[]{:S(2)}, u32[]{:S(2)}) collective-permute-start(bf16[512,1024]{1,0:T(8,128)(2,1)} %collective-permute-done.43.refs_4_), channel_id=1, source_target_pairs={{0,8},{2,10},{4,12},{6,14},{8,24},{10,26},{12,28},{14,30},{24,16},... | collective-permute-start | bytes 3145736 | tf_op jit(solution)/shard_map/top_line/ppermute | solution.py:919
  302.4 10.1 %collective-permute-start.48 = (bf16[512,1024]{1,0:T(8,128)(2,1)}, bf16[512,1024]{1,0:T(8,128)(2,1)}, u32[]{:S(2)}, u32[]{:S(2)}) collective-permute-start(bf16[512,1024]{1,0:T(8,128)(2,1)} %collective-permute-done.44.refs_6_), channel_id=1, source_target_pairs={{0,1},{1,0},{2,3},{3,2},{4,5},{5,4},{6,7},{7,6},{8,9},{9,8},{10,11... | collective-permute-start | bytes 3145736 | tf_op jit(solution)/shard_map/ppermute | solution.py:922
  302.9 36.4 %collective-permute-start.52 = (bf16[4,144,1024]{2,1,0:T(8,128)(2,1)}, bf16[4,144,1024]{2,1,0:T(8,128)(2,1)S(1)}, u32[]{:S(2)}, u32[]{:S(2)}) collective-permute-start(bf16[4,144,1024]{2,1,0:T(8,128)(2,1)} %get-tuple-element.193.lefts_ref.refs_0_.refs_4_.refs_8_), channel_id=1, source_target_pairs={{0,1},{1,0},{2,3},{3,2},{4,5},{5,4},{6,7},{7,6},{8,9},{9,8},{10,11... | collective-permute-start | bytes 3538952 | tf_op jit(solution)/shard_map/ppermute | solution.py:922
  304.8 22.8 %collective-permute-start.49 = (bf16[144,1024]{1,0:T(8,128)(2,1)S(1)}, bf16[144,1024]{1,0:T(8,128)(2,1)S(1)}, u32[]{:S(2)}, u32[]{:S(2)}) collective-permute-start(bf16[144,1024]{1,0:T(8,128)(2,1)S(1)} %slice_bitcast_fusion.8), channel_id=1, source_target_pairs={{0,2},{2,0},{4,6},{6,4},{8,10},{10,8},{12,14},{14,12},{16,18},{18,... | collective-permute-start | bytes 884744 | tf_op jit(solution)/shard_map/spread/ppermute | solution.py:912
  307.8 19.9 %collective-permute-start.50 = (bf16[144,1024]{1,0:T(8,128)(2,1)S(1)}, bf16[144,1024]{1,0:T(8,128)(2,1)S(1)}, u32[]{:S(2)}, u32[]{:S(2)}) collective-permute-start(bf16[144,1024]{1,0:T(8,128)(2,1)S(1)} %slice_bitcast_fusion.8), channel_id=1, source_target_pairs={{0,4},{2,6},{4,0},{6,2},{8,12},{10,14},{12,8},{14,10},{16,20},{18,... | collective-permute-start | bytes 884744 | tf_op jit(solution)/shard_map/spread/ppermute | solution.py:912
  309.3 18.4 %collective-permute-start.51 = (bf16[144,1024]{1,0:T(8,128)(2,1)S(1)}, bf16[144,1024]{1,0:T(8,128)(2,1)S(1)}, u32[]{:S(2)}, u32[]{:S(2)}) collective-permute-start(bf16[144,1024]{1,0:T(8,128)(2,1)S(1)} %slice_bitcast_fusion.8), channel_id=1, source_target_pairs={{0,6},{2,4},{4,2},{6,0},{8,14},{10,12},{12,10},{14,8},{16,22},{18,... | collective-permute-start | bytes 884744 | tf_op jit(solution)/shard_map/spread/ppermute | solution.py:912
  335.7 11.8 %collective-permute-start.54 = (bf16[144,1024]{1,0:T(8,128)(2,1)S(1)}, bf16[144,1024]{1,0:T(8,128)(2,1)S(1)}, u32[]{:S(2)}, u32[]{:S(2)}) collective-permute-start(bf16[144,1024]{1,0:T(8,128)(2,1)S(1)} %slice_bitcast_fusion.7), channel_id=1, source_target_pairs={{0,2},{2,0},{4,6},{6,4},{8,10},{10,8},{12,14},{14,12},{16,18},{18,... | collective-permute-start | bytes 884744 | tf_op jit(solution)/shard_map/spread/ppermute | solution.py:912
  337.2 15.4 %collective-permute-start.55 = (bf16[144,1024]{1,0:T(8,128)(2,1)S(1)}, bf16[144,1024]{1,0:T(8,128)(2,1)S(1)}, u32[]{:S(2)}, u32[]{:S(2)}) collective-permute-start(bf16[144,1024]{1,0:T(8,128)(2,1)S(1)} %slice_bitcast_fusion.7), channel_id=1, source_target_pairs={{0,4},{2,6},{4,0},{6,2},{8,12},{10,14},{12,8},{14,10},{16,20},{18,... | collective-permute-start | bytes 884744 | tf_op jit(solution)/shard_map/spread/ppermute | solution.py:912
  338.7 13.9 %collective-permute-start.56 = (bf16[144,1024]{1,0:T(8,128)(2,1)S(1)}, bf16[144,1024]{1,0:T(8,128)(2,1)S(1)}, u32[]{:S(2)}, u32[]{:S(2)}) collective-permute-start(bf16[144,1024]{1,0:T(8,128)(2,1)S(1)} %slice_bitcast_fusion.7), channel_id=1, source_target_pairs={{0,6},{2,4},{4,2},{6,0},{8,14},{10,12},{12,10},{14,8},{16,22},{18,... | collective-permute-start | bytes 884744 | tf_op jit(solution)/shard_map/spread/ppermute | solution.py:912
  339.3 13.3 %collective-permute-start.57 = (bf16[2,144,512]{2,1,0:T(8,128)(2,1)}, bf16[2,144,512]{2,1,0:T(8,128)(2,1)S(1)}, u32[]{:S(2)}, u32[]{:S(2)}) collective-permute-start(bf16[2,144,512]{2,1,0:T(8,128)(2,1)} %get-tuple-element.232), channel_id=1, source_target_pairs={{0,1},{1,0},{2,3},{3,2},{4,5},{5,4},{6,7},{7,6},{8,9},{9,8},{10,11... | collective-permute-start | bytes 884744 | tf_op jit(solution)/shard_map/ppermute | solution.py:922
  352.6 43.8 %collective-permute-start.58 = (bf16[4,64,2048]{2,1,0:T(8,128)(2,1)}, bf16[4,64,2048]{2,1,0:T(8,128)(2,1)S(1)}, u32[]{:S(2)}, u32[]{:S(2)}) collective-permute-start(bf16[4,64,2048]{2,1,0:T(8,128)(2,1)} %get-tuple-element.233), channel_id=1, source_target_pairs={{0,2},{2,0},{4,6},{6,4},{8,10},{10,8},{12,14},{14,12},{16,18},{18,... | collective-permute-start | bytes 3145736 | tf_op jit(solution)/shard_map/readout_across/ppermute | solution.py:912
  353.9 42.5 %collective-permute-start.59 = (bf16[4,64,2048]{2,1,0:T(8,128)(2,1)}, bf16[4,64,2048]{2,1,0:T(8,128)(2,1)S(1)}, u32[]{:S(2)}, u32[]{:S(2)}) collective-permute-start(bf16[4,64,2048]{2,1,0:T(8,128)(2,1)} %get-tuple-element.234), channel_id=1, source_target_pairs={{0,4},{2,6},{4,0},{6,2},{8,12},{10,14},{12,8},{14,10},{16,20},{18,... | collective-permute-start | bytes 3145736 | tf_op jit(solution)/shard_map/readout_across/ppermute | solution.py:912
  399.1 33.7 %collective-permute-start.63 = (bf16[576,1024]{1,0:T(8,128)(2,1)S(1)}, bf16[576,1024]{1,0:T(8,128)(2,1)}, u32[]{:S(2)}, u32[]{:S(2)}) collective-permute-start(bf16[576,1024]{1,0:T(8,128)(2,1)S(1)} %constant_dynamic-update-slice_fusion.44.refs_2_), channel_id=1, source_target_pairs={{0,1},{1,0},{2,3},{3,2},{4,5},{5,4},{6,7},{7,6},{8,9},{9,8},{10,11... | collective-permute-start | bytes 3538952 | tf_op jit(solution)/shard_map/spread_swap/ppermute | solution.py:922
  400.7 32.1 %collective-permute-start.64 = (bf16[576,1024]{1,0:T(8,128)(2,1)S(1)}, bf16[576,1024]{1,0:T(8,128)(2,1)}, u32[]{:S(2)}, u32[]{:S(2)}) collective-permute-start(bf16[576,1024]{1,0:T(8,128)(2,1)S(1)} %constant_dynamic-update-slice_fusion.40.refs_0_), channel_id=1, source_target_pairs={{0,1},{1,0},{2,3},{3,2},{4,5},{5,4},{6,7},{7,6},{8,9},{9,8},{10,11... | collective-permute-start | bytes 3538952 | tf_op jit(solution)/shard_map/spread_swap/ppermute | solution.py:922
  401.1 31.8 %collective-permute-start.60 = (bf16[2,64,2048]{2,1,0:T(8,128)(2,1)}, bf16[2,64,2048]{2,1,0:T(8,128)(2,1)S(1)}, u32[]{:S(2)}, u32[]{:S(2)}) collective-permute-start(bf16[2,64,2048]{2,1,0:T(8,128)(2,1)} %add_convert_fusion.8), channel_id=1, source_target_pairs={{0,2},{2,0},{4,6},{6,4},{8,10},{10,8},{12,14},{14,12},{16,18},{18,... | collective-permute-start | bytes 1572872 | tf_op jit(solution)/shard_map/readout_onward/ppermute | solution.py:912
  402.5 30.3 %collective-permute-start.61 = (bf16[2,64,2048]{2,1,0:T(8,128)(2,1)}, bf16[2,64,2048]{2,1,0:T(8,128)(2,1)}, u32[]{:S(2)}, u32[]{:S(2)}) collective-permute-start(bf16[2,64,2048]{2,1,0:T(8,128)(2,1)} %add_convert_fusion.7), channel_id=1, source_target_pairs={{0,4},{2,6},{4,0},{6,2},{8,12},{10,14},{12,8},{14,10},{16,20},{18,... | collective-permute-start | bytes 1572872 | tf_op jit(solution)/shard_map/readout_onward/ppermute | solution.py:912
  436.2 53.5 %collective-permute-start.65 = (bf16[4,576,512]{2,1,0:T(8,128)(2,1)}, bf16[4,576,512]{2,1,0:T(8,128)(2,1)S(1)}, u32[]{:S(2)}, u32[]{:S(2)}) collective-permute-start(bf16[4,576,512]{2,1,0:T(8,128)(2,1)} %get-tuple-element.274), channel_id=1, source_target_pairs={{0,2},{2,0},{4,6},{6,4},{8,10},{10,8},{12,14},{14,12},{16,18},{18,... | collective-permute-start | bytes 7077896 | tf_op jit(solution)/shard_map/middle_0_across/ppermute | solution.py:912
  437.6 53.3 %collective-permute-start.66 = (bf16[4,576,512]{2,1,0:T(8,128)(2,1)}, bf16[4,576,512]{2,1,0:T(8,128)(2,1)}, u32[]{:S(2)}, u32[]{:S(2)}) collective-permute-start(bf16[4,576,512]{2,1,0:T(8,128)(2,1)} %get-tuple-element.275), channel_id=1, source_target_pairs={{0,4},{2,6},{4,0},{6,2},{8,12},{10,14},{12,8},{14,10},{16,20},{18,... | collective-permute-start | bytes 7077896 | tf_op jit(solution)/shard_map/middle_0_across/ppermute | solution.py:912
  440.7 153.8 %reduce-scatter.5.cloned.1.call-start = ((), (), s32[]{:S(2)}) async-start(), calls=%async_computation.4 | async-start | bytes 2949120 | tf_op jit(solution)/shard_map/middle_1_levels/reduce_scatter | solution.py:1415
  495.0 27.1 %collective-permute-start.70 = (bf16[2,576,512]{2,1,0:T(8,128)(2,1)}, bf16[2,576,512]{2,1,0:T(8,128)(2,1)S(1)}, u32[]{:S(2)}, u32[]{:S(2)}) collective-permute-start(bf16[2,576,512]{2,1,0:T(8,128)(2,1)} %add_convert_fusion.1), channel_id=1, source_target_pairs={{0,2},{2,0},{4,6},{6,4},{8,10},{10,8},{12,14},{14,12},{16,18},{18,... | collective-permute-start | bytes 3538952 | tf_op jit(solution)/shard_map/middle_0_onward/ppermute | solution.py:912
  496.3 26.8 %collective-permute-start.71 = (bf16[2,576,512]{2,1,0:T(8,128)(2,1)}, bf16[2,576,512]{2,1,0:T(8,128)(2,1)S(1)}, u32[]{:S(2)}, u32[]{:S(2)}) collective-permute-start(bf16[2,576,512]{2,1,0:T(8,128)(2,1)} %add_convert_fusion), channel_id=1, source_target_pairs={{0,4},{2,6},{4,0},{6,2},{8,12},{10,14},{12,8},{14,10},{16,20},{18,... | collective-permute-start | bytes 3538952 | tf_op jit(solution)/shard_map/middle_0_onward/ppermute | solution.py:912
  530.1 28.9 %collective-permute-start.72 = (bf16[4,320,512]{2,1,0:T(8,128)(2,1)}, bf16[4,320,512]{2,1,0:T(8,128)(2,1)}, u32[]{:S(2)}, u32[]{:S(2)}) collective-permute-start(bf16[4,320,512]{2,1,0:T(8,128)(2,1)} %get-tuple-element.295), channel_id=1, source_target_pairs={{0,2},{2,0},{4,6},{6,4},{8,10},{10,8},{12,14},{14,12},{16,18},{18,... | collective-permute-start | bytes 3932168 | tf_op jit(solution)/shard_map/last_across/ppermute | solution.py:912
  530.8 28.6 %collective-permute-start.73 = (bf16[4,320,512]{2,1,0:T(8,128)(2,1)}, bf16[4,320,512]{2,1,0:T(8,128)(2,1)}, u32[]{:S(2)}, u32[]{:S(2)}) collective-permute-start(bf16[4,320,512]{2,1,0:T(8,128)(2,1)} %get-tuple-element.296), channel_id=1, source_target_pairs={{0,4},{2,6},{4,0},{6,2},{8,12},{10,14},{12,8},{14,10},{16,20},{18,... | collective-permute-start | bytes 3932168 | tf_op jit(solution)/shard_map/last_across/ppermute | solution.py:912
  532.0 23.5 %collective-permute-start.79 = (bf16[576,512]{1,0:T(8,128)(2,1)}, bf16[576,512]{1,0:T(8,128)(2,1)}, u32[]{:S(2)}, u32[]{:S(2)}) collective-permute-start(bf16[576,512]{1,0:T(8,128)(2,1)} %fusion.8), channel_id=1, source_target_pairs={{0,8},{2,10},{4,12},{6,14},{8,24},{10,26},{12,28},{14,30},{24,16},... | collective-permute-start | bytes 1769480 | tf_op jit(solution)/shard_map/middle_0_line/ppermute | solution.py:919
  557.2 15.4 %collective-permute-start.80 = (bf16[576,512]{1,0:T(8,128)(2,1)S(1)}, bf16[576,512]{1,0:T(8,128)(2,1)S(1)}, u32[]{:S(2)}, u32[]{:S(2)}) collective-permute-start(bf16[576,512]{1,0:T(8,128)(2,1)S(1)} %add_convert_fusion.4), channel_id=1, source_target_pairs={{0,8},{2,10},{4,12},{6,14},{8,24},{10,26},{12,28},{14,30},{24,16},... | collective-permute-start | bytes 1769480 | tf_op jit(solution)/shard_map/middle_0_line/ppermute | solution.py:919
  560.6 13.9 %collective-permute-start.75 = (bf16[2,320,512]{2,1,0:T(8,128)(2,1)S(1)}, bf16[2,320,512]{2,1,0:T(8,128)(2,1)S(1)}, u32[]{:S(2)}, u32[]{:S(2)}) collective-permute-start(bf16[2,320,512]{2,1,0:T(8,128)(2,1)S(1)} %add_convert_fusion.3), channel_id=1, source_target_pairs={{0,4},{2,6},{4,0},{6,2},{8,12},{10,14},{12,8},{14,10},{16,20},{18,... | collective-permute-start | bytes 1966088 | tf_op jit(solution)/shard_map/last_onward/ppermute | solution.py:912
  563.6 13.5 %collective-permute-start.76 = (bf16[2,320,512]{2,1,0:T(8,128)(2,1)S(1)}, bf16[2,320,512]{2,1,0:T(8,128)(2,1)S(1)}, u32[]{:S(2)}, u32[]{:S(2)}) collective-permute-start(bf16[2,320,512]{2,1,0:T(8,128)(2,1)S(1)} %add_convert_fusion.2), channel_id=1, source_target_pairs={{0,2},{2,0},{4,6},{6,4},{8,10},{10,8},{12,14},{14,12},{16,18},{18,... | collective-permute-start | bytes 1966088 | tf_op jit(solution)/shard_map/last_onward/ppermute | solution.py:912
  572.8 17.2 %collective-permute-start.81 = (bf16[576,512]{1,0:T(8,128)(2,1)S(1)}, bf16[576,512]{1,0:T(8,128)(2,1)S(1)}, u32[]{:S(2)}, u32[]{:S(2)}) collective-permute-start(bf16[576,512]{1,0:T(8,128)(2,1)S(1)} %fusion.1), channel_id=1, source_target_pairs={{0,8},{2,10},{4,12},{6,14},{8,24},{10,26},{12,28},{14,30},{24,16},... | collective-permute-start | bytes 1769480 | tf_op jit(solution)/shard_map/middle_0_line/ppermute | solution.py:919
  579.9 14.3 %collective-permute-start.77 = (bf16[320,512]{1,0:T(8,128)(2,1)S(1)}, bf16[320,512]{1,0:T(8,128)(2,1)S(1)}, u32[]{:S(2)}, u32[]{:S(2)}) collective-permute-start(bf16[320,512]{1,0:T(8,128)(2,1)S(1)} %fusion.9), channel_id=1, source_target_pairs={{0,8},{2,10},{4,12},{6,14},{8,24},{10,26},{12,28},{14,30},{24,16},... | collective-permute-start | bytes 983048 | tf_op jit(solution)/shard_map/last_line/ppermute | solution.py:919
  (92 other events, 1002.5 us)
Sparse Core Ops, SparseCore 0:
  114.9 58.5 all-gather.1
  440.8 25.2 reduce-scatter.2
  497.4 55.4 reduce-scatter.4

commit v5 on v4

--- a/solution.py
+++ b/solution.py
@@ -586,15 +586,13 @@
 
                 lax.fori_loop(0, C // 128, spread, 0)
                 lax.fori_loop(0, width // 128, shift, 0)
-            for row_tap in range(3):
-
-                def part(i, carry, row_tap=row_tap):
-                    cut = pl.ds(pl.multiple_of(i * size, size), size)
-                    target = pl.ds(pl.multiple_of(row_tap * 3 * C + i * size, size), size)
-                    grad[target, :] = low(dot_sums(taps[:, cut], shifted[row_tap]))
-                    return carry
-
-                lax.fori_loop(0, 3 * C // size, part, 0)
+            def part(i, carry):
+                cut = pl.ds(pl.multiple_of(lax.rem(i, 3 * C // size) * size, size), size)
+                target = pl.ds(pl.multiple_of(i * size, size), size)
+                grad[target, :] = low(dot_sums(taps[:, cut], shifted[i // (3 * C // size)]))
+                return carry
+
+            lax.fori_loop(0, 9 * C // size, part, 0)
         for number, (copies, left, right) in enumerate(waits):
             if middle is not None and number == 0:
                 continue
@@ -875,11 +873,11 @@
                 side[:, part * SIDE : (part + 1) * SIDE] = mine_ref[4, :, :SIDE]
                 side[:, (1 - part) * SIDE : (2 - part) * SIDE] = other_ref[4, :, :SIDE]
 
+        pos[...] = side[:, :cells]
         turned = jnp.transpose(side[...])
-        pos[...] = turned[:cells]
         for number in range(6):
-            gains[number // 3, number % 3 : number % 3 + 1, :] = turned[cells + number : cells + number + 1]
-            biases[number // 3, number % 3 : number % 3 + 1, :] = turned[cells + 6 + number : cells + 7 + number]
+            gains[number % 3, number // 3 : number // 3 + 1, :] = turned[cells + number : cells + number + 1]
+            biases[number % 3, number // 3 : number // 3 + 1, :] = turned[cells + 6 + number : cells + 7 + number]
         bias[...] = turned[cells + 12 : cells + MISC]
 
     return call(
@@ -887,7 +885,7 @@
         "place_last",
         [core, mine, other],
         [SMEM, IN, IN],
-        [shaped(2, rows, 2 * half)] * 2 + [shaped(cells, rows)] + [shaped(2, 3, rows)] * 2 + [shaped(4, rows)],
+        [shaped(2, rows, 2 * half)] * 2 + [shaped(rows, cells)] + [shaped(3, 2, rows)] * 2 + [shaped(4, rows)],
         [IN] * 6,
         [pltpu.VMEM((rows, 2 * SIDE), jnp.float32)],
         0,
@@ -977,11 +975,11 @@
             for core, held in enumerate((array, other)):
                 self.found.append((held, first + i * self.rows, self.at + 16 * core + 4 * far + step))
 
-    def line(self, second, third):
+    def line(self, second=(), third=(), first=()):
         with jax.named_scope(self.name + "_line"):
-            one = self.move.along(self.own)
+            one = self.move.along(after(self.own, *first) if first else self.own)
             two = self.move.along(after(one, *second) if second else one)
-            three = self.move.along(after(two, *third))
+            three = self.move.along(after(two, *third) if third else two)
         self.passed = (one, two, three)
         self.held = jnp.concatenate([self.own, one, two, three])
 
@@ -996,10 +994,11 @@
             other = self.move.swap(after(self.held, *earlier) if earlier else self.held)
         self.keep(self.held, 0, range(4), other=other)
 
-    def plane_first(self):
+    def plane_first(self, *earlier):
         half = self.rows // 2
+        own = after(self.own, *earlier) if earlier else self.own
         with jax.named_scope(self.name + "_plane"):
-            first, second = self.sides = self.move.flip(self.own, 1), self.move.flip(self.own, 2)
+            first, second = self.sides = self.move.flip(own, 1), self.move.flip(own, 2)
             self.fars = (self.move.flip(first[:half], 2), self.move.flip(second[half:], 1))
             self.passed = (jnp.concatenate([self.own, first, second, *self.fars]),)
 
@@ -1218,11 +1217,11 @@
             Piece(move, jnp.concatenate(stack) if len(stack) > 1 else stack[0], name)
             for stack, name in zip(stacks, ("one", "two", "three", "four", "top"))
         ]
-        top.plane_first()
-        one.line((), top.sides)
+        one.line()
+        top.plane_first(one.passed[0])
         two.line(one.passed[1:2], one.passed[2:])
         three.line(two.passed[1:2], two.passed[2:])
-        four.levels(three.passed[1])
+        four.line(first=three.passed[2:])
         cross(move, [one], [], *top.fars)
         cross(move, [two], [one], one.first)
         one.settle_line(one.first)
@@ -1230,13 +1229,13 @@
         cross(move, [three], [two], two.first)
         two.settle_line(two.first)
         settle(move, [two], [one], two.first)
-        top.pass_on(two.first)
-        cross(move, [], [three], three.first)
+        top.pass_on(four.passed[1])
+        cross(move, [], [three], three.first, four.passed[2])
         three.settle_line(three.first)
         settle(move, [three], [two], three.first)
-        cross(move, [four], [], three.far_first, top.passed[1])
+        cross(move, [four], [], three.far_first)
         top.pass_on(three.far_first)
-        settle(move, [], [three], three.far_first)
+        settle(move, [], [three], three.far_first, top.passed[1])
         lies = {
             "head_0": [(one, 0, rows, 0, 0, C), (one, rows, rows, 0, C, HEAD - C)],
             "middle_0": [(two, 0, cut, 0, 0, C), (three, 0, cut, cut, 0, C)],
@@ -1323,18 +1322,19 @@
     lefts_other_0 = swap(lefts_0)
     if paired:
         settle(move, [four], [], pooled)
-        cross(move, [], [four])
+        cross(move, [], [four], top.passed[2])
         top.pass_on(pooled)
         four.settle_line(pooled)
         settle(move, [], [four])
     first_1, mid_1, last_1 = matrix("first_1"), matrix("middle_1"), matrix("last_1")
+    if paired:
+        top.end_line(pooled)
+        pooled = tie(pooled, top.passed[3])
     lefts_1, pre1_1, pre2_1, pre3_1, first_1, last_1 = forward_block(
         table, 1, half_side, pooled, None, misc, first_1, mid_1, last_1
     )
     first_0, last_0, first_1, last_1 = [whole_matrix(array) for array in (first_0, last_0, first_1, last_1)]
     lefts_other_1 = swap(lefts_1)
-    if paired:
-        top.end_line(lefts_1)
     readout_bias = misc[12:].T.reshape(1, width)
     output, grad_top, grad_readout_b, grad_logits, grad_logits_other = readout(
         table, grid_live, tie(lefts_1, lefts_other_0), readout_bias, cotangent[0], matrix("readout")
@@ -1413,7 +1413,7 @@
         sum_middle_0.onward(*waited)
         with jax.named_scope("middle_1_levels"):
             owned_1 = lax.psum_scatter(
-                after(middle_terms_1, *waited).reshape(-1, C),
+                middle_terms_1.reshape(-1, C),
                 "dp",
                 axis_index_groups=move.lines(),
                 scatter_dimension=0,
@@ -1449,6 +1449,8 @@
         sum_last.finish(middle_owned)
         first_grad, last_grad, pos_grad, gain_grad, bias_grad, readout_grad = place_last(core, *halves(move, sum_last.owned, 5), cells)
         readout_grad = readout_grad.T
+        pos_grad = pos_grad.T
+        gain_grad, bias_grad = jnp.swapaxes(gain_grad, 0, 1), jnp.swapaxes(bias_grad, 0, 1)
     else:
         readout_owned = scattered(readout_terms)[0]
         middle_owned = jnp.concatenate([scattered(terms) for terms in (crossed_terms, middle_terms_1)])

time: 638 us -> 611 us (0.958)
  local copies, waits for them, and re-layouts: 62.9 us -> 43.5 us
    unnamed x167 -> x150, local copies, waits for them, and re-layouts: 37.5 us -> 22.7 us
    ppermute x33, waiting for transfers between devices: 34.7 us -> 21.1 us  [swap(): return lax.ppermute(value, 'fsdp', [(0, 1), (1, 0)])]
    ppermute x18 -> x21, waiting for transfers between devices: 140 us -> 152 us  [along(): return lax.ppermute(value, 'dp', pairs)]
    ppermute x18 -> x21, starting transfers between devices: 18.4 us -> 16.6 us  [along(): return lax.ppermute(value, 'dp', pairs)]
  transfers between devices with their start and end apart: 88 -> 90, of which waited for: 44 -> 47; matrix products, arithmetic and copies ran while one was open for 8% -> 7% of each run, Pallas kernels for 33% -> 34%
where the time goes in v5:
time: 611 us; the launch traced here: 601 us
  waiting for transfers between devices  249 us (41%)
  Pallas kernels  208 us (34%)
  starting transfers between devices  60.7 us (10%)
  local copies, waits for them, and re-layouts  43.5 us (7%)
  other arithmetic  23.9 us (4%)
  between operations  16.2 us (3%)
    pallas_call x14, Pallas kernels, call(): pl.pallas_call(kernel, name=name, out_shape=outs, in_specs=in_specs, out_...  208 us
    ppermute x21, waiting for transfers between devices, along(): return lax.ppermute(value, 'dp', pairs)  152 us
    ppermute x34, waiting for transfers between devices, flip(): return lax.ppermute(value, 'dp', [(i, i ^ bits) for i in range(self.dp)])  76.1 us
    ppermute x34, starting transfers between devices, flip(): return lax.ppermute(value, 'dp', [(i, i ^ bits) for i in range(self.dp)])  38.8 us
    unnamed x150, local copies, waits for them, and re-layouts  22.7 us
    ppermute x33, waiting for transfers between devices, swap(): return lax.ppermute(value, 'fsdp', [(0, 1), (1, 0)])  21.1 us
    ppermute x21, starting transfers between devices, along(): return lax.ppermute(value, 'dp', pairs)  16.6 us
    convert_element_type x11, other arithmetic, low(): return value.astype(jnp.bfloat16)  12.6 us
  transfers between devices with their start and end apart: 90, of which 47 were waited for; matrix products, arithmetic and copies ran while one was open for 7% of the time, Pallas kernels for 34%

profile of v5, /device:TPU:0, one launch (start us, length us, event | category | flops | bytes accessed | tf_op | source)
XLA Modules:
  0.0 601.0 jit_solution(5090117770710470878)
XLA Ops:
  11.6 3.1 collective-permute-start
  15.8 2.6 collective-permute-start.12
  21.5 1.9 collective-permute-start.3
  25.7 5.8 collective-permute-done.1
  33.7 1.6 collective-permute-start.6
  35.2 2.8 collective-permute-done.2
  40.2 3.4 collective-permute-start.13
  44.2 4.5 collective-permute-done.13
  48.7 2.5 collective-permute-start.14
  51.3 5.1 collective-permute-done.14
  56.6 3.9 collective-permute-done.9.refs_5_.refs_31_
  62.7 9.1 %collective-permute-done.20 = bf16[208,1024]{1,0:T(8,128)(2,1)S(1)} collective-permute-done((bf16[208,1024]{1,0:T(8,128)(2,1)S(1)}, bf16[208,1024]{1,0:T(8,128)(2,1)S(1)}, u32[]{:S(2)}, u32[]{:S(2)}) %collective-permute-start.20) | collective-permute-done | bytes 426016 | tf_op jit(solution)/shard_map/three_line/ppermute | solution.py:917
  71.9 11.9 %collective-permute-done.21 = bf16[208,1024]{1,0:T(8,128)(2,1)S(1)} collective-permute-done((bf16[208,1024]{1,0:T(8,128)(2,1)S(1)}, bf16[208,1024]{1,0:T(8,128)(2,1)S(1)}, u32[]{:S(2)}, u32[]{:S(2)}) %collective-permute-start.21) | collective-permute-done | bytes 426016 | tf_op jit(solution)/shard_map/three_line/ppermute | solution.py:917
  84.0 8.9 %collective-permute-done.22 = bf16[208,1024]{1,0:T(8,128)(2,1)S(1)} collective-permute-done((bf16[208,1024]{1,0:T(8,128)(2,1)S(1)}, bf16[208,1024]{1,0:T(8,128)(2,1)S(1)}, u32[]{:S(2)}, u32[]{:S(2)}) %collective-permute-start.22) | collective-permute-done | bytes 426016 | tf_op jit(solution)/shard_map/three_line/ppermute | solution.py:917
  93.4 1.6 collective-permute-done.16.refs_9_.refs_15_.refs_35_.refs_8_
  96.5 2.3 collective-permute-start.24
  98.9 16.0 %collective-permute-done.28 = bf16[288,1024]{1,0:T(8,128)(2,1)S(1)} collective-permute-done((bf16[288,1024]{1,0:T(8,128)(2,1)S(1)}, bf16[288,1024]{1,0:T(8,128)(2,1)S(1)}, u32[]{:S(2)}, u32[]{:S(2)}) %collective-permute-start.28) | collective-permute-done | bytes 589856 | tf_op jit(solution)/shard_map/four_line/ppermute | solution.py:917
  114.9 17.1 %collective-permute-done.29 = bf16[288,1024]{1,0:T(8,128)(2,1)S(1)} collective-permute-done((bf16[288,1024]{1,0:T(8,128)(2,1)S(1)}, bf16[288,1024]{1,0:T(8,128)(2,1)S(1)}, u32[]{:S(2)}, u32[]{:S(2)}) %collective-permute-start.29) | collective-permute-done | bytes 589856 | tf_op jit(solution)/shard_map/four_line/ppermute | solution.py:917
  135.0 7.6 %collective-permute-done.23.refs_17_.refs_4_.refs_24_.refs_10_ = bf16[1120,1024]{1,0:T(8,128)(2,1)S(1)} collective-permute-done((bf16[1120,1024]{1,0:T(8,128)(2,1)S(1)}, bf16[1120,1024]{1,0:T(8,128)(2,1)S(1)}, u32[]{:S(2)}, u32[]{:S(2)}) %collective-permute-start.23) | collective-permute-done | bytes 2293792 | tf_op jit(solution)/shard_map/three_two_plane/ppermute | solution.py:910
  147.0 1.8 collective-permute-start.32
  149.5 15.8 %collective-permute-done.33.refs_2_ = bf16[512,1024]{1,0:T(8,128)(2,1)} collective-permute-done((bf16[512,1024]{1,0:T(8,128)(2,1)}, bf16[512,1024]{1,0:T(8,128)(2,1)}, u32[]{:S(2)}, u32[]{:S(2)}) %collective-permute-start.33) | collective-permute-done | bytes 1048608 | tf_op jit(solution)/shard_map/top_line/ppermute | solution.py:917
  166.0 3.3 collective-permute-done.11.refs_6_.refs_32_
  173.6 1.6 pad_maximum_fusion.refs_16_.refs_4_
  175.3 2.4 collective-permute-done.27.refs_22_.refs_3_.refs_23_.refs_15_
  180.3 2.0 collective-permute-done.26.refs_20_.refs_7_.refs_27_.refs_13_
  182.2 31.0 %forward_block.2 = (f32[16,1024]{1,0:T(8,128)}, f32[144,1024]{1,0:T(8,128)}, f32[576,1024]{1,0:T(8,128)}, bf16[3,576,1024]{2,1,0:T(8,128)(2,1)}, f32[576,1024]{1...) custom-call(s32[165]{0:T(256)} %bitcast.127, ...), custom_call_target="tpu_custom_call" | custom-call | flops 265751104 | bytes 697303 | tf_op jit(solution)/shard_map/forward_block/pallas_call | solution.py:144
  213.4 15.5 %collective-permute-done.38.refs_12_.refs_0_ = bf16[1152,1024]{1,0:T(8,128)(2,1)} collective-permute-done((bf16[1152,1024]{1,0:T(8,128)(2,1)}, bf16[1152,1024]{1,0:T(8,128)(2,1)}, u32[]{:S(2)}, u32[]{:S(2)}) %collective-permute-start.38) | collective-permute-done | bytes 2359328 | tf_op jit(solution)/shard_map/four_plane/ppermute | solution.py:910
  231.9 1.7 collective-permute-start.43
  233.9 6.2 %collective-permute-done.37.refs_6_ = bf16[512,1024]{1,0:T(8,128)(2,1)} collective-permute-done((bf16[512,1024]{1,0:T(8,128)(2,1)}, bf16[512,1024]{1,0:T(8,128)(2,1)}, u32[]{:S(2)}, u32[]{:S(2)}) %collective-permute-start.37) | collective-permute-done | bytes 1048608 | tf_op jit(solution)/shard_map/top_line/ppermute | solution.py:917
  240.1 19.2 %collective-permute-done.43.refs_18_.refs_6_ = bf16[576,1024]{1,0:T(8,128)(2,1)S(1)} collective-permute-done((bf16[576,1024]{1,0:T(8,128)(2,1)S(1)}, bf16[576,1024]{1,0:T(8,128)(2,1)S(1)}, u32[]{:S(2)}, u32[]{:S(2)}) %collective-permute-start.43) | collective-permute-done | bytes 1179680 | tf_op jit(solution)/shard_map/four_plane/ppermute | solution.py:910
  260.8 4.6 collective-permute-done.44.refs_19_.refs_7_
  268.7 16.6 %forward_block.3 = (bf16[4,144,1024]{2,1,0:T(8,128)(2,1)}, f32[144,1024]{1,0:T(8,128)}, f32[144,1024]{1,0:T(8,128)}, f32[144,1024]{1,0:T(8,128)}, bf16[1024,1024...) custom-call(s32[165]{0:T(256)} %bitcast.128, f32[144,1024]{1,0:T(8,128)} %get-tuple-element.191.refs_0_.u_in, ...), custom_call_target="tpu_custom_call" | custom-call | flops 66437776 | bytes 520355 | tf_op jit(solution)/shard_map/forward_block/pallas_call | solution.py:144
  292.7 15.2 %readout.1 = (bf16[144,4096]{1,0:T(8,128)(2,1)}, f32[144,1024]{1,0:T(8,128)}, f32[1,4096]{1,0:T(1,128)}, bf16[144,2048]{1,0:T(8,128)(2,1)}, bf16[144,2048]{1,0:T(8,128)(2,1)}) custom-call(s32[165]{0:T(256)} %bitcast.129, s32[1]{0:T(128)S(6)} %copy.74.live_ref, bf16[4,144,1024]{2,1,0:T(8,128)(2,1)} %get-tuple-element.202.lefts_ref.refs_0_.refs_4_.refs_8_, ...), custom_call_target="tpu_custom_call" | custom-call | flops 603979776 | bytes 2686976 | tf_op jit(solution)/shard_map/readout/pallas_call | solution.py:144
  308.0 6.3 %back_last.2 = (f32[144,1024]{1,0:T(8,128)}, bf16[2,144,1024]{2,1,0:T(8,128)(2,1)}, bf16[2,144,512]{2,1,0:T(8,128)(2,1)}, f32[4,1024]{1,0:T(4,128)}) custom-call(s32[165]{0:T(256)} %bitcast.130, f32[144,1024]{1,0:T(8,128)} %get-tuple-element.209.grad_ref, f32[144,1024]{1,0:T(8,128)} %get-tuple-element.191.refs_0_.u_in, ...), custom_call_target="tpu_custom_call" | custom-call | flops 75497472 | bytes 1409024 | tf_op jit(solution)/shard_map/back_last/pallas_call | solution.py:144
  318.9 7.3 %weight_terms.3 = (bf16[4,64,2048]{2,1,0:T(8,128)(2,1)}, bf16[4,64,2048]{2,1,0:T(8,128)(2,1)}, bf16[2,64,2048]{2,1,0:T(8,128)(2,1)}, bf16[2,64,2048]{2,1,0:T(8,128)(2,1)}, bf16[4,64,2048]{2,1,0:T(8,128)(2,1)}) custom-call(s32[165]{0:T(256)} %bitcast.131, bf16[4,144,1024]{2,1,0:T(8,128)(2,1)} %get-tuple-element.202.lefts_ref.refs_0_.refs_4_.refs_8_, ...), custom_call_target="tpu_custom_call" | custom-call | flops 301989888 | bytes 1343488 | tf_op jit(solution)/shard_map/weight_terms/pallas_call | solution.py:144
  326.2 6.0 collective-permute-done.58
  335.3 17.3 %back_first.2 = (f32[144,1024]{1,0:T(8,128)}, f32[2,1024]{1,0:T(2,128)}, bf16[1,144,1024]{2,1,0:T(8,128)(2,1)}, bf16[144,512]{1,0:T(8,128)(2,1)}) custom-call(s32[165]{0:T(256)} %bitcast.132, bf16[2,144,1024]{2,1,0:T(8,128)(2,1)} %get-tuple-element.228.grads_in.refs_9_, f32[144,1024]{1,0:T(8,128)} %get-tuple-element.229.pre1_in, ...), custom_call_target="tpu_custom_call" | custom-call | flops 754974720 | bytes 6127616 | tf_op jit(solution)/shard_map/back_first/pallas_call | solution.py:144
  352.6 23.2 %back_last.3 = (f32[576,1024]{1,0:T(8,128)}, bf16[2,576,1024]{2,1,0:T(8,128)(2,1)}, bf16[2,576,512]{2,1,0:T(8,128)(2,1)}, f32[4,1024]{1,0:T(4,128)}) custom-call(s32[165]{0:T(256)} %bitcast.133, f32[144,1024]{1,0:T(8,128)} %get-tuple-element.232.grad_ref, f32[576,1024]{1,0:T(8,128)} %get-tuple-element.233.u_in, f32[576,1024]{1,0:T(8,128)} %get-tuple-element.234.pre3_in, ...), custom_call_target="tpu_custom_call" | custom-call | flops 301989888 | bytes 4063232 | tf_op jit(solution)/shard_map/back_last/pallas_call | solution.py:144
  384.9 26.5 %weight_terms.4 = (bf16[4,576,512]{2,1,0:T(8,128)(2,1)}, bf16[4,576,512]{2,1,0:T(8,128)(2,1)}, bf16[2,576,512]{2,1,0:T(8,128)(2,1)}, bf16[2,576,512]{2,1,0:T(8,128)(2,1)}, bf16[4,576,512]{2,1,0:T(8,128)(2,1)}) custom-call(s32[165]{0:T(256)} %bitcast.134, bf16[3,576,1024]{2,1,0:T(8,128)(2,1)} %get-tuple-element.201.refs_0_.refs_12_, ...), custom_call_target="tpu_custom_call" | custom-call | flops 2717908992 | bytes 3538944 | tf_op jit(solution)/shard_map/weight_terms/pallas_call | solution.py:144
  411.5 2.2 add_convert_fusion.6
  419.0 15.0 %plane_terms.1 = bf16[4,288,1024]{2,1,0:T(8,128)(2,1)} custom-call(s32[165]{0:T(256)} %bitcast.135, bf16[576,1024]{1,0:T(8,128)(2,1)} %copy-done.30, bf16[576,1024]{1,0:T(8,128)(2,1)} %collective-permute-done.67.refs_1_, bf16[576,1024]{1,0:T(8,128)(2,1)} %copy-done.29, bf16[576,1024]{1,0:T(8,128)(2,1)} %collective-permute-done.66.refs_3_), custom_call_target="tpu_custom_call" | custom-call | flops 905969664 | bytes 1769472 | tf_op jit(solution)/shard_map/plane_terms/pallas_call | solution.py:144
  434.0 29.0 %back_first.3 = (f32[576,1024]{1,0:T(8,128)}, f32[2,1024]{1,0:T(2,128)}, bf16[1,576,1024]{2,1,0:T(8,128)(2,1)}, bf16[576,512]{1,0:T(8,128)(2,1)}, bf16[1024,384]{1,0:T(8,128)(2,1)}, /*index=5*/bf16[1024,384]{1,0:T(8,128)(2,1)}) custom-call(s32[165]{0:T(256)} %bitcast.136, bf16[2,576,1024]{2,1,0:T(8,128)(2,1)} %get-tuple-element.274.refs_1_.grads_in, ...), custom_call_target="tpu_custom_call" | custom-call | flops 3019898880 | bytes 8781824 | tf_op jit(solution)/shard_map/back_first/pallas_call | solution.py:144
  463.0 4.6 collective-permute-done.68
  470.1 2.7 add_convert_fusion.1
  475.6 3.0 collective-permute-done.70.refs_7_
  479.6 13.7 %weight_terms.5 = (bf16[4,320,512]{2,1,0:T(8,128)(2,1)}, bf16[4,320,512]{2,1,0:T(8,128)(2,1)}, bf16[2,320,512]{2,1,0:T(8,128)(2,1)}, bf16[2,320,512]{2,1,0:T(8,128)(2,1)}, bf16[4,320,512]{2,1,0:T(8,128)(2,1)}) custom-call(s32[165]{0:T(256)} %bitcast.137, bf16[3,576,1024]{2,1,0:T(8,128)(2,1)} %get-tuple-element.201.refs_0_.refs_12_, ...), custom_call_target="tpu_custom_call" | custom-call | flops 754974720 | bytes 3997696 | tf_op jit(solution)/shard_map/weight_terms/pallas_call | solution.py:144
  493.3 6.3 %collective-permute-done.73 = bf16[2,576,512]{2,1,0:T(8,128)(2,1)S(1)} collective-permute-done((bf16[2,576,512]{2,1,0:T(8,128)(2,1)}, bf16[2,576,512]{2,1,0:T(8,128)(2,1)S(1)}, u32[]{:S(2)}, u32[]{:S(2)}) %collective-permute-start.73) | collective-permute-done | bytes 1179680 | tf_op jit(solution)/shard_map/middle_0_onward/ppermute | solution.py:910
  501.4 3.6 convert_add_fusion
  513.6 1.9 place_halves.2
  515.5 16.9 %collective-permute-done.82 = bf16[576,512]{1,0:T(8,128)(2,1)} collective-permute-done((bf16[576,512]{1,0:T(8,128)(2,1)}, bf16[576,512]{1,0:T(8,128)(2,1)}, u32[]{:S(2)}, u32[]{:S(2)}) %collective-permute-start.82) | collective-permute-done | bytes 589856 | tf_op jit(solution)/shard_map/middle_0_line/ppermute | solution.py:917
  532.4 1.6 add_convert_fusion.4
  534.1 2.1 collective-permute-done.75
  542.2 7.1 %collective-permute-done.83 = bf16[576,512]{1,0:T(8,128)(2,1)S(1)} collective-permute-done((bf16[576,512]{1,0:T(8,128)(2,1)S(1)}, bf16[576,512]{1,0:T(8,128)(2,1)S(1)}, u32[]{:S(2)}, u32[]{:S(2)}) %collective-permute-start.83) | collective-permute-done | bytes 589856 | tf_op jit(solution)/shard_map/middle_0_line/ppermute | solution.py:917
  549.6 1.7 collective-permute-done.78
  551.3 2.5 collective-permute-done.79
  553.8 2.9 convert_add_fusion.2
  556.8 1.9 collective-permute-start.80
  558.7 8.1 %collective-permute-done.84 = bf16[576,512]{1,0:T(8,128)(2,1)S(1)} collective-permute-done((bf16[576,512]{1,0:T(8,128)(2,1)S(1)}, bf16[576,512]{1,0:T(8,128)(2,1)S(1)}, u32[]{:S(2)}, u32[]{:S(2)}) %collective-permute-start.84) | collective-permute-done | bytes 589856 | tf_op jit(solution)/shard_map/middle_0_line/ppermute | solution.py:917
  567.9 3.1 collective-permute-done.80
  572.0 3.1 place_halves.3
  575.1 4.0 collective-permute-done.81
  579.3 8.0 %collective-permute-done.86 = bf16[320,512]{1,0:T(8,128)(2,1)S(1)} collective-permute-done((bf16[320,512]{1,0:T(8,128)(2,1)S(1)}, bf16[320,512]{1,0:T(8,128)(2,1)S(1)}, u32[]{:S(2)}, u32[]{:S(2)}) %collective-permute-start.86) | collective-permute-done | bytes 327712 | tf_op jit(solution)/shard_map/last_line/ppermute | solution.py:917
  588.1 1.6 collective-permute-done.87.other_ref
  590.5 1.9 place_last.1
  (346 shorter events, 101.6 us)
Async XLA Ops:
  7.2 502.4 %reduce-scatter.3.cloned.1.call-start = ((), (), s32[]{:S(2)}) async-start(), calls=%async_computation.2 | async-start | bytes 1310720 | tf_op jit(solution)/shard_map/readout_line/reduce_scatter | solution.py:1114
  11.6 9.8 %collective-permute-start = (bf16[96,1024]{1,0:T(8,128)(2,1)S(1)}, bf16[96,1024]{1,0:T(8,128)(2,1)S(1)}, u32[]{:S(2)}, u32[]{:S(2)}) collective-permute-start(bf16[96,1024]{1,0:T(8,128)(2,1)S(1)} %pad_maximum_fusion.5), channel_id=1, source_target_pairs={{0,8},{2,10},{4,12},{6,14},{8,24},{10,26},{12,28},{14,30},{24,16},... | collective-permute-start | bytes 589832 | tf_op jit(solution)/shard_map/one_line/ppermute | solution.py:917
  15.8 24.4 %collective-permute-start.12 = (bf16[144,1024]{1,0:T(8,128)(2,1)S(1)}, bf16[144,1024]{1,0:T(8,128)(2,1)S(1)}, u32[]{:S(2)}, u32[]{:S(2)}) collective-permute-start(bf16[144,1024]{1,0:T(8,128)(2,1)S(1)} %get-tuple-element.324), channel_id=1, source_target_pairs={{0,8},{2,10},{4,12},{6,14},{8,24},{10,26},{12,28},{14,30},{24,16},... | collective-permute-start | bytes 884744 | tf_op jit(solution)/shard_map/two_line/ppermute | solution.py:917
  21.5 10.8 %collective-permute-start.3 = (bf16[128,1024]{1,0:T(8,128)(2,1)S(1)}, bf16[128,1024]{1,0:T(8,128)(2,1)S(1)}, u32[]{:S(2)}, u32[]{:S(2)}) collective-permute-start(bf16[128,1024]{1,0:T(8,128)(2,1)S(1)} %pad_maximum_fusion.4), channel_id=1, source_target_pairs={{0,2},{2,0},{4,6},{6,4},{8,10},{10,8},{12,14},{14,12},{16,18},{18,... | collective-permute-start | bytes 786440 | tf_op jit(solution)/shard_map/top_plane/ppermute | solution.py:910
  23.3 10.3 %collective-permute-start.5 = (bf16[128,1024]{1,0:T(8,128)(2,1)S(1)}, bf16[128,1024]{1,0:T(8,128)(2,1)S(1)}, u32[]{:S(2)}, u32[]{:S(2)}) collective-permute-start(bf16[128,1024]{1,0:T(8,128)(2,1)S(1)} %pad_maximum_fusion.4), channel_id=1, source_target_pairs={{0,4},{2,6},{4,0},{6,2},{8,12},{10,14},{12,8},{14,10},{16,20},{18,... | collective-permute-start | bytes 786440 | tf_op jit(solution)/shard_map/top_plane/ppermute | solution.py:910
  38.7 17.8 %collective-permute-start.7 = (bf16[384,1024]{1,0:T(8,128)(2,1)S(1)}, bf16[384,1024]{1,0:T(8,128)(2,1)S(1)}, u32[]{:S(2)}, u32[]{:S(2)}) collective-permute-start(bf16[384,1024]{1,0:T(8,128)(2,1)S(1)} %constant_dynamic-update-slice_fusion.refs_1_.refs_27_), channel_id=1, source_target_pairs={{0,2},{2,0},{4,6},{6,4},{8,10},{10,8},{12,14},{14,12},{16,18},{18,... | collective-permute-start | bytes 2359304 | tf_op jit(solution)/shard_map/one_plane/ppermute | solution.py:910
  43.6 16.9 %collective-permute-start.9 = (bf16[384,1024]{1,0:T(8,128)(2,1)S(1)}, bf16[384,1024]{1,0:T(8,128)(2,1)S(1)}, u32[]{:S(2)}, u32[]{:S(2)}) collective-permute-start(bf16[384,1024]{1,0:T(8,128)(2,1)S(1)} %constant_dynamic-update-slice_fusion.refs_1_.refs_27_), channel_id=1, source_target_pairs={{0,4},{2,6},{4,0},{6,2},{8,12},{10,14},{12,8},{14,10},{16,20},{18,... | collective-permute-start | bytes 2359304 | tf_op jit(solution)/shard_map/one_plane/ppermute | solution.py:910
  60.5 32.8 %collective-permute-start.15 = (bf16[768,1024]{1,0:T(8,128)(2,1)S(1)}, bf16[768,1024]{1,0:T(8,128)(2,1)S(1)}, u32[]{:S(2)}, u32[]{:S(2)}) collective-permute-start(bf16[768,1024]{1,0:T(8,128)(2,1)S(1)} %slice_dynamic-update-slice_fusion.3), channel_id=1, source_target_pairs={{0,2},{2,0},{4,6},{6,4},{8,10},{10,8},{12,14},{14,12},{16,18},{18,... | collective-permute-start | bytes 4718600 | tf_op jit(solution)/shard_map/two_one_plane/ppermute | solution.py:910
  60.6 11.1 %collective-permute-start.20 = (bf16[208,1024]{1,0:T(8,128)(2,1)S(1)}, bf16[208,1024]{1,0:T(8,128)(2,1)S(1)}, u32[]{:S(2)}, u32[]{:S(2)}) collective-permute-start(bf16[208,1024]{1,0:T(8,128)(2,1)S(1)} %pad_maximum_fusion.3), channel_id=1, source_target_pairs={{0,8},{2,10},{4,12},{6,14},{8,24},{10,26},{12,28},{14,30},{24,16},... | collective-permute-start | bytes 1277960 | tf_op jit(solution)/shard_map/three_line/ppermute | solution.py:917
  61.4 33.6 %collective-permute-start.16 = (bf16[768,1024]{1,0:T(8,128)(2,1)S(1)}, bf16[768,1024]{1,0:T(8,128)(2,1)S(1)}, u32[]{:S(2)}, u32[]{:S(2)}) collective-permute-start(bf16[768,1024]{1,0:T(8,128)(2,1)S(1)} %slice_dynamic-update-slice_fusion.2), channel_id=1, source_target_pairs={{0,4},{2,6},{4,0},{6,2},{8,12},{10,14},{12,8},{14,10},{16,20},{18,... | collective-permute-start | bytes 4718600 | tf_op jit(solution)/shard_map/two_one_plane/ppermute | solution.py:910
  71.7 12.1 %collective-permute-start.21 = (bf16[208,1024]{1,0:T(8,128)(2,1)S(1)}, bf16[208,1024]{1,0:T(8,128)(2,1)S(1)}, u32[]{:S(2)}, u32[]{:S(2)}) collective-permute-start(bf16[208,1024]{1,0:T(8,128)(2,1)S(1)} %collective-permute-done.20), channel_id=1, source_target_pairs={{0,8},{2,10},{4,12},{6,14},{8,24},{10,26},{12,28},{14,30},{24,16},... | collective-permute-start | bytes 1277960 | tf_op jit(solution)/shard_map/three_line/ppermute | solution.py:917
  95.0 47.6 %collective-permute-start.23 = (bf16[1120,1024]{1,0:T(8,128)(2,1)S(1)}, bf16[1120,1024]{1,0:T(8,128)(2,1)S(1)}, u32[]{:S(2)}, u32[]{:S(2)}) collective-permute-start(bf16[1120,1024]{1,0:T(8,128)(2,1)S(1)} %slice_dynamic-update-slice_fusion.1), channel_id=1, source_target_pairs={{0,2},{2,0},{4,6},{6,4},{8,10},{10,8},{12,14},{14,12},{16,18},{18,... | collective-permute-start | bytes 6881288 | tf_op jit(solution)/shard_map/three_two_plane/ppermute | solution.py:910
  96.5 47.2 %collective-permute-start.24 = (bf16[1120,1024]{1,0:T(8,128)(2,1)S(1)}, bf16[1120,1024]{1,0:T(8,128)(2,1)}, u32[]{:S(2)}, u32[]{:S(2)}) collective-permute-start(bf16[1120,1024]{1,0:T(8,128)(2,1)S(1)} %slice_dynamic-update-slice_fusion), channel_id=1, source_target_pairs={{0,4},{2,6},{4,0},{6,2},{8,12},{10,14},{12,8},{14,10},{16,20},{18,... | collective-permute-start | bytes 6881288 | tf_op jit(solution)/shard_map/three_two_plane/ppermute | solution.py:910
  98.8 16.0 %collective-permute-start.28 = (bf16[288,1024]{1,0:T(8,128)(2,1)S(1)}, bf16[288,1024]{1,0:T(8,128)(2,1)S(1)}, u32[]{:S(2)}, u32[]{:S(2)}) collective-permute-start(bf16[288,1024]{1,0:T(8,128)(2,1)S(1)} %slice_bitcast_fusion.6), channel_id=1, source_target_pairs={{0,8},{2,10},{4,12},{6,14},{8,24},{10,26},{12,28},{14,30},{24,16},... | collective-permute-start | bytes 1769480 | tf_op jit(solution)/shard_map/four_line/ppermute | solution.py:917
  114.9 17.1 %collective-permute-start.29 = (bf16[288,1024]{1,0:T(8,128)(2,1)S(1)}, bf16[288,1024]{1,0:T(8,128)(2,1)S(1)}, u32[]{:S(2)}, u32[]{:S(2)}) collective-permute-start(bf16[288,1024]{1,0:T(8,128)(2,1)S(1)} %collective-permute-done.28), channel_id=1, source_target_pairs={{0,8},{2,10},{4,12},{6,14},{8,24},{10,26},{12,28},{14,30},{24,16},... | collective-permute-start | bytes 1769480 | tf_op jit(solution)/shard_map/four_line/ppermute | solution.py:917
  132.0 14.2 %collective-permute-start.30 = (bf16[288,1024]{1,0:T(8,128)(2,1)S(1)}, bf16[288,1024]{1,0:T(8,128)(2,1)S(1)}, u32[]{:S(2)}, u32[]{:S(2)}) collective-permute-start(bf16[288,1024]{1,0:T(8,128)(2,1)S(1)} %collective-permute-done.29), channel_id=1, source_target_pairs={{0,8},{2,10},{4,12},{6,14},{8,24},{10,26},{12,28},{14,30},{24,16},... | collective-permute-start | bytes 1769480 | tf_op jit(solution)/shard_map/four_line/ppermute | solution.py:917
  134.1 14.7 %collective-permute-start.10 = (bf16[384,1024]{1,0:T(8,128)(2,1)S(1)}, bf16[384,1024]{1,0:T(8,128)(2,1)S(1)}, u32[]{:S(2)}, u32[]{:S(2)}) collective-permute-start(bf16[384,1024]{1,0:T(8,128)(2,1)S(1)} %collective-permute-done.7.refs_3_.refs_29_), channel_id=1, source_target_pairs={{0,1},{1,0},{2,3},{3,2},{4,5},{5,4},{6,7},{7,6},{8,9},{9,8},{10,11... | collective-permute-start | bytes 2359304 | tf_op jit(solution)/shard_map/swap/ppermute | solution.py:920
  134.8 30.6 %collective-permute-start.33 = (bf16[512,1024]{1,0:T(8,128)(2,1)}, bf16[512,1024]{1,0:T(8,128)(2,1)}, u32[]{:S(2)}, u32[]{:S(2)}) collective-permute-start(bf16[512,1024]{1,0:T(8,128)(2,1)} %constant_dynamic-update-slice_fusion.32.refs_0_), channel_id=1, source_target_pairs={{0,8},{2,10},{4,12},{6,14},{8,24},{10,26},{12,28},{14,30},{24,16},... | collective-permute-start | bytes 3145736 | tf_op jit(solution)/shard_map/top_line/ppermute | solution.py:917
  146.2 19.2 %collective-permute-start.31 = (bf16[416,1024]{1,0:T(8,128)(2,1)S(1)}, bf16[416,1024]{1,0:T(8,128)(2,1)S(1)}, u32[]{:S(2)}, u32[]{:S(2)}) collective-permute-start(bf16[416,1024]{1,0:T(8,128)(2,1)S(1)} %slice.224), channel_id=1, source_target_pairs={{0,2},{2,0},{4,6},{6,4},{8,10},{10,8},{12,14},{14,12},{16,18},{18,... | collective-permute-start | bytes 2555912 | tf_op jit(solution)/shard_map/three_plane/ppermute | solution.py:910
  147.0 18.9 %collective-permute-start.32 = (bf16[416,1024]{1,0:T(8,128)(2,1)S(1)}, bf16[416,1024]{1,0:T(8,128)(2,1)S(1)}, u32[]{:S(2)}, u32[]{:S(2)}) collective-permute-start(bf16[416,1024]{1,0:T(8,128)(2,1)S(1)} %slice.225), channel_id=1, source_target_pairs={{0,4},{2,6},{4,0},{6,2},{8,12},{10,14},{12,8},{14,10},{16,20},{18,... | collective-permute-start | bytes 2555912 | tf_op jit(solution)/shard_map/three_plane/ppermute | solution.py:910
  148.8 22.2 %collective-permute-start.17 = (bf16[768,1024]{1,0:T(8,128)(2,1)S(1)}, bf16[768,1024]{1,0:T(8,128)(2,1)S(1)}, u32[]{:S(2)}, u32[]{:S(2)}) collective-permute-start(bf16[768,1024]{1,0:T(8,128)(2,1)S(1)} %collective-permute-done.15.refs_7_.refs_13_.refs_33_.refs_6_), channel_id=1, source_target_pairs={{0,1},{1,0},{2,3},{3,2},{4,5},{5,4},{6,7},{7,6},{8,9},{9,8},{10,11... | collective-permute-start | bytes 4718600 | tf_op jit(solution)/shard_map/swap/ppermute | solution.py:920
  148.8 22.4 %collective-permute-start.18 = (bf16[768,1024]{1,0:T(8,128)(2,1)S(1)}, bf16[768,1024]{1,0:T(8,128)(2,1)S(1)}, u32[]{:S(2)}, u32[]{:S(2)}) collective-permute-start(bf16[768,1024]{1,0:T(8,128)(2,1)S(1)} %collective-permute-done.16.refs_9_.refs_15_.refs_35_.refs_8_), channel_id=1, source_target_pairs={{0,1},{1,0},{2,3},{3,2},{4,5},{5,4},{6,7},{7,6},{8,9},{9,8},{10,11... | collective-permute-start | bytes 4718600 | tf_op jit(solution)/shard_map/swap/ppermute | solution.py:920
  171.0 9.2 %collective-permute-start.25 = (bf16[1120,1024]{1,0:T(8,128)(2,1)S(1)}, bf16[1120,1024]{1,0:T(8,128)(2,1)}, u32[]{:S(2)}, u32[]{:S(2)}) collective-permute-start(bf16[1120,1024]{1,0:T(8,128)(2,1)S(1)} %collective-permute-done.23.refs_17_.refs_4_.refs_24_.refs_10_), channel_id=1, source_target_pairs={{0,1},{1,0},{2,3},{3,2},{4,5},{5,4},{6,7},{7,6},{8,9},{9,8},{10,11... | collective-permute-start | bytes 6881288 | tf_op jit(solution)/shard_map/swap/ppermute | solution.py:920
  175.2 53.7 %collective-permute-start.38 = (bf16[1152,1024]{1,0:T(8,128)(2,1)}, bf16[1152,1024]{1,0:T(8,128)(2,1)}, u32[]{:S(2)}, u32[]{:S(2)}) collective-permute-start(bf16[1152,1024]{1,0:T(8,128)(2,1)} %pad_maximum_fusion.refs_16_.refs_4_), channel_id=1, source_target_pairs={{0,2},{2,0},{4,6},{6,4},{8,10},{10,8},{12,14},{14,12},{16,18},{18,... | collective-permute-start | bytes 7077896 | tf_op jit(solution)/shard_map/four_plane/ppermute | solution.py:910
  175.2 53.8 %collective-permute-start.39 = (bf16[1152,1024]{1,0:T(8,128)(2,1)}, bf16[1152,1024]{1,0:T(8,128)(2,1)}, u32[]{:S(2)}, u32[]{:S(2)}) collective-permute-start(bf16[1152,1024]{1,0:T(8,128)(2,1)} %pad_maximum_fusion.refs_16_.refs_4_), channel_id=1, source_target_pairs={{0,4},{2,6},{4,0},{6,2},{8,12},{10,14},{12,8},{14,10},{16,20},{18,... | collective-permute-start | bytes 7077896 | tf_op jit(solution)/shard_map/four_plane/ppermute | solution.py:910
  178.9 34.5 %collective-permute-start.36 = (bf16[512,1024]{1,0:T(8,128)(2,1)}, bf16[512,1024]{1,0:T(8,128)(2,1)}, u32[]{:S(2)}, u32[]{:S(2)}) collective-permute-start(bf16[512,1024]{1,0:T(8,128)(2,1)} %collective-permute-done.33.refs_2_), channel_id=1, source_target_pairs={{0,8},{2,10},{4,12},{6,14},{8,24},{10,26},{12,28},{14,30},{24,16},... | collective-permute-start | bytes 3145736 | tf_op jit(solution)/shard_map/top_line/ppermute | solution.py:917
  213.2 47.1 %collective-permute-start.42 = (bf16[1152,1024]{1,0:T(8,128)(2,1)}, bf16[1152,1024]{1,0:T(8,128)(2,1)}, u32[]{:S(2)}, u32[]{:S(2)}) collective-permute-start(bf16[1152,1024]{1,0:T(8,128)(2,1)} %pad_maximum_fusion.refs_16_.refs_4_), channel_id=1, source_target_pairs={{0,1},{1,0},{2,3},{3,2},{4,5},{5,4},{6,7},{7,6},{8,9},{9,8},{10,11... | collective-permute-start | bytes 7077896 | tf_op jit(solution)/shard_map/swap/ppermute | solution.py:920
  213.4 26.7 %collective-permute-start.37 = (bf16[512,1024]{1,0:T(8,128)(2,1)}, bf16[512,1024]{1,0:T(8,128)(2,1)}, u32[]{:S(2)}, u32[]{:S(2)}) collective-permute-start(bf16[512,1024]{1,0:T(8,128)(2,1)} %collective-permute-done.36.refs_4_), channel_id=1, source_target_pairs={{0,8},{2,10},{4,12},{6,14},{8,24},{10,26},{12,28},{14,30},{24,16},... | collective-permute-start | bytes 3145736 | tf_op jit(solution)/shard_map/top_line/ppermute | solution.py:917
  231.9 27.4 %collective-permute-start.43 = (bf16[576,1024]{1,0:T(8,128)(2,1)S(1)}, bf16[576,1024]{1,0:T(8,128)(2,1)S(1)}, u32[]{:S(2)}, u32[]{:S(2)}) collective-permute-start(bf16[576,1024]{1,0:T(8,128)(2,1)S(1)} %slice.185), channel_id=1, source_target_pairs={{0,2},{2,0},{4,6},{6,4},{8,10},{10,8},{12,14},{14,12},{16,18},{18,... | collective-permute-start | bytes 3538952 | tf_op jit(solution)/shard_map/four_plane/ppermute | solution.py:910
  233.6 26.7 %collective-permute-start.45 = (bf16[576,1024]{1,0:T(8,128)(2,1)S(1)}, bf16[576,1024]{1,0:T(8,128)(2,1)S(1)}, u32[]{:S(2)}, u32[]{:S(2)}) collective-permute-start(bf16[576,1024]{1,0:T(8,128)(2,1)S(1)} %slice.186), channel_id=1, source_target_pairs={{0,4},{2,6},{4,0},{6,2},{8,12},{10,14},{12,8},{14,10},{16,20},{18,... | collective-permute-start | bytes 3538952 | tf_op jit(solution)/shard_map/four_plane/ppermute | solution.py:910
  233.9 54.7 %collective-permute-start.47 = (bf16[3,576,1024]{2,1,0:T(8,128)(2,1)S(1)}, bf16[3,576,1024]{2,1,0:T(8,128)(2,1)}, u32[]{:S(2)}, u32[]{:S(2)}) collective-permute-start(bf16[3,576,1024]{2,1,0:T(8,128)(2,1)S(1)} %copy-done.1), channel_id=1, source_target_pairs={{0,1},{1,0},{2,3},{3,2},{4,5},{5,4},{6,7},{7,6},{8,9},{9,8},{10,11... | collective-permute-start | bytes 10616840 | tf_op jit(solution)/shard_map/ppermute | solution.py:920
  240.1 28.1 %collective-permute-start.40 = (bf16[1152,1024]{1,0:T(8,128)(2,1)}, bf16[1152,1024]{1,0:T(8,128)(2,1)}, u32[]{:S(2)}, u32[]{:S(2)}) collective-permute-start(bf16[1152,1024]{1,0:T(8,128)(2,1)} %collective-permute-done.38.refs_12_.refs_0_), channel_id=1, source_target_pairs={{0,1},{1,0},{2,3},{3,2},{4,5},{5,4},{6,7},{7,6},{8,9},{9,8},{10,11... | collective-permute-start | bytes 7077896 | tf_op jit(solution)/shard_map/swap/ppermute | solution.py:920
  259.3 9.1 %collective-permute-start.41 = (bf16[1152,1024]{1,0:T(8,128)(2,1)}, bf16[1152,1024]{1,0:T(8,128)(2,1)}, u32[]{:S(2)}, u32[]{:S(2)}) collective-permute-start(bf16[1152,1024]{1,0:T(8,128)(2,1)} %collective-permute-done.39.refs_14_.refs_2_), channel_id=1, source_target_pairs={{0,1},{1,0},{2,3},{3,2},{4,5},{5,4},{6,7},{7,6},{8,9},{9,8},{10,11... | collective-permute-start | bytes 7077896 | tf_op jit(solution)/shard_map/swap/ppermute | solution.py:920
  265.5 19.9 %collective-permute-start.48 = (bf16[512,1024]{1,0:T(8,128)(2,1)}, bf16[512,1024]{1,0:T(8,128)(2,1)}, u32[]{:S(2)}, u32[]{:S(2)}) collective-permute-start(bf16[512,1024]{1,0:T(8,128)(2,1)} %constant_dynamic-update-slice_fusion.32.refs_0_), channel_id=1, source_target_pairs={{0,1},{1,0},{2,3},{3,2},{4,5},{5,4},{6,7},{7,6},{8,9},{9,8},{10,11... | collective-permute-start | bytes 3145736 | tf_op jit(solution)/shard_map/ppermute | solution.py:920
  267.2 19.4 %collective-permute-start.49 = (bf16[512,1024]{1,0:T(8,128)(2,1)}, bf16[512,1024]{1,0:T(8,128)(2,1)}, u32[]{:S(2)}, u32[]{:S(2)}) collective-permute-start(bf16[512,1024]{1,0:T(8,128)(2,1)} %collective-permute-done.33.refs_2_), channel_id=1, source_target_pairs={{0,1},{1,0},{2,3},{3,2},{4,5},{5,4},{6,7},{7,6},{8,9},{9,8},{10,11... | collective-permute-start | bytes 3145736 | tf_op jit(solution)/shard_map/ppermute | solution.py:920
  268.2 19.8 %collective-permute-start.50 = (bf16[512,1024]{1,0:T(8,128)(2,1)}, bf16[512,1024]{1,0:T(8,128)(2,1)}, u32[]{:S(2)}, u32[]{:S(2)}) collective-permute-start(bf16[512,1024]{1,0:T(8,128)(2,1)} %collective-permute-done.36.refs_4_), channel_id=1, source_target_pairs={{0,1},{1,0},{2,3},{3,2},{4,5},{5,4},{6,7},{7,6},{8,9},{9,8},{10,11... | collective-permute-start | bytes 3145736 | tf_op jit(solution)/shard_map/ppermute | solution.py:920
  268.3 24.4 %collective-permute-start.51 = (bf16[512,1024]{1,0:T(8,128)(2,1)}, bf16[512,1024]{1,0:T(8,128)(2,1)}, u32[]{:S(2)}, u32[]{:S(2)}) collective-permute-start(bf16[512,1024]{1,0:T(8,128)(2,1)} %collective-permute-done.37.refs_6_), channel_id=1, source_target_pairs={{0,1},{1,0},{2,3},{3,2},{4,5},{5,4},{6,7},{7,6},{8,9},{9,8},{10,11... | collective-permute-start | bytes 3145736 | tf_op jit(solution)/shard_map/ppermute | solution.py:920
  285.4 33.5 %collective-permute-start.55 = (bf16[4,144,1024]{2,1,0:T(8,128)(2,1)}, bf16[4,144,1024]{2,1,0:T(8,128)(2,1)}, u32[]{:S(2)}, u32[]{:S(2)}) collective-permute-start(bf16[4,144,1024]{2,1,0:T(8,128)(2,1)} %get-tuple-element.202.lefts_ref.refs_0_.refs_4_.refs_8_), channel_id=1, source_target_pairs={{0,1},{1,0},{2,3},{3,2},{4,5},{5,4},{6,7},{7,6},{8,9},{9,8},{10,11... | collective-permute-start | bytes 3538952 | tf_op jit(solution)/shard_map/ppermute | solution.py:920
  286.5 21.4 %collective-permute-start.52 = (bf16[144,1024]{1,0:T(8,128)(2,1)S(1)}, bf16[144,1024]{1,0:T(8,128)(2,1)S(1)}, u32[]{:S(2)}, u32[]{:S(2)}) collective-permute-start(bf16[144,1024]{1,0:T(8,128)(2,1)S(1)} %slice_bitcast_fusion.8), channel_id=1, source_target_pairs={{0,2},{2,0},{4,6},{6,4},{8,10},{10,8},{12,14},{14,12},{16,18},{18,... | collective-permute-start | bytes 884744 | tf_op jit(solution)/shard_map/spread/ppermute | solution.py:910
  288.0 20.0 %collective-permute-start.53 = (bf16[144,1024]{1,0:T(8,128)(2,1)S(1)}, bf16[144,1024]{1,0:T(8,128)(2,1)}, u32[]{:S(2)}, u32[]{:S(2)}) collective-permute-start(bf16[144,1024]{1,0:T(8,128)(2,1)S(1)} %slice_bitcast_fusion.8), channel_id=1, source_target_pairs={{0,4},{2,6},{4,0},{6,2},{8,12},{10,14},{12,8},{14,10},{16,20},{18,... | collective-permute-start | bytes 884744 | tf_op jit(solution)/shard_map/spread/ppermute | solution.py:910
  288.6 19.3 %collective-permute-start.54 = (bf16[144,1024]{1,0:T(8,128)(2,1)S(1)}, bf16[144,1024]{1,0:T(8,128)(2,1)S(1)}, u32[]{:S(2)}, u32[]{:S(2)}) collective-permute-start(bf16[144,1024]{1,0:T(8,128)(2,1)S(1)} %slice_bitcast_fusion.8), channel_id=1, source_target_pairs={{0,6},{2,4},{4,2},{6,0},{8,14},{10,12},{12,10},{14,8},{16,22},{18,... | collective-permute-start | bytes 884744 | tf_op jit(solution)/shard_map/spread/ppermute | solution.py:910
  315.3 10.8 %collective-permute-start.57 = (bf16[144,1024]{1,0:T(8,128)(2,1)S(1)}, bf16[144,1024]{1,0:T(8,128)(2,1)S(1)}, u32[]{:S(2)}, u32[]{:S(2)}) collective-permute-start(bf16[144,1024]{1,0:T(8,128)(2,1)S(1)} %slice_bitcast_fusion.7), channel_id=1, source_target_pairs={{0,2},{2,0},{4,6},{6,4},{8,10},{10,8},{12,14},{14,12},{16,18},{18,... | collective-permute-start | bytes 884744 | tf_op jit(solution)/shard_map/spread/ppermute | solution.py:910
  316.7 15.4 %collective-permute-start.58 = (bf16[144,1024]{1,0:T(8,128)(2,1)S(1)}, bf16[144,1024]{1,0:T(8,128)(2,1)S(1)}, u32[]{:S(2)}, u32[]{:S(2)}) collective-permute-start(bf16[144,1024]{1,0:T(8,128)(2,1)S(1)} %slice_bitcast_fusion.7), channel_id=1, source_target_pairs={{0,4},{2,6},{4,0},{6,2},{8,12},{10,14},{12,8},{14,10},{16,20},{18,... | collective-permute-start | bytes 884744 | tf_op jit(solution)/shard_map/spread/ppermute | solution.py:910
  317.4 14.8 %collective-permute-start.59 = (bf16[144,1024]{1,0:T(8,128)(2,1)S(1)}, bf16[144,1024]{1,0:T(8,128)(2,1)S(1)}, u32[]{:S(2)}, u32[]{:S(2)}) collective-permute-start(bf16[144,1024]{1,0:T(8,128)(2,1)S(1)} %slice_bitcast_fusion.7), channel_id=1, source_target_pairs={{0,6},{2,4},{4,2},{6,0},{8,14},{10,12},{12,10},{14,8},{16,22},{18,... | collective-permute-start | bytes 884744 | tf_op jit(solution)/shard_map/spread/ppermute | solution.py:910
  318.9 14.0 %collective-permute-start.60 = (bf16[2,144,512]{2,1,0:T(8,128)(2,1)}, bf16[2,144,512]{2,1,0:T(8,128)(2,1)S(1)}, u32[]{:S(2)}, u32[]{:S(2)}) collective-permute-start(bf16[2,144,512]{2,1,0:T(8,128)(2,1)} %get-tuple-element.239), channel_id=1, source_target_pairs={{0,1},{1,0},{2,3},{3,2},{4,5},{5,4},{6,7},{7,6},{8,9},{9,8},{10,11... | collective-permute-start | bytes 884744 | tf_op jit(solution)/shard_map/ppermute | solution.py:920
  333.7 42.1 %collective-permute-start.61 = (bf16[4,64,2048]{2,1,0:T(8,128)(2,1)}, bf16[4,64,2048]{2,1,0:T(8,128)(2,1)S(1)}, u32[]{:S(2)}, u32[]{:S(2)}) collective-permute-start(bf16[4,64,2048]{2,1,0:T(8,128)(2,1)} %get-tuple-element.240), channel_id=1, source_target_pairs={{0,2},{2,0},{4,6},{6,4},{8,10},{10,8},{12,14},{14,12},{16,18},{18,... | collective-permute-start | bytes 3145736 | tf_op jit(solution)/shard_map/readout_across/ppermute | solution.py:910
  334.4 41.5 %collective-permute-start.62 = (bf16[4,64,2048]{2,1,0:T(8,128)(2,1)}, bf16[4,64,2048]{2,1,0:T(8,128)(2,1)S(1)}, u32[]{:S(2)}, u32[]{:S(2)}) collective-permute-start(bf16[4,64,2048]{2,1,0:T(8,128)(2,1)} %get-tuple-element.241), channel_id=1, source_target_pairs={{0,4},{2,6},{4,0},{6,2},{8,12},{10,14},{12,8},{14,10},{16,20},{18,... | collective-permute-start | bytes 3145736 | tf_op jit(solution)/shard_map/readout_across/ppermute | solution.py:910
  378.5 32.9 %collective-permute-start.66 = (bf16[576,1024]{1,0:T(8,128)(2,1)S(1)}, bf16[576,1024]{1,0:T(8,128)(2,1)}, u32[]{:S(2)}, u32[]{:S(2)}) collective-permute-start(bf16[576,1024]{1,0:T(8,128)(2,1)S(1)} %constant_dynamic-update-slice_fusion.44.refs_2_), channel_id=1, source_target_pairs={{0,1},{1,0},{2,3},{3,2},{4,5},{5,4},{6,7},{7,6},{8,9},{9,8},{10,11... | collective-permute-start | bytes 3538952 | tf_op jit(solution)/shard_map/spread_swap/ppermute | solution.py:920
  380.9 30.6 %collective-permute-start.67 = (bf16[576,1024]{1,0:T(8,128)(2,1)S(1)}, bf16[576,1024]{1,0:T(8,128)(2,1)}, u32[]{:S(2)}, u32[]{:S(2)}) collective-permute-start(bf16[576,1024]{1,0:T(8,128)(2,1)S(1)} %constant_dynamic-update-slice_fusion.40.refs_0_), channel_id=1, source_target_pairs={{0,1},{1,0},{2,3},{3,2},{4,5},{5,4},{6,7},{7,6},{8,9},{9,8},{10,11... | collective-permute-start | bytes 3538952 | tf_op jit(solution)/shard_map/spread_swap/ppermute | solution.py:920
  381.5 30.0 %collective-permute-start.63 = (bf16[2,64,2048]{2,1,0:T(8,128)(2,1)}, bf16[2,64,2048]{2,1,0:T(8,128)(2,1)S(1)}, u32[]{:S(2)}, u32[]{:S(2)}) collective-permute-start(bf16[2,64,2048]{2,1,0:T(8,128)(2,1)} %add_convert_fusion.8), channel_id=1, source_target_pairs={{0,2},{2,0},{4,6},{6,4},{8,10},{10,8},{12,14},{14,12},{16,18},{18,... | collective-permute-start | bytes 1572872 | tf_op jit(solution)/shard_map/readout_onward/ppermute | solution.py:910
  382.5 29.0 %collective-permute-start.64 = (bf16[2,64,2048]{2,1,0:T(8,128)(2,1)}, bf16[2,64,2048]{2,1,0:T(8,128)(2,1)}, u32[]{:S(2)}, u32[]{:S(2)}) collective-permute-start(bf16[2,64,2048]{2,1,0:T(8,128)(2,1)} %add_convert_fusion.7), channel_id=1, source_target_pairs={{0,4},{2,6},{4,0},{6,2},{8,12},{10,14},{12,8},{14,10},{16,20},{18,... | collective-permute-start | bytes 1572872 | tf_op jit(solution)/shard_map/readout_onward/ppermute | solution.py:910
  414.7 52.9 %collective-permute-start.68 = (bf16[4,576,512]{2,1,0:T(8,128)(2,1)}, bf16[4,576,512]{2,1,0:T(8,128)(2,1)S(1)}, u32[]{:S(2)}, u32[]{:S(2)}) collective-permute-start(bf16[4,576,512]{2,1,0:T(8,128)(2,1)} %get-tuple-element.281), channel_id=1, source_target_pairs={{0,2},{2,0},{4,6},{6,4},{8,10},{10,8},{12,14},{14,12},{16,18},{18,... | collective-permute-start | bytes 7077896 | tf_op jit(solution)/shard_map/middle_0_across/ppermute | solution.py:910
  415.4 52.9 %collective-permute-start.69 = (bf16[4,576,512]{2,1,0:T(8,128)(2,1)}, bf16[4,576,512]{2,1,0:T(8,128)(2,1)}, u32[]{:S(2)}, u32[]{:S(2)}) collective-permute-start(bf16[4,576,512]{2,1,0:T(8,128)(2,1)} %get-tuple-element.282), channel_id=1, source_target_pairs={{0,4},{2,6},{4,0},{6,2},{8,12},{10,14},{12,8},{14,10},{16,20},{18,... | collective-permute-start | bytes 7077896 | tf_op jit(solution)/shard_map/middle_0_across/ppermute | solution.py:910
  418.9 152.2 %reduce-scatter.5.cloned.1.call-start = ((), (), s32[]{:S(2)}) async-start(), calls=%async_computation.3 | async-start | bytes 2949120 | tf_op jit(solution)/shard_map/middle_1_levels/reduce_scatter | solution.py:1415
  472.7 26.9 %collective-permute-start.73 = (bf16[2,576,512]{2,1,0:T(8,128)(2,1)}, bf16[2,576,512]{2,1,0:T(8,128)(2,1)S(1)}, u32[]{:S(2)}, u32[]{:S(2)}) collective-permute-start(bf16[2,576,512]{2,1,0:T(8,128)(2,1)} %add_convert_fusion.1), channel_id=1, source_target_pairs={{0,2},{2,0},{4,6},{6,4},{8,10},{10,8},{12,14},{14,12},{16,18},{18,... | collective-permute-start | bytes 3538952 | tf_op jit(solution)/shard_map/middle_0_onward/ppermute | solution.py:910
  473.6 26.8 %collective-permute-start.74 = (bf16[2,576,512]{2,1,0:T(8,128)(2,1)}, bf16[2,576,512]{2,1,0:T(8,128)(2,1)S(1)}, u32[]{:S(2)}, u32[]{:S(2)}) collective-permute-start(bf16[2,576,512]{2,1,0:T(8,128)(2,1)} %add_convert_fusion), channel_id=1, source_target_pairs={{0,4},{2,6},{4,0},{6,2},{8,12},{10,14},{12,8},{14,10},{16,20},{18,... | collective-permute-start | bytes 3538952 | tf_op jit(solution)/shard_map/middle_0_onward/ppermute | solution.py:910
  507.4 28.9 %collective-permute-start.75 = (bf16[4,320,512]{2,1,0:T(8,128)(2,1)}, bf16[4,320,512]{2,1,0:T(8,128)(2,1)}, u32[]{:S(2)}, u32[]{:S(2)}) collective-permute-start(bf16[4,320,512]{2,1,0:T(8,128)(2,1)} %get-tuple-element.302), channel_id=1, source_target_pairs={{0,2},{2,0},{4,6},{6,4},{8,10},{10,8},{12,14},{14,12},{16,18},{18,... | collective-permute-start | bytes 3932168 | tf_op jit(solution)/shard_map/last_across/ppermute | solution.py:910
  508.4 28.4 %collective-permute-start.76 = (bf16[4,320,512]{2,1,0:T(8,128)(2,1)}, bf16[4,320,512]{2,1,0:T(8,128)(2,1)}, u32[]{:S(2)}, u32[]{:S(2)}) collective-permute-start(bf16[4,320,512]{2,1,0:T(8,128)(2,1)} %get-tuple-element.303), channel_id=1, source_target_pairs={{0,4},{2,6},{4,0},{6,2},{8,12},{10,14},{12,8},{14,10},{16,20},{18,... | collective-permute-start | bytes 3932168 | tf_op jit(solution)/shard_map/last_across/ppermute | solution.py:910
  509.6 22.8 %collective-permute-start.82 = (bf16[576,512]{1,0:T(8,128)(2,1)}, bf16[576,512]{1,0:T(8,128)(2,1)}, u32[]{:S(2)}, u32[]{:S(2)}) collective-permute-start(bf16[576,512]{1,0:T(8,128)(2,1)} %fusion.8), channel_id=1, source_target_pairs={{0,8},{2,10},{4,12},{6,14},{8,24},{10,26},{12,28},{14,30},{24,16},... | collective-permute-start | bytes 1769480 | tf_op jit(solution)/shard_map/middle_0_line/ppermute | solution.py:917
  534.0 15.3 %collective-permute-start.83 = (bf16[576,512]{1,0:T(8,128)(2,1)S(1)}, bf16[576,512]{1,0:T(8,128)(2,1)S(1)}, u32[]{:S(2)}, u32[]{:S(2)}) collective-permute-start(bf16[576,512]{1,0:T(8,128)(2,1)S(1)} %add_convert_fusion.4), channel_id=1, source_target_pairs={{0,8},{2,10},{4,12},{6,14},{8,24},{10,26},{12,28},{14,30},{24,16},... | collective-permute-start | bytes 1769480 | tf_op jit(solution)/shard_map/middle_0_line/ppermute | solution.py:917
  538.0 13.3 %collective-permute-start.78 = (bf16[2,320,512]{2,1,0:T(8,128)(2,1)S(1)}, bf16[2,320,512]{2,1,0:T(8,128)(2,1)S(1)}, u32[]{:S(2)}, u32[]{:S(2)}) collective-permute-start(bf16[2,320,512]{2,1,0:T(8,128)(2,1)S(1)} %add_convert_fusion.3), channel_id=1, source_target_pairs={{0,4},{2,6},{4,0},{6,2},{8,12},{10,14},{12,8},{14,10},{16,20},{18,... | collective-permute-start | bytes 1966088 | tf_op jit(solution)/shard_map/last_onward/ppermute | solution.py:910
  540.8 13.1 %collective-permute-start.79 = (bf16[2,320,512]{2,1,0:T(8,128)(2,1)S(1)}, bf16[2,320,512]{2,1,0:T(8,128)(2,1)S(1)}, u32[]{:S(2)}, u32[]{:S(2)}) collective-permute-start(bf16[2,320,512]{2,1,0:T(8,128)(2,1)S(1)} %add_convert_fusion.2), channel_id=1, source_target_pairs={{0,2},{2,0},{4,6},{6,4},{8,10},{10,8},{12,14},{14,12},{16,18},{18,... | collective-permute-start | bytes 1966088 | tf_op jit(solution)/shard_map/last_onward/ppermute | solution.py:910
  549.5 17.2 %collective-permute-start.84 = (bf16[576,512]{1,0:T(8,128)(2,1)S(1)}, bf16[576,512]{1,0:T(8,128)(2,1)S(1)}, u32[]{:S(2)}, u32[]{:S(2)}) collective-permute-start(bf16[576,512]{1,0:T(8,128)(2,1)S(1)} %fusion.1), channel_id=1, source_target_pairs={{0,8},{2,10},{4,12},{6,14},{8,24},{10,26},{12,28},{14,30},{24,16},... | collective-permute-start | bytes 1769480 | tf_op jit(solution)/shard_map/middle_0_line/ppermute | solution.py:917
  556.8 14.2 %collective-permute-start.80 = (bf16[320,512]{1,0:T(8,128)(2,1)S(1)}, bf16[320,512]{1,0:T(8,128)(2,1)S(1)}, u32[]{:S(2)}, u32[]{:S(2)}) collective-permute-start(bf16[320,512]{1,0:T(8,128)(2,1)S(1)} %fusion.9), channel_id=1, source_target_pairs={{0,8},{2,10},{4,12},{6,14},{8,24},{10,26},{12,28},{14,30},{24,16},... | collective-permute-start | bytes 983048 | tf_op jit(solution)/shard_map/last_line/ppermute | solution.py:917
  (87 other events, 1027.4 us)
Sparse Core Ops, SparseCore 0:
  419.1 24.7 reduce-scatter.2
  475.7 54.4 reduce-scatter.4

commit v6 on v5

--- a/solution.py
+++ b/solution.py
@@ -110,6 +110,18 @@
     def copies(self):
         return len(self.moves)
 
+    def firsts(self, places):
+        return [
+            to_row + (places[place] * stride if place is not None else jnp.int32(0))
+            for _, _, _, _, place, stride, to_row, _, _, _ in self.moves
+        ]
+
+    def ends(self, places):
+        return [
+            to_row + rows + (places[place] * stride if place is not None else 0)
+            for _, _, _, _, place, stride, to_row, _, rows, _ in self.moves
+        ]
+
     def bind(self, refs, places, matrix, sems, to_blocks=False, base=0):
         made = []
         for number, block, row, column, place, stride, to_row, to_column, rows, columns in self.moves:
@@ -174,11 +186,19 @@
         start(copies)
         return copies
 
-    def store(self, blocks, refs, places, matrix):
+    def plan(self, blocks, refs, places, matrix):
         copies = blocks.bind(refs, places, matrix, self.sems, to_blocks=True, base=self.used)
         self.used += len(copies)
-        start(copies)
         self.sent += copies
+        return copies
+
+    def plan_in(self, blocks, refs, places, matrix):
+        copies = blocks.bind(refs, places, matrix, self.sems, base=self.used)
+        self.used += len(copies)
+        return copies
+
+    def store(self, blocks, refs, places, matrix):
+        start(self.plan(blocks, refs, places, matrix))
 
     def finish(self):
         wait(self.sent)
@@ -586,10 +606,24 @@
 
                 lax.fori_loop(0, C // 128, spread, 0)
                 lax.fori_loop(0, width // 128, shift, 0)
+            stage = 3 * C // size
+            out_copies = traffic.plan(out_blocks, targets, table_ref, grad)
+            ends = out_blocks.ends(table_ref)
+
             def part(i, carry):
-                cut = pl.ds(pl.multiple_of(lax.rem(i, 3 * C // size) * size, size), size)
+                cut = pl.ds(pl.multiple_of(lax.rem(i, stage) * size, size), size)
                 target = pl.ds(pl.multiple_of(i * size, size), size)
-                grad[target, :] = low(dot_sums(taps[:, cut], shifted[i // (3 * C // size)]))
+                grad[target, :] = low(dot_sums(taps[:, cut], shifted[i // stage]))
+
+                @pl.when(lax.rem(i, stage) == stage - 1)
+                def _():
+                    ready = (i + 1) * size
+                    for copy, end in zip(out_copies, ends):
+
+                        @pl.when((end <= ready) & (end > ready - 3 * C))
+                        def _(copy=copy):
+                            copy.start()
+
                 return carry
 
             lax.fori_loop(0, 9 * C // size, part, 0)
@@ -603,7 +637,8 @@
                 grad[target, :] = low(dot_sums(left[:, cut], right[...]))
 
             tiles(C, TILE, part)
-        traffic.store(out_blocks, targets, table_ref, grad)
+        if middle is None:
+            traffic.store(out_blocks, targets, table_ref, grad)
         traffic.finish()
 
     outs = [shaped(*array.shape, dtype=bf16) for array in out_blocks.operands]
@@ -706,18 +741,28 @@
         firsts = [refs.pop(0) for _ in range(n_first)]
         grad_u, sums, grad_pre1, other = [refs.pop(0) for _ in range(4)]
         turned = [refs.pop(0), refs.pop(0)] if closing else None
-        wm, wi, grad_ref, pre1_ref, direct_ref, taps, above, below, work, parts, sems = refs
+        wm, wi, grad_ref, pre1_ref, direct_ref, taps, above, work, parts, sems = refs
         traffic = Traffic(sems)
         given = traffic.begin(grads_in.at[1], grad_ref)
-        middle_copies = traffic.load(w_middle, middles, table_ref, wm)
+        middle_copies = traffic.plan_in(w_middle, middles, table_ref, wm)
+        stages = [lax.div(first, 3 * C) for first in w_middle.firsts(table_ref)]
+
+        def of_stage(stage, act):
+            for copy, own in zip(middle_copies, stages):
+
+                @pl.when(own == stage)
+                def _(copy=copy):
+                    act(copy)
+
+        for stage in range(3):
+            of_stage(stage, lambda copy: copy.start())
         pre1_copy = traffic.begin(pre1_in, pre1_ref)
         first_copies = traffic.load(w_first, firsts, table_ref, wi)
         direct_copy = traffic.begin(direct_in, direct_ref)
         parts[...] = jnp.zeros_like(parts)
         zeros = jnp.zeros((PAD, TILE), jnp.float32)
-        for ref in (above, below):
-            ref[:PAD, :] = zeros
-            ref[PAD + cells :, :] = zeros
+        above[:PAD, :] = zeros
+        above[PAD + cells :, :] = zeros
         given.wait()
 
         def spread(i, carry):
@@ -729,26 +774,29 @@
             return carry
 
         lax.fori_loop(0, C // 128, spread, 0)
-        wait(middle_copies)
-
-        def middle(i, carry):
-            def row(tap):
+        for tap in range(3):
+            of_stage(tap, lambda copy: copy.wait())
+
+            def middle(i, carry, tap=tap):
+                cut = pl.ds(pl.multiple_of(i * TILE, TILE), TILE)
                 total = None
                 for column in range(3):
                     source = pl.ds(pl.multiple_of((3 * tap + column) * C + i * TILE, TILE), TILE)
                     term = dot_rows(taps[:, column * C : (column + 1) * C], wm[source, :])
                     total = term if total is None else total + term
-                return total
-
-            above[PAD : PAD + cells, :] = row(0)
-            below[PAD : PAD + cells, :] = row(2)
-            cut = pl.ds(pl.multiple_of(i * TILE, TILE), TILE)
-            work[:, cut] = (
-                row(1) + above[PAD + side : PAD + side + cells, :] + below[PAD - side : PAD - side + cells, :]
-            )
-            return carry
-
-        lax.fori_loop(0, C // TILE, middle, 0)
+                if tap == 1:
+                    work[:, cut] += total
+                else:
+                    shift = side if tap == 0 else -side
+                    above[PAD : PAD + cells, :] = total
+                    moved = above[PAD + shift : PAD + shift + cells, :]
+                    if tap == 0:
+                        work[:, cut] = moved
+                    else:
+                        work[:, cut] += moved
+                return carry
+
+            lax.fori_loop(0, C // TILE, middle, 0)
         gain = misc_ref[3 * number : 3 * number + 1, :]
         bias = misc_ref[6 + 3 * number : 7 + 3 * number, :]
         pre1_copy.wait()
@@ -810,7 +858,6 @@
         pltpu.VMEM((cells, C), f32),
         pltpu.VMEM((cells, C), f32),
         pltpu.VMEM((cells, 3 * C), bf16),
-        pltpu.VMEM((cells + 2 * PAD, TILE), f32),
         pltpu.VMEM((cells + 2 * PAD, TILE), f32),
         pltpu.VMEM((cells, C), f32),
         pltpu.VMEM((16, C), f32),
@@ -1230,7 +1277,7 @@
         two.settle_line(two.first)
         settle(move, [two], [one], two.first)
         top.pass_on(four.passed[1])
-        cross(move, [], [three], three.first, four.passed[2])
+        cross(move, [], [three], three.first, four.held)
         three.settle_line(three.first)
         settle(move, [three], [two], three.first)
         cross(move, [four], [], three.far_first)
@@ -1326,16 +1373,16 @@
         top.pass_on(pooled)
         four.settle_line(pooled)
         settle(move, [], [four])
+    readout_bias = misc[12:].T.reshape(1, width)
     first_1, mid_1, last_1 = matrix("first_1"), matrix("middle_1"), matrix("last_1")
     if paired:
         top.end_line(pooled)
-        pooled = tie(pooled, top.passed[3])
+        pooled = tie(pooled, top.passed[3], readout_bias)
     lefts_1, pre1_1, pre2_1, pre3_1, first_1, last_1 = forward_block(
         table, 1, half_side, pooled, None, misc, first_1, mid_1, last_1
     )
     first_0, last_0, first_1, last_1 = [whole_matrix(array) for array in (first_0, last_0, first_1, last_1)]
     lefts_other_1 = swap(lefts_1)
-    readout_bias = misc[12:].T.reshape(1, width)
     output, grad_top, grad_readout_b, grad_logits, grad_logits_other = readout(
         table, grid_live, tie(lefts_1, lefts_other_0), readout_bias, cotangent[0], matrix("readout")
     )
@@ -1349,7 +1396,6 @@
         table, 1, half_side, grad_top, pooled, pre3_1, pre2_1, misc, last_1
     )
     if paired:
-        spread = Spread(move, grads_1[1], grad_logits_other)
         grads_other_1 = tie(grads_other_1, grad_logits_other)
     grads_other_1 = swap(grads_other_1)
     readout_terms = weight_terms(
@@ -1361,9 +1407,9 @@
     )
     if paired:
         sum_readout = Sum(move, readout_terms, "readout", levels=True)
-        spread.sides = after(spread.sides, *readout_terms)
-        sum_readout.across(grads_other_1, *spread.sides)
-        grads_1 = tie(grads_1, *readout_terms, *spread.sides)
+        spread = Spread(move, grads_1[1], *readout_terms)
+        sum_readout.across(grads_other_1)
+        grads_1 = tie(grads_1, *readout_terms, grads_other_1)
     else:
         middle_terms_1 = weight_terms(
             table,

time: 611 us -> 605 us (level)
    ppermute x34, waiting for transfers between devices: 76.1 us -> 56.4 us  [flip(): return lax.ppermute(value, 'dp', [(i, i ^ bits) for i in range(self.dp)])]
    ppermute x21, waiting for transfers between devices: 152 us -> 166 us  [along(): return lax.ppermute(value, 'dp', pairs)]
    ppermute x34, starting transfers between devices: 38.8 us -> 32.4 us  [flip(): return lax.ppermute(value, 'dp', [(i, i ^ bits) for i in range(self.dp)])]
    unnamed x150 -> x148, local copies, waits for them, and re-layouts: 22.7 us -> 23.9 us
  transfers between devices with their start and end apart: 90 -> 90, of which waited for: 47 -> 45; matrix products, arithmetic and copies ran while one was open for 7% -> 7% of each run, Pallas kernels for 34% -> 34%
where the time goes in v6:
time: 605 us; the launch traced here: 594 us
  waiting for transfers between devices  249 us (41%)
  Pallas kernels  204 us (34%)
  starting transfers between devices  55.2 us (9%)
  local copies, waits for them, and re-layouts  46.3 us (8%)
  other arithmetic  23.3 us (4%)
  between operations  16.3 us (3%)
    pallas_call x14, Pallas kernels, call(): pl.pallas_call(kernel, name=name, out_shape=outs, in_specs=in_specs, out_...  204 us
    ppermute x21, waiting for transfers between devices, along(): return lax.ppermute(value, 'dp', pairs)  166 us
    ppermute x34, waiting for transfers between devices, flip(): return lax.ppermute(value, 'dp', [(i, i ^ bits) for i in range(self.dp)])  56.4 us
    ppermute x34, starting transfers between devices, flip(): return lax.ppermute(value, 'dp', [(i, i ^ bits) for i in range(self.dp)])  32.4 us
    ppermute x33, waiting for transfers between devices, swap(): return lax.ppermute(value, 'fsdp', [(0, 1), (1, 0)])  26.7 us
    unnamed x148, local copies, waits for them, and re-layouts  23.9 us
    ppermute x21, starting transfers between devices, along(): return lax.ppermute(value, 'dp', pairs)  16.5 us
  transfers between devices with their start and end apart: 90, of which 45 were waited for; matrix products, arithmetic and copies ran while one was open for 7% of the time, Pallas kernels for 34%

profile of v6, /device:TPU:0, one launch (start us, length us, event | category | flops | bytes accessed | tf_op | source)
XLA Modules:
  0.0 594.0 jit_solution(10210947811578233612)
XLA Ops:
  11.6 3.1 collective-permute-start
  15.8 2.6 collective-permute-start.12
  21.5 1.9 collective-permute-start.3
  25.7 5.8 collective-permute-done.1
  35.2 2.8 collective-permute-done.2
  40.2 3.4 collective-permute-start.13
  44.2 4.5 collective-permute-done.13
  48.7 2.5 collective-permute-start.14
  51.3 5.1 collective-permute-done.14
  56.6 3.9 collective-permute-done.9.refs_5_.refs_31_
  62.7 9.1 %collective-permute-done.20 = bf16[208,1024]{1,0:T(8,128)(2,1)S(1)} collective-permute-done((bf16[208,1024]{1,0:T(8,128)(2,1)S(1)}, bf16[208,1024]{1,0:T(8,128)(2,1)S(1)}, u32[]{:S(2)}, u32[]{:S(2)}) %collective-permute-start.20) | collective-permute-done | bytes 426016 | tf_op jit(solution)/shard_map/three_line/ppermute | solution.py:964
  71.9 11.9 %collective-permute-done.21 = bf16[208,1024]{1,0:T(8,128)(2,1)S(1)} collective-permute-done((bf16[208,1024]{1,0:T(8,128)(2,1)S(1)}, bf16[208,1024]{1,0:T(8,128)(2,1)S(1)}, u32[]{:S(2)}, u32[]{:S(2)}) %collective-permute-start.21) | collective-permute-done | bytes 426016 | tf_op jit(solution)/shard_map/three_line/ppermute | solution.py:964
  84.0 8.8 %collective-permute-done.22 = bf16[208,1024]{1,0:T(8,128)(2,1)S(1)} collective-permute-done((bf16[208,1024]{1,0:T(8,128)(2,1)S(1)}, bf16[208,1024]{1,0:T(8,128)(2,1)S(1)}, u32[]{:S(2)}, u32[]{:S(2)}) %collective-permute-start.22) | collective-permute-done | bytes 426016 | tf_op jit(solution)/shard_map/three_line/ppermute | solution.py:964
  96.5 2.3 collective-permute-start.24
  98.9 16.0 %collective-permute-done.28 = bf16[288,1024]{1,0:T(8,128)(2,1)S(1)} collective-permute-done((bf16[288,1024]{1,0:T(8,128)(2,1)S(1)}, bf16[288,1024]{1,0:T(8,128)(2,1)S(1)}, u32[]{:S(2)}, u32[]{:S(2)}) %collective-permute-start.28) | collective-permute-done | bytes 589856 | tf_op jit(solution)/shard_map/four_line/ppermute | solution.py:964
  114.9 17.1 %collective-permute-done.29 = bf16[288,1024]{1,0:T(8,128)(2,1)S(1)} collective-permute-done((bf16[288,1024]{1,0:T(8,128)(2,1)S(1)}, bf16[288,1024]{1,0:T(8,128)(2,1)S(1)}, u32[]{:S(2)}, u32[]{:S(2)}) %collective-permute-start.29) | collective-permute-done | bytes 589856 | tf_op jit(solution)/shard_map/four_line/ppermute | solution.py:964
  135.0 11.2 %collective-permute-done.30 = bf16[288,1024]{1,0:T(8,128)(2,1)S(1)} collective-permute-done((bf16[288,1024]{1,0:T(8,128)(2,1)S(1)}, bf16[288,1024]{1,0:T(8,128)(2,1)S(1)}, u32[]{:S(2)}, u32[]{:S(2)}) %collective-permute-start.30) | collective-permute-done | bytes 589856 | tf_op jit(solution)/shard_map/four_line/ppermute | solution.py:964
  146.2 1.7 pad_maximum_fusion.refs_16_.refs_4_
  147.9 1.8 slice.224
  150.7 14.7 %collective-permute-done.33.refs_2_ = bf16[512,1024]{1,0:T(8,128)(2,1)} collective-permute-done((bf16[512,1024]{1,0:T(8,128)(2,1)}, bf16[512,1024]{1,0:T(8,128)(2,1)}, u32[]{:S(2)}, u32[]{:S(2)}) %collective-permute-start.33) | collective-permute-done | bytes 1048608 | tf_op jit(solution)/shard_map/top_line/ppermute | solution.py:964
  166.0 4.0 collective-permute-done.11.refs_6_.refs_32_
  172.4 2.4 collective-permute-done.35.refs_26_.refs_11_.refs_31_.refs_19_
  174.9 6.9 %collective-permute-done.27.refs_22_.refs_3_.refs_23_.refs_15_ = bf16[832,1024]{1,0:T(8,128)(2,1)S(1)} collective-permute-done((bf16[832,1024]{1,0:T(8,128)(2,1)S(1)}, bf16[832,1024]{1,0:T(8,128)(2,1)S(1)}, u32[]{:S(2)}, u32[]{:S(2)}) %collective-permute-start.27) | collective-permute-done | bytes 1703968 | tf_op jit(solution)/shard_map/swap/ppermute | solution.py:967
  184.3 31.1 %forward_block.2 = (f32[16,1024]{1,0:T(8,128)}, f32[144,1024]{1,0:T(8,128)}, f32[576,1024]{1,0:T(8,128)}, bf16[3,576,1024]{2,1,0:T(8,128)(2,1)}, f32[576,1024]{1...) custom-call(s32[165]{0:T(256)} %bitcast.127, ...), custom_call_target="tpu_custom_call" | custom-call | flops 265751104 | bytes 697303 | tf_op jit(solution)/shard_map/forward_block/pallas_call | solution.py:156
  215.9 10.4 %collective-permute-done.38.refs_12_.refs_0_ = bf16[1152,1024]{1,0:T(8,128)(2,1)} collective-permute-done((bf16[1152,1024]{1,0:T(8,128)(2,1)}, bf16[1152,1024]{1,0:T(8,128)(2,1)}, u32[]{:S(2)}, u32[]{:S(2)}) %collective-permute-start.38) | collective-permute-done | bytes 2359328 | tf_op jit(solution)/shard_map/four_plane/ppermute | solution.py:957
  226.3 2.4 collective-permute-done.39.refs_14_.refs_2_
  232.0 10.5 %collective-permute-done.37.refs_6_ = bf16[512,1024]{1,0:T(8,128)(2,1)} collective-permute-done((bf16[512,1024]{1,0:T(8,128)(2,1)}, bf16[512,1024]{1,0:T(8,128)(2,1)}, u32[]{:S(2)}, u32[]{:S(2)}) %collective-permute-start.37) | collective-permute-done | bytes 1048608 | tf_op jit(solution)/shard_map/top_line/ppermute | solution.py:964
  242.5 16.5 %collective-permute-done.43.refs_18_.refs_6_ = bf16[576,1024]{1,0:T(8,128)(2,1)S(1)} collective-permute-done((bf16[576,1024]{1,0:T(8,128)(2,1)S(1)}, bf16[576,1024]{1,0:T(8,128)(2,1)S(1)}, u32[]{:S(2)}, u32[]{:S(2)}) %collective-permute-start.43) | collective-permute-done | bytes 1179680 | tf_op jit(solution)/shard_map/four_plane/ppermute | solution.py:957
  260.6 4.7 collective-permute-done.44.refs_19_.refs_7_
  270.3 2.0 reshape.64.bias_ref
  272.3 16.6 %forward_block.3 = (bf16[4,144,1024]{2,1,0:T(8,128)(2,1)}, f32[144,1024]{1,0:T(8,128)}, f32[144,1024]{1,0:T(8,128)}, f32[144,1024]{1,0:T(8,128)}, bf16[1024,1024...) custom-call(s32[165]{0:T(256)} %bitcast.128, f32[144,1024]{1,0:T(8,128)} %get-tuple-element.189.refs_0_.u_in, ...), custom_call_target="tpu_custom_call" | custom-call | flops 66437776 | bytes 520355 | tf_op jit(solution)/shard_map/forward_block/pallas_call | solution.py:156
  291.0 2.7 collective-permute-start.54
  294.4 15.2 %readout.1 = (bf16[144,4096]{1,0:T(8,128)(2,1)}, f32[144,1024]{1,0:T(8,128)}, f32[1,4096]{1,0:T(1,128)}, bf16[144,2048]{1,0:T(8,128)(2,1)}, bf16[144,2048]{1,0:T(8,128)(2,1)}) custom-call(s32[165]{0:T(256)} %bitcast.129, s32[1]{0:T(128)S(6)} %copy.74.live_ref, bf16[4,144,1024]{2,1,0:T(8,128)(2,1)} %get-tuple-element.199.lefts_ref.refs_0_.refs_4_.refs_8_, ...), custom_call_target="tpu_custom_call" | custom-call | flops 603979776 | bytes 2686976 | tf_op jit(solution)/shard_map/readout/pallas_call | solution.py:156
  309.7 6.3 %back_last.2 = (f32[144,1024]{1,0:T(8,128)}, bf16[2,144,1024]{2,1,0:T(8,128)(2,1)}, bf16[2,144,512]{2,1,0:T(8,128)(2,1)}, f32[4,1024]{1,0:T(4,128)}) custom-call(s32[165]{0:T(256)} %bitcast.130, f32[144,1024]{1,0:T(8,128)} %get-tuple-element.206.grad_ref, f32[144,1024]{1,0:T(8,128)} %get-tuple-element.189.refs_0_.u_in, ...), custom_call_target="tpu_custom_call" | custom-call | flops 75497472 | bytes 1409024 | tf_op jit(solution)/shard_map/back_last/pallas_call | solution.py:156
  316.8 7.3 %weight_terms.3 = (bf16[4,64,2048]{2,1,0:T(8,128)(2,1)}, bf16[4,64,2048]{2,1,0:T(8,128)(2,1)}, bf16[2,64,2048]{2,1,0:T(8,128)(2,1)}, bf16[2,64,2048]{2,1,0:T(8,128)(2,1)}, bf16[4,64,2048]{2,1,0:T(8,128)(2,1)}) custom-call(s32[165]{0:T(256)} %bitcast.131, bf16[4,144,1024]{2,1,0:T(8,128)(2,1)} %get-tuple-element.199.lefts_ref.refs_0_.refs_4_.refs_8_, ...), custom_call_target="tpu_custom_call" | custom-call | flops 301989888 | bytes 1343488 | tf_op jit(solution)/shard_map/weight_terms/pallas_call | solution.py:156
  325.7 1.8 collective-permute-start.60
  329.2 15.1 %back_first.2 = (f32[144,1024]{1,0:T(8,128)}, f32[2,1024]{1,0:T(2,128)}, bf16[1,144,1024]{2,1,0:T(8,128)(2,1)}, bf16[144,512]{1,0:T(8,128)(2,1)}) custom-call(s32[165]{0:T(256)} %bitcast.132, bf16[2,144,1024]{2,1,0:T(8,128)(2,1)} %get-tuple-element.223.grads_in.refs_9_, f32[144,1024]{1,0:T(8,128)} %get-tuple-element.224.pre1_in, ...), custom_call_target="tpu_custom_call" | custom-call | flops 754974720 | bytes 6127616 | tf_op jit(solution)/shard_map/back_first/pallas_call | solution.py:156
  344.3 23.6 %back_last.3 = (f32[576,1024]{1,0:T(8,128)}, bf16[2,576,1024]{2,1,0:T(8,128)(2,1)}, bf16[2,576,512]{2,1,0:T(8,128)(2,1)}, f32[4,1024]{1,0:T(4,128)}) custom-call(s32[165]{0:T(256)} %bitcast.133, f32[144,1024]{1,0:T(8,128)} %get-tuple-element.227.grad_ref, f32[576,1024]{1,0:T(8,128)} %get-tuple-element.228.u_in, f32[576,1024]{1,0:T(8,128)} %get-tuple-element.229.pre3_in, ...), custom_call_target="tpu_custom_call" | custom-call | flops 301989888 | bytes 4063232 | tf_op jit(solution)/shard_map/back_last/pallas_call | solution.py:156
  375.2 1.7 collective-permute-start.63
  379.5 24.9 %weight_terms.4 = (bf16[4,576,512]{2,1,0:T(8,128)(2,1)}, bf16[4,576,512]{2,1,0:T(8,128)(2,1)}, bf16[2,576,512]{2,1,0:T(8,128)(2,1)}, bf16[2,576,512]{2,1,0:T(8,128)(2,1)}, bf16[4,576,512]{2,1,0:T(8,128)(2,1)}) custom-call(s32[165]{0:T(256)} %bitcast.134, bf16[3,576,1024]{2,1,0:T(8,128)(2,1)} %get-tuple-element.198.refs_0_.refs_12_, ...), custom_call_target="tpu_custom_call" | custom-call | flops 2717908992 | bytes 3538944 | tf_op jit(solution)/shard_map/weight_terms/pallas_call | solution.py:156
  404.5 2.4 add_convert_fusion.6
  411.4 15.0 %plane_terms.1 = bf16[4,288,1024]{2,1,0:T(8,128)(2,1)} custom-call(s32[165]{0:T(256)} %bitcast.135, bf16[576,1024]{1,0:T(8,128)(2,1)} %copy-done.29, bf16[576,1024]{1,0:T(8,128)(2,1)} %collective-permute-done.67.refs_1_, bf16[576,1024]{1,0:T(8,128)(2,1)} %copy-done.28, bf16[576,1024]{1,0:T(8,128)(2,1)} %collective-permute-done.66.refs_3_), custom_call_target="tpu_custom_call" | custom-call | flops 905969664 | bytes 1769472 | tf_op jit(solution)/shard_map/plane_terms/pallas_call | solution.py:156
  426.4 28.1 %back_first.3 = (f32[576,1024]{1,0:T(8,128)}, f32[2,1024]{1,0:T(2,128)}, bf16[1,576,1024]{2,1,0:T(8,128)(2,1)}, bf16[576,512]{1,0:T(8,128)(2,1)}, bf16[1024,384]{1,0:T(8,128)(2,1)}, /*index=5*/bf16[1024,384]{1,0:T(8,128)(2,1)}) custom-call(s32[165]{0:T(256)} %bitcast.136, bf16[2,576,1024]{2,1,0:T(8,128)(2,1)} %get-tuple-element.268.refs_1_.grads_in, ...), custom_call_target="tpu_custom_call" | custom-call | flops 3019898880 | bytes 8781824 | tf_op jit(solution)/shard_map/back_first/pallas_call | solution.py:156
  454.5 6.4 %collective-permute-done.68 = bf16[4,576,512]{2,1,0:T(8,128)(2,1)S(1)} collective-permute-done((bf16[4,576,512]{2,1,0:T(8,128)(2,1)}, bf16[4,576,512]{2,1,0:T(8,128)(2,1)S(1)}, u32[]{:S(2)}, u32[]{:S(2)}) %collective-permute-start.68) | collective-permute-done | bytes 2359328 | tf_op jit(solution)/shard_map/middle_0_across/ppermute | solution.py:957
  463.2 2.7 add_convert_fusion.1
  467.9 3.0 collective-permute-done.70.refs_7_
  471.9 13.7 %weight_terms.5 = (bf16[4,320,512]{2,1,0:T(8,128)(2,1)}, bf16[4,320,512]{2,1,0:T(8,128)(2,1)}, bf16[2,320,512]{2,1,0:T(8,128)(2,1)}, bf16[2,320,512]{2,1,0:T(8,128)(2,1)}, bf16[4,320,512]{2,1,0:T(8,128)(2,1)}) custom-call(s32[165]{0:T(256)} %bitcast.137, bf16[3,576,1024]{2,1,0:T(8,128)(2,1)} %get-tuple-element.198.refs_0_.refs_12_, ...), custom_call_target="tpu_custom_call" | custom-call | flops 754974720 | bytes 3997696 | tf_op jit(solution)/shard_map/weight_terms/pallas_call | solution.py:156
  485.6 7.0 %collective-permute-done.73 = bf16[2,576,512]{2,1,0:T(8,128)(2,1)S(1)} collective-permute-done((bf16[2,576,512]{2,1,0:T(8,128)(2,1)}, bf16[2,576,512]{2,1,0:T(8,128)(2,1)S(1)}, u32[]{:S(2)}, u32[]{:S(2)}) %collective-permute-start.73) | collective-permute-done | bytes 1179680 | tf_op jit(solution)/shard_map/middle_0_onward/ppermute | solution.py:957
  494.0 3.7 convert_add_fusion
  506.2 1.9 place_halves.2
  508.1 17.4 %collective-permute-done.82 = bf16[576,512]{1,0:T(8,128)(2,1)} collective-permute-done((bf16[576,512]{1,0:T(8,128)(2,1)}, bf16[576,512]{1,0:T(8,128)(2,1)}, u32[]{:S(2)}, u32[]{:S(2)}) %collective-permute-start.82) | collective-permute-done | bytes 589856 | tf_op jit(solution)/shard_map/middle_0_line/ppermute | solution.py:964
  525.5 1.6 add_convert_fusion.4
  534.5 7.9 %collective-permute-done.83 = bf16[576,512]{1,0:T(8,128)(2,1)S(1)} collective-permute-done((bf16[576,512]{1,0:T(8,128)(2,1)S(1)}, bf16[576,512]{1,0:T(8,128)(2,1)S(1)}, u32[]{:S(2)}, u32[]{:S(2)}) %collective-permute-start.83) | collective-permute-done | bytes 589856 | tf_op jit(solution)/shard_map/middle_0_line/ppermute | solution.py:964
  542.7 1.7 collective-permute-done.78
  544.3 2.6 collective-permute-done.79
  546.9 2.8 convert_add_fusion.2
  549.8 1.9 collective-permute-start.80
  551.7 8.1 %collective-permute-done.84 = bf16[576,512]{1,0:T(8,128)(2,1)S(1)} collective-permute-done((bf16[576,512]{1,0:T(8,128)(2,1)S(1)}, bf16[576,512]{1,0:T(8,128)(2,1)S(1)}, u32[]{:S(2)}, u32[]{:S(2)}) %collective-permute-start.84) | collective-permute-done | bytes 589856 | tf_op jit(solution)/shard_map/middle_0_line/ppermute | solution.py:964
  560.9 3.0 collective-permute-done.80
  565.0 3.1 place_halves.3
  568.1 4.0 collective-permute-done.81
  572.3 8.0 %collective-permute-done.86 = bf16[320,512]{1,0:T(8,128)(2,1)S(1)} collective-permute-done((bf16[320,512]{1,0:T(8,128)(2,1)S(1)}, bf16[320,512]{1,0:T(8,128)(2,1)S(1)}, u32[]{:S(2)}, u32[]{:S(2)}) %collective-permute-start.86) | collective-permute-done | bytes 327712 | tf_op jit(solution)/shard_map/last_line/ppermute | solution.py:964
  581.1 1.6 collective-permute-done.87.other_ref
  583.5 1.9 place_last.1
  (344 shorter events, 92.3 us)
Async XLA Ops:
  7.2 495.0 %reduce-scatter.3.cloned.1.call-start = ((), (), s32[]{:S(2)}) async-start(), calls=%async_computation.2 | async-start | bytes 1310720 | tf_op jit(solution)/shard_map/readout_line/reduce_scatter | solution.py:1161
  11.6 9.8 %collective-permute-start = (bf16[96,1024]{1,0:T(8,128)(2,1)S(1)}, bf16[96,1024]{1,0:T(8,128)(2,1)S(1)}, u32[]{:S(2)}, u32[]{:S(2)}) collective-permute-start(bf16[96,1024]{1,0:T(8,128)(2,1)S(1)} %pad_maximum_fusion.5), channel_id=1, source_target_pairs={{0,8},{2,10},{4,12},{6,14},{8,24},{10,26},{12,28},{14,30},{24,16},... | collective-permute-start | bytes 589832 | tf_op jit(solution)/shard_map/one_line/ppermute | solution.py:964
  15.8 24.4 %collective-permute-start.12 = (bf16[144,1024]{1,0:T(8,128)(2,1)S(1)}, bf16[144,1024]{1,0:T(8,128)(2,1)S(1)}, u32[]{:S(2)}, u32[]{:S(2)}) collective-permute-start(bf16[144,1024]{1,0:T(8,128)(2,1)S(1)} %get-tuple-element.318), channel_id=1, source_target_pairs={{0,8},{2,10},{4,12},{6,14},{8,24},{10,26},{12,28},{14,30},{24,16},... | collective-permute-start | bytes 884744 | tf_op jit(solution)/shard_map/two_line/ppermute | solution.py:964
  21.5 10.8 %collective-permute-start.3 = (bf16[128,1024]{1,0:T(8,128)(2,1)S(1)}, bf16[128,1024]{1,0:T(8,128)(2,1)S(1)}, u32[]{:S(2)}, u32[]{:S(2)}) collective-permute-start(bf16[128,1024]{1,0:T(8,128)(2,1)S(1)} %pad_maximum_fusion.4), channel_id=1, source_target_pairs={{0,2},{2,0},{4,6},{6,4},{8,10},{10,8},{12,14},{14,12},{16,18},{18,... | collective-permute-start | bytes 786440 | tf_op jit(solution)/shard_map/top_plane/ppermute | solution.py:957
  23.3 10.3 %collective-permute-start.5 = (bf16[128,1024]{1,0:T(8,128)(2,1)S(1)}, bf16[128,1024]{1,0:T(8,128)(2,1)S(1)}, u32[]{:S(2)}, u32[]{:S(2)}) collective-permute-start(bf16[128,1024]{1,0:T(8,128)(2,1)S(1)} %pad_maximum_fusion.4), channel_id=1, source_target_pairs={{0,4},{2,6},{4,0},{6,2},{8,12},{10,14},{12,8},{14,10},{16,20},{18,... | collective-permute-start | bytes 786440 | tf_op jit(solution)/shard_map/top_plane/ppermute | solution.py:957
  38.7 17.8 %collective-permute-start.7 = (bf16[384,1024]{1,0:T(8,128)(2,1)S(1)}, bf16[384,1024]{1,0:T(8,128)(2,1)S(1)}, u32[]{:S(2)}, u32[]{:S(2)}) collective-permute-start(bf16[384,1024]{1,0:T(8,128)(2,1)S(1)} %constant_dynamic-update-slice_fusion.refs_1_.refs_27_), channel_id=1, source_target_pairs={{0,2},{2,0},{4,6},{6,4},{8,10},{10,8},{12,14},{14,12},{16,18},{18,... | collective-permute-start | bytes 2359304 | tf_op jit(solution)/shard_map/one_plane/ppermute | solution.py:957
  43.6 16.9 %collective-permute-start.9 = (bf16[384,1024]{1,0:T(8,128)(2,1)S(1)}, bf16[384,1024]{1,0:T(8,128)(2,1)S(1)}, u32[]{:S(2)}, u32[]{:S(2)}) collective-permute-start(bf16[384,1024]{1,0:T(8,128)(2,1)S(1)} %constant_dynamic-update-slice_fusion.refs_1_.refs_27_), channel_id=1, source_target_pairs={{0,4},{2,6},{4,0},{6,2},{8,12},{10,14},{12,8},{14,10},{16,20},{18,... | collective-permute-start | bytes 2359304 | tf_op jit(solution)/shard_map/one_plane/ppermute | solution.py:957
  60.5 32.8 %collective-permute-start.15 = (bf16[768,1024]{1,0:T(8,128)(2,1)S(1)}, bf16[768,1024]{1,0:T(8,128)(2,1)S(1)}, u32[]{:S(2)}, u32[]{:S(2)}) collective-permute-start(bf16[768,1024]{1,0:T(8,128)(2,1)S(1)} %slice_dynamic-update-slice_fusion.3), channel_id=1, source_target_pairs={{0,2},{2,0},{4,6},{6,4},{8,10},{10,8},{12,14},{14,12},{16,18},{18,... | collective-permute-start | bytes 4718600 | tf_op jit(solution)/shard_map/two_one_plane/ppermute | solution.py:957
  60.6 11.1 %collective-permute-start.20 = (bf16[208,1024]{1,0:T(8,128)(2,1)S(1)}, bf16[208,1024]{1,0:T(8,128)(2,1)S(1)}, u32[]{:S(2)}, u32[]{:S(2)}) collective-permute-start(bf16[208,1024]{1,0:T(8,128)(2,1)S(1)} %pad_maximum_fusion.3), channel_id=1, source_target_pairs={{0,8},{2,10},{4,12},{6,14},{8,24},{10,26},{12,28},{14,30},{24,16},... | collective-permute-start | bytes 1277960 | tf_op jit(solution)/shard_map/three_line/ppermute | solution.py:964
  61.4 33.6 %collective-permute-start.16 = (bf16[768,1024]{1,0:T(8,128)(2,1)S(1)}, bf16[768,1024]{1,0:T(8,128)(2,1)S(1)}, u32[]{:S(2)}, u32[]{:S(2)}) collective-permute-start(bf16[768,1024]{1,0:T(8,128)(2,1)S(1)} %slice_dynamic-update-slice_fusion.2), channel_id=1, source_target_pairs={{0,4},{2,6},{4,0},{6,2},{8,12},{10,14},{12,8},{14,10},{16,20},{18,... | collective-permute-start | bytes 4718600 | tf_op jit(solution)/shard_map/two_one_plane/ppermute | solution.py:957
  71.7 12.1 %collective-permute-start.21 = (bf16[208,1024]{1,0:T(8,128)(2,1)S(1)}, bf16[208,1024]{1,0:T(8,128)(2,1)S(1)}, u32[]{:S(2)}, u32[]{:S(2)}) collective-permute-start(bf16[208,1024]{1,0:T(8,128)(2,1)S(1)} %collective-permute-done.20), channel_id=1, source_target_pairs={{0,8},{2,10},{4,12},{6,14},{8,24},{10,26},{12,28},{14,30},{24,16},... | collective-permute-start | bytes 1277960 | tf_op jit(solution)/shard_map/three_line/ppermute | solution.py:964
  95.0 52.8 %collective-permute-start.23 = (bf16[1120,1024]{1,0:T(8,128)(2,1)S(1)}, bf16[1120,1024]{1,0:T(8,128)(2,1)S(1)}, u32[]{:S(2)}, u32[]{:S(2)}) collective-permute-start(bf16[1120,1024]{1,0:T(8,128)(2,1)S(1)} %slice_dynamic-update-slice_fusion.1), channel_id=1, source_target_pairs={{0,2},{2,0},{4,6},{6,4},{8,10},{10,8},{12,14},{14,12},{16,18},{18,... | collective-permute-start | bytes 6881288 | tf_op jit(solution)/shard_map/three_two_plane/ppermute | solution.py:957
  96.5 51.4 %collective-permute-start.24 = (bf16[1120,1024]{1,0:T(8,128)(2,1)S(1)}, bf16[1120,1024]{1,0:T(8,128)(2,1)}, u32[]{:S(2)}, u32[]{:S(2)}) collective-permute-start(bf16[1120,1024]{1,0:T(8,128)(2,1)S(1)} %slice_dynamic-update-slice_fusion), channel_id=1, source_target_pairs={{0,4},{2,6},{4,0},{6,2},{8,12},{10,14},{12,8},{14,10},{16,20},{18,... | collective-permute-start | bytes 6881288 | tf_op jit(solution)/shard_map/three_two_plane/ppermute | solution.py:957
  98.8 16.0 %collective-permute-start.28 = (bf16[288,1024]{1,0:T(8,128)(2,1)S(1)}, bf16[288,1024]{1,0:T(8,128)(2,1)S(1)}, u32[]{:S(2)}, u32[]{:S(2)}) collective-permute-start(bf16[288,1024]{1,0:T(8,128)(2,1)S(1)} %slice_bitcast_fusion.6), channel_id=1, source_target_pairs={{0,8},{2,10},{4,12},{6,14},{8,24},{10,26},{12,28},{14,30},{24,16},... | collective-permute-start | bytes 1769480 | tf_op jit(solution)/shard_map/four_line/ppermute | solution.py:964
  114.9 17.1 %collective-permute-start.29 = (bf16[288,1024]{1,0:T(8,128)(2,1)S(1)}, bf16[288,1024]{1,0:T(8,128)(2,1)S(1)}, u32[]{:S(2)}, u32[]{:S(2)}) collective-permute-start(bf16[288,1024]{1,0:T(8,128)(2,1)S(1)} %collective-permute-done.28), channel_id=1, source_target_pairs={{0,8},{2,10},{4,12},{6,14},{8,24},{10,26},{12,28},{14,30},{24,16},... | collective-permute-start | bytes 1769480 | tf_op jit(solution)/shard_map/four_line/ppermute | solution.py:964
  132.0 14.2 %collective-permute-start.30 = (bf16[288,1024]{1,0:T(8,128)(2,1)S(1)}, bf16[288,1024]{1,0:T(8,128)(2,1)S(1)}, u32[]{:S(2)}, u32[]{:S(2)}) collective-permute-start(bf16[288,1024]{1,0:T(8,128)(2,1)S(1)} %collective-permute-done.29), channel_id=1, source_target_pairs={{0,8},{2,10},{4,12},{6,14},{8,24},{10,26},{12,28},{14,30},{24,16},... | collective-permute-start | bytes 1769480 | tf_op jit(solution)/shard_map/four_line/ppermute | solution.py:964
  134.7 15.3 %collective-permute-start.10 = (bf16[384,1024]{1,0:T(8,128)(2,1)S(1)}, bf16[384,1024]{1,0:T(8,128)(2,1)S(1)}, u32[]{:S(2)}, u32[]{:S(2)}) collective-permute-start(bf16[384,1024]{1,0:T(8,128)(2,1)S(1)} %collective-permute-done.7.refs_3_.refs_29_), channel_id=1, source_target_pairs={{0,1},{1,0},{2,3},{3,2},{4,5},{5,4},{6,7},{7,6},{8,9},{9,8},{10,11... | collective-permute-start | bytes 2359304 | tf_op jit(solution)/shard_map/swap/ppermute | solution.py:967
  134.7 30.6 %collective-permute-start.33 = (bf16[512,1024]{1,0:T(8,128)(2,1)}, bf16[512,1024]{1,0:T(8,128)(2,1)}, u32[]{:S(2)}, u32[]{:S(2)}) collective-permute-start(bf16[512,1024]{1,0:T(8,128)(2,1)} %constant_dynamic-update-slice_fusion.32.refs_0_), channel_id=1, source_target_pairs={{0,8},{2,10},{4,12},{6,14},{8,24},{10,26},{12,28},{14,30},{24,16},... | collective-permute-start | bytes 3145736 | tf_op jit(solution)/shard_map/top_line/ppermute | solution.py:964
  149.8 15.6 %collective-permute-start.31 = (bf16[416,1024]{1,0:T(8,128)(2,1)S(1)}, bf16[416,1024]{1,0:T(8,128)(2,1)S(1)}, u32[]{:S(2)}, u32[]{:S(2)}) collective-permute-start(bf16[416,1024]{1,0:T(8,128)(2,1)S(1)} %slice.224), channel_id=1, source_target_pairs={{0,2},{2,0},{4,6},{6,4},{8,10},{10,8},{12,14},{14,12},{16,18},{18,... | collective-permute-start | bytes 2555912 | tf_op jit(solution)/shard_map/three_plane/ppermute | solution.py:957
  149.8 16.1 %collective-permute-start.32 = (bf16[416,1024]{1,0:T(8,128)(2,1)S(1)}, bf16[416,1024]{1,0:T(8,128)(2,1)S(1)}, u32[]{:S(2)}, u32[]{:S(2)}) collective-permute-start(bf16[416,1024]{1,0:T(8,128)(2,1)S(1)} %slice.225), channel_id=1, source_target_pairs={{0,4},{2,6},{4,0},{6,2},{8,12},{10,14},{12,8},{14,10},{16,20},{18,... | collective-permute-start | bytes 2555912 | tf_op jit(solution)/shard_map/three_plane/ppermute | solution.py:957
  149.9 21.2 %collective-permute-start.17 = (bf16[768,1024]{1,0:T(8,128)(2,1)S(1)}, bf16[768,1024]{1,0:T(8,128)(2,1)S(1)}, u32[]{:S(2)}, u32[]{:S(2)}) collective-permute-start(bf16[768,1024]{1,0:T(8,128)(2,1)S(1)} %collective-permute-done.15.refs_7_.refs_13_.refs_33_.refs_6_), channel_id=1, source_target_pairs={{0,1},{1,0},{2,3},{3,2},{4,5},{5,4},{6,7},{7,6},{8,9},{9,8},{10,11... | collective-permute-start | bytes 4718600 | tf_op jit(solution)/shard_map/swap/ppermute | solution.py:967
  150.0 21.3 %collective-permute-start.18 = (bf16[768,1024]{1,0:T(8,128)(2,1)S(1)}, bf16[768,1024]{1,0:T(8,128)(2,1)S(1)}, u32[]{:S(2)}, u32[]{:S(2)}) collective-permute-start(bf16[768,1024]{1,0:T(8,128)(2,1)S(1)} %collective-permute-done.16.refs_9_.refs_15_.refs_35_.refs_8_), channel_id=1, source_target_pairs={{0,1},{1,0},{2,3},{3,2},{4,5},{5,4},{6,7},{7,6},{8,9},{9,8},{10,11... | collective-permute-start | bytes 4718600 | tf_op jit(solution)/shard_map/swap/ppermute | solution.py:967
  170.7 11.1 %collective-permute-start.27 = (bf16[832,1024]{1,0:T(8,128)(2,1)S(1)}, bf16[832,1024]{1,0:T(8,128)(2,1)S(1)}, u32[]{:S(2)}, u32[]{:S(2)}) collective-permute-start(bf16[832,1024]{1,0:T(8,128)(2,1)S(1)} %get-tuple-element.178.refs_21_.refs_2_.refs_22_.refs_14_), channel_id=1, source_target_pairs={{0,1},{1,0},{2,3},{3,2},{4,5},{5,4},{6,7},{7,6},{8,9},{9,8},{10,11... | collective-permute-start | bytes 5111816 | tf_op jit(solution)/shard_map/swap/ppermute | solution.py:967
  171.1 13.2 %collective-permute-start.25 = (bf16[1120,1024]{1,0:T(8,128)(2,1)S(1)}, bf16[1120,1024]{1,0:T(8,128)(2,1)}, u32[]{:S(2)}, u32[]{:S(2)}) collective-permute-start(bf16[1120,1024]{1,0:T(8,128)(2,1)S(1)} %collective-permute-done.23.refs_17_.refs_4_.refs_24_.refs_10_), channel_id=1, source_target_pairs={{0,1},{1,0},{2,3},{3,2},{4,5},{5,4},{6,7},{7,6},{8,9},{9,8},{10,11... | collective-permute-start | bytes 6881288 | tf_op jit(solution)/shard_map/swap/ppermute | solution.py:967
  171.3 13.0 %collective-permute-start.26 = (bf16[1120,1024]{1,0:T(8,128)(2,1)}, bf16[1120,1024]{1,0:T(8,128)(2,1)}, u32[]{:S(2)}, u32[]{:S(2)}) collective-permute-start(bf16[1120,1024]{1,0:T(8,128)(2,1)} %collective-permute-done.24.refs_19_.refs_6_.refs_26_.refs_12_), channel_id=1, source_target_pairs={{0,1},{1,0},{2,3},{3,2},{4,5},{5,4},{6,7},{7,6},{8,9},{9,8},{10,11... | collective-permute-start | bytes 6881288 | tf_op jit(solution)/shard_map/swap/ppermute | solution.py:967
  172.4 53.8 %collective-permute-start.38 = (bf16[1152,1024]{1,0:T(8,128)(2,1)}, bf16[1152,1024]{1,0:T(8,128)(2,1)}, u32[]{:S(2)}, u32[]{:S(2)}) collective-permute-start(bf16[1152,1024]{1,0:T(8,128)(2,1)} %pad_maximum_fusion.refs_16_.refs_4_), channel_id=1, source_target_pairs={{0,2},{2,0},{4,6},{6,4},{8,10},{10,8},{12,14},{14,12},{16,18},{18,... | collective-permute-start | bytes 7077896 | tf_op jit(solution)/shard_map/four_plane/ppermute | solution.py:957
  174.9 53.8 %collective-permute-start.39 = (bf16[1152,1024]{1,0:T(8,128)(2,1)}, bf16[1152,1024]{1,0:T(8,128)(2,1)}, u32[]{:S(2)}, u32[]{:S(2)}) collective-permute-start(bf16[1152,1024]{1,0:T(8,128)(2,1)} %pad_maximum_fusion.refs_16_.refs_4_), channel_id=1, source_target_pairs={{0,4},{2,6},{4,0},{6,2},{8,12},{10,14},{12,8},{14,10},{16,20},{18,... | collective-permute-start | bytes 7077896 | tf_op jit(solution)/shard_map/four_plane/ppermute | solution.py:957
  183.0 32.9 %collective-permute-start.36 = (bf16[512,1024]{1,0:T(8,128)(2,1)}, bf16[512,1024]{1,0:T(8,128)(2,1)}, u32[]{:S(2)}, u32[]{:S(2)}) collective-permute-start(bf16[512,1024]{1,0:T(8,128)(2,1)} %collective-permute-done.33.refs_2_), channel_id=1, source_target_pairs={{0,8},{2,10},{4,12},{6,14},{8,24},{10,26},{12,28},{14,30},{24,16},... | collective-permute-start | bytes 3145736 | tf_op jit(solution)/shard_map/top_line/ppermute | solution.py:964
  215.4 44.7 %collective-permute-start.42 = (bf16[1152,1024]{1,0:T(8,128)(2,1)}, bf16[1152,1024]{1,0:T(8,128)(2,1)}, u32[]{:S(2)}, u32[]{:S(2)}) collective-permute-start(bf16[1152,1024]{1,0:T(8,128)(2,1)} %pad_maximum_fusion.refs_16_.refs_4_), channel_id=1, source_target_pairs={{0,1},{1,0},{2,3},{3,2},{4,5},{5,4},{6,7},{7,6},{8,9},{9,8},{10,11... | collective-permute-start | bytes 7077896 | tf_op jit(solution)/shard_map/swap/ppermute | solution.py:967
  215.8 26.7 %collective-permute-start.37 = (bf16[512,1024]{1,0:T(8,128)(2,1)}, bf16[512,1024]{1,0:T(8,128)(2,1)}, u32[]{:S(2)}, u32[]{:S(2)}) collective-permute-start(bf16[512,1024]{1,0:T(8,128)(2,1)} %collective-permute-done.36.refs_4_), channel_id=1, source_target_pairs={{0,8},{2,10},{4,12},{6,14},{8,24},{10,26},{12,28},{14,30},{24,16},... | collective-permute-start | bytes 3145736 | tf_op jit(solution)/shard_map/top_line/ppermute | solution.py:964
  231.6 27.5 %collective-permute-start.43 = (bf16[576,1024]{1,0:T(8,128)(2,1)S(1)}, bf16[576,1024]{1,0:T(8,128)(2,1)S(1)}, u32[]{:S(2)}, u32[]{:S(2)}) collective-permute-start(bf16[576,1024]{1,0:T(8,128)(2,1)S(1)} %slice.186), channel_id=1, source_target_pairs={{0,2},{2,0},{4,6},{6,4},{8,10},{10,8},{12,14},{14,12},{16,18},{18,... | collective-permute-start | bytes 3538952 | tf_op jit(solution)/shard_map/four_plane/ppermute | solution.py:957
  231.6 27.5 %collective-permute-start.45 = (bf16[576,1024]{1,0:T(8,128)(2,1)S(1)}, bf16[576,1024]{1,0:T(8,128)(2,1)S(1)}, u32[]{:S(2)}, u32[]{:S(2)}) collective-permute-start(bf16[576,1024]{1,0:T(8,128)(2,1)S(1)} %slice.187), channel_id=1, source_target_pairs={{0,4},{2,6},{4,0},{6,2},{8,12},{10,14},{12,8},{14,10},{16,20},{18,... | collective-permute-start | bytes 3538952 | tf_op jit(solution)/shard_map/four_plane/ppermute | solution.py:957
  232.0 59.0 %collective-permute-start.47 = (bf16[3,576,1024]{2,1,0:T(8,128)(2,1)S(1)}, bf16[3,576,1024]{2,1,0:T(8,128)(2,1)}, u32[]{:S(2)}, u32[]{:S(2)}) collective-permute-start(bf16[3,576,1024]{2,1,0:T(8,128)(2,1)S(1)} %copy-done.1), channel_id=1, source_target_pairs={{0,1},{1,0},{2,3},{3,2},{4,5},{5,4},{6,7},{7,6},{8,9},{9,8},{10,11... | collective-permute-start | bytes 10616840 | tf_op jit(solution)/shard_map/ppermute | solution.py:967
  242.5 25.5 %collective-permute-start.40 = (bf16[1152,1024]{1,0:T(8,128)(2,1)}, bf16[1152,1024]{1,0:T(8,128)(2,1)}, u32[]{:S(2)}, u32[]{:S(2)}) collective-permute-start(bf16[1152,1024]{1,0:T(8,128)(2,1)} %collective-permute-done.38.refs_12_.refs_0_), channel_id=1, source_target_pairs={{0,1},{1,0},{2,3},{3,2},{4,5},{5,4},{6,7},{7,6},{8,9},{9,8},{10,11... | collective-permute-start | bytes 7077896 | tf_op jit(solution)/shard_map/swap/ppermute | solution.py:967
  265.3 23.6 %collective-permute-start.48 = (bf16[512,1024]{1,0:T(8,128)(2,1)}, bf16[512,1024]{1,0:T(8,128)(2,1)}, u32[]{:S(2)}, u32[]{:S(2)}) collective-permute-start(bf16[512,1024]{1,0:T(8,128)(2,1)} %constant_dynamic-update-slice_fusion.32.refs_0_), channel_id=1, source_target_pairs={{0,1},{1,0},{2,3},{3,2},{4,5},{5,4},{6,7},{7,6},{8,9},{9,8},{10,11... | collective-permute-start | bytes 3145736 | tf_op jit(solution)/shard_map/ppermute | solution.py:967
  267.0 23.1 %collective-permute-start.49 = (bf16[512,1024]{1,0:T(8,128)(2,1)}, bf16[512,1024]{1,0:T(8,128)(2,1)}, u32[]{:S(2)}, u32[]{:S(2)}) collective-permute-start(bf16[512,1024]{1,0:T(8,128)(2,1)} %collective-permute-done.33.refs_2_), channel_id=1, source_target_pairs={{0,1},{1,0},{2,3},{3,2},{4,5},{5,4},{6,7},{7,6},{8,9},{9,8},{10,11... | collective-permute-start | bytes 3145736 | tf_op jit(solution)/shard_map/ppermute | solution.py:967
  268.0 22.5 %collective-permute-start.50 = (bf16[512,1024]{1,0:T(8,128)(2,1)}, bf16[512,1024]{1,0:T(8,128)(2,1)}, u32[]{:S(2)}, u32[]{:S(2)}) collective-permute-start(bf16[512,1024]{1,0:T(8,128)(2,1)} %collective-permute-done.36.refs_4_), channel_id=1, source_target_pairs={{0,1},{1,0},{2,3},{3,2},{4,5},{5,4},{6,7},{7,6},{8,9},{9,8},{10,11... | collective-permute-start | bytes 3145736 | tf_op jit(solution)/shard_map/ppermute | solution.py:967
  268.2 26.2 %collective-permute-start.51 = (bf16[512,1024]{1,0:T(8,128)(2,1)}, bf16[512,1024]{1,0:T(8,128)(2,1)}, u32[]{:S(2)}, u32[]{:S(2)}) collective-permute-start(bf16[512,1024]{1,0:T(8,128)(2,1)} %collective-permute-done.37.refs_6_), channel_id=1, source_target_pairs={{0,1},{1,0},{2,3},{3,2},{4,5},{5,4},{6,7},{7,6},{8,9},{9,8},{10,11... | collective-permute-start | bytes 3145736 | tf_op jit(solution)/shard_map/ppermute | solution.py:967
  288.9 27.6 %collective-permute-start.55 = (bf16[4,144,1024]{2,1,0:T(8,128)(2,1)}, bf16[4,144,1024]{2,1,0:T(8,128)(2,1)}, u32[]{:S(2)}, u32[]{:S(2)}) collective-permute-start(bf16[4,144,1024]{2,1,0:T(8,128)(2,1)} %get-tuple-element.199.lefts_ref.refs_0_.refs_4_.refs_8_), channel_id=1, source_target_pairs={{0,1},{1,0},{2,3},{3,2},{4,5},{5,4},{6,7},{7,6},{8,9},{9,8},{10,11... | collective-permute-start | bytes 3538952 | tf_op jit(solution)/shard_map/ppermute | solution.py:967
  290.1 19.5 %collective-permute-start.52 = (bf16[144,1024]{1,0:T(8,128)(2,1)S(1)}, bf16[144,1024]{1,0:T(8,128)(2,1)}, u32[]{:S(2)}, u32[]{:S(2)}) collective-permute-start(bf16[144,1024]{1,0:T(8,128)(2,1)S(1)} %slice_bitcast_fusion.8), channel_id=1, source_target_pairs={{0,2},{2,0},{4,6},{6,4},{8,10},{10,8},{12,14},{14,12},{16,18},{18,... | collective-permute-start | bytes 884744 | tf_op jit(solution)/shard_map/spread/ppermute | solution.py:957
  290.5 19.1 %collective-permute-start.53 = (bf16[144,1024]{1,0:T(8,128)(2,1)S(1)}, bf16[144,1024]{1,0:T(8,128)(2,1)}, u32[]{:S(2)}, u32[]{:S(2)}) collective-permute-start(bf16[144,1024]{1,0:T(8,128)(2,1)S(1)} %slice_bitcast_fusion.8), channel_id=1, source_target_pairs={{0,4},{2,6},{4,0},{6,2},{8,12},{10,14},{12,8},{14,10},{16,20},{18,... | collective-permute-start | bytes 884744 | tf_op jit(solution)/shard_map/spread/ppermute | solution.py:957
  291.0 18.6 %collective-permute-start.54 = (bf16[144,1024]{1,0:T(8,128)(2,1)S(1)}, bf16[144,1024]{1,0:T(8,128)(2,1)S(1)}, u32[]{:S(2)}, u32[]{:S(2)}) collective-permute-start(bf16[144,1024]{1,0:T(8,128)(2,1)S(1)} %slice_bitcast_fusion.8), channel_id=1, source_target_pairs={{0,6},{2,4},{4,2},{6,0},{8,14},{10,12},{12,10},{14,8},{16,22},{18,... | collective-permute-start | bytes 884744 | tf_op jit(solution)/shard_map/spread/ppermute | solution.py:957
  324.8 43.1 %collective-permute-start.58 = (bf16[4,64,2048]{2,1,0:T(8,128)(2,1)}, bf16[4,64,2048]{2,1,0:T(8,128)(2,1)S(1)}, u32[]{:S(2)}, u32[]{:S(2)}) collective-permute-start(bf16[4,64,2048]{2,1,0:T(8,128)(2,1)} %get-tuple-element.233), channel_id=1, source_target_pairs={{0,2},{2,0},{4,6},{6,4},{8,10},{10,8},{12,14},{14,12},{16,18},{18,... | collective-permute-start | bytes 3145736 | tf_op jit(solution)/shard_map/readout_across/ppermute | solution.py:957
  325.1 43.6 %collective-permute-start.59 = (bf16[4,64,2048]{2,1,0:T(8,128)(2,1)}, bf16[4,64,2048]{2,1,0:T(8,128)(2,1)S(1)}, u32[]{:S(2)}, u32[]{:S(2)}) collective-permute-start(bf16[4,64,2048]{2,1,0:T(8,128)(2,1)} %get-tuple-element.234), channel_id=1, source_target_pairs={{0,4},{2,6},{4,0},{6,2},{8,12},{10,14},{12,8},{14,10},{16,20},{18,... | collective-permute-start | bytes 3145736 | tf_op jit(solution)/shard_map/readout_across/ppermute | solution.py:957
  325.7 42.2 %collective-permute-start.60 = (bf16[144,1024]{1,0:T(8,128)(2,1)S(1)}, bf16[144,1024]{1,0:T(8,128)(2,1)S(1)}, u32[]{:S(2)}, u32[]{:S(2)}) collective-permute-start(bf16[144,1024]{1,0:T(8,128)(2,1)S(1)} %slice_bitcast_fusion.7), channel_id=1, source_target_pairs={{0,2},{2,0},{4,6},{6,4},{8,10},{10,8},{12,14},{14,12},{16,18},{18,... | collective-permute-start | bytes 884744 | tf_op jit(solution)/shard_map/spread/ppermute | solution.py:957
  327.4 40.5 %collective-permute-start.61 = (bf16[144,1024]{1,0:T(8,128)(2,1)S(1)}, bf16[144,1024]{1,0:T(8,128)(2,1)S(1)}, u32[]{:S(2)}, u32[]{:S(2)}) collective-permute-start(bf16[144,1024]{1,0:T(8,128)(2,1)S(1)} %slice_bitcast_fusion.7), channel_id=1, source_target_pairs={{0,4},{2,6},{4,0},{6,2},{8,12},{10,14},{12,8},{14,10},{16,20},{18,... | collective-permute-start | bytes 884744 | tf_op jit(solution)/shard_map/spread/ppermute | solution.py:957
  329.0 39.0 %collective-permute-start.62 = (bf16[144,1024]{1,0:T(8,128)(2,1)S(1)}, bf16[144,1024]{1,0:T(8,128)(2,1)S(1)}, u32[]{:S(2)}, u32[]{:S(2)}) collective-permute-start(bf16[144,1024]{1,0:T(8,128)(2,1)S(1)} %slice_bitcast_fusion.7), channel_id=1, source_target_pairs={{0,6},{2,4},{4,2},{6,0},{8,14},{10,12},{12,10},{14,8},{16,22},{18,... | collective-permute-start | bytes 884744 | tf_op jit(solution)/shard_map/spread/ppermute | solution.py:957
  371.2 33.2 %collective-permute-start.66 = (bf16[576,1024]{1,0:T(8,128)(2,1)S(1)}, bf16[576,1024]{1,0:T(8,128)(2,1)}, u32[]{:S(2)}, u32[]{:S(2)}) collective-permute-start(bf16[576,1024]{1,0:T(8,128)(2,1)S(1)} %constant_dynamic-update-slice_fusion.44.refs_2_), channel_id=1, source_target_pairs={{0,1},{1,0},{2,3},{3,2},{4,5},{5,4},{6,7},{7,6},{8,9},{9,8},{10,11... | collective-permute-start | bytes 3538952 | tf_op jit(solution)/shard_map/spread_swap/ppermute | solution.py:967
  374.8 29.6 %collective-permute-start.67 = (bf16[576,1024]{1,0:T(8,128)(2,1)S(1)}, bf16[576,1024]{1,0:T(8,128)(2,1)}, u32[]{:S(2)}, u32[]{:S(2)}) collective-permute-start(bf16[576,1024]{1,0:T(8,128)(2,1)S(1)} %constant_dynamic-update-slice_fusion.40.refs_0_), channel_id=1, source_target_pairs={{0,1},{1,0},{2,3},{3,2},{4,5},{5,4},{6,7},{7,6},{8,9},{9,8},{10,11... | collective-permute-start | bytes 3538952 | tf_op jit(solution)/shard_map/spread_swap/ppermute | solution.py:967
  375.2 29.2 %collective-permute-start.63 = (bf16[2,64,2048]{2,1,0:T(8,128)(2,1)}, bf16[2,64,2048]{2,1,0:T(8,128)(2,1)}, u32[]{:S(2)}, u32[]{:S(2)}) collective-permute-start(bf16[2,64,2048]{2,1,0:T(8,128)(2,1)} %add_convert_fusion.8), channel_id=1, source_target_pairs={{0,2},{2,0},{4,6},{6,4},{8,10},{10,8},{12,14},{14,12},{16,18},{18,... | collective-permute-start | bytes 1572872 | tf_op jit(solution)/shard_map/readout_onward/ppermute | solution.py:957
  376.9 27.5 %collective-permute-start.64 = (bf16[2,64,2048]{2,1,0:T(8,128)(2,1)S(1)}, bf16[2,64,2048]{2,1,0:T(8,128)(2,1)}, u32[]{:S(2)}, u32[]{:S(2)}) collective-permute-start(bf16[2,64,2048]{2,1,0:T(8,128)(2,1)S(1)} %add_convert_fusion.7), channel_id=1, source_target_pairs={{0,4},{2,6},{4,0},{6,2},{8,12},{10,14},{12,8},{14,10},{16,20},{18,... | collective-permute-start | bytes 1572872 | tf_op jit(solution)/shard_map/readout_onward/ppermute | solution.py:957
  407.9 53.0 %collective-permute-start.68 = (bf16[4,576,512]{2,1,0:T(8,128)(2,1)}, bf16[4,576,512]{2,1,0:T(8,128)(2,1)S(1)}, u32[]{:S(2)}, u32[]{:S(2)}) collective-permute-start(bf16[4,576,512]{2,1,0:T(8,128)(2,1)} %get-tuple-element.275), channel_id=1, source_target_pairs={{0,2},{2,0},{4,6},{6,4},{8,10},{10,8},{12,14},{14,12},{16,18},{18,... | collective-permute-start | bytes 7077896 | tf_op jit(solution)/shard_map/middle_0_across/ppermute | solution.py:957
  408.2 52.8 %collective-permute-start.69 = (bf16[4,576,512]{2,1,0:T(8,128)(2,1)}, bf16[4,576,512]{2,1,0:T(8,128)(2,1)}, u32[]{:S(2)}, u32[]{:S(2)}) collective-permute-start(bf16[4,576,512]{2,1,0:T(8,128)(2,1)} %get-tuple-element.276), channel_id=1, source_target_pairs={{0,4},{2,6},{4,0},{6,2},{8,12},{10,14},{12,8},{14,10},{16,20},{18,... | collective-permute-start | bytes 7077896 | tf_op jit(solution)/shard_map/middle_0_across/ppermute | solution.py:957
  411.3 152.8 %reduce-scatter.5.cloned.1.call-start = ((), (), s32[]{:S(2)}) async-start(), calls=%async_computation.3 | async-start | bytes 2949120 | tf_op jit(solution)/shard_map/middle_1_levels/reduce_scatter | solution.py:1461
  465.8 26.8 %collective-permute-start.73 = (bf16[2,576,512]{2,1,0:T(8,128)(2,1)}, bf16[2,576,512]{2,1,0:T(8,128)(2,1)S(1)}, u32[]{:S(2)}, u32[]{:S(2)}) collective-permute-start(bf16[2,576,512]{2,1,0:T(8,128)(2,1)} %add_convert_fusion.1), channel_id=1, source_target_pairs={{0,2},{2,0},{4,6},{6,4},{8,10},{10,8},{12,14},{14,12},{16,18},{18,... | collective-permute-start | bytes 3538952 | tf_op jit(solution)/shard_map/middle_0_onward/ppermute | solution.py:957
  466.8 26.2 %collective-permute-start.74 = (bf16[2,576,512]{2,1,0:T(8,128)(2,1)}, bf16[2,576,512]{2,1,0:T(8,128)(2,1)S(1)}, u32[]{:S(2)}, u32[]{:S(2)}) collective-permute-start(bf16[2,576,512]{2,1,0:T(8,128)(2,1)} %add_convert_fusion), channel_id=1, source_target_pairs={{0,4},{2,6},{4,0},{6,2},{8,12},{10,14},{12,8},{14,10},{16,20},{18,... | collective-permute-start | bytes 3538952 | tf_op jit(solution)/shard_map/middle_0_onward/ppermute | solution.py:957
  500.0 28.4 %collective-permute-start.75 = (bf16[4,320,512]{2,1,0:T(8,128)(2,1)}, bf16[4,320,512]{2,1,0:T(8,128)(2,1)}, u32[]{:S(2)}, u32[]{:S(2)}) collective-permute-start(bf16[4,320,512]{2,1,0:T(8,128)(2,1)} %get-tuple-element.296), channel_id=1, source_target_pairs={{0,2},{2,0},{4,6},{6,4},{8,10},{10,8},{12,14},{14,12},{16,18},{18,... | collective-permute-start | bytes 3932168 | tf_op jit(solution)/shard_map/last_across/ppermute | solution.py:957
  501.3 28.3 %collective-permute-start.76 = (bf16[4,320,512]{2,1,0:T(8,128)(2,1)}, bf16[4,320,512]{2,1,0:T(8,128)(2,1)}, u32[]{:S(2)}, u32[]{:S(2)}) collective-permute-start(bf16[4,320,512]{2,1,0:T(8,128)(2,1)} %get-tuple-element.297), channel_id=1, source_target_pairs={{0,4},{2,6},{4,0},{6,2},{8,12},{10,14},{12,8},{14,10},{16,20},{18,... | collective-permute-start | bytes 3932168 | tf_op jit(solution)/shard_map/last_across/ppermute | solution.py:957
  502.2 23.3 %collective-permute-start.82 = (bf16[576,512]{1,0:T(8,128)(2,1)}, bf16[576,512]{1,0:T(8,128)(2,1)}, u32[]{:S(2)}, u32[]{:S(2)}) collective-permute-start(bf16[576,512]{1,0:T(8,128)(2,1)} %fusion.8), channel_id=1, source_target_pairs={{0,8},{2,10},{4,12},{6,14},{8,24},{10,26},{12,28},{14,30},{24,16},... | collective-permute-start | bytes 1769480 | tf_op jit(solution)/shard_map/middle_0_line/ppermute | solution.py:964
  527.1 15.3 %collective-permute-start.83 = (bf16[576,512]{1,0:T(8,128)(2,1)S(1)}, bf16[576,512]{1,0:T(8,128)(2,1)S(1)}, u32[]{:S(2)}, u32[]{:S(2)}) collective-permute-start(bf16[576,512]{1,0:T(8,128)(2,1)S(1)} %add_convert_fusion.4), channel_id=1, source_target_pairs={{0,8},{2,10},{4,12},{6,14},{8,24},{10,26},{12,28},{14,30},{24,16},... | collective-permute-start | bytes 1769480 | tf_op jit(solution)/shard_map/middle_0_line/ppermute | solution.py:964
  530.9 13.5 %collective-permute-start.78 = (bf16[2,320,512]{2,1,0:T(8,128)(2,1)S(1)}, bf16[2,320,512]{2,1,0:T(8,128)(2,1)S(1)}, u32[]{:S(2)}, u32[]{:S(2)}) collective-permute-start(bf16[2,320,512]{2,1,0:T(8,128)(2,1)S(1)} %add_convert_fusion.3), channel_id=1, source_target_pairs={{0,4},{2,6},{4,0},{6,2},{8,12},{10,14},{12,8},{14,10},{16,20},{18,... | collective-permute-start | bytes 1966088 | tf_op jit(solution)/shard_map/last_onward/ppermute | solution.py:957
  533.3 13.6 %collective-permute-start.79 = (bf16[2,320,512]{2,1,0:T(8,128)(2,1)S(1)}, bf16[2,320,512]{2,1,0:T(8,128)(2,1)S(1)}, u32[]{:S(2)}, u32[]{:S(2)}) collective-permute-start(bf16[2,320,512]{2,1,0:T(8,128)(2,1)S(1)} %add_convert_fusion.2), channel_id=1, source_target_pairs={{0,2},{2,0},{4,6},{6,4},{8,10},{10,8},{12,14},{14,12},{16,18},{18,... | collective-permute-start | bytes 1966088 | tf_op jit(solution)/shard_map/last_onward/ppermute | solution.py:957
  542.6 17.2 %collective-permute-start.84 = (bf16[576,512]{1,0:T(8,128)(2,1)S(1)}, bf16[576,512]{1,0:T(8,128)(2,1)S(1)}, u32[]{:S(2)}, u32[]{:S(2)}) collective-permute-start(bf16[576,512]{1,0:T(8,128)(2,1)S(1)} %fusion.1), channel_id=1, source_target_pairs={{0,8},{2,10},{4,12},{6,14},{8,24},{10,26},{12,28},{14,30},{24,16},... | collective-permute-start | bytes 1769480 | tf_op jit(solution)/shard_map/middle_0_line/ppermute | solution.py:964
  549.8 14.2 %collective-permute-start.80 = (bf16[320,512]{1,0:T(8,128)(2,1)S(1)}, bf16[320,512]{1,0:T(8,128)(2,1)S(1)}, u32[]{:S(2)}, u32[]{:S(2)}) collective-permute-start(bf16[320,512]{1,0:T(8,128)(2,1)S(1)} %fusion.9), channel_id=1, source_target_pairs={{0,8},{2,10},{4,12},{6,14},{8,24},{10,26},{12,28},{14,30},{24,16},... | collective-permute-start | bytes 983048 | tf_op jit(solution)/shard_map/last_line/ppermute | solution.py:964
  (86 other events, 1100.7 us)
Sparse Core Ops, SparseCore 0:
  411.4 25.5 reduce-scatter.2
  468.0 55.8 reduce-scatter.4

commit v7 on v6

--- a/solution.py
+++ b/solution.py
@@ -232,7 +232,18 @@
         wi, wm, wo, taps, lefts, above, below, work, pairs, pre1, pre2, pre3, sems = refs
         traffic = Traffic(sems)
         first_copies = traffic.load(w_first, firsts, table_ref, wi)
-        middle_copies = traffic.load(w_middle, middles, table_ref, wm)
+        middle_copies = traffic.plan_in(w_middle, middles, table_ref, wm)
+        stages = [lax.div(first, 3 * C) for first in w_middle.firsts(table_ref)]
+
+        def of_stage(stage, act):
+            for copy, own in zip(middle_copies, stages):
+
+                @pl.when(own == stage)
+                def _(copy=copy):
+                    act(copy)
+
+        for stage in range(3):
+            of_stage(stage, lambda copy: copy.start())
         last_copies = traffic.load(w_last, lasts, table_ref, wo)
         wait(first_copies)
         traffic.send(wi.at[:, pl.ds(0, C)], wi_out)
@@ -287,15 +298,23 @@
         for ref in (above, below):
             ref[:PAD, :] = zeros
             ref[PAD + cells :, :] = zeros
-        wait(middle_copies)
-
-        def middle(cut):
-            above[PAD : PAD + cells, :] = dot(taps[...], wm[0 : 3 * C, cut])
-            below[PAD : PAD + cells, :] = dot(taps[...], wm[6 * C : 9 * C, cut])
-            same = dot(taps[...], wm[3 * C : 6 * C, cut])
-            pre2[:, cut] = same + above[PAD - side : PAD - side + cells, :] + below[PAD + side : PAD + side + cells, :]
-
-        tiles(C, TILE, middle)
+        for tap in range(3):
+            of_stage(tap, lambda copy: copy.wait())
+
+            def middle(cut, tap=tap):
+                total = dot(taps[...], wm[3 * C * tap : 3 * C * (tap + 1), cut])
+                if tap == 1:
+                    pre2[:, cut] += total
+                else:
+                    shift = -side if tap == 0 else side
+                    above[PAD : PAD + cells, :] = total
+                    moved = above[PAD + shift : PAD + shift + cells, :]
+                    if tap == 0:
+                        pre2[:, cut] = moved
+                    else:
+                        pre2[:, cut] += moved
+
+            tiles(C, TILE, middle)
         traffic.send(pre2, pre2_out)
 
         def keep_second(rows, value):
@@ -396,8 +415,9 @@
         core = table_ref[CORE]
         grad_stream[...] = jnp.zeros((cells, C), jnp.float32)
         given.wait()
-        wait(copies)
         for part in range(2):
+            middle = (len(copies) + 1) // 2
+            wait(copies[middle:] if part else copies[:middle])
 
             def step(cut, part=part):
                 here = pl.ds(pl.multiple_of(part * half + cut.start, cut_size), cut_size)

time: 605 us -> 591 us (0.977)
  Pallas kernels: 204 us -> 192 us
    pallas_call x14, Pallas kernels: 204 us -> 192 us  [call(): pl.pallas_call(kernel, name=name, out_shape=outs, in_specs=in_specs, out_...]
  transfers between devices with their start and end apart: 90 -> 90, of which waited for: 45 -> 46; matrix products, arithmetic and copies ran while one was open for 7% -> 7% of each run, Pallas kernels for 34% -> 32%
where the time goes in v7:
time: 591 us; the launch traced here: 585 us
  waiting for transfers between devices  253 us (43%)
  Pallas kernels  192 us (32%)
  starting transfers between devices  55.8 us (9%)
  local copies, waits for them, and re-layouts  45.5 us (8%)
  other arithmetic  23.3 us (4%)
  between operations  16.1 us (3%)
    pallas_call x14, Pallas kernels, call(): pl.pallas_call(kernel, name=name, out_shape=outs, in_specs=in_specs, out_...  192 us
    ppermute x21, waiting for transfers between devices, along(): return lax.ppermute(value, 'dp', pairs)  167 us
    ppermute x34, waiting for transfers between devices, flip(): return lax.ppermute(value, 'dp', [(i, i ^ bits) for i in range(self.dp)])  59.6 us
    ppermute x34, starting transfers between devices, flip(): return lax.ppermute(value, 'dp', [(i, i ^ bits) for i in range(self.dp)])  32.5 us
    ppermute x33, waiting for transfers between devices, swap(): return lax.ppermute(value, 'fsdp', [(0, 1), (1, 0)])  26.7 us
    unnamed x148, local copies, waits for them, and re-layouts  23.1 us
    ppermute x21, starting transfers between devices, along(): return lax.ppermute(value, 'dp', pairs)  17 us
    convert_element_type x11, other arithmetic, low(): return value.astype(jnp.bfloat16)  12 us
  transfers between devices with their start and end apart: 90, of which 46 were waited for; matrix products, arithmetic and copies ran while one was open for 7% of the time, Pallas kernels for 32%

profile of v7, /device:TPU:0, one launch (start us, length us, event | category | flops | bytes accessed | tf_op | source)
XLA Modules:
  0.0 585.4 jit_solution(17813487669938062051)
XLA Ops:
  11.6 3.1 collective-permute-start
  15.8 2.6 collective-permute-start.12
  21.5 1.9 collective-permute-start.3
  25.7 5.8 collective-permute-done.1
  35.2 2.8 collective-permute-done.2
  40.2 3.4 collective-permute-start.13
  44.2 4.5 collective-permute-done.13
  48.7 2.5 collective-permute-start.14
  51.3 5.1 collective-permute-done.14
  56.6 3.9 collective-permute-done.9.refs_5_.refs_31_
  62.7 9.1 %collective-permute-done.20 = bf16[208,1024]{1,0:T(8,128)(2,1)S(1)} collective-permute-done((bf16[208,1024]{1,0:T(8,128)(2,1)S(1)}, bf16[208,1024]{1,0:T(8,128)(2,1)S(1)}, u32[]{:S(2)}, u32[]{:S(2)}) %collective-permute-start.20) | collective-permute-done | bytes 426016 | tf_op jit(solution)/shard_map/three_line/ppermute | solution.py:984
  71.9 11.9 %collective-permute-done.21 = bf16[208,1024]{1,0:T(8,128)(2,1)S(1)} collective-permute-done((bf16[208,1024]{1,0:T(8,128)(2,1)S(1)}, bf16[208,1024]{1,0:T(8,128)(2,1)S(1)}, u32[]{:S(2)}, u32[]{:S(2)}) %collective-permute-start.21) | collective-permute-done | bytes 426016 | tf_op jit(solution)/shard_map/three_line/ppermute | solution.py:984
  84.0 8.8 %collective-permute-done.22 = bf16[208,1024]{1,0:T(8,128)(2,1)S(1)} collective-permute-done((bf16[208,1024]{1,0:T(8,128)(2,1)S(1)}, bf16[208,1024]{1,0:T(8,128)(2,1)S(1)}, u32[]{:S(2)}, u32[]{:S(2)}) %collective-permute-start.22) | collective-permute-done | bytes 426016 | tf_op jit(solution)/shard_map/three_line/ppermute | solution.py:984
  96.5 2.3 collective-permute-start.24
  98.9 16.0 %collective-permute-done.28 = bf16[288,1024]{1,0:T(8,128)(2,1)S(1)} collective-permute-done((bf16[288,1024]{1,0:T(8,128)(2,1)S(1)}, bf16[288,1024]{1,0:T(8,128)(2,1)S(1)}, u32[]{:S(2)}, u32[]{:S(2)}) %collective-permute-start.28) | collective-permute-done | bytes 589856 | tf_op jit(solution)/shard_map/four_line/ppermute | solution.py:984
  114.9 17.1 %collective-permute-done.29 = bf16[288,1024]{1,0:T(8,128)(2,1)S(1)} collective-permute-done((bf16[288,1024]{1,0:T(8,128)(2,1)S(1)}, bf16[288,1024]{1,0:T(8,128)(2,1)S(1)}, u32[]{:S(2)}, u32[]{:S(2)}) %collective-permute-start.29) | collective-permute-done | bytes 589856 | tf_op jit(solution)/shard_map/four_line/ppermute | solution.py:984
  135.0 11.2 %collective-permute-done.30 = bf16[288,1024]{1,0:T(8,128)(2,1)S(1)} collective-permute-done((bf16[288,1024]{1,0:T(8,128)(2,1)S(1)}, bf16[288,1024]{1,0:T(8,128)(2,1)S(1)}, u32[]{:S(2)}, u32[]{:S(2)}) %collective-permute-start.30) | collective-permute-done | bytes 589856 | tf_op jit(solution)/shard_map/four_line/ppermute | solution.py:984
  146.2 1.7 pad_maximum_fusion.refs_16_.refs_4_
  147.9 1.8 slice.224
  150.7 14.7 %collective-permute-done.33.refs_2_ = bf16[512,1024]{1,0:T(8,128)(2,1)} collective-permute-done((bf16[512,1024]{1,0:T(8,128)(2,1)}, bf16[512,1024]{1,0:T(8,128)(2,1)}, u32[]{:S(2)}, u32[]{:S(2)}) %collective-permute-start.33) | collective-permute-done | bytes 1048608 | tf_op jit(solution)/shard_map/top_line/ppermute | solution.py:984
  166.0 4.0 collective-permute-done.11.refs_6_.refs_32_
  172.4 2.4 collective-permute-done.35.refs_26_.refs_11_.refs_31_.refs_19_
  174.9 6.9 %collective-permute-done.27.refs_22_.refs_3_.refs_23_.refs_15_ = bf16[832,1024]{1,0:T(8,128)(2,1)S(1)} collective-permute-done((bf16[832,1024]{1,0:T(8,128)(2,1)S(1)}, bf16[832,1024]{1,0:T(8,128)(2,1)S(1)}, u32[]{:S(2)}, u32[]{:S(2)}) %collective-permute-start.27) | collective-permute-done | bytes 1703968 | tf_op jit(solution)/shard_map/swap/ppermute | solution.py:987
  184.8 31.8 %forward_block.2 = (f32[16,1024]{1,0:T(8,128)}, f32[144,1024]{1,0:T(8,128)}, f32[576,1024]{1,0:T(8,128)}, bf16[3,576,1024]{2,1,0:T(8,128)(2,1)}, f32[576,1024]{1...) custom-call(s32[165]{0:T(256)} %bitcast.127, ...), custom_call_target="tpu_custom_call" | custom-call | flops 265751104 | bytes 697303 | tf_op jit(solution)/shard_map/forward_block/pallas_call | solution.py:156
  217.0 9.3 %collective-permute-done.38.refs_12_.refs_0_ = bf16[1152,1024]{1,0:T(8,128)(2,1)} collective-permute-done((bf16[1152,1024]{1,0:T(8,128)(2,1)}, bf16[1152,1024]{1,0:T(8,128)(2,1)}, u32[]{:S(2)}, u32[]{:S(2)}) %collective-permute-start.38) | collective-permute-done | bytes 2359328 | tf_op jit(solution)/shard_map/four_plane/ppermute | solution.py:977
  226.3 2.4 collective-permute-done.39.refs_14_.refs_2_
  232.0 11.7 %collective-permute-done.37.refs_6_ = bf16[512,1024]{1,0:T(8,128)(2,1)} collective-permute-done((bf16[512,1024]{1,0:T(8,128)(2,1)}, bf16[512,1024]{1,0:T(8,128)(2,1)}, u32[]{:S(2)}, u32[]{:S(2)}) %collective-permute-start.37) | collective-permute-done | bytes 1048608 | tf_op jit(solution)/shard_map/top_line/ppermute | solution.py:984
  243.7 15.4 %collective-permute-done.43.refs_18_.refs_6_ = bf16[576,1024]{1,0:T(8,128)(2,1)S(1)} collective-permute-done((bf16[576,1024]{1,0:T(8,128)(2,1)S(1)}, bf16[576,1024]{1,0:T(8,128)(2,1)S(1)}, u32[]{:S(2)}, u32[]{:S(2)}) %collective-permute-start.43) | collective-permute-done | bytes 1179680 | tf_op jit(solution)/shard_map/four_plane/ppermute | solution.py:977
  260.6 4.7 collective-permute-done.44.refs_19_.refs_7_
  270.3 2.0 reshape.64.bias_ref
  272.3 14.9 %forward_block.3 = (bf16[4,144,1024]{2,1,0:T(8,128)(2,1)}, f32[144,1024]{1,0:T(8,128)}, f32[144,1024]{1,0:T(8,128)}, f32[144,1024]{1,0:T(8,128)}, bf16[1024,1024...) custom-call(s32[165]{0:T(256)} %bitcast.128, f32[144,1024]{1,0:T(8,128)} %get-tuple-element.189.refs_0_.u_in, ...), custom_call_target="tpu_custom_call" | custom-call | flops 66437776 | bytes 520355 | tf_op jit(solution)/shard_map/forward_block/pallas_call | solution.py:156
  289.4 2.7 collective-permute-start.54
  292.7 14.1 %readout.1 = (bf16[144,4096]{1,0:T(8,128)(2,1)}, f32[144,1024]{1,0:T(8,128)}, f32[1,4096]{1,0:T(1,128)}, bf16[144,2048]{1,0:T(8,128)(2,1)}, bf16[144,2048]{1,0:T(8,128)(2,1)}) custom-call(s32[165]{0:T(256)} %bitcast.129, s32[1]{0:T(128)S(6)} %copy.74.live_ref, bf16[4,144,1024]{2,1,0:T(8,128)(2,1)} %get-tuple-element.199.lefts_ref.refs_0_.refs_4_.refs_8_, ...), custom_call_target="tpu_custom_call" | custom-call | flops 603979776 | bytes 2686976 | tf_op jit(solution)/shard_map/readout/pallas_call | solution.py:156
  306.9 6.3 %back_last.2 = (f32[144,1024]{1,0:T(8,128)}, bf16[2,144,1024]{2,1,0:T(8,128)(2,1)}, bf16[2,144,512]{2,1,0:T(8,128)(2,1)}, f32[4,1024]{1,0:T(4,128)}) custom-call(s32[165]{0:T(256)} %bitcast.130, f32[144,1024]{1,0:T(8,128)} %get-tuple-element.206.grad_ref, f32[144,1024]{1,0:T(8,128)} %get-tuple-element.189.refs_0_.u_in, ...), custom_call_target="tpu_custom_call" | custom-call | flops 75497472 | bytes 1409024 | tf_op jit(solution)/shard_map/back_last/pallas_call | solution.py:156
  314.0 7.3 %weight_terms.3 = (bf16[4,64,2048]{2,1,0:T(8,128)(2,1)}, bf16[4,64,2048]{2,1,0:T(8,128)(2,1)}, bf16[2,64,2048]{2,1,0:T(8,128)(2,1)}, bf16[2,64,2048]{2,1,0:T(8,128)(2,1)}, bf16[4,64,2048]{2,1,0:T(8,128)(2,1)}) custom-call(s32[165]{0:T(256)} %bitcast.131, bf16[4,144,1024]{2,1,0:T(8,128)(2,1)} %get-tuple-element.199.lefts_ref.refs_0_.refs_4_.refs_8_, ...), custom_call_target="tpu_custom_call" | custom-call | flops 301989888 | bytes 1343488 | tf_op jit(solution)/shard_map/weight_terms/pallas_call | solution.py:156
  322.9 1.8 collective-permute-start.60
  326.4 15.1 %back_first.2 = (f32[144,1024]{1,0:T(8,128)}, f32[2,1024]{1,0:T(2,128)}, bf16[1,144,1024]{2,1,0:T(8,128)(2,1)}, bf16[144,512]{1,0:T(8,128)(2,1)}) custom-call(s32[165]{0:T(256)} %bitcast.132, bf16[2,144,1024]{2,1,0:T(8,128)(2,1)} %get-tuple-element.223.grads_in.refs_9_, f32[144,1024]{1,0:T(8,128)} %get-tuple-element.224.pre1_in, ...), custom_call_target="tpu_custom_call" | custom-call | flops 754974720 | bytes 6127616 | tf_op jit(solution)/shard_map/back_first/pallas_call | solution.py:156
  341.5 13.7 %back_last.3 = (f32[576,1024]{1,0:T(8,128)}, bf16[2,576,1024]{2,1,0:T(8,128)(2,1)}, bf16[2,576,512]{2,1,0:T(8,128)(2,1)}, f32[4,1024]{1,0:T(4,128)}) custom-call(s32[165]{0:T(256)} %bitcast.133, f32[144,1024]{1,0:T(8,128)} %get-tuple-element.227.grad_ref, f32[576,1024]{1,0:T(8,128)} %get-tuple-element.228.u_in, f32[576,1024]{1,0:T(8,128)} %get-tuple-element.229.pre3_in, ...), custom_call_target="tpu_custom_call" | custom-call | flops 301989888 | bytes 4063232 | tf_op jit(solution)/shard_map/back_last/pallas_call | solution.py:156
  355.3 5.1 collective-permute-done.62
  367.6 1.8 collective-permute-start.63
  371.0 24.9 %weight_terms.4 = (bf16[4,576,512]{2,1,0:T(8,128)(2,1)}, bf16[4,576,512]{2,1,0:T(8,128)(2,1)}, bf16[2,576,512]{2,1,0:T(8,128)(2,1)}, bf16[2,576,512]{2,1,0:T(8,128)(2,1)}, bf16[4,576,512]{2,1,0:T(8,128)(2,1)}) custom-call(s32[165]{0:T(256)} %bitcast.134, bf16[3,576,1024]{2,1,0:T(8,128)(2,1)} %get-tuple-element.198.refs_0_.refs_12_, ...), custom_call_target="tpu_custom_call" | custom-call | flops 2717908992 | bytes 3538944 | tf_op jit(solution)/shard_map/weight_terms/pallas_call | solution.py:156
  396.0 2.4 add_convert_fusion.6
  403.8 15.0 %plane_terms.1 = bf16[4,288,1024]{2,1,0:T(8,128)(2,1)} custom-call(s32[165]{0:T(256)} %bitcast.135, bf16[576,1024]{1,0:T(8,128)(2,1)} %copy-done.29, bf16[576,1024]{1,0:T(8,128)(2,1)} %collective-permute-done.67.refs_1_, bf16[576,1024]{1,0:T(8,128)(2,1)} %copy-done.28, bf16[576,1024]{1,0:T(8,128)(2,1)} %collective-permute-done.66.refs_3_), custom_call_target="tpu_custom_call" | custom-call | flops 905969664 | bytes 1769472 | tf_op jit(solution)/shard_map/plane_terms/pallas_call | solution.py:156
  418.8 28.0 %back_first.3 = (f32[576,1024]{1,0:T(8,128)}, f32[2,1024]{1,0:T(2,128)}, bf16[1,576,1024]{2,1,0:T(8,128)(2,1)}, bf16[576,512]{1,0:T(8,128)(2,1)}, bf16[1024,384]{1,0:T(8,128)(2,1)}, /*index=5*/bf16[1024,384]{1,0:T(8,128)(2,1)}) custom-call(s32[165]{0:T(256)} %bitcast.136, bf16[2,576,1024]{2,1,0:T(8,128)(2,1)} %get-tuple-element.268.refs_1_.grads_in, ...), custom_call_target="tpu_custom_call" | custom-call | flops 3019898880 | bytes 8781824 | tf_op jit(solution)/shard_map/back_first/pallas_call | solution.py:156
  446.8 5.6 collective-permute-done.68
  454.8 2.7 add_convert_fusion.1
  460.4 3.0 collective-permute-done.70.refs_7_
  464.4 13.7 %weight_terms.5 = (bf16[4,320,512]{2,1,0:T(8,128)(2,1)}, bf16[4,320,512]{2,1,0:T(8,128)(2,1)}, bf16[2,320,512]{2,1,0:T(8,128)(2,1)}, bf16[2,320,512]{2,1,0:T(8,128)(2,1)}, bf16[4,320,512]{2,1,0:T(8,128)(2,1)}) custom-call(s32[165]{0:T(256)} %bitcast.137, bf16[3,576,1024]{2,1,0:T(8,128)(2,1)} %get-tuple-element.198.refs_0_.refs_12_, ...), custom_call_target="tpu_custom_call" | custom-call | flops 754974720 | bytes 3997696 | tf_op jit(solution)/shard_map/weight_terms/pallas_call | solution.py:156
  478.1 6.4 %collective-permute-done.73 = bf16[2,576,512]{2,1,0:T(8,128)(2,1)S(1)} collective-permute-done((bf16[2,576,512]{2,1,0:T(8,128)(2,1)}, bf16[2,576,512]{2,1,0:T(8,128)(2,1)S(1)}, u32[]{:S(2)}, u32[]{:S(2)}) %collective-permute-start.73) | collective-permute-done | bytes 1179680 | tf_op jit(solution)/shard_map/middle_0_onward/ppermute | solution.py:977
  486.3 3.6 convert_add_fusion
  498.4 1.9 place_halves.2
  500.3 16.8 %collective-permute-done.82 = bf16[576,512]{1,0:T(8,128)(2,1)} collective-permute-done((bf16[576,512]{1,0:T(8,128)(2,1)}, bf16[576,512]{1,0:T(8,128)(2,1)}, u32[]{:S(2)}, u32[]{:S(2)}) %collective-permute-start.82) | collective-permute-done | bytes 589856 | tf_op jit(solution)/shard_map/middle_0_line/ppermute | solution.py:984
  518.8 2.5 collective-permute-done.75
  526.0 8.0 %collective-permute-done.83 = bf16[576,512]{1,0:T(8,128)(2,1)S(1)} collective-permute-done((bf16[576,512]{1,0:T(8,128)(2,1)S(1)}, bf16[576,512]{1,0:T(8,128)(2,1)S(1)}, u32[]{:S(2)}, u32[]{:S(2)}) %collective-permute-start.83) | collective-permute-done | bytes 589856 | tf_op jit(solution)/shard_map/middle_0_line/ppermute | solution.py:984
  534.3 2.2 collective-permute-done.78
  536.4 2.1 collective-permute-done.79
  538.5 2.8 convert_add_fusion.2
  541.4 1.9 collective-permute-start.80
  543.3 8.1 %collective-permute-done.84 = bf16[576,512]{1,0:T(8,128)(2,1)S(1)} collective-permute-done((bf16[576,512]{1,0:T(8,128)(2,1)S(1)}, bf16[576,512]{1,0:T(8,128)(2,1)S(1)}, u32[]{:S(2)}, u32[]{:S(2)}) %collective-permute-start.84) | collective-permute-done | bytes 589856 | tf_op jit(solution)/shard_map/middle_0_line/ppermute | solution.py:984
  552.5 3.0 collective-permute-done.80
  556.6 3.1 place_halves.3
  559.7 4.0 collective-permute-done.81
  563.9 8.0 %collective-permute-done.86 = bf16[320,512]{1,0:T(8,128)(2,1)S(1)} collective-permute-done((bf16[320,512]{1,0:T(8,128)(2,1)S(1)}, bf16[320,512]{1,0:T(8,128)(2,1)S(1)}, u32[]{:S(2)}, u32[]{:S(2)}) %collective-permute-start.86) | collective-permute-done | bytes 327712 | tf_op jit(solution)/shard_map/last_line/ppermute | solution.py:984
  575.1 1.9 place_last.1
  (344 shorter events, 94.6 us)
Async XLA Ops:
  7.2 487.2 %reduce-scatter.3.cloned.1.call-start = ((), (), s32[]{:S(2)}) async-start(), calls=%async_computation.2 | async-start | bytes 1310720 | tf_op jit(solution)/shard_map/readout_line/reduce_scatter | solution.py:1181
  11.6 9.8 %collective-permute-start = (bf16[96,1024]{1,0:T(8,128)(2,1)S(1)}, bf16[96,1024]{1,0:T(8,128)(2,1)S(1)}, u32[]{:S(2)}, u32[]{:S(2)}) collective-permute-start(bf16[96,1024]{1,0:T(8,128)(2,1)S(1)} %pad_maximum_fusion.5), channel_id=1, source_target_pairs={{0,8},{2,10},{4,12},{6,14},{8,24},{10,26},{12,28},{14,30},{24,16},... | collective-permute-start | bytes 589832 | tf_op jit(solution)/shard_map/one_line/ppermute | solution.py:984
  15.8 24.4 %collective-permute-start.12 = (bf16[144,1024]{1,0:T(8,128)(2,1)S(1)}, bf16[144,1024]{1,0:T(8,128)(2,1)S(1)}, u32[]{:S(2)}, u32[]{:S(2)}) collective-permute-start(bf16[144,1024]{1,0:T(8,128)(2,1)S(1)} %get-tuple-element.318), channel_id=1, source_target_pairs={{0,8},{2,10},{4,12},{6,14},{8,24},{10,26},{12,28},{14,30},{24,16},... | collective-permute-start | bytes 884744 | tf_op jit(solution)/shard_map/two_line/ppermute | solution.py:984
  21.5 10.8 %collective-permute-start.3 = (bf16[128,1024]{1,0:T(8,128)(2,1)S(1)}, bf16[128,1024]{1,0:T(8,128)(2,1)S(1)}, u32[]{:S(2)}, u32[]{:S(2)}) collective-permute-start(bf16[128,1024]{1,0:T(8,128)(2,1)S(1)} %pad_maximum_fusion.4), channel_id=1, source_target_pairs={{0,2},{2,0},{4,6},{6,4},{8,10},{10,8},{12,14},{14,12},{16,18},{18,... | collective-permute-start | bytes 786440 | tf_op jit(solution)/shard_map/top_plane/ppermute | solution.py:977
  23.3 10.3 %collective-permute-start.5 = (bf16[128,1024]{1,0:T(8,128)(2,1)S(1)}, bf16[128,1024]{1,0:T(8,128)(2,1)S(1)}, u32[]{:S(2)}, u32[]{:S(2)}) collective-permute-start(bf16[128,1024]{1,0:T(8,128)(2,1)S(1)} %pad_maximum_fusion.4), channel_id=1, source_target_pairs={{0,4},{2,6},{4,0},{6,2},{8,12},{10,14},{12,8},{14,10},{16,20},{18,... | collective-permute-start | bytes 786440 | tf_op jit(solution)/shard_map/top_plane/ppermute | solution.py:977
  38.7 17.8 %collective-permute-start.7 = (bf16[384,1024]{1,0:T(8,128)(2,1)S(1)}, bf16[384,1024]{1,0:T(8,128)(2,1)S(1)}, u32[]{:S(2)}, u32[]{:S(2)}) collective-permute-start(bf16[384,1024]{1,0:T(8,128)(2,1)S(1)} %constant_dynamic-update-slice_fusion.refs_1_.refs_27_), channel_id=1, source_target_pairs={{0,2},{2,0},{4,6},{6,4},{8,10},{10,8},{12,14},{14,12},{16,18},{18,... | collective-permute-start | bytes 2359304 | tf_op jit(solution)/shard_map/one_plane/ppermute | solution.py:977
  43.6 16.9 %collective-permute-start.9 = (bf16[384,1024]{1,0:T(8,128)(2,1)S(1)}, bf16[384,1024]{1,0:T(8,128)(2,1)S(1)}, u32[]{:S(2)}, u32[]{:S(2)}) collective-permute-start(bf16[384,1024]{1,0:T(8,128)(2,1)S(1)} %constant_dynamic-update-slice_fusion.refs_1_.refs_27_), channel_id=1, source_target_pairs={{0,4},{2,6},{4,0},{6,2},{8,12},{10,14},{12,8},{14,10},{16,20},{18,... | collective-permute-start | bytes 2359304 | tf_op jit(solution)/shard_map/one_plane/ppermute | solution.py:977
  60.5 32.8 %collective-permute-start.15 = (bf16[768,1024]{1,0:T(8,128)(2,1)S(1)}, bf16[768,1024]{1,0:T(8,128)(2,1)S(1)}, u32[]{:S(2)}, u32[]{:S(2)}) collective-permute-start(bf16[768,1024]{1,0:T(8,128)(2,1)S(1)} %slice_dynamic-update-slice_fusion.3), channel_id=1, source_target_pairs={{0,2},{2,0},{4,6},{6,4},{8,10},{10,8},{12,14},{14,12},{16,18},{18,... | collective-permute-start | bytes 4718600 | tf_op jit(solution)/shard_map/two_one_plane/ppermute | solution.py:977
  60.6 11.1 %collective-permute-start.20 = (bf16[208,1024]{1,0:T(8,128)(2,1)S(1)}, bf16[208,1024]{1,0:T(8,128)(2,1)S(1)}, u32[]{:S(2)}, u32[]{:S(2)}) collective-permute-start(bf16[208,1024]{1,0:T(8,128)(2,1)S(1)} %pad_maximum_fusion.3), channel_id=1, source_target_pairs={{0,8},{2,10},{4,12},{6,14},{8,24},{10,26},{12,28},{14,30},{24,16},... | collective-permute-start | bytes 1277960 | tf_op jit(solution)/shard_map/three_line/ppermute | solution.py:984
  61.4 33.6 %collective-permute-start.16 = (bf16[768,1024]{1,0:T(8,128)(2,1)S(1)}, bf16[768,1024]{1,0:T(8,128)(2,1)S(1)}, u32[]{:S(2)}, u32[]{:S(2)}) collective-permute-start(bf16[768,1024]{1,0:T(8,128)(2,1)S(1)} %slice_dynamic-update-slice_fusion.2), channel_id=1, source_target_pairs={{0,4},{2,6},{4,0},{6,2},{8,12},{10,14},{12,8},{14,10},{16,20},{18,... | collective-permute-start | bytes 4718600 | tf_op jit(solution)/shard_map/two_one_plane/ppermute | solution.py:977
  71.7 12.1 %collective-permute-start.21 = (bf16[208,1024]{1,0:T(8,128)(2,1)S(1)}, bf16[208,1024]{1,0:T(8,128)(2,1)S(1)}, u32[]{:S(2)}, u32[]{:S(2)}) collective-permute-start(bf16[208,1024]{1,0:T(8,128)(2,1)S(1)} %collective-permute-done.20), channel_id=1, source_target_pairs={{0,8},{2,10},{4,12},{6,14},{8,24},{10,26},{12,28},{14,30},{24,16},... | collective-permute-start | bytes 1277960 | tf_op jit(solution)/shard_map/three_line/ppermute | solution.py:984
  95.0 52.8 %collective-permute-start.23 = (bf16[1120,1024]{1,0:T(8,128)(2,1)S(1)}, bf16[1120,1024]{1,0:T(8,128)(2,1)S(1)}, u32[]{:S(2)}, u32[]{:S(2)}) collective-permute-start(bf16[1120,1024]{1,0:T(8,128)(2,1)S(1)} %slice_dynamic-update-slice_fusion.1), channel_id=1, source_target_pairs={{0,2},{2,0},{4,6},{6,4},{8,10},{10,8},{12,14},{14,12},{16,18},{18,... | collective-permute-start | bytes 6881288 | tf_op jit(solution)/shard_map/three_two_plane/ppermute | solution.py:977
  96.5 51.4 %collective-permute-start.24 = (bf16[1120,1024]{1,0:T(8,128)(2,1)S(1)}, bf16[1120,1024]{1,0:T(8,128)(2,1)}, u32[]{:S(2)}, u32[]{:S(2)}) collective-permute-start(bf16[1120,1024]{1,0:T(8,128)(2,1)S(1)} %slice_dynamic-update-slice_fusion), channel_id=1, source_target_pairs={{0,4},{2,6},{4,0},{6,2},{8,12},{10,14},{12,8},{14,10},{16,20},{18,... | collective-permute-start | bytes 6881288 | tf_op jit(solution)/shard_map/three_two_plane/ppermute | solution.py:977
  98.8 16.0 %collective-permute-start.28 = (bf16[288,1024]{1,0:T(8,128)(2,1)S(1)}, bf16[288,1024]{1,0:T(8,128)(2,1)S(1)}, u32[]{:S(2)}, u32[]{:S(2)}) collective-permute-start(bf16[288,1024]{1,0:T(8,128)(2,1)S(1)} %slice_bitcast_fusion.6), channel_id=1, source_target_pairs={{0,8},{2,10},{4,12},{6,14},{8,24},{10,26},{12,28},{14,30},{24,16},... | collective-permute-start | bytes 1769480 | tf_op jit(solution)/shard_map/four_line/ppermute | solution.py:984
  114.9 17.1 %collective-permute-start.29 = (bf16[288,1024]{1,0:T(8,128)(2,1)S(1)}, bf16[288,1024]{1,0:T(8,128)(2,1)S(1)}, u32[]{:S(2)}, u32[]{:S(2)}) collective-permute-start(bf16[288,1024]{1,0:T(8,128)(2,1)S(1)} %collective-permute-done.28), channel_id=1, source_target_pairs={{0,8},{2,10},{4,12},{6,14},{8,24},{10,26},{12,28},{14,30},{24,16},... | collective-permute-start | bytes 1769480 | tf_op jit(solution)/shard_map/four_line/ppermute | solution.py:984
  132.0 14.2 %collective-permute-start.30 = (bf16[288,1024]{1,0:T(8,128)(2,1)S(1)}, bf16[288,1024]{1,0:T(8,128)(2,1)S(1)}, u32[]{:S(2)}, u32[]{:S(2)}) collective-permute-start(bf16[288,1024]{1,0:T(8,128)(2,1)S(1)} %collective-permute-done.29), channel_id=1, source_target_pairs={{0,8},{2,10},{4,12},{6,14},{8,24},{10,26},{12,28},{14,30},{24,16},... | collective-permute-start | bytes 1769480 | tf_op jit(solution)/shard_map/four_line/ppermute | solution.py:984
  134.7 15.3 %collective-permute-start.10 = (bf16[384,1024]{1,0:T(8,128)(2,1)S(1)}, bf16[384,1024]{1,0:T(8,128)(2,1)S(1)}, u32[]{:S(2)}, u32[]{:S(2)}) collective-permute-start(bf16[384,1024]{1,0:T(8,128)(2,1)S(1)} %collective-permute-done.7.refs_3_.refs_29_), channel_id=1, source_target_pairs={{0,1},{1,0},{2,3},{3,2},{4,5},{5,4},{6,7},{7,6},{8,9},{9,8},{10,11... | collective-permute-start | bytes 2359304 | tf_op jit(solution)/shard_map/swap/ppermute | solution.py:987
  134.7 30.6 %collective-permute-start.33 = (bf16[512,1024]{1,0:T(8,128)(2,1)}, bf16[512,1024]{1,0:T(8,128)(2,1)}, u32[]{:S(2)}, u32[]{:S(2)}) collective-permute-start(bf16[512,1024]{1,0:T(8,128)(2,1)} %constant_dynamic-update-slice_fusion.32.refs_0_), channel_id=1, source_target_pairs={{0,8},{2,10},{4,12},{6,14},{8,24},{10,26},{12,28},{14,30},{24,16},... | collective-permute-start | bytes 3145736 | tf_op jit(solution)/shard_map/top_line/ppermute | solution.py:984
  149.8 15.6 %collective-permute-start.31 = (bf16[416,1024]{1,0:T(8,128)(2,1)S(1)}, bf16[416,1024]{1,0:T(8,128)(2,1)S(1)}, u32[]{:S(2)}, u32[]{:S(2)}) collective-permute-start(bf16[416,1024]{1,0:T(8,128)(2,1)S(1)} %slice.224), channel_id=1, source_target_pairs={{0,2},{2,0},{4,6},{6,4},{8,10},{10,8},{12,14},{14,12},{16,18},{18,... | collective-permute-start | bytes 2555912 | tf_op jit(solution)/shard_map/three_plane/ppermute | solution.py:977
  149.8 16.1 %collective-permute-start.32 = (bf16[416,1024]{1,0:T(8,128)(2,1)S(1)}, bf16[416,1024]{1,0:T(8,128)(2,1)S(1)}, u32[]{:S(2)}, u32[]{:S(2)}) collective-permute-start(bf16[416,1024]{1,0:T(8,128)(2,1)S(1)} %slice.225), channel_id=1, source_target_pairs={{0,4},{2,6},{4,0},{6,2},{8,12},{10,14},{12,8},{14,10},{16,20},{18,... | collective-permute-start | bytes 2555912 | tf_op jit(solution)/shard_map/three_plane/ppermute | solution.py:977
  149.9 21.2 %collective-permute-start.17 = (bf16[768,1024]{1,0:T(8,128)(2,1)S(1)}, bf16[768,1024]{1,0:T(8,128)(2,1)S(1)}, u32[]{:S(2)}, u32[]{:S(2)}) collective-permute-start(bf16[768,1024]{1,0:T(8,128)(2,1)S(1)} %collective-permute-done.15.refs_7_.refs_13_.refs_33_.refs_6_), channel_id=1, source_target_pairs={{0,1},{1,0},{2,3},{3,2},{4,5},{5,4},{6,7},{7,6},{8,9},{9,8},{10,11... | collective-permute-start | bytes 4718600 | tf_op jit(solution)/shard_map/swap/ppermute | solution.py:987
  150.0 21.3 %collective-permute-start.18 = (bf16[768,1024]{1,0:T(8,128)(2,1)S(1)}, bf16[768,1024]{1,0:T(8,128)(2,1)S(1)}, u32[]{:S(2)}, u32[]{:S(2)}) collective-permute-start(bf16[768,1024]{1,0:T(8,128)(2,1)S(1)} %collective-permute-done.16.refs_9_.refs_15_.refs_35_.refs_8_), channel_id=1, source_target_pairs={{0,1},{1,0},{2,3},{3,2},{4,5},{5,4},{6,7},{7,6},{8,9},{9,8},{10,11... | collective-permute-start | bytes 4718600 | tf_op jit(solution)/shard_map/swap/ppermute | solution.py:987
  170.7 11.1 %collective-permute-start.27 = (bf16[832,1024]{1,0:T(8,128)(2,1)S(1)}, bf16[832,1024]{1,0:T(8,128)(2,1)S(1)}, u32[]{:S(2)}, u32[]{:S(2)}) collective-permute-start(bf16[832,1024]{1,0:T(8,128)(2,1)S(1)} %get-tuple-element.178.refs_21_.refs_2_.refs_22_.refs_14_), channel_id=1, source_target_pairs={{0,1},{1,0},{2,3},{3,2},{4,5},{5,4},{6,7},{7,6},{8,9},{9,8},{10,11... | collective-permute-start | bytes 5111816 | tf_op jit(solution)/shard_map/swap/ppermute | solution.py:987
  171.1 13.7 %collective-permute-start.25 = (bf16[1120,1024]{1,0:T(8,128)(2,1)S(1)}, bf16[1120,1024]{1,0:T(8,128)(2,1)}, u32[]{:S(2)}, u32[]{:S(2)}) collective-permute-start(bf16[1120,1024]{1,0:T(8,128)(2,1)S(1)} %collective-permute-done.23.refs_17_.refs_4_.refs_24_.refs_10_), channel_id=1, source_target_pairs={{0,1},{1,0},{2,3},{3,2},{4,5},{5,4},{6,7},{7,6},{8,9},{9,8},{10,11... | collective-permute-start | bytes 6881288 | tf_op jit(solution)/shard_map/swap/ppermute | solution.py:987
  171.3 13.5 %collective-permute-start.26 = (bf16[1120,1024]{1,0:T(8,128)(2,1)}, bf16[1120,1024]{1,0:T(8,128)(2,1)}, u32[]{:S(2)}, u32[]{:S(2)}) collective-permute-start(bf16[1120,1024]{1,0:T(8,128)(2,1)} %collective-permute-done.24.refs_19_.refs_6_.refs_26_.refs_12_), channel_id=1, source_target_pairs={{0,1},{1,0},{2,3},{3,2},{4,5},{5,4},{6,7},{7,6},{8,9},{9,8},{10,11... | collective-permute-start | bytes 6881288 | tf_op jit(solution)/shard_map/swap/ppermute | solution.py:987
  172.4 53.8 %collective-permute-start.38 = (bf16[1152,1024]{1,0:T(8,128)(2,1)}, bf16[1152,1024]{1,0:T(8,128)(2,1)}, u32[]{:S(2)}, u32[]{:S(2)}) collective-permute-start(bf16[1152,1024]{1,0:T(8,128)(2,1)} %pad_maximum_fusion.refs_16_.refs_4_), channel_id=1, source_target_pairs={{0,2},{2,0},{4,6},{6,4},{8,10},{10,8},{12,14},{14,12},{16,18},{18,... | collective-permute-start | bytes 7077896 | tf_op jit(solution)/shard_map/four_plane/ppermute | solution.py:977
  174.9 53.8 %collective-permute-start.39 = (bf16[1152,1024]{1,0:T(8,128)(2,1)}, bf16[1152,1024]{1,0:T(8,128)(2,1)}, u32[]{:S(2)}, u32[]{:S(2)}) collective-permute-start(bf16[1152,1024]{1,0:T(8,128)(2,1)} %pad_maximum_fusion.refs_16_.refs_4_), channel_id=1, source_target_pairs={{0,4},{2,6},{4,0},{6,2},{8,12},{10,14},{12,8},{14,10},{16,20},{18,... | collective-permute-start | bytes 7077896 | tf_op jit(solution)/shard_map/four_plane/ppermute | solution.py:977
  183.0 34.0 %collective-permute-start.36 = (bf16[512,1024]{1,0:T(8,128)(2,1)}, bf16[512,1024]{1,0:T(8,128)(2,1)}, u32[]{:S(2)}, u32[]{:S(2)}) collective-permute-start(bf16[512,1024]{1,0:T(8,128)(2,1)} %collective-permute-done.33.refs_2_), channel_id=1, source_target_pairs={{0,8},{2,10},{4,12},{6,14},{8,24},{10,26},{12,28},{14,30},{24,16},... | collective-permute-start | bytes 3145736 | tf_op jit(solution)/shard_map/top_line/ppermute | solution.py:984
  216.6 43.5 %collective-permute-start.42 = (bf16[1152,1024]{1,0:T(8,128)(2,1)}, bf16[1152,1024]{1,0:T(8,128)(2,1)}, u32[]{:S(2)}, u32[]{:S(2)}) collective-permute-start(bf16[1152,1024]{1,0:T(8,128)(2,1)} %pad_maximum_fusion.refs_16_.refs_4_), channel_id=1, source_target_pairs={{0,1},{1,0},{2,3},{3,2},{4,5},{5,4},{6,7},{7,6},{8,9},{9,8},{10,11... | collective-permute-start | bytes 7077896 | tf_op jit(solution)/shard_map/swap/ppermute | solution.py:987
  217.0 26.7 %collective-permute-start.37 = (bf16[512,1024]{1,0:T(8,128)(2,1)}, bf16[512,1024]{1,0:T(8,128)(2,1)}, u32[]{:S(2)}, u32[]{:S(2)}) collective-permute-start(bf16[512,1024]{1,0:T(8,128)(2,1)} %collective-permute-done.36.refs_4_), channel_id=1, source_target_pairs={{0,8},{2,10},{4,12},{6,14},{8,24},{10,26},{12,28},{14,30},{24,16},... | collective-permute-start | bytes 3145736 | tf_op jit(solution)/shard_map/top_line/ppermute | solution.py:984
  231.6 27.5 %collective-permute-start.43 = (bf16[576,1024]{1,0:T(8,128)(2,1)S(1)}, bf16[576,1024]{1,0:T(8,128)(2,1)S(1)}, u32[]{:S(2)}, u32[]{:S(2)}) collective-permute-start(bf16[576,1024]{1,0:T(8,128)(2,1)S(1)} %slice.186), channel_id=1, source_target_pairs={{0,2},{2,0},{4,6},{6,4},{8,10},{10,8},{12,14},{14,12},{16,18},{18,... | collective-permute-start | bytes 3538952 | tf_op jit(solution)/shard_map/four_plane/ppermute | solution.py:977
  231.6 27.5 %collective-permute-start.45 = (bf16[576,1024]{1,0:T(8,128)(2,1)S(1)}, bf16[576,1024]{1,0:T(8,128)(2,1)S(1)}, u32[]{:S(2)}, u32[]{:S(2)}) collective-permute-start(bf16[576,1024]{1,0:T(8,128)(2,1)S(1)} %slice.187), channel_id=1, source_target_pairs={{0,4},{2,6},{4,0},{6,2},{8,12},{10,14},{12,8},{14,10},{16,20},{18,... | collective-permute-start | bytes 3538952 | tf_op jit(solution)/shard_map/four_plane/ppermute | solution.py:977
  232.0 57.4 %collective-permute-start.47 = (bf16[3,576,1024]{2,1,0:T(8,128)(2,1)S(1)}, bf16[3,576,1024]{2,1,0:T(8,128)(2,1)}, u32[]{:S(2)}, u32[]{:S(2)}) collective-permute-start(bf16[3,576,1024]{2,1,0:T(8,128)(2,1)S(1)} %copy-done.1), channel_id=1, source_target_pairs={{0,1},{1,0},{2,3},{3,2},{4,5},{5,4},{6,7},{7,6},{8,9},{9,8},{10,11... | collective-permute-start | bytes 10616840 | tf_op jit(solution)/shard_map/ppermute | solution.py:987
  243.7 24.3 %collective-permute-start.40 = (bf16[1152,1024]{1,0:T(8,128)(2,1)}, bf16[1152,1024]{1,0:T(8,128)(2,1)}, u32[]{:S(2)}, u32[]{:S(2)}) collective-permute-start(bf16[1152,1024]{1,0:T(8,128)(2,1)} %collective-permute-done.38.refs_12_.refs_0_), channel_id=1, source_target_pairs={{0,1},{1,0},{2,3},{3,2},{4,5},{5,4},{6,7},{7,6},{8,9},{9,8},{10,11... | collective-permute-start | bytes 7077896 | tf_op jit(solution)/shard_map/swap/ppermute | solution.py:987
  265.3 21.9 %collective-permute-start.48 = (bf16[512,1024]{1,0:T(8,128)(2,1)}, bf16[512,1024]{1,0:T(8,128)(2,1)}, u32[]{:S(2)}, u32[]{:S(2)}) collective-permute-start(bf16[512,1024]{1,0:T(8,128)(2,1)} %constant_dynamic-update-slice_fusion.32.refs_0_), channel_id=1, source_target_pairs={{0,1},{1,0},{2,3},{3,2},{4,5},{5,4},{6,7},{7,6},{8,9},{9,8},{10,11... | collective-permute-start | bytes 3145736 | tf_op jit(solution)/shard_map/ppermute | solution.py:987
  267.0 21.5 %collective-permute-start.49 = (bf16[512,1024]{1,0:T(8,128)(2,1)}, bf16[512,1024]{1,0:T(8,128)(2,1)}, u32[]{:S(2)}, u32[]{:S(2)}) collective-permute-start(bf16[512,1024]{1,0:T(8,128)(2,1)} %collective-permute-done.33.refs_2_), channel_id=1, source_target_pairs={{0,1},{1,0},{2,3},{3,2},{4,5},{5,4},{6,7},{7,6},{8,9},{9,8},{10,11... | collective-permute-start | bytes 3145736 | tf_op jit(solution)/shard_map/ppermute | solution.py:987
  268.0 20.8 %collective-permute-start.50 = (bf16[512,1024]{1,0:T(8,128)(2,1)}, bf16[512,1024]{1,0:T(8,128)(2,1)}, u32[]{:S(2)}, u32[]{:S(2)}) collective-permute-start(bf16[512,1024]{1,0:T(8,128)(2,1)} %collective-permute-done.36.refs_4_), channel_id=1, source_target_pairs={{0,1},{1,0},{2,3},{3,2},{4,5},{5,4},{6,7},{7,6},{8,9},{9,8},{10,11... | collective-permute-start | bytes 3145736 | tf_op jit(solution)/shard_map/ppermute | solution.py:987
  268.2 24.5 %collective-permute-start.51 = (bf16[512,1024]{1,0:T(8,128)(2,1)}, bf16[512,1024]{1,0:T(8,128)(2,1)}, u32[]{:S(2)}, u32[]{:S(2)}) collective-permute-start(bf16[512,1024]{1,0:T(8,128)(2,1)} %collective-permute-done.37.refs_6_), channel_id=1, source_target_pairs={{0,1},{1,0},{2,3},{3,2},{4,5},{5,4},{6,7},{7,6},{8,9},{9,8},{10,11... | collective-permute-start | bytes 3145736 | tf_op jit(solution)/shard_map/ppermute | solution.py:987
  287.2 26.5 %collective-permute-start.55 = (bf16[4,144,1024]{2,1,0:T(8,128)(2,1)}, bf16[4,144,1024]{2,1,0:T(8,128)(2,1)}, u32[]{:S(2)}, u32[]{:S(2)}) collective-permute-start(bf16[4,144,1024]{2,1,0:T(8,128)(2,1)} %get-tuple-element.199.lefts_ref.refs_0_.refs_4_.refs_8_), channel_id=1, source_target_pairs={{0,1},{1,0},{2,3},{3,2},{4,5},{5,4},{6,7},{7,6},{8,9},{9,8},{10,11... | collective-permute-start | bytes 3538952 | tf_op jit(solution)/shard_map/ppermute | solution.py:987
  288.4 18.3 %collective-permute-start.52 = (bf16[144,1024]{1,0:T(8,128)(2,1)S(1)}, bf16[144,1024]{1,0:T(8,128)(2,1)}, u32[]{:S(2)}, u32[]{:S(2)}) collective-permute-start(bf16[144,1024]{1,0:T(8,128)(2,1)S(1)} %slice_bitcast_fusion.8), channel_id=1, source_target_pairs={{0,2},{2,0},{4,6},{6,4},{8,10},{10,8},{12,14},{14,12},{16,18},{18,... | collective-permute-start | bytes 884744 | tf_op jit(solution)/shard_map/spread/ppermute | solution.py:977
  288.8 18.0 %collective-permute-start.53 = (bf16[144,1024]{1,0:T(8,128)(2,1)S(1)}, bf16[144,1024]{1,0:T(8,128)(2,1)}, u32[]{:S(2)}, u32[]{:S(2)}) collective-permute-start(bf16[144,1024]{1,0:T(8,128)(2,1)S(1)} %slice_bitcast_fusion.8), channel_id=1, source_target_pairs={{0,4},{2,6},{4,0},{6,2},{8,12},{10,14},{12,8},{14,10},{16,20},{18,... | collective-permute-start | bytes 884744 | tf_op jit(solution)/shard_map/spread/ppermute | solution.py:977
  289.4 17.4 %collective-permute-start.54 = (bf16[144,1024]{1,0:T(8,128)(2,1)S(1)}, bf16[144,1024]{1,0:T(8,128)(2,1)S(1)}, u32[]{:S(2)}, u32[]{:S(2)}) collective-permute-start(bf16[144,1024]{1,0:T(8,128)(2,1)S(1)} %slice_bitcast_fusion.8), channel_id=1, source_target_pairs={{0,6},{2,4},{4,2},{6,0},{8,14},{10,12},{12,10},{14,8},{16,22},{18,... | collective-permute-start | bytes 884744 | tf_op jit(solution)/shard_map/spread/ppermute | solution.py:977
  322.0 38.4 %collective-permute-start.58 = (bf16[4,64,2048]{2,1,0:T(8,128)(2,1)}, bf16[4,64,2048]{2,1,0:T(8,128)(2,1)S(1)}, u32[]{:S(2)}, u32[]{:S(2)}) collective-permute-start(bf16[4,64,2048]{2,1,0:T(8,128)(2,1)} %get-tuple-element.233), channel_id=1, source_target_pairs={{0,2},{2,0},{4,6},{6,4},{8,10},{10,8},{12,14},{14,12},{16,18},{18,... | collective-permute-start | bytes 3145736 | tf_op jit(solution)/shard_map/readout_across/ppermute | solution.py:977
  322.3 38.8 %collective-permute-start.59 = (bf16[4,64,2048]{2,1,0:T(8,128)(2,1)}, bf16[4,64,2048]{2,1,0:T(8,128)(2,1)S(1)}, u32[]{:S(2)}, u32[]{:S(2)}) collective-permute-start(bf16[4,64,2048]{2,1,0:T(8,128)(2,1)} %get-tuple-element.234), channel_id=1, source_target_pairs={{0,4},{2,6},{4,0},{6,2},{8,12},{10,14},{12,8},{14,10},{16,20},{18,... | collective-permute-start | bytes 3145736 | tf_op jit(solution)/shard_map/readout_across/ppermute | solution.py:977
  322.9 32.4 %collective-permute-start.60 = (bf16[144,1024]{1,0:T(8,128)(2,1)S(1)}, bf16[144,1024]{1,0:T(8,128)(2,1)S(1)}, u32[]{:S(2)}, u32[]{:S(2)}) collective-permute-start(bf16[144,1024]{1,0:T(8,128)(2,1)S(1)} %slice_bitcast_fusion.7), channel_id=1, source_target_pairs={{0,2},{2,0},{4,6},{6,4},{8,10},{10,8},{12,14},{14,12},{16,18},{18,... | collective-permute-start | bytes 884744 | tf_op jit(solution)/shard_map/spread/ppermute | solution.py:977
  324.7 30.6 %collective-permute-start.61 = (bf16[144,1024]{1,0:T(8,128)(2,1)S(1)}, bf16[144,1024]{1,0:T(8,128)(2,1)S(1)}, u32[]{:S(2)}, u32[]{:S(2)}) collective-permute-start(bf16[144,1024]{1,0:T(8,128)(2,1)S(1)} %slice_bitcast_fusion.7), channel_id=1, source_target_pairs={{0,4},{2,6},{4,0},{6,2},{8,12},{10,14},{12,8},{14,10},{16,20},{18,... | collective-permute-start | bytes 884744 | tf_op jit(solution)/shard_map/spread/ppermute | solution.py:977
  326.2 34.3 %collective-permute-start.62 = (bf16[144,1024]{1,0:T(8,128)(2,1)S(1)}, bf16[144,1024]{1,0:T(8,128)(2,1)S(1)}, u32[]{:S(2)}, u32[]{:S(2)}) collective-permute-start(bf16[144,1024]{1,0:T(8,128)(2,1)S(1)} %slice_bitcast_fusion.7), channel_id=1, source_target_pairs={{0,6},{2,4},{4,2},{6,0},{8,14},{10,12},{12,10},{14,8},{16,22},{18,... | collective-permute-start | bytes 884744 | tf_op jit(solution)/shard_map/spread/ppermute | solution.py:977
  363.6 32.3 %collective-permute-start.66 = (bf16[576,1024]{1,0:T(8,128)(2,1)S(1)}, bf16[576,1024]{1,0:T(8,128)(2,1)}, u32[]{:S(2)}, u32[]{:S(2)}) collective-permute-start(bf16[576,1024]{1,0:T(8,128)(2,1)S(1)} %constant_dynamic-update-slice_fusion.44.refs_2_), channel_id=1, source_target_pairs={{0,1},{1,0},{2,3},{3,2},{4,5},{5,4},{6,7},{7,6},{8,9},{9,8},{10,11... | collective-permute-start | bytes 3538952 | tf_op jit(solution)/shard_map/spread_swap/ppermute | solution.py:987
  367.2 28.7 %collective-permute-start.67 = (bf16[576,1024]{1,0:T(8,128)(2,1)S(1)}, bf16[576,1024]{1,0:T(8,128)(2,1)}, u32[]{:S(2)}, u32[]{:S(2)}) collective-permute-start(bf16[576,1024]{1,0:T(8,128)(2,1)S(1)} %constant_dynamic-update-slice_fusion.40.refs_0_), channel_id=1, source_target_pairs={{0,1},{1,0},{2,3},{3,2},{4,5},{5,4},{6,7},{7,6},{8,9},{9,8},{10,11... | collective-permute-start | bytes 3538952 | tf_op jit(solution)/shard_map/spread_swap/ppermute | solution.py:987
  367.6 28.3 %collective-permute-start.63 = (bf16[2,64,2048]{2,1,0:T(8,128)(2,1)}, bf16[2,64,2048]{2,1,0:T(8,128)(2,1)}, u32[]{:S(2)}, u32[]{:S(2)}) collective-permute-start(bf16[2,64,2048]{2,1,0:T(8,128)(2,1)} %add_convert_fusion.8), channel_id=1, source_target_pairs={{0,2},{2,0},{4,6},{6,4},{8,10},{10,8},{12,14},{14,12},{16,18},{18,... | collective-permute-start | bytes 1572872 | tf_op jit(solution)/shard_map/readout_onward/ppermute | solution.py:977
  369.4 26.5 %collective-permute-start.64 = (bf16[2,64,2048]{2,1,0:T(8,128)(2,1)S(1)}, bf16[2,64,2048]{2,1,0:T(8,128)(2,1)}, u32[]{:S(2)}, u32[]{:S(2)}) collective-permute-start(bf16[2,64,2048]{2,1,0:T(8,128)(2,1)S(1)} %add_convert_fusion.7), channel_id=1, source_target_pairs={{0,4},{2,6},{4,0},{6,2},{8,12},{10,14},{12,8},{14,10},{16,20},{18,... | collective-permute-start | bytes 1572872 | tf_op jit(solution)/shard_map/readout_onward/ppermute | solution.py:977
  399.4 53.0 %collective-permute-start.68 = (bf16[4,576,512]{2,1,0:T(8,128)(2,1)}, bf16[4,576,512]{2,1,0:T(8,128)(2,1)S(1)}, u32[]{:S(2)}, u32[]{:S(2)}) collective-permute-start(bf16[4,576,512]{2,1,0:T(8,128)(2,1)} %get-tuple-element.275), channel_id=1, source_target_pairs={{0,2},{2,0},{4,6},{6,4},{8,10},{10,8},{12,14},{14,12},{16,18},{18,... | collective-permute-start | bytes 7077896 | tf_op jit(solution)/shard_map/middle_0_across/ppermute | solution.py:977
  400.5 52.8 %collective-permute-start.69 = (bf16[4,576,512]{2,1,0:T(8,128)(2,1)}, bf16[4,576,512]{2,1,0:T(8,128)(2,1)}, u32[]{:S(2)}, u32[]{:S(2)}) collective-permute-start(bf16[4,576,512]{2,1,0:T(8,128)(2,1)} %get-tuple-element.276), channel_id=1, source_target_pairs={{0,4},{2,6},{4,0},{6,2},{8,12},{10,14},{12,8},{14,10},{16,20},{18,... | collective-permute-start | bytes 7077896 | tf_op jit(solution)/shard_map/middle_0_across/ppermute | solution.py:977
  403.7 152.0 %reduce-scatter.5.cloned.1.call-start = ((), (), s32[]{:S(2)}) async-start(), calls=%async_computation.3 | async-start | bytes 2949120 | tf_op jit(solution)/shard_map/middle_1_levels/reduce_scatter | solution.py:1481
  457.4 27.1 %collective-permute-start.73 = (bf16[2,576,512]{2,1,0:T(8,128)(2,1)}, bf16[2,576,512]{2,1,0:T(8,128)(2,1)S(1)}, u32[]{:S(2)}, u32[]{:S(2)}) collective-permute-start(bf16[2,576,512]{2,1,0:T(8,128)(2,1)} %add_convert_fusion.1), channel_id=1, source_target_pairs={{0,2},{2,0},{4,6},{6,4},{8,10},{10,8},{12,14},{14,12},{16,18},{18,... | collective-permute-start | bytes 3538952 | tf_op jit(solution)/shard_map/middle_0_onward/ppermute | solution.py:977
  458.4 26.9 %collective-permute-start.74 = (bf16[2,576,512]{2,1,0:T(8,128)(2,1)}, bf16[2,576,512]{2,1,0:T(8,128)(2,1)S(1)}, u32[]{:S(2)}, u32[]{:S(2)}) collective-permute-start(bf16[2,576,512]{2,1,0:T(8,128)(2,1)} %add_convert_fusion), channel_id=1, source_target_pairs={{0,4},{2,6},{4,0},{6,2},{8,12},{10,14},{12,8},{14,10},{16,20},{18,... | collective-permute-start | bytes 3538952 | tf_op jit(solution)/shard_map/middle_0_onward/ppermute | solution.py:977
  492.3 29.0 %collective-permute-start.75 = (bf16[4,320,512]{2,1,0:T(8,128)(2,1)}, bf16[4,320,512]{2,1,0:T(8,128)(2,1)}, u32[]{:S(2)}, u32[]{:S(2)}) collective-permute-start(bf16[4,320,512]{2,1,0:T(8,128)(2,1)} %get-tuple-element.296), channel_id=1, source_target_pairs={{0,2},{2,0},{4,6},{6,4},{8,10},{10,8},{12,14},{14,12},{16,18},{18,... | collective-permute-start | bytes 3932168 | tf_op jit(solution)/shard_map/last_across/ppermute | solution.py:977
  493.2 28.6 %collective-permute-start.76 = (bf16[4,320,512]{2,1,0:T(8,128)(2,1)}, bf16[4,320,512]{2,1,0:T(8,128)(2,1)}, u32[]{:S(2)}, u32[]{:S(2)}) collective-permute-start(bf16[4,320,512]{2,1,0:T(8,128)(2,1)} %get-tuple-element.297), channel_id=1, source_target_pairs={{0,4},{2,6},{4,0},{6,2},{8,12},{10,14},{12,8},{14,10},{16,20},{18,... | collective-permute-start | bytes 3932168 | tf_op jit(solution)/shard_map/last_across/ppermute | solution.py:977
  494.4 22.7 %collective-permute-start.82 = (bf16[576,512]{1,0:T(8,128)(2,1)}, bf16[576,512]{1,0:T(8,128)(2,1)}, u32[]{:S(2)}, u32[]{:S(2)}) collective-permute-start(bf16[576,512]{1,0:T(8,128)(2,1)} %fusion.8), channel_id=1, source_target_pairs={{0,8},{2,10},{4,12},{6,14},{8,24},{10,26},{12,28},{14,30},{24,16},... | collective-permute-start | bytes 1769480 | tf_op jit(solution)/shard_map/middle_0_line/ppermute | solution.py:984
  518.7 15.3 %collective-permute-start.83 = (bf16[576,512]{1,0:T(8,128)(2,1)S(1)}, bf16[576,512]{1,0:T(8,128)(2,1)S(1)}, u32[]{:S(2)}, u32[]{:S(2)}) collective-permute-start(bf16[576,512]{1,0:T(8,128)(2,1)S(1)} %add_convert_fusion.4), channel_id=1, source_target_pairs={{0,8},{2,10},{4,12},{6,14},{8,24},{10,26},{12,28},{14,30},{24,16},... | collective-permute-start | bytes 1769480 | tf_op jit(solution)/shard_map/middle_0_line/ppermute | solution.py:984
  523.1 13.3 %collective-permute-start.78 = (bf16[2,320,512]{2,1,0:T(8,128)(2,1)S(1)}, bf16[2,320,512]{2,1,0:T(8,128)(2,1)S(1)}, u32[]{:S(2)}, u32[]{:S(2)}) collective-permute-start(bf16[2,320,512]{2,1,0:T(8,128)(2,1)S(1)} %add_convert_fusion.3), channel_id=1, source_target_pairs={{0,4},{2,6},{4,0},{6,2},{8,12},{10,14},{12,8},{14,10},{16,20},{18,... | collective-permute-start | bytes 1966088 | tf_op jit(solution)/shard_map/last_onward/ppermute | solution.py:977
  525.3 13.2 %collective-permute-start.79 = (bf16[2,320,512]{2,1,0:T(8,128)(2,1)S(1)}, bf16[2,320,512]{2,1,0:T(8,128)(2,1)S(1)}, u32[]{:S(2)}, u32[]{:S(2)}) collective-permute-start(bf16[2,320,512]{2,1,0:T(8,128)(2,1)S(1)} %add_convert_fusion.2), channel_id=1, source_target_pairs={{0,2},{2,0},{4,6},{6,4},{8,10},{10,8},{12,14},{14,12},{16,18},{18,... | collective-permute-start | bytes 1966088 | tf_op jit(solution)/shard_map/last_onward/ppermute | solution.py:977
  534.2 17.2 %collective-permute-start.84 = (bf16[576,512]{1,0:T(8,128)(2,1)S(1)}, bf16[576,512]{1,0:T(8,128)(2,1)S(1)}, u32[]{:S(2)}, u32[]{:S(2)}) collective-permute-start(bf16[576,512]{1,0:T(8,128)(2,1)S(1)} %fusion.1), channel_id=1, source_target_pairs={{0,8},{2,10},{4,12},{6,14},{8,24},{10,26},{12,28},{14,30},{24,16},... | collective-permute-start | bytes 1769480 | tf_op jit(solution)/shard_map/middle_0_line/ppermute | solution.py:984
  541.4 14.2 %collective-permute-start.80 = (bf16[320,512]{1,0:T(8,128)(2,1)S(1)}, bf16[320,512]{1,0:T(8,128)(2,1)S(1)}, u32[]{:S(2)}, u32[]{:S(2)}) collective-permute-start(bf16[320,512]{1,0:T(8,128)(2,1)S(1)} %fusion.9), channel_id=1, source_target_pairs={{0,8},{2,10},{4,12},{6,14},{8,24},{10,26},{12,28},{14,30},{24,16},... | collective-permute-start | bytes 983048 | tf_op jit(solution)/shard_map/last_line/ppermute | solution.py:984
  (86 other events, 1105.9 us)
Sparse Core Ops, SparseCore 0:
  403.8 24.7 reduce-scatter.2
  460.5 54.4 reduce-scatter.4
